TPU v7x, 128 devices: a whole 4x4x4 slice. The times are simulated.
128 devices in a mesh: hst: 4 (over x), row: 32 (over z, y, core).
Axes of the slice: x: 4, y: 4, z: 4, core: 2. Of those that a mesh axis runs over, the one named last changes fastest.
Arguments:
- tables: bfloat16 [16, 32768, 160], P('hst', 'row'), may hold values from -1.75 to 1.75
- indices: int32 [16384, 16, 8], P(None, 'hst'), may hold values from 0 to 32767
- lengths: int32 [16384, 16], P(None, 'hst'), may hold values from 1 to 8
- feature_order: int32 [16], replicated, may hold values from 0 to 15, each once
- proj_weight: bfloat16 [24, 16], replicated, may hold values from -1.5 to 1.5
- fm_gain: float32 [384], replicated, may hold values from 0.25 to 1.75
- up_weight: bfloat16 [384, 1024], replicated, may hold values from -0.3125 to 0.3125
- down_weight: bfloat16 [1024, 1280], replicated, may hold values from -0.1875 to 0.1875
- compress_weight: bfloat16 [8, 16], replicated, may hold values from -1.5 to 1.5
- out_gain: float32 [16, 160], replicated, may hold values from 0.25 to 1.75
Outputs:
- wukong_out: bfloat16 [16384, 16, 160], P(('hst', 'row'))
Inputs may be any that keep to these rules, and one draw needn't show every extreme that they name: `feature_order`: each of 0 to 15 once.
All inputs are finite; a program needn't handle non-finite values.
Results may differ from a plain program's by a relative error of at most 0.017.
Values may be sent and summed in bfloat16 or wider, within the bound.
No kernel may reach another device: no remote copies, remote signals or barrier semaphores. Data moves between devices by JAX's collectives and lax.ppermute only.
A program may use at most 192 MiB of HBM per device.

v0:
```python
import math

import jax
import jax.numpy as jnp
from jax import lax
from jax.sharding import PartitionSpec as P


def layer_norm(values, gain):
    center = values - jnp.mean(values, axis=-1, keepdims=True)
    spread = jnp.mean(center * center, axis=-1, keepdims=True)
    return center / jnp.sqrt(spread + 1e-05) * gain


def pool_block(table_shard, index_block, length_block, row_base):
    row_count = table_shard.shape[1]
    slot_count = index_block.shape[2]
    slot_ids = jnp.arange(slot_count, dtype=jnp.int32)
    usable = slot_ids[None, None, :] < length_block[:, :, None]
    local_index = jnp.where(usable, index_block - row_base, -1)
    row_ids = jnp.arange(row_count, dtype=jnp.int32)
    counts = jnp.sum((local_index[..., None] == row_ids).astype(jnp.float32), axis=2).astype(
        jnp.bfloat16
    )
    return jnp.einsum("bjr,jre->bje", counts, table_shard, preferred_element_type=jnp.float32)


def pool_rows(table_shard, index_rows, length_rows, row_base):
    total_rows, tables_here, slot_count = index_rows.shape
    block_size = math.gcd(total_rows, 1024)
    blocks = total_rows // block_size
    pooled = lax.map(
        lambda pair: pool_block(table_shard, pair[0], pair[1], row_base),
        (
            index_rows.reshape(blocks, block_size, tables_here, slot_count),
            length_rows.reshape(blocks, block_size, tables_here),
        ),
    )
    return pooled.reshape(total_rows, tables_here, table_shard.shape[2])


def on_device(
    tables,
    indices,
    lengths,
    feature_order,
    proj_weight,
    fm_gain,
    up_weight,
    down_weight,
    compress_weight,
    out_gain,
):
    hosts = lax.axis_size("hst")
    row_devs = lax.axis_size("row")
    row_base = lax.axis_index("row") * tables.shape[1]
    total_rows, tables_here, slot_count = indices.shape
    per_device = total_rows // (hosts * row_devs)
    index_order = indices.reshape(hosts, row_devs, per_device, tables_here, slot_count)
    index_order = jnp.transpose(index_order, (1, 0, 2, 3, 4)).reshape(
        total_rows, tables_here, slot_count
    )
    length_order = lengths.reshape(hosts, row_devs, per_device, tables_here)
    length_order = jnp.transpose(length_order, (1, 0, 2, 3)).reshape(total_rows, tables_here)
    summed_rows = lax.psum_scatter(
        pool_rows(tables, index_order, length_order, row_base).astype(jnp.bfloat16),
        "row",
        scatter_dimension=0,
        tiled=True,
    )
    gathered = lax.all_to_all(summed_rows, "hst", split_axis=0, concat_axis=1, tiled=True)
    features = gathered.shape[1]
    emb_dim = gathered.shape[2]
    placing = (feature_order[:, None] == jnp.arange(features, dtype=jnp.int32)[None, :]).astype(
        jnp.bfloat16
    )
    embedded = jnp.einsum(
        "bje,jk->bke", gathered, placing, preferred_element_type=jnp.float32
    ).astype(jnp.bfloat16)
    batch_rows = embedded.shape[0]
    projected = jnp.einsum(
        "kf,bfe->bke", proj_weight, embedded, preferred_element_type=jnp.float32
    ).astype(jnp.bfloat16)
    interaction = jnp.einsum(
        "bfe,bke->bfk", embedded, projected, preferred_element_type=jnp.float32
    )
    normed = layer_norm(interaction.reshape(batch_rows, -1), fm_gain).astype(jnp.bfloat16)
    hidden = jnp.maximum(
        jnp.dot(normed, up_weight, preferred_element_type=jnp.float32), 0.0
    ).astype(jnp.bfloat16)
    fm_block = jnp.dot(hidden, down_weight, preferred_element_type=jnp.float32).reshape(
        batch_rows, compress_weight.shape[0], emb_dim
    )
    compressed = jnp.einsum(
        "mf,bfe->bme", compress_weight, embedded, preferred_element_type=jnp.float32
    )
    summed = jnp.concatenate([fm_block, compressed], axis=1) + embedded.astype(jnp.float32)
    result = layer_norm(
        summed.reshape(batch_rows, features * emb_dim), out_gain.reshape(features * emb_dim)
    )
    return result.reshape(batch_rows, features, emb_dim).astype(jnp.bfloat16)


def solution(mesh):
    in_specs = (
        P("hst", "row", None),
        P(None, "hst", None),
        P(None, "hst"),
        P(),
        P(),
        P(),
        P(),
        P(),
        P(),
        P(),
    )
    out_specs = P(("hst", "row"), None, None)
    return jax.shard_map(
        on_device, mesh=mesh, in_specs=in_specs, out_specs=out_specs, check_vma=False
    )
```

profile of v0, /device:TPU:0, one launch (start us, length us, event | category | flops | bytes accessed | tf_op | source)
XLA Modules:
  0.0 1173.0 jit_solution(15259720392138914090)
XLA Ops:
  6.5 23.8 %copy.65 = s32[4,32,128,4,8]{4,3,2,0,1:T(4,128)} copy(s32[4,32,128,4,8]{2,4,1,0,3:T(8,128)} %bitcast.78) | data formatting | bytes 4194304 | tf_op jit(solution)/shard_map/transpose | solution.py:60
  35.3 936.0 %while.10 = (s32[]{:T(128)}, bf16[16,1024,4,160]{1,3,2,0:T(8,128)(2,1)}, s32[16,1024,4]{2,1,0:T(8,128)}, s32[16,1024,4,8]{3,2,1,0:T(4,128)}, s32[]{:T(128)}, /*index=5*/bf16[4,1024,160]{1,2,0:T(8,128)(2,1)}, s32[]{:T(128)}) while((s32[]{:T(128)}, bf16[16,1024,4,160]{1,3,2,0:T(8,128)(2,1)}, s32[16,1024,4]{2,1,0:T(8,128)}, ...), condition=%wide.region_2.3_spmd, body=%wide.region_0.2_spmd.sunk | while | flops 1438744576 | bytes 26395252 | solution.py:32
  41.2 46.2 %convert_reduce_fusion.2 = bf16[1024,4,1024]{2,1,0:T(4,128)(2,1)S(1)} fusion(s32[1024,4,8]{2,1,0:T(4,128)S(1)} %bitcast_select_fusion.2), kind=kLoop, calls=%fused_computation.clone.1 | loop fusion | flops 96468992 | bytes 8519680 | tf_op jit(solution)/shard_map/while/body/eval_jaxpr/reduce_sum | solution.py:22
  99.7 46.2 %convert_reduce_fusion.2 = bf16[1024,4,1024]{2,1,0:T(4,128)(2,1)S(1)} fusion(s32[1024,4,8]{2,1,0:T(4,128)S(1)} %bitcast_select_fusion.2), kind=kLoop, calls=%fused_computation.clone.1 | loop fusion | flops 96468992 | bytes 8519680 | tf_op jit(solution)/shard_map/while/body/eval_jaxpr/reduce_sum | solution.py:22
  158.2 46.2 %convert_reduce_fusion.2 = bf16[1024,4,1024]{2,1,0:T(4,128)(2,1)S(1)} fusion(s32[1024,4,8]{2,1,0:T(4,128)S(1)} %bitcast_select_fusion.2), kind=kLoop, calls=%fused_computation.clone.1 | loop fusion | flops 96468992 | bytes 8519680 | tf_op jit(solution)/shard_map/while/body/eval_jaxpr/reduce_sum | solution.py:22
  216.7 46.2 %convert_reduce_fusion.2 = bf16[1024,4,1024]{2,1,0:T(4,128)(2,1)S(1)} fusion(s32[1024,4,8]{2,1,0:T(4,128)S(1)} %bitcast_select_fusion.2), kind=kLoop, calls=%fused_computation.clone.1 | loop fusion | flops 96468992 | bytes 8519680 | tf_op jit(solution)/shard_map/while/body/eval_jaxpr/reduce_sum | solution.py:22
  275.2 46.2 %convert_reduce_fusion.2 = bf16[1024,4,1024]{2,1,0:T(4,128)(2,1)S(1)} fusion(s32[1024,4,8]{2,1,0:T(4,128)S(1)} %bitcast_select_fusion.2), kind=kLoop, calls=%fused_computation.clone.1 | loop fusion | flops 96468992 | bytes 8519680 | tf_op jit(solution)/shard_map/while/body/eval_jaxpr/reduce_sum | solution.py:22
  333.6 46.2 %convert_reduce_fusion.2 = bf16[1024,4,1024]{2,1,0:T(4,128)(2,1)S(1)} fusion(s32[1024,4,8]{2,1,0:T(4,128)S(1)} %bitcast_select_fusion.2), kind=kLoop, calls=%fused_computation.clone.1 | loop fusion | flops 96468992 | bytes 8519680 | tf_op jit(solution)/shard_map/while/body/eval_jaxpr/reduce_sum | solution.py:22
  392.1 46.2 %convert_reduce_fusion.2 = bf16[1024,4,1024]{2,1,0:T(4,128)(2,1)S(1)} fusion(s32[1024,4,8]{2,1,0:T(4,128)S(1)} %bitcast_select_fusion.2), kind=kLoop, calls=%fused_computation.clone.1 | loop fusion | flops 96468992 | bytes 8519680 | tf_op jit(solution)/shard_map/while/body/eval_jaxpr/reduce_sum | solution.py:22
  438.3 6.5 bitcast_dynamic-update-slice_fusion.2
  450.7 46.2 %convert_reduce_fusion.2 = bf16[1024,4,1024]{2,1,0:T(4,128)(2,1)S(1)} fusion(s32[1024,4,8]{2,1,0:T(4,128)S(1)} %bitcast_select_fusion.2), kind=kLoop, calls=%fused_computation.clone.1 | loop fusion | flops 96468992 | bytes 8519680 | tf_op jit(solution)/shard_map/while/body/eval_jaxpr/reduce_sum | solution.py:22
  496.9 6.5 bitcast_dynamic-update-slice_fusion.2
  509.2 46.2 %convert_reduce_fusion.2 = bf16[1024,4,1024]{2,1,0:T(4,128)(2,1)S(1)} fusion(s32[1024,4,8]{2,1,0:T(4,128)S(1)} %bitcast_select_fusion.2), kind=kLoop, calls=%fused_computation.clone.1 | loop fusion | flops 96468992 | bytes 8519680 | tf_op jit(solution)/shard_map/while/body/eval_jaxpr/reduce_sum | solution.py:22
  567.7 46.2 %convert_reduce_fusion.2 = bf16[1024,4,1024]{2,1,0:T(4,128)(2,1)S(1)} fusion(s32[1024,4,8]{2,1,0:T(4,128)S(1)} %bitcast_select_fusion.2), kind=kLoop, calls=%fused_computation.clone.1 | loop fusion | flops 96468992 | bytes 8519680 | tf_op jit(solution)/shard_map/while/body/eval_jaxpr/reduce_sum | solution.py:22
  626.2 46.2 %convert_reduce_fusion.2 = bf16[1024,4,1024]{2,1,0:T(4,128)(2,1)S(1)} fusion(s32[1024,4,8]{2,1,0:T(4,128)S(1)} %bitcast_select_fusion.2), kind=kLoop, calls=%fused_computation.clone.1 | loop fusion | flops 96468992 | bytes 8519680 | tf_op jit(solution)/shard_map/while/body/eval_jaxpr/reduce_sum | solution.py:22
  684.7 46.2 %convert_reduce_fusion.2 = bf16[1024,4,1024]{2,1,0:T(4,128)(2,1)S(1)} fusion(s32[1024,4,8]{2,1,0:T(4,128)S(1)} %bitcast_select_fusion.2), kind=kLoop, calls=%fused_computation.clone.1 | loop fusion | flops 96468992 | bytes 8519680 | tf_op jit(solution)/shard_map/while/body/eval_jaxpr/reduce_sum | solution.py:22
  743.2 46.2 %convert_reduce_fusion.2 = bf16[1024,4,1024]{2,1,0:T(4,128)(2,1)S(1)} fusion(s32[1024,4,8]{2,1,0:T(4,128)S(1)} %bitcast_select_fusion.2), kind=kLoop, calls=%fused_computation.clone.1 | loop fusion | flops 96468992 | bytes 8519680 | tf_op jit(solution)/shard_map/while/body/eval_jaxpr/reduce_sum | solution.py:22
  801.7 46.2 %convert_reduce_fusion.2 = bf16[1024,4,1024]{2,1,0:T(4,128)(2,1)S(1)} fusion(s32[1024,4,8]{2,1,0:T(4,128)S(1)} %bitcast_select_fusion.2), kind=kLoop, calls=%fused_computation.clone.1 | loop fusion | flops 96468992 | bytes 8519680 | tf_op jit(solution)/shard_map/while/body/eval_jaxpr/reduce_sum | solution.py:22
  860.2 46.2 %convert_reduce_fusion.2 = bf16[1024,4,1024]{2,1,0:T(4,128)(2,1)S(1)} fusion(s32[1024,4,8]{2,1,0:T(4,128)S(1)} %bitcast_select_fusion.2), kind=kLoop, calls=%fused_computation.clone.1 | loop fusion | flops 96468992 | bytes 8519680 | tf_op jit(solution)/shard_map/while/body/eval_jaxpr/reduce_sum | solution.py:22
  918.7 46.2 %convert_reduce_fusion.2 = bf16[1024,4,1024]{2,1,0:T(4,128)(2,1)S(1)} fusion(s32[1024,4,8]{2,1,0:T(4,128)S(1)} %bitcast_select_fusion.2), kind=kLoop, calls=%fused_computation.clone.1 | loop fusion | flops 96468992 | bytes 8519680 | tf_op jit(solution)/shard_map/while/body/eval_jaxpr/reduce_sum | solution.py:22
  964.9 6.4 bitcast_dynamic-update-slice_fusion.2
  971.3 17.5 %copy.66 = bf16[16,4,20,8,1024]{4,3,0,2,1:T(8,128)(2,1)} copy(bf16[16,4,20,8,1024]{4,3,2,1,0:T(8,128)(2,1)} %bitcast.74) | data formatting | bytes 41943040 | tf_op jit(solution)/shard_map/convert_element_type | solution.py:66
  988.9 130.9 %reduce-scatter.2.cloned.1.call-done = bf16[512,4,160]{0,2,1:T(8,128)(2,1)} async-done(((bf16[16384,4,160]{0,2,1:T(8,128)(2,1)}), bf16[512,4,160]{0,2,1:T(8,128)(2,1)}) %reduce-scatter.2.cloned.1.call-update) | async-done | bytes 655376 | tf_op jit(solution)/shard_map/reduce_scatter | solution.py:65
  1126.6 14.6 %all-to-all-done = bf16[512,4,160]{2,1,0:T(4,128)(2,1)} async-done(((bf16[512,4,160]{2,1,0:T(4,128)(2,1)}), bf16[512,4,160]{2,1,0:T(4,128)(2,1)}, u32[]{:S(2)}, u32[]{:S(2)}) %all-to-all-start) | async-done | bytes 655392 | tf_op jit(solution)/shard_map/all_to_all | solution.py:71
  (116 shorter events, 213.8 us)
Async XLA Ops:
  6.5 1152.5 %copy-start = (bf16[1024,1280]{1,0:T(8,128)(2,1)S(1)}, bf16[1024,1280]{1,0:T(8,128)(2,1)}, u32[]{:S(2)}) copy-start(bf16[1024,1280]{1,0:T(8,128)(2,1)} %param.19) | copy-start | bytes 7864324
  6.5 1113.3 %reduce-scatter.2.cloned.1.call-start = ((), (), s32[]{:S(2)}) async-start(), calls=%async_computation.2 | async-start | bytes 21626880 | tf_op jit(solution)/shard_map/reduce_scatter | solution.py:65
  6.5 23.8 %copy-start.1 = (s32[16384,4]{0,1:T(4,128)S(1)}, s32[16384,4]{0,1:T(4,128)}, u32[]{:S(2)}) copy-start(s32[16384,4]{0,1:T(4,128)} %param.14) | copy-start | bytes 786436
  41.2 46.2 %copy-start.6 = (bf16[4,1024,160]{1,2,0:T(8,128)(2,1)S(1)}, bf16[4,1024,160]{1,2,0:T(8,128)(2,1)}, u32[]{:S(2)}) copy-start(bf16[4,1024,160]{1,2,0:T(8,128)(2,1)} %get-tuple-element.126) | copy-start | bytes 3932164 | tf_op jit(solution)/shard_map/while
  99.7 46.2 %copy-start.6 = (bf16[4,1024,160]{1,2,0:T(8,128)(2,1)S(1)}, bf16[4,1024,160]{1,2,0:T(8,128)(2,1)}, u32[]{:S(2)}) copy-start(bf16[4,1024,160]{1,2,0:T(8,128)(2,1)} %get-tuple-element.126) | copy-start | bytes 3932164 | tf_op jit(solution)/shard_map/while
  158.2 46.2 %copy-start.6 = (bf16[4,1024,160]{1,2,0:T(8,128)(2,1)S(1)}, bf16[4,1024,160]{1,2,0:T(8,128)(2,1)}, u32[]{:S(2)}) copy-start(bf16[4,1024,160]{1,2,0:T(8,128)(2,1)} %get-tuple-element.126) | copy-start | bytes 3932164 | tf_op jit(solution)/shard_map/while
  216.7 46.2 %copy-start.6 = (bf16[4,1024,160]{1,2,0:T(8,128)(2,1)S(1)}, bf16[4,1024,160]{1,2,0:T(8,128)(2,1)}, u32[]{:S(2)}) copy-start(bf16[4,1024,160]{1,2,0:T(8,128)(2,1)} %get-tuple-element.126) | copy-start | bytes 3932164 | tf_op jit(solution)/shard_map/while
  275.1 46.2 %copy-start.6 = (bf16[4,1024,160]{1,2,0:T(8,128)(2,1)S(1)}, bf16[4,1024,160]{1,2,0:T(8,128)(2,1)}, u32[]{:S(2)}) copy-start(bf16[4,1024,160]{1,2,0:T(8,128)(2,1)} %get-tuple-element.126) | copy-start | bytes 3932164 | tf_op jit(solution)/shard_map/while
  333.6 46.2 %copy-start.6 = (bf16[4,1024,160]{1,2,0:T(8,128)(2,1)S(1)}, bf16[4,1024,160]{1,2,0:T(8,128)(2,1)}, u32[]{:S(2)}) copy-start(bf16[4,1024,160]{1,2,0:T(8,128)(2,1)} %get-tuple-element.126) | copy-start | bytes 3932164 | tf_op jit(solution)/shard_map/while
  392.1 46.2 %copy-start.6 = (bf16[4,1024,160]{1,2,0:T(8,128)(2,1)S(1)}, bf16[4,1024,160]{1,2,0:T(8,128)(2,1)}, u32[]{:S(2)}) copy-start(bf16[4,1024,160]{1,2,0:T(8,128)(2,1)} %get-tuple-element.126) | copy-start | bytes 3932164 | tf_op jit(solution)/shard_map/while
  450.6 46.2 %copy-start.6 = (bf16[4,1024,160]{1,2,0:T(8,128)(2,1)S(1)}, bf16[4,1024,160]{1,2,0:T(8,128)(2,1)}, u32[]{:S(2)}) copy-start(bf16[4,1024,160]{1,2,0:T(8,128)(2,1)} %get-tuple-element.126) | copy-start | bytes 3932164 | tf_op jit(solution)/shard_map/while
  509.2 46.2 %copy-start.6 = (bf16[4,1024,160]{1,2,0:T(8,128)(2,1)S(1)}, bf16[4,1024,160]{1,2,0:T(8,128)(2,1)}, u32[]{:S(2)}) copy-start(bf16[4,1024,160]{1,2,0:T(8,128)(2,1)} %get-tuple-element.126) | copy-start | bytes 3932164 | tf_op jit(solution)/shard_map/while
  567.7 46.2 %copy-start.6 = (bf16[4,1024,160]{1,2,0:T(8,128)(2,1)S(1)}, bf16[4,1024,160]{1,2,0:T(8,128)(2,1)}, u32[]{:S(2)}) copy-start(bf16[4,1024,160]{1,2,0:T(8,128)(2,1)} %get-tuple-element.126) | copy-start | bytes 3932164 | tf_op jit(solution)/shard_map/while
  626.2 46.2 %copy-start.6 = (bf16[4,1024,160]{1,2,0:T(8,128)(2,1)S(1)}, bf16[4,1024,160]{1,2,0:T(8,128)(2,1)}, u32[]{:S(2)}) copy-start(bf16[4,1024,160]{1,2,0:T(8,128)(2,1)} %get-tuple-element.126) | copy-start | bytes 3932164 | tf_op jit(solution)/shard_map/while
  684.7 46.2 %copy-start.6 = (bf16[4,1024,160]{1,2,0:T(8,128)(2,1)S(1)}, bf16[4,1024,160]{1,2,0:T(8,128)(2,1)}, u32[]{:S(2)}) copy-start(bf16[4,1024,160]{1,2,0:T(8,128)(2,1)} %get-tuple-element.126) | copy-start | bytes 3932164 | tf_op jit(solution)/shard_map/while
  743.2 46.2 %copy-start.6 = (bf16[4,1024,160]{1,2,0:T(8,128)(2,1)S(1)}, bf16[4,1024,160]{1,2,0:T(8,128)(2,1)}, u32[]{:S(2)}) copy-start(bf16[4,1024,160]{1,2,0:T(8,128)(2,1)} %get-tuple-element.126) | copy-start | bytes 3932164 | tf_op jit(solution)/shard_map/while
  801.7 46.2 %copy-start.6 = (bf16[4,1024,160]{1,2,0:T(8,128)(2,1)S(1)}, bf16[4,1024,160]{1,2,0:T(8,128)(2,1)}, u32[]{:S(2)}) copy-start(bf16[4,1024,160]{1,2,0:T(8,128)(2,1)} %get-tuple-element.126) | copy-start | bytes 3932164 | tf_op jit(solution)/shard_map/while
  860.2 46.2 %copy-start.6 = (bf16[4,1024,160]{1,2,0:T(8,128)(2,1)S(1)}, bf16[4,1024,160]{1,2,0:T(8,128)(2,1)}, u32[]{:S(2)}) copy-start(bf16[4,1024,160]{1,2,0:T(8,128)(2,1)} %get-tuple-element.126) | copy-start | bytes 3932164 | tf_op jit(solution)/shard_map/while
  918.7 46.2 %copy-start.6 = (bf16[4,1024,160]{1,2,0:T(8,128)(2,1)S(1)}, bf16[4,1024,160]{1,2,0:T(8,128)(2,1)}, u32[]{:S(2)}) copy-start(bf16[4,1024,160]{1,2,0:T(8,128)(2,1)} %get-tuple-element.126) | copy-start | bytes 3932164 | tf_op jit(solution)/shard_map/while
  988.9 137.7 %copy-start.2 = (f32[16,160]{1,0:T(8,128)S(1)}, f32[16,160]{1,0:T(8,128)}, u32[]{:S(2)}) copy-start(f32[16,160]{1,0:T(8,128)} %param.21) | copy-start | bytes 30724
  1122.1 22.9 %copy-start.5 = (s32[16]{0:T(128)S(1)}, s32[16]{0:T(128)}, u32[]{:S(2)}) copy-start(s32[16]{0:T(128)} %param.15) | copy-start | bytes 196
  1122.1 19.2 %all-to-all-start = ((bf16[512,4,160]{2,1,0:T(4,128)(2,1)}), bf16[512,4,160]{2,1,0:T(4,128)(2,1)}, u32[]{:S(2)}, u32[]{:S(2)}) async-start(bf16[512,4,160]{2,1,0:T(4,128)(2,1)} %copy.50), calls=%async_computation.1 | async-start | bytes 2097152 | tf_op jit(solution)/shard_map/all_to_all | solution.py:71
  1141.3 7.1 copy-start.3
  1159.0 4.7 copy-start.4
Sparse Core Ops, SparseCore 0:
  989.0 130.7 reduce-scatter.1
where the time goes:
time: 1180 us; the launch traced here: 1170 us
  other arithmetic  822 us (70%)
  waiting for transfers between devices  146 us (12%)
  matrix products  112 us (9%)
  local copies, waits for them, and re-layouts  75.7 us (6%)
  between operations  13.5 us (1%)
    reduce_sum x16, other arithmetic, pool_block(): jnp.sum((local_index[..., None] == row_ids).astype(jnp.float32), axis=2)  739 us
    reduce_scatter x1, waiting for transfers between devices, on_device(): lax.psum_scatter(pool_rows(tables, index_order, length_order, row_base).a...  131 us
    dot_general x16, matrix products, pool_block(): jnp.einsum('bjr,jre->bje', counts, table_shard, preferred_element_type=jn...  103 us
    select_n x16, other arithmetic, pool_block(): local_index = jnp.where(usable, index_block - row_base, -1)  76.5 us
    transpose x1, local copies, waits for them, and re-layouts, on_device(): jnp.transpose(index_order, (1, 0, 2, 3, 4))  23.8 us
  transfers between devices with their start and end apart: 2, of which 2 were waited for; matrix products, arithmetic and copies ran while one was open for 0% of the time, Pallas kernels for 0%

commit v1 on v0

v1 whole, which is shorter than its diff:
```python
import functools

import jax
import jax.numpy as jnp
from jax import lax
from jax.experimental import pallas as pl
from jax.experimental.pallas import tpu as pltpu
from jax.sharding import PartitionSpec as P

LANES = 128
ROWS_DEV = 1024
SUB = 256
GATHER = 8
BLOCKS = GATHER * ROWS_DEV // SUB
BAG_BLOCKS = 16
STEPS = BAG_BLOCKS // 2


def prep_kernel(pos_ref, idx_ref, len_ref, keys_ref, lid_ref, mask_ref):
    host, z, y, core = pos_ref[0], pos_ref[1], pos_ref[2], pos_ref[3]
    table = pl.program_id(0)
    over_z = table % 2 == 0
    slot = lax.broadcasted_iota(jnp.int32, (8, LANES), 0)
    pick = lax.broadcasted_iota(jnp.int32, (len_ref.shape[0], LANES), 0)
    for n in range(BAG_BLOCKS):
        dest, hrel = n // 4, n % 4
        owner_host = (host + hrel) & 3
        row_dev = jnp.where(
            over_z,
            z * 8 + ((y + dest) & 3) * 2 + core,
            ((z + dest) & 3) * 8 + y * 2 + core,
        )
        start = pl.multiple_of((owner_host * 32 + row_dev) * LANES, LANES)
        v = idx_ref[0, :, pl.ds(start, LANES)]
        used = jnp.sum(
            jnp.where(pick == table, len_ref[:, pl.ds(start, LANES)], 0), axis=0, keepdims=True
        )
        at_z, at_y, at_core = v >> 13, (v >> 11) & 3, (v >> 10) & 1
        here = jnp.where(over_z, at_y - y, at_z - z) == 0
        shard = jnp.where(over_z, (at_z - z) & 3, (at_y - y) & 3) * 2 + (at_core ^ core)
        local = shard * ROWS_DEV + (v & (ROWS_DEV - 1))
        local = jnp.where(here & (slot < used), local, -1)
        for s in range(8):
            lid_ref[0, s, n : n + 1, :] = local[s : s + 1, :]
    for g in range(BAG_BLOCKS // 8):
        rows = pl.ds(g * 8, 8)
        lids = [lid_ref[0, s, rows, :] for s in range(8)]
        high = [x >> 8 for x in lids]
        low = [(x & (SUB - 1)).astype(jnp.float32) for x in lids]

        def one_block(blk, mask):
            at = [h == blk for h in high]
            up = [jnp.where(a, l, 511.0) for a, l in zip(at, low)]
            down = [jnp.where(a, l, -1.0) for a, l in zip(at, low)]
            first = functools.reduce(jnp.minimum, up)
            last = functools.reduce(jnp.maximum, down)
            n_first = sum(jnp.where(u == first, 1.0, 0.0) for u in up)
            n_last = sum(jnp.where(d == last, 1.0, 0.0) for d in down)
            total = sum(jnp.where(a, 1.0, 0.0) for a in at)
            more = (n_first + n_last) < total
            keys_ref[0, blk, 0, rows, :] = first
            keys_ref[0, blk, 1, rows, :] = n_first
            keys_ref[0, blk, 2, rows, :] = jnp.where(last == first, -1.0, last)
            keys_ref[0, blk, 3, rows, :] = n_last
            return mask | jnp.where(more, jnp.int32(1) << blk, 0)

        mask_ref[0, rows, :] = lax.fori_loop(
            0, BLOCKS, one_block, jnp.zeros((8, LANES), jnp.int32)
        )


def prep(pos, idx, lens):
    tables = idx.shape[0]
    return pl.pallas_call(
        prep_kernel,
        grid=(tables,),
        in_specs=[
            pl.BlockSpec(memory_space=pltpu.SMEM),
            pl.BlockSpec((1,) + idx.shape[1:], lambda j: (j, 0, 0)),
            pl.BlockSpec(lens.shape, lambda j: (0, 0)),
        ],
        out_specs=[
            pl.BlockSpec((1, BLOCKS, 4, BAG_BLOCKS, LANES), lambda j: (j, 0, 0, 0, 0)),
            pl.BlockSpec((1, 8, BAG_BLOCKS, LANES), lambda j: (j, 0, 0, 0)),
            pl.BlockSpec((1, BAG_BLOCKS, LANES), lambda j: (j, 0, 0)),
        ],
        out_shape=[
            jax.ShapeDtypeStruct((tables, BLOCKS, 4, BAG_BLOCKS, LANES), jnp.float32),
            jax.ShapeDtypeStruct((tables, 8, BAG_BLOCKS, LANES), jnp.int32),
            jax.ShapeDtypeStruct((tables, BAG_BLOCKS, LANES), jnp.int32),
        ],
        compiler_params=pltpu.CompilerParams(vmem_limit_bytes=32 << 20),
        cost_estimate=pl.CostEstimate(
            flops=40_000_000, bytes_accessed=9_000_000, transcendentals=0
        ),
        name="prep",
    )(pos, idx, lens)


def pool_kernel(mask_ref, keys_ref, lid_ref, *rest):
    tabs = rest[:GATHER]
    outs = rest[GATHER : GATHER + 4]
    acc, counts, extra = rest[GATHER + 4 :]
    step = pl.program_id(0)
    row_ids = [
        (lax.broadcasted_iota(jnp.int32, (16, LANES), 0) + c * 16)
        .astype(jnp.float32)
        .astype(jnp.bfloat16)
        for c in range(SUB // 16)
    ]

    def wide(x):
        return jnp.broadcast_to(x, (16, LANES)).astype(jnp.bfloat16)

    for blk in range(BLOCKS):
        for half in range(2):
            row = pl.ds(2 * step + half, 1)
            k1, m1, k2, m2 = (wide(keys_ref[0, blk, v, row, :]) for v in range(4))
            for c in range(SUB // 16):
                counts[
                    blk * SUB + c * 16 : blk * SUB + (c + 1) * 16,
                    half * LANES : (half + 1) * LANES,
                ] = jnp.where(
                    k1 == row_ids[c], m1, jnp.where(k2 == row_ids[c], m2, jnp.bfloat16(0))
                )
    total = None
    for g in range(GATHER):
        part = jnp.dot(
            tabs[g][...],
            counts[g * ROWS_DEV : (g + 1) * ROWS_DEV, :],
            preferred_element_type=jnp.float32,
        )
        total = part if total is None else total + part
    acc[...] = total

    mask = mask_ref[2 * step] | mask_ref[2 * step + 1]

    @pl.when(mask != 0)
    def _():
        def fix(blk, carry):
            @pl.when(((mask >> blk) & 1) == 1)
            def _():
                for half in range(2):
                    row = pl.ds(2 * step + half, 1)
                    k1 = keys_ref[0, blk, 0, row, :]
                    k2 = keys_ref[0, blk, 2, row, :]
                    left = []
                    for s in range(8):
                        x = lid_ref[0, s, row, :]
                        low = jnp.where(
                            (x >> 8) == blk, (x & (SUB - 1)).astype(jnp.float32), -1.0
                        )
                        left.append(wide(jnp.where((low == k1) | (low == k2), -1.0, low)))
                    for c in range(SUB // 16):
                        n = jnp.zeros((16, LANES), jnp.bfloat16)
                        for k in left:
                            n = n + jnp.where(k == row_ids[c], jnp.bfloat16(1), jnp.bfloat16(0))
                        extra[c * 16 : (c + 1) * 16, half * LANES : (half + 1) * LANES] = n
                columns = pl.ds(pl.multiple_of((blk & 3) * SUB, SUB), SUB)
                for g in range(GATHER):

                    @pl.when((blk >> 2) == g)
                    def _(g=g):
                        acc[...] += jnp.dot(
                            tabs[g][:, columns], extra[...], preferred_element_type=jnp.float32
                        )

            return carry

        lax.fori_loop(0, BLOCKS, fix, 0)

    result = acc[...].astype(jnp.bfloat16)
    place = (step % 2) * 2
    for d in range(4):

        @pl.when(step // 2 == d)
        def _(d=d):
            outs[d][pl.ds(place, 1), :, :] = result[None, :, :LANES]
            outs[d][pl.ds(place + 1, 1), :, :] = result[None, :, LANES:]


def pool(table, mask, keys, lids, shards):
    emb, rows = shards[0].shape
    return pl.pallas_call(
        pool_kernel,
        grid=(STEPS,),
        in_specs=[
            pl.BlockSpec(memory_space=pltpu.SMEM),
            pl.BlockSpec((1,) + keys.shape[1:], lambda i: (table, 0, 0, 0, 0)),
            pl.BlockSpec((1,) + lids.shape[1:], lambda i: (table, 0, 0, 0)),
        ]
        + [pl.BlockSpec((emb, rows), lambda i: (0, 0))] * GATHER,
        out_specs=[pl.BlockSpec((4, emb, LANES), lambda i: (0, 0, 0))] * 4,
        out_shape=[jax.ShapeDtypeStruct((4, emb, LANES), jnp.bfloat16)] * 4,
        scratch_shapes=[
            pltpu.VMEM((emb, 2 * LANES), jnp.float32),
            pltpu.VMEM((GATHER * rows, 2 * LANES), jnp.bfloat16),
            pltpu.VMEM((SUB, 2 * LANES), jnp.bfloat16),
        ],
        compiler_params=pltpu.CompilerParams(vmem_limit_bytes=32 << 20),
        cost_estimate=pl.CostEstimate(
            flops=2 * GATHER * rows * 2048 * 256, bytes_accessed=5_000_000, transcendentals=0
        ),
        name="pool",
    )(mask, keys, lids, *shards)


def tail_kernel(
    host_ref,
    order_ref,
    proj_ref,
    compress_ref,
    *rest,
):
    parts = rest[:4]
    fm_gain_ref, up_ref, down_ref, gain_ref, out_ref, emb, gram, summed = rest[4:]
    host = host_ref[0]
    for d in range(4):
        source = (host - d) & 3
        for j in range(4):
            at = order_ref[source * 4 + j]
            emb[pl.ds(at, 1), :, :] = parts[d][j : j + 1, :, :].astype(jnp.float32)
    feats, width, lanes = emb.shape
    rank = proj_ref.shape[0]

    for f in range(feats):
        x = emb[f]
        for g in range(f + 1):
            dot = jnp.sum(x * emb[g], axis=0, keepdims=True)
            gram[f, g : g + 1, :] = dot
            if g != f:
                gram[g, f : f + 1, :] = dot
    rows = []
    for k in range(rank):
        row = None
        for g in range(feats):
            term = proj_ref[k, g] * gram[g]
            row = term if row is None else row + term
        rows.append(row)
    inv = 1.0 / (rank * feats)
    mean = jnp.sum(sum(rows), axis=0, keepdims=True) * inv
    rows = [r - mean for r in rows]
    spread = jnp.sum(sum(r * r for r in rows), axis=0, keepdims=True) * inv
    scale = 1.0 / jnp.sqrt(spread + 1e-05)
    normed = jnp.concatenate(
        [rows[k] * scale * fm_gain_ref[:, k : k + 1] for k in range(rank)], axis=0
    ).astype(jnp.bfloat16)
    hidden = jnp.maximum(
        jnp.dot(up_ref[...], normed, preferred_element_type=jnp.float32), 0.0
    ).astype(jnp.bfloat16)
    half = feats // 2
    for m in range(half):
        block = jnp.dot(
            down_ref[m * width : (m + 1) * width, :], hidden, preferred_element_type=jnp.float32
        )
        summed[m] = block + emb[m]
        acc = emb[half + m]
        for f in range(feats):
            acc = acc + compress_ref[m, f] * emb[f]
        summed[half + m] = acc
    inv = 1.0 / (feats * width)
    total = summed[0]
    for f in range(1, feats):
        total = total + summed[f]
    mean = jnp.sum(total, axis=0, keepdims=True) * inv
    square = None
    for f in range(feats):
        c = summed[f] - mean
        square = c * c if square is None else square + c * c
    spread = jnp.sum(square, axis=0, keepdims=True) * inv
    scale = 1.0 / jnp.sqrt(spread + 1e-05)
    for f in range(feats):
        out_ref[f] = ((summed[f] - mean) * scale * gain_ref[:, f : f + 1]).astype(jnp.bfloat16)


def tail(host, order, proj, compress, parts, fm_gain, up, down, gain):
    feats, width = order.shape[0], parts[0].shape[1]
    smem = pl.BlockSpec(memory_space=pltpu.SMEM)
    vmem = pl.BlockSpec(memory_space=pltpu.VMEM)
    return pl.pallas_call(
        tail_kernel,
        in_specs=[smem] * 4 + [vmem] * 8,
        out_specs=vmem,
        out_shape=jax.ShapeDtypeStruct((feats, width, LANES), jnp.bfloat16),
        scratch_shapes=[
            pltpu.VMEM((feats, width, LANES), jnp.float32),
            pltpu.VMEM((feats, feats, LANES), jnp.float32),
            pltpu.VMEM((feats, width, LANES), jnp.float32),
        ],
        compiler_params=pltpu.CompilerParams(vmem_limit_bytes=32 << 20),
        cost_estimate=pl.CostEstimate(
            flops=1_000_000_000, bytes_accessed=8_000_000, transcendentals=0
        ),
        name="tail",
    )(host, order, proj, compress, *parts, fm_gain, up, down, gain)


def row_moves(axis, step):
    pairs = []
    for z in range(4):
        for y in range(4):
            for core in range(2):
                to = {
                    "z": (((z + step) % 4) * 8 + y * 2 + core),
                    "y": (z * 8 + ((y + step) % 4) * 2 + core),
                    "core": (z * 8 + y * 2 + (core + step) % 2),
                }[axis]
                pairs.append((z * 8 + y * 2 + core, to))
    return pairs


def gather_shards(shard, axis):
    near = [shard]
    for rel in range(1, 4):
        near.append(lax.ppermute(shard, "row", row_moves(axis, 4 - rel)))
    far = [lax.ppermute(x, "row", row_moves("core", 1)) for x in near]
    return [x for pair in zip(near, far) for x in pair]


def exchange(blocks, axis):
    total = blocks[0].astype(jnp.float32)
    for d in range(1, 4):
        total = total + lax.ppermute(blocks[d], "row", row_moves(axis, d)).astype(jnp.float32)
    return total.astype(jnp.bfloat16)


def on_device(
    tables,
    indices,
    lengths,
    feature_order,
    proj_weight,
    fm_gain,
    up_weight,
    down_weight,
    compress_weight,
    out_gain,
):
    host = lax.axis_index("hst")
    row = lax.axis_index("row")
    pos = jnp.stack([host, row // 8, (row // 2) % 4, row % 2]).astype(jnp.int32)
    n_tables = tables.shape[0]
    feats, emb = out_gain.shape
    rank = proj_weight.shape[0]
    width = up_weight.shape[1]

    flipped = jnp.swapaxes(tables, 1, 2)
    shards = [
        gather_shards(flipped[j], "z" if j % 2 == 0 else "y") for j in range(n_tables)
    ]
    keys, lids, masks = prep(pos, jnp.transpose(indices, (1, 2, 0)), lengths.T)
    masks = lax.reduce(masks, jnp.int32(0), lax.bitwise_or, (2,))
    sums = []
    for j in range(n_tables):
        blocks = pool(j, masks[j], keys, lids, shards[j])
        sums.append(exchange(blocks, "y" if j % 2 == 0 else "z"))

    parts = []
    for d in range(4):
        block = jnp.stack([s[d] for s in sums])
        if d:
            block = lax.ppermute(block, "hst", [(h, (h + d) % 4) for h in range(4)])
        parts.append(block)
    up = jnp.transpose(up_weight.reshape(feats, rank, width), (2, 1, 0)).reshape(
        width, rank * feats
    )
    result = tail(
        pos[:1],
        feature_order,
        proj_weight.astype(jnp.float32),
        compress_weight.astype(jnp.float32),
        parts,
        fm_gain.reshape(feats, rank),
        up,
        down_weight.T,
        out_gain.T,
    )
    return jnp.transpose(result, (2, 0, 1))


def solution(mesh):
    in_specs = (
        P("hst", "row", None),
        P(None, "hst", None),
        P(None, "hst"),
        P(),
        P(),
        P(),
        P(),
        P(),
        P(),
        P(),
    )
    out_specs = P(("hst", "row"), None, None)
    return jax.shard_map(
        on_device, mesh=mesh, in_specs=in_specs, out_specs=out_specs, check_vma=False
    )
```

time: 1180 us -> 175 us (0.15)
  other arithmetic: 822 us -> 4.15 us
  waiting for transfers between devices: 146 us -> 32.1 us
  matrix products: 112 us -> 0 us
  Pallas kernels: 0 us -> 69.8 us
  local copies, waits for them, and re-layouts: 75.7 us -> 21.7 us
  starting transfers between devices: 4.42 us -> 46.5 us
  between operations: 13.5 us -> 0.33 us
    reduce_sum x19 -> x0, other arithmetic: 743 us -> none  [the longest x16 739 us: pool_block(): jnp.sum((local_index[..., None] == row_ids).astype(jnp.float32), axis=2)]
    reduce_scatter x1 -> x0, waiting for transfers between devices: 131 us -> none  [on_device(): lax.psum_scatter(pool_rows(tables, index_order, length_order, row_base).a...]
    dot_general x20 -> x0, matrix products: 112 us -> none  [the longest x16 103 us: pool_block(): jnp.einsum('bjr,jre->bje', counts, table_shard, preferred_element_type=jn...]
    select_n x16 -> x0, other arithmetic: 76.5 us -> none  [pool_block(): local_index = jnp.where(usable, index_block - row_base, -1)]
    pallas_call x0 -> x6, Pallas kernels: none -> 69.8 us  [the longest x4 57.4 us: pool(): pl.pallas_call(pool_kernel, grid=(STEPS,), in_specs=[pl.BlockSpec(memory_...]
    ppermute x0 -> x43, starting transfers between devices: none -> 46.5 us  [the longest x12 20.3 us: gather_shards(): near.append(lax.ppermute(shard, 'row', row_moves(axis, 4 - rel)))]
    ppermute x0 -> x43, waiting for transfers between devices: none -> 32.1 us  [the longest x12 24.8 us: gather_shards(): near.append(lax.ppermute(shard, 'row', row_moves(axis, 4 - rel)))]
    transpose x1, local copies, waits for them, and re-layouts: 23.8 us -> 1.35 us  [on_device(): jnp.transpose(up_weight.reshape(feats, rank, width), (2, 1, 0))]
  transfers between devices with their start and end apart: 2 -> 43, of which waited for: 2 -> 9; matrix products, arithmetic and copies ran while one was open for 0% -> 7% of each run, Pallas kernels for 0% -> 37%
where the time goes in v1:
time: 175 us
  Pallas kernels  69.8 us (40%)
  starting transfers between devices  46.5 us (27%)
  waiting for transfers between devices  32.1 us (18%)
  local copies, waits for them, and re-layouts  21.7 us (12%)
  other arithmetic  4.15 us (2%)
    pallas_call x4, Pallas kernels, pool(): pl.pallas_call(pool_kernel, grid=(STEPS,), in_specs=[pl.BlockSpec(memory_...  57.4 us
    ppermute x12, waiting for transfers between devices, gather_shards(): near.append(lax.ppermute(shard, 'row', row_moves(axis, 4 - rel)))  24.8 us
    ppermute x12, starting transfers between devices, gather_shards(): near.append(lax.ppermute(shard, 'row', row_moves(axis, 4 - rel)))  20.3 us
    ppermute x12, starting transfers between devices, exchange(): lax.ppermute(blocks[d], 'row', row_moves(axis, d)).astype(jnp.float32)  17.6 us
    unnamed x38, local copies, waits for them, and re-layouts  14.6 us
    ppermute x12, waiting for transfers between devices, exchange(): lax.ppermute(blocks[d], 'row', row_moves(axis, d)).astype(jnp.float32)  7.2 us
    pallas_call x1, Pallas kernels, prep(): pl.pallas_call(prep_kernel, grid=(tables,), in_specs=[pl.BlockSpec(memory...  6.88 us
    pallas_call x1, Pallas kernels, tail(): pl.pallas_call(tail_kernel, in_specs=[smem] * 4 + [vmem] * 8, out_specs=v...  5.52 us
  transfers between devices with their start and end apart: 43, of which 9 were waited for; matrix products, arithmetic and copies ran while one was open for 7% of the time, Pallas kernels for 37%

profile of v1, /device:TPU:0, one launch (start us, length us, event | category | flops | bytes accessed | tf_op | source)
XLA Modules:
  0.0 174.6 jit_solution(4931164833952862822)
XLA Ops:
  1.5 4.2 %collective-permute-start.1 = (bf16[160,1024]{1,0:T(8,128)(2,1)S(1)}, bf16[160,1024]{1,0:T(8,128)(2,1)S(1)}, u32[]{:S(2)}, u32[]{:S(2)}) collective-permute-start(bf16[160,1024]{1,0:T(8,128)(2,1)S(1)} %get-tuple-element.43.rest_0_), channel_id=1, source_target_pairs={{0,24},{1,25},{2,26},{3,27},{4,28},{5,29},{6,30},{7,31},{8,0},{9,1... | collective-permute-start | bytes 983048 | tf_op jit(solution)/shard_map/ppermute | solution.py:315
  7.0 3.0 %collective-permute-start.11 = (bf16[160,1024]{1,0:T(8,128)(2,1)S(1)}, bf16[160,1024]{1,0:T(8,128)(2,1)}, u32[]{:S(2)}, u32[]{:S(2)}) collective-permute-start(bf16[160,1024]{1,0:T(8,128)(2,1)S(1)} %get-tuple-element.46.rest_0_), channel_id=1, source_target_pairs={{0,6},{1,7},{2,0},{3,1},{4,2},{5,3},{6,4},{7,5},{8,14},{9,15},{10,... | collective-permute-start | bytes 983048 | tf_op jit(solution)/shard_map/ppermute | solution.py:315
  10.0 9.7 %collective-permute-done.1.rest_2_ = bf16[160,1024]{1,0:T(8,128)(2,1)S(1)} collective-permute-done((bf16[160,1024]{1,0:T(8,128)(2,1)S(1)}, bf16[160,1024]{1,0:T(8,128)(2,1)S(1)}, u32[]{:S(2)}, u32[]{:S(2)}) %collective-permute-start.1) | collective-permute-done | bytes 327712 | tf_op jit(solution)/shard_map/ppermute | solution.py:315
  19.7 3.2 %collective-permute-start.13 = (bf16[160,1024]{1,0:T(8,128)(2,1)S(1)}, bf16[160,1024]{1,0:T(8,128)(2,1)}, u32[]{:S(2)}, u32[]{:S(2)}) collective-permute-start(bf16[160,1024]{1,0:T(8,128)(2,1)S(1)} %get-tuple-element.46.rest_0_), channel_id=1, source_target_pairs={{0,4},{1,5},{2,6},{3,7},{4,0},{5,1},{6,2},{7,3},{8,12},{9,13},{10,... | collective-permute-start | bytes 983048 | tf_op jit(solution)/shard_map/ppermute | solution.py:315
  24.4 3.7 %collective-permute-start.21 = (bf16[160,1024]{1,0:T(8,128)(2,1)S(1)}, bf16[160,1024]{1,0:T(8,128)(2,1)}, u32[]{:S(2)}, u32[]{:S(2)}) collective-permute-start(bf16[160,1024]{1,0:T(8,128)(2,1)S(1)} %get-tuple-element.45.rest_0_), channel_id=1, source_target_pairs={{0,24},{1,25},{2,26},{3,27},{4,28},{5,29},{6,30},{7,31},{8,0},{9,1... | collective-permute-start | bytes 983048 | tf_op jit(solution)/shard_map/ppermute | solution.py:315
  28.1 3.9 %collective-permute-done.13.rest_4_ = bf16[160,1024]{1,0:T(8,128)(2,1)} collective-permute-done((bf16[160,1024]{1,0:T(8,128)(2,1)S(1)}, bf16[160,1024]{1,0:T(8,128)(2,1)}, u32[]{:S(2)}, u32[]{:S(2)}) %collective-permute-start.13) | collective-permute-done | bytes 327712 | tf_op jit(solution)/shard_map/ppermute | solution.py:315
  32.0 4.8 %collective-permute-done.15.rest_6_ = bf16[160,1024]{1,0:T(8,128)(2,1)} collective-permute-done((bf16[160,1024]{1,0:T(8,128)(2,1)S(1)}, bf16[160,1024]{1,0:T(8,128)(2,1)}, u32[]{:S(2)}, u32[]{:S(2)}) %collective-permute-start.15) | collective-permute-done | bytes 327712 | tf_op jit(solution)/shard_map/ppermute | solution.py:315
  37.3 5.4 %collective-permute-done.21.rest_2_ = bf16[160,1024]{1,0:T(8,128)(2,1)} collective-permute-done((bf16[160,1024]{1,0:T(8,128)(2,1)S(1)}, bf16[160,1024]{1,0:T(8,128)(2,1)}, u32[]{:S(2)}, u32[]{:S(2)}) %collective-permute-start.21) | collective-permute-done | bytes 327712 | tf_op jit(solution)/shard_map/ppermute | solution.py:315
  43.7 6.9 %prep.1 = (f32[4,32,4,16,128]{4,3,2,1,0:T(8,128)S(1)}, s32[4,8,16,128]{3,2,1,0:T(8,128)S(1)}, s32[4,16,128]{2,1,0:T(8,128)S(1)}) custom-call(s32[4]{0:T(128)S(1)} %pad_add_fusion.pos_ref, s32[4,8,16384]{2,1,0:T(8,128)S(1)} %bitcast.31, s32[4,16384]{1,0:T(4,128)S(1)} %bitcast.33), custom_call_target="tpu_custom_call" | custom-call | flops 40000000 | bytes 9000000 | tf_op jit(solution)/shard_map/prep/pallas_call | solution.py:74
  54.0 2.6 %collective-permute-start.31 = (bf16[160,1024]{1,0:T(8,128)(2,1)S(1)}, bf16[160,1024]{1,0:T(8,128)(2,1)S(1)}, u32[]{:S(2)}, u32[]{:S(2)}) collective-permute-start(bf16[160,1024]{1,0:T(8,128)(2,1)S(1)} %get-tuple-element.44.rest_0_), channel_id=1, source_target_pairs={{0,6},{1,7},{2,0},{3,1},{4,2},{5,3},{6,4},{7,5},{8,14},{9,15},{10,... | collective-permute-start | bytes 983048 | tf_op jit(solution)/shard_map/ppermute | solution.py:315
  57.2 2.2 %copy-done.4 = f32[4,32,4,16,128]{4,3,2,1,0:T(8,128)S(1)} copy-done((f32[4,32,4,16,128]{4,3,2,1,0:T(8,128)S(1)}, f32[4,32,4,16,128]{4,3,2,1,0:T(8,128)}, u32[]{:S(2)}) %copy-start.4) | copy-done | bytes 4194328
  64.2 14.5 %pool.4 = (bf16[4,160,128]{2,1,0:T(8,128)(2,1)S(1)}, bf16[4,160,128]{2,1,0:T(8,128)(2,1)S(1)}, bf16[4,160,128]{2,1,0:T(8,128)(2,1)S(1)}, bf16[4,160,128]{2,1,0:T(8,128)(2,1)S(1)}) custom-call(s32[16]{0:T(128)S(1)} %get-tuple-element.63.mask_ref, f32[4,32,4,16,128]{4,3,2,1,0:T(8,128)S(1)} %copy-done.4, s32[4,8,16,128]{3,2,1,0:T(8,128)S(1)} %copy-done.14, ...), custom_call_target="tpu_custom_call" | custom-call | flops 8589934592 | bytes 5000000 | tf_op jit(solution)/shard_map/pool/pallas_call | solution.py:184
  81.1 14.6 %pool.5 = (bf16[4,160,128]{2,1,0:T(8,128)(2,1)S(1)}, bf16[4,160,128]{2,1,0:T(8,128)(2,1)S(1)}, bf16[4,160,128]{2,1,0:T(8,128)(2,1)S(1)}, bf16[4,160,128]{2,1,0:T(8,128)(2,1)S(1)}) custom-call(s32[16]{0:T(128)S(1)} %get-tuple-element.66.mask_ref, f32[4,32,4,16,128]{4,3,2,1,0:T(8,128)S(1)} %copy-done.4, s32[4,8,16,128]{3,2,1,0:T(8,128)S(1)} %copy-done.14, ...), custom_call_target="tpu_custom_call" | custom-call | flops 8589934592 | bytes 5000000 | tf_op jit(solution)/shard_map/pool/pallas_call | solution.py:184
  97.8 2.2 %collective-permute-start.7 = (bf16[4,160,128]{2,1,0:T(8,128)(2,1)S(1)}, bf16[4,160,128]{2,1,0:T(8,128)(2,1)S(1)}, u32[]{:S(2)}, u32[]{:S(2)}) collective-permute-start(bf16[4,160,128]{2,1,0:T(8,128)(2,1)S(1)} %get-tuple-element.28), channel_id=1, source_target_pairs={{0,2},{1,3},{2,4},{3,5},{4,6},{5,7},{6,0},{7,1},{8,10},{9,11},{10,... | collective-permute-start | bytes 491528 | tf_op jit(solution)/shard_map/ppermute | solution.py:323
  100.1 14.5 %pool.6 = (bf16[4,160,128]{2,1,0:T(8,128)(2,1)S(1)}, bf16[4,160,128]{2,1,0:T(8,128)(2,1)S(1)}, bf16[4,160,128]{2,1,0:T(8,128)(2,1)S(1)}, bf16[4,160,128]{2,1,0:T(8,128)(2,1)S(1)}) custom-call(s32[16]{0:T(128)S(1)} %get-tuple-element.65.mask_ref, f32[4,32,4,16,128]{4,3,2,1,0:T(8,128)S(1)} %copy-done.4, s32[4,8,16,128]{3,2,1,0:T(8,128)S(1)} %copy-done.14, ...), custom_call_target="tpu_custom_call" | custom-call | flops 8589934592 | bytes 5000000 | tf_op jit(solution)/shard_map/pool/pallas_call | solution.py:184
  115.7 2.3 %collective-permute-start.9 = (bf16[4,160,128]{2,1,0:T(8,128)(2,1)S(1)}, bf16[4,160,128]{2,1,0:T(8,128)(2,1)S(1)}, u32[]{:S(2)}, u32[]{:S(2)}) collective-permute-start(bf16[4,160,128]{2,1,0:T(8,128)(2,1)S(1)} %get-tuple-element.30), channel_id=1, source_target_pairs={{0,6},{1,7},{2,0},{3,1},{4,2},{5,3},{6,4},{7,5},{8,14},{9,15},{10,... | collective-permute-start | bytes 491528 | tf_op jit(solution)/shard_map/ppermute | solution.py:323
  118.0 5.4 %collective-permute-start.18 = (bf16[4,160,128]{2,1,0:T(8,128)(2,1)S(1)}, bf16[4,160,128]{2,1,0:T(8,128)(2,1)S(1)}, u32[]{:S(2)}, u32[]{:S(2)}) collective-permute-start(bf16[4,160,128]{2,1,0:T(8,128)(2,1)S(1)} %get-tuple-element.33), channel_id=1, source_target_pairs={{0,16},{1,17},{2,18},{3,19},{4,20},{5,21},{6,22},{7,23},{8,24},{9,... | collective-permute-start | bytes 491528 | tf_op jit(solution)/shard_map/ppermute | solution.py:323
  123.4 13.8 %pool.7 = (bf16[4,160,128]{2,1,0:T(8,128)(2,1)S(1)}, bf16[4,160,128]{2,1,0:T(8,128)(2,1)S(1)}, bf16[4,160,128]{2,1,0:T(8,128)(2,1)S(1)}, bf16[4,160,128]{2,1,0:T(8,128)(2,1)S(1)}) custom-call(s32[16]{0:T(128)S(1)} %get-tuple-element.64.mask_ref, f32[4,32,4,16,128]{4,3,2,1,0:T(8,128)S(1)} %copy-done.4, s32[4,8,16,128]{3,2,1,0:T(8,128)S(1)} %copy-done.14, ...), custom_call_target="tpu_custom_call" | custom-call | flops 8589934592 | bytes 5000000 | tf_op jit(solution)/shard_map/pool/pallas_call | solution.py:184
  139.1 2.3 %collective-permute-start.29 = (bf16[4,160,128]{2,1,0:T(8,128)(2,1)S(1)}, bf16[4,160,128]{2,1,0:T(8,128)(2,1)S(1)}, u32[]{:S(2)}, u32[]{:S(2)}) collective-permute-start(bf16[4,160,128]{2,1,0:T(8,128)(2,1)S(1)} %get-tuple-element.38), channel_id=1, source_target_pairs={{0,6},{1,7},{2,0},{3,1},{4,2},{5,3},{6,4},{7,5},{8,14},{9,15},{10,... | collective-permute-start | bytes 491528 | tf_op jit(solution)/shard_map/ppermute | solution.py:323
  144.3 3.0 %collective-permute-done.27 = bf16[4,160,128]{2,1,0:T(8,128)(2,1)S(1)} collective-permute-done((bf16[4,160,128]{2,1,0:T(8,128)(2,1)S(1)}, bf16[4,160,128]{2,1,0:T(8,128)(2,1)S(1)}, u32[]{:S(2)}, u32[]{:S(2)}) %collective-permute-start.27) | collective-permute-done | bytes 163872 | tf_op jit(solution)/shard_map/ppermute | solution.py:323
  148.5 2.7 %collective-permute-done.37 = bf16[4,160,128]{2,1,0:T(8,128)(2,1)S(1)} collective-permute-done((bf16[4,160,128]{2,1,0:T(8,128)(2,1)S(1)}, bf16[4,160,128]{2,1,0:T(8,128)(2,1)S(1)}, u32[]{:S(2)}, u32[]{:S(2)}) %collective-permute-start.37) | collective-permute-done | bytes 163872 | tf_op jit(solution)/shard_map/ppermute | solution.py:323
  154.0 3.1 %collective-permute-start.42 = (bf16[4,160,128]{2,1,0:T(8,128)(2,1)}, bf16[4,160,128]{2,1,0:T(8,128)(2,1)}, u32[]{:S(2)}, u32[]{:S(2)}) collective-permute-start(bf16[4,160,128]{2,1,0:T(8,128)(2,1)} %pad_maximum_fusion.3), channel_id=1, source_target_pairs={{0,96},{32,0},{64,32},{96,64},{1,97},{33,1},{65,33},{97,65},{2,98}... | collective-permute-start | bytes 491528 | tf_op jit(solution)/shard_map/ppermute | solution.py:362
  160.6 3.0 %copy.25 = bf16[1024,1280]{0,1:T(8,128)(2,1)S(1)} copy(bf16[1024,1280]{1,0:T(8,128)(2,1)} %param.17) | data formatting | bytes 5242880 | tf_op args[7]
  169.0 5.5 %tail.1 = bf16[16,160,128]{2,1,0:T(8,128)(2,1)} custom-call(s32[1]{0:T(128)} %bitcast.host_ref, s32[16]{0:T(128)S(1)} %copy-done.2, f32[24,16]{1,0:T(8,128)S(1)} %copy.27.proj_ref, f32[8,16]{1,0:T(8,128)S(1)} %convert_element_type.67.compress_ref, bf16[4,160,128]{2,1,0:T(8,128)(2,1)S(1)} %pad_maximum_fusion.rest_0_, ...), custom_call_target="tpu_custom_call" | custom-call | flops 1000000000 | bytes 8000000 | tf_op jit(solution)/shard_map/tail/pallas_call | solution.py:280
  (127 shorter events, 37.7 us)
Async XLA Ops:
  1.5 18.2 %collective-permute-start.1 = (bf16[160,1024]{1,0:T(8,128)(2,1)S(1)}, bf16[160,1024]{1,0:T(8,128)(2,1)S(1)}, u32[]{:S(2)}, u32[]{:S(2)}) collective-permute-start(bf16[160,1024]{1,0:T(8,128)(2,1)S(1)} %get-tuple-element.43.rest_0_), channel_id=1, source_target_pairs={{0,24},{1,25},{2,26},{3,27},{4,28},{5,29},{6,30},{7,31},{8,0},{9,1... | collective-permute-start | bytes 983048 | tf_op jit(solution)/shard_map/ppermute | solution.py:315
  5.7 17.9 %collective-permute-start.5 = (bf16[160,1024]{1,0:T(8,128)(2,1)S(1)}, bf16[160,1024]{1,0:T(8,128)(2,1)S(1)}, u32[]{:S(2)}, u32[]{:S(2)}) collective-permute-start(bf16[160,1024]{1,0:T(8,128)(2,1)S(1)} %get-tuple-element.43.rest_0_), channel_id=1, source_target_pairs={{0,8},{1,9},{2,10},{3,11},{4,12},{5,13},{6,14},{7,15},{8,16},{9,17... | collective-permute-start | bytes 983048 | tf_op jit(solution)/shard_map/ppermute | solution.py:315
  7.0 21.1 %collective-permute-start.11 = (bf16[160,1024]{1,0:T(8,128)(2,1)S(1)}, bf16[160,1024]{1,0:T(8,128)(2,1)}, u32[]{:S(2)}, u32[]{:S(2)}) collective-permute-start(bf16[160,1024]{1,0:T(8,128)(2,1)S(1)} %get-tuple-element.46.rest_0_), channel_id=1, source_target_pairs={{0,6},{1,7},{2,0},{3,1},{4,2},{5,3},{6,4},{7,5},{8,14},{9,15},{10,... | collective-permute-start | bytes 983048 | tf_op jit(solution)/shard_map/ppermute | solution.py:315
  24.4 18.3 %collective-permute-start.21 = (bf16[160,1024]{1,0:T(8,128)(2,1)S(1)}, bf16[160,1024]{1,0:T(8,128)(2,1)}, u32[]{:S(2)}, u32[]{:S(2)}) collective-permute-start(bf16[160,1024]{1,0:T(8,128)(2,1)S(1)} %get-tuple-element.45.rest_0_), channel_id=1, source_target_pairs={{0,24},{1,25},{2,26},{3,27},{4,28},{5,29},{6,30},{7,31},{8,0},{9,1... | collective-permute-start | bytes 983048 | tf_op jit(solution)/shard_map/ppermute | solution.py:315
  28.1 25.4 %collective-permute-start.23 = (bf16[160,1024]{1,0:T(8,128)(2,1)S(1)}, bf16[160,1024]{1,0:T(8,128)(2,1)}, u32[]{:S(2)}, u32[]{:S(2)}) collective-permute-start(bf16[160,1024]{1,0:T(8,128)(2,1)S(1)} %get-tuple-element.45.rest_0_), channel_id=1, source_target_pairs={{0,16},{1,17},{2,18},{3,19},{4,20},{5,21},{6,22},{7,23},{8,24},{9,... | collective-permute-start | bytes 983048 | tf_op jit(solution)/shard_map/ppermute | solution.py:315
  32.0 22.0 %collective-permute-start.25 = (bf16[160,1024]{1,0:T(8,128)(2,1)S(1)}, bf16[160,1024]{1,0:T(8,128)(2,1)}, u32[]{:S(2)}, u32[]{:S(2)}) collective-permute-start(bf16[160,1024]{1,0:T(8,128)(2,1)S(1)} %get-tuple-element.45.rest_0_), channel_id=1, source_target_pairs={{0,8},{1,9},{2,10},{3,11},{4,12},{5,13},{6,14},{7,15},{8,16},{9,17... | collective-permute-start | bytes 983048 | tf_op jit(solution)/shard_map/ppermute | solution.py:315
  36.8 19.8 %collective-permute-start.2 = (bf16[160,1024]{1,0:T(8,128)(2,1)}, bf16[160,1024]{1,0:T(8,128)(2,1)}, u32[]{:S(2)}, u32[]{:S(2)}) collective-permute-start(bf16[160,1024]{1,0:T(8,128)(2,1)} %copy-done.5), channel_id=1, source_target_pairs={{0,1},{1,0},{2,3},{3,2},{4,5},{5,4},{6,7},{7,6},{8,9},{9,8},{10,11... | collective-permute-start | bytes 983048 | tf_op jit(solution)/shard_map/ppermute | solution.py:316
  36.8 19.8 %collective-permute-start.4 = (bf16[160,1024]{1,0:T(8,128)(2,1)}, bf16[160,1024]{1,0:T(8,128)(2,1)}, u32[]{:S(2)}, u32[]{:S(2)}) collective-permute-start(bf16[160,1024]{1,0:T(8,128)(2,1)} %copy-done.7), channel_id=1, source_target_pairs={{0,1},{1,0},{2,3},{3,2},{4,5},{5,4},{6,7},{7,6},{8,9},{9,8},{10,11... | collective-permute-start | bytes 983048 | tf_op jit(solution)/shard_map/ppermute | solution.py:316
  53.5 25.3 %collective-permute-start.20 = (bf16[160,1024]{1,0:T(8,128)(2,1)S(1)}, bf16[160,1024]{1,0:T(8,128)(2,1)S(1)}, u32[]{:S(2)}, u32[]{:S(2)}) collective-permute-start(bf16[160,1024]{1,0:T(8,128)(2,1)S(1)} %get-tuple-element.45.rest_0_), channel_id=1, source_target_pairs={{0,1},{1,0},{2,3},{3,2},{4,5},{5,4},{6,7},{7,6},{8,9},{9,8},{10,11... | collective-permute-start | bytes 983048 | tf_op jit(solution)/shard_map/ppermute | solution.py:316
  54.0 25.2 %collective-permute-start.31 = (bf16[160,1024]{1,0:T(8,128)(2,1)S(1)}, bf16[160,1024]{1,0:T(8,128)(2,1)S(1)}, u32[]{:S(2)}, u32[]{:S(2)}) collective-permute-start(bf16[160,1024]{1,0:T(8,128)(2,1)S(1)} %get-tuple-element.44.rest_0_), channel_id=1, source_target_pairs={{0,6},{1,7},{2,0},{3,1},{4,2},{5,3},{6,4},{7,5},{8,14},{9,15},{10,... | collective-permute-start | bytes 983048 | tf_op jit(solution)/shard_map/ppermute | solution.py:315
  56.6 23.9 %collective-permute-start.12 = (bf16[160,1024]{1,0:T(8,128)(2,1)}, bf16[160,1024]{1,0:T(8,128)(2,1)S(1)}, u32[]{:S(2)}, u32[]{:S(2)}) collective-permute-start(bf16[160,1024]{1,0:T(8,128)(2,1)} %collective-permute-done.11.rest_2_), channel_id=1, source_target_pairs={{0,1},{1,0},{2,3},{3,2},{4,5},{5,4},{6,7},{7,6},{8,9},{9,8},{10,11... | collective-permute-start | bytes 983048 | tf_op jit(solution)/shard_map/ppermute | solution.py:316
  56.6 23.9 %collective-permute-start.14 = (bf16[160,1024]{1,0:T(8,128)(2,1)}, bf16[160,1024]{1,0:T(8,128)(2,1)S(1)}, u32[]{:S(2)}, u32[]{:S(2)}) collective-permute-start(bf16[160,1024]{1,0:T(8,128)(2,1)} %collective-permute-done.13.rest_4_), channel_id=1, source_target_pairs={{0,1},{1,0},{2,3},{3,2},{4,5},{5,4},{6,7},{7,6},{8,9},{9,8},{10,11... | collective-permute-start | bytes 983048 | tf_op jit(solution)/shard_map/ppermute | solution.py:316
  57.1 23.9 %collective-permute-start.16 = (bf16[160,1024]{1,0:T(8,128)(2,1)}, bf16[160,1024]{1,0:T(8,128)(2,1)S(1)}, u32[]{:S(2)}, u32[]{:S(2)}) collective-permute-start(bf16[160,1024]{1,0:T(8,128)(2,1)} %collective-permute-done.15.rest_6_), channel_id=1, source_target_pairs={{0,1},{1,0},{2,3},{3,2},{4,5},{5,4},{6,7},{7,6},{8,9},{9,8},{10,11... | collective-permute-start | bytes 983048 | tf_op jit(solution)/shard_map/ppermute | solution.py:316
  79.2 18.0 %collective-permute-start.35 = (bf16[160,1024]{1,0:T(8,128)(2,1)S(1)}, bf16[160,1024]{1,0:T(8,128)(2,1)S(1)}, u32[]{:S(2)}, u32[]{:S(2)}) collective-permute-start(bf16[160,1024]{1,0:T(8,128)(2,1)S(1)} %get-tuple-element.44.rest_0_), channel_id=1, source_target_pairs={{0,2},{1,3},{2,4},{3,5},{4,6},{5,7},{6,0},{7,1},{8,10},{9,11},{10,... | collective-permute-start | bytes 983048 | tf_op jit(solution)/shard_map/ppermute | solution.py:315
  80.5 17.2 %collective-permute-start.24 = (bf16[160,1024]{1,0:T(8,128)(2,1)}, bf16[160,1024]{1,0:T(8,128)(2,1)S(1)}, u32[]{:S(2)}, u32[]{:S(2)}) collective-permute-start(bf16[160,1024]{1,0:T(8,128)(2,1)} %collective-permute-done.23.rest_4_), channel_id=1, source_target_pairs={{0,1},{1,0},{2,3},{3,2},{4,5},{5,4},{6,7},{7,6},{8,9},{9,8},{10,11... | collective-permute-start | bytes 983048 | tf_op jit(solution)/shard_map/ppermute | solution.py:316
  95.7 18.8 %collective-permute-start.30 = (bf16[160,1024]{1,0:T(8,128)(2,1)S(1)}, bf16[160,1024]{1,0:T(8,128)(2,1)S(1)}, u32[]{:S(2)}, u32[]{:S(2)}) collective-permute-start(bf16[160,1024]{1,0:T(8,128)(2,1)S(1)} %get-tuple-element.44.rest_0_), channel_id=1, source_target_pairs={{0,1},{1,0},{2,3},{3,2},{4,5},{5,4},{6,7},{7,6},{8,9},{9,8},{10,11... | collective-permute-start | bytes 983048 | tf_op jit(solution)/shard_map/ppermute | solution.py:316
  97.2 18.5 %collective-permute-start.32 = (bf16[160,1024]{1,0:T(8,128)(2,1)S(1)}, bf16[160,1024]{1,0:T(8,128)(2,1)S(1)}, u32[]{:S(2)}, u32[]{:S(2)}) collective-permute-start(bf16[160,1024]{1,0:T(8,128)(2,1)S(1)} %collective-permute-done.31.rest_2_), channel_id=1, source_target_pairs={{0,1},{1,0},{2,3},{3,2},{4,5},{5,4},{6,7},{7,6},{8,9},{9,8},{10,11... | collective-permute-start | bytes 983048 | tf_op jit(solution)/shard_map/ppermute | solution.py:316
  97.2 20.8 %collective-permute-start.34 = (bf16[160,1024]{1,0:T(8,128)(2,1)S(1)}, bf16[160,1024]{1,0:T(8,128)(2,1)S(1)}, u32[]{:S(2)}, u32[]{:S(2)}) collective-permute-start(bf16[160,1024]{1,0:T(8,128)(2,1)S(1)} %collective-permute-done.33.rest_4_), channel_id=1, source_target_pairs={{0,1},{1,0},{2,3},{3,2},{4,5},{5,4},{6,7},{7,6},{8,9},{9,8},{10,11... | collective-permute-start | bytes 983048 | tf_op jit(solution)/shard_map/ppermute | solution.py:316
  97.8 20.3 %collective-permute-start.36 = (bf16[160,1024]{1,0:T(8,128)(2,1)S(1)}, bf16[160,1024]{1,0:T(8,128)(2,1)S(1)}, u32[]{:S(2)}, u32[]{:S(2)}) collective-permute-start(bf16[160,1024]{1,0:T(8,128)(2,1)S(1)} %collective-permute-done.35.rest_6_), channel_id=1, source_target_pairs={{0,1},{1,0},{2,3},{3,2},{4,5},{5,4},{6,7},{7,6},{8,9},{9,8},{10,11... | collective-permute-start | bytes 983048 | tf_op jit(solution)/shard_map/ppermute | solution.py:316
  97.8 39.4 %collective-permute-start.7 = (bf16[4,160,128]{2,1,0:T(8,128)(2,1)S(1)}, bf16[4,160,128]{2,1,0:T(8,128)(2,1)S(1)}, u32[]{:S(2)}, u32[]{:S(2)}) collective-permute-start(bf16[4,160,128]{2,1,0:T(8,128)(2,1)S(1)} %get-tuple-element.28), channel_id=1, source_target_pairs={{0,2},{1,3},{2,4},{3,5},{4,6},{5,7},{6,0},{7,1},{8,10},{9,11},{10,... | collective-permute-start | bytes 491528 | tf_op jit(solution)/shard_map/ppermute | solution.py:323
  114.6 22.8 %collective-permute-start.8 = (bf16[4,160,128]{2,1,0:T(8,128)(2,1)S(1)}, bf16[4,160,128]{2,1,0:T(8,128)(2,1)S(1)}, u32[]{:S(2)}, u32[]{:S(2)}) collective-permute-start(bf16[4,160,128]{2,1,0:T(8,128)(2,1)S(1)} %get-tuple-element.29), channel_id=1, source_target_pairs={{0,4},{1,5},{2,6},{3,7},{4,0},{5,1},{6,2},{7,3},{8,12},{9,13},{10,... | collective-permute-start | bytes 491528 | tf_op jit(solution)/shard_map/ppermute | solution.py:323
  115.7 22.7 %collective-permute-start.9 = (bf16[4,160,128]{2,1,0:T(8,128)(2,1)S(1)}, bf16[4,160,128]{2,1,0:T(8,128)(2,1)S(1)}, u32[]{:S(2)}, u32[]{:S(2)}) collective-permute-start(bf16[4,160,128]{2,1,0:T(8,128)(2,1)S(1)} %get-tuple-element.30), channel_id=1, source_target_pairs={{0,6},{1,7},{2,0},{3,1},{4,2},{5,3},{6,4},{7,5},{8,14},{9,15},{10,... | collective-permute-start | bytes 491528 | tf_op jit(solution)/shard_map/ppermute | solution.py:323
  118.0 21.1 %collective-permute-start.17 = (bf16[4,160,128]{2,1,0:T(8,128)(2,1)S(1)}, bf16[4,160,128]{2,1,0:T(8,128)(2,1)S(1)}, u32[]{:S(2)}, u32[]{:S(2)}) collective-permute-start(bf16[4,160,128]{2,1,0:T(8,128)(2,1)S(1)} %get-tuple-element.32), channel_id=1, source_target_pairs={{0,8},{1,9},{2,10},{3,11},{4,12},{5,13},{6,14},{7,15},{8,16},{9,17... | collective-permute-start | bytes 491528 | tf_op jit(solution)/shard_map/ppermute | solution.py:323
  118.0 23.4 %collective-permute-start.18 = (bf16[4,160,128]{2,1,0:T(8,128)(2,1)S(1)}, bf16[4,160,128]{2,1,0:T(8,128)(2,1)S(1)}, u32[]{:S(2)}, u32[]{:S(2)}) collective-permute-start(bf16[4,160,128]{2,1,0:T(8,128)(2,1)S(1)} %get-tuple-element.33), channel_id=1, source_target_pairs={{0,16},{1,17},{2,18},{3,19},{4,20},{5,21},{6,22},{7,23},{8,24},{9,... | collective-permute-start | bytes 491528 | tf_op jit(solution)/shard_map/ppermute | solution.py:323
  (37 other events, 308.3 us)

commit v2 on v1

--- a/solution.py
+++ b/solution.py
@@ -103,7 +103,7 @@
     acc, counts, extra = rest[GATHER + 4 :]
     step = pl.program_id(0)
     row_ids = [
-        (lax.broadcasted_iota(jnp.int32, (16, LANES), 0) + c * 16)
+        (lax.broadcasted_iota(jnp.int32, (16, 2 * LANES), 0) + c * 16)
         .astype(jnp.float32)
         .astype(jnp.bfloat16)
         for c in range(SUB // 16)
@@ -113,16 +113,17 @@
         return jnp.broadcast_to(x, (16, LANES)).astype(jnp.bfloat16)
 
     for blk in range(BLOCKS):
-        for half in range(2):
-            row = pl.ds(2 * step + half, 1)
-            k1, m1, k2, m2 = (wide(keys_ref[0, blk, v, row, :]) for v in range(4))
-            for c in range(SUB // 16):
-                counts[
-                    blk * SUB + c * 16 : blk * SUB + (c + 1) * 16,
-                    half * LANES : (half + 1) * LANES,
-                ] = jnp.where(
-                    k1 == row_ids[c], m1, jnp.where(k2 == row_ids[c], m2, jnp.bfloat16(0))
-                )
+        k1, m1, k2, m2 = (
+            jnp.concatenate(
+                [wide(keys_ref[0, blk, v, pl.ds(2 * step + half, 1), :]) for half in range(2)],
+                axis=1,
+            )
+            for v in range(4)
+        )
+        for c in range(SUB // 16):
+            counts[blk * SUB + c * 16 : blk * SUB + (c + 1) * 16, :] = jnp.where(
+                k1 == row_ids[c], m1, jnp.where(k2 == row_ids[c], m2, jnp.bfloat16(0))
+            )
     total = None
     for g in range(GATHER):
         part = jnp.dot(
@@ -154,7 +155,7 @@
                     for c in range(SUB // 16):
                         n = jnp.zeros((16, LANES), jnp.bfloat16)
                         for k in left:
-                            n = n + jnp.where(k == row_ids[c], jnp.bfloat16(1), jnp.bfloat16(0))
+                            n = n + jnp.where(k == row_ids[c][:, :LANES], jnp.bfloat16(1), jnp.bfloat16(0))
                         extra[c * 16 : (c + 1) * 16, half * LANES : (half + 1) * LANES] = n
                 columns = pl.ds(pl.multiple_of((blk & 3) * SUB, SUB), SUB)
                 for g in range(GATHER):
@@ -212,14 +213,15 @@
     compress_ref,
     *rest,
 ):
-    parts = rest[:4]
-    fm_gain_ref, up_ref, down_ref, gain_ref, out_ref, emb, gram, summed = rest[4:]
+    parts = rest[:8]
+    fm_gain_ref, up_ref, down_ref, gain_ref, out_ref, emb, gram, summed = rest[8:]
     host = host_ref[0]
     for d in range(4):
         source = (host - d) & 3
         for j in range(4):
             at = order_ref[source * 4 + j]
-            emb[pl.ds(at, 1), :, :] = parts[d][j : j + 1, :, :].astype(jnp.float32)
+            part, k = (parts[d], j) if j < 3 else (parts[4 + d], 0)
+            emb[pl.ds(at, 1), :, :] = part[k : k + 1, :, :].astype(jnp.float32)
     feats, width, lanes = emb.shape
     rank = proj_ref.shape[0]
 
@@ -279,7 +281,7 @@
     vmem = pl.BlockSpec(memory_space=pltpu.VMEM)
     return pl.pallas_call(
         tail_kernel,
-        in_specs=[smem] * 4 + [vmem] * 8,
+        in_specs=[smem] * 4 + [vmem] * 12,
         out_specs=vmem,
         out_shape=jax.ShapeDtypeStruct((feats, width, LANES), jnp.bfloat16),
         scratch_shapes=[
@@ -309,12 +311,14 @@
     return pairs
 
 
-def gather_shards(shard, axis):
-    near = [shard]
-    for rel in range(1, 4):
-        near.append(lax.ppermute(shard, "row", row_moves(axis, 4 - rel)))
-    far = [lax.ppermute(x, "row", row_moves("core", 1)) for x in near]
-    return [x for pair in zip(near, far) for x in pair]
+def near_shards(shard, axis):
+    return [
+        lax.ppermute(shard, "row", row_moves(axis, 4 - rel)) for rel in range(1, 4)
+    ]
+
+
+def other_core(x):
+    return lax.ppermute(x, "row", row_moves("core", 1))
 
 
 def exchange(blocks, axis):
@@ -345,25 +349,40 @@
     width = up_weight.shape[1]
 
     flipped = jnp.swapaxes(tables, 1, 2)
-    shards = [
-        gather_shards(flipped[j], "z" if j % 2 == 0 else "y") for j in range(n_tables)
-    ]
+    axes = ["z" if j % 2 == 0 else "y" for j in range(n_tables)]
+    own = [flipped[j] for j in range(n_tables)]
+    own_far = [other_core(x) for x in own]
+    near = [near_shards(own[j], axes[j]) for j in range(2)]
     keys, lids, masks = prep(pos, jnp.transpose(indices, (1, 2, 0)), lengths.T)
     masks = lax.reduce(masks, jnp.int32(0), lax.bitwise_or, (2,))
-    sums = []
-    for j in range(n_tables):
-        blocks = pool(j, masks[j], keys, lids, shards[j])
-        sums.append(exchange(blocks, "y" if j % 2 == 0 else "z"))
-
-    parts = []
-    for d in range(4):
-        block = jnp.stack([s[d] for s in sums])
-        if d:
-            block = lax.ppermute(block, "hst", [(h, (h + d) % 4) for h in range(4)])
-        parts.append(block)
     up = jnp.transpose(up_weight.reshape(feats, rank, width), (2, 1, 0)).reshape(
         width, rank * feats
     )
+    down = down_weight.T
+    near, masks, up, down, own = lax.optimization_barrier((near, masks, up, down, own))
+    far = [[other_core(x) for x in near[j]] for j in range(2)]
+    near += [near_shards(own[j], axes[j]) for j in range(2, n_tables)]
+    sums = []
+    masks = [masks[j] for j in range(n_tables)]
+    for j in range(n_tables):
+        shards = [own[j], own_far[j]] + [x for pair in zip(near[j], far[j]) for x in pair]
+        blocks = pool(j, masks[j], keys, lids, shards)
+        if j + 2 < n_tables:
+            near[j + 2], masks[j + 1 :], blocks = lax.optimization_barrier(
+                (near[j + 2], masks[j + 1 :], blocks)
+            )
+            far.append([other_core(x) for x in near[j + 2]])
+        elif j + 1 < n_tables:
+            masks[j + 1], blocks = lax.optimization_barrier((masks[j + 1], blocks))
+        sums.append(exchange(blocks, "y" if j % 2 == 0 else "z"))
+
+    parts = []
+    for group in (sums[:3], sums[3:]):
+        for d in range(4):
+            block = jnp.stack([x[d] for x in group])
+            if d:
+                block = lax.ppermute(block, "hst", [(h, (h + d) % 4) for h in range(4)])
+            parts.append(block)
     result = tail(
         pos[:1],
         feature_order,
@@ -372,7 +391,7 @@
         parts,
         fm_gain.reshape(feats, rank),
         up,
-        down_weight.T,
+        down,
         out_gain.T,
     )
     return jnp.transpose(result, (2, 0, 1))

time: 175 us -> 172 us (0.983)
  Pallas kernels: 69.8 us -> 46.3 us
  waiting for transfers between devices: 32.1 us -> 50.7 us
  starting transfers between devices: 46.5 us -> 51.7 us
  local copies, waits for them, and re-layouts: 21.7 us -> 17.9 us
    pallas_call x4, Pallas kernels: 57.4 us -> 34 us  [pool(): pl.pallas_call(pool_kernel, grid=(STEPS,), in_specs=[pl.BlockSpec(memory_...]
    ppermute x12, waiting for transfers between devices: 7.2 us -> 23.2 us  [exchange(): lax.ppermute(blocks[d], 'row', row_moves(axis, d)).astype(jnp.float32)]
    ppermute x3 -> x6, starting transfers between devices: 5.22 us -> 12.7 us  [on_device(): block = lax.ppermute(block, 'hst', [(h, (h + d) % 4) for h in range(4)])]
    unnamed x38 -> x22, local copies, waits for them, and re-layouts: 14.6 us -> 8.91 us
    ppermute x12, starting transfers between devices: 17.6 us -> 15.5 us  [exchange(): lax.ppermute(blocks[d], 'row', row_moves(axis, d)).astype(jnp.float32)]
  transfers between devices with their start and end apart: 43 -> 46, of which waited for: 9 -> 14; matrix products, arithmetic and copies ran while one was open for 7% -> 8% of each run, Pallas kernels for 37% -> 19%
where the time goes in v2:
time: 172 us; the launch traced here: 171 us
  starting transfers between devices  51.7 us (30%)
  waiting for transfers between devices  50.7 us (29%)
  Pallas kernels  46.3 us (27%)
  local copies, waits for them, and re-layouts  17.9 us (10%)
  other arithmetic  4.08 us (2%)
    pallas_call x4, Pallas kernels, pool(): pl.pallas_call(pool_kernel, grid=(STEPS,), in_specs=[pl.BlockSpec(memory_...  34 us
    ppermute x12, waiting for transfers between devices, near_shards(): lax.ppermute(shard, 'row', row_moves(axis, 4 - rel))  26.3 us
    ppermute x12, waiting for transfers between devices, exchange(): lax.ppermute(blocks[d], 'row', row_moves(axis, d)).astype(jnp.float32)  23.2 us
    ppermute x12, starting transfers between devices, near_shards(): lax.ppermute(shard, 'row', row_moves(axis, 4 - rel))  20.3 us
    ppermute x12, starting transfers between devices, exchange(): lax.ppermute(blocks[d], 'row', row_moves(axis, d)).astype(jnp.float32)  15.5 us
    ppermute x6, starting transfers between devices, on_device(): block = lax.ppermute(block, 'hst', [(h, (h + d) % 4) for h in range(4)])  12.7 us
    unnamed x22, local copies, waits for them, and re-layouts  8.91 us
    pallas_call x1, Pallas kernels, prep(): pl.pallas_call(prep_kernel, grid=(tables,), in_specs=[pl.BlockSpec(memory...  6.88 us
  transfers between devices with their start and end apart: 46, of which 14 were waited for; matrix products, arithmetic and copies ran while one was open for 8% of the time, Pallas kernels for 19%

profile of v2, /device:TPU:0, one launch (start us, length us, event | category | flops | bytes accessed | tf_op | source)
XLA Modules:
  0.0 171.1 jit_solution(1619691757722273004)
XLA Ops:
  0.0 2.3 %slice_bitcast_fusion = (bf16[160,1024]{1,0:T(8,128)(2,1)S(1)}, bf16[160,1024]{1,0:T(8,128)(2,1)S(1)}, bf16[160,1024]{1,0:T(8,128)(2,1)}, bf16[160,1024]{1,0:T(8,128)(2,1)}) fusion(bf16[4,160,1024]{2,1,0:T(8,128)(2,1)} %bitcast.35), kind=kLoop, calls=%fused_computation | loop fusion | bytes 2621440 | tf_op jit(solution)/shard_map/squeeze | solution.py:353
  2.4 4.1 %collective-permute-start = (bf16[160,1024]{1,0:T(8,128)(2,1)}, bf16[160,1024]{1,0:T(8,128)(2,1)}, u32[]{:S(2)}, u32[]{:S(2)}) collective-permute-start(bf16[160,1024]{1,0:T(8,128)(2,1)} %get-tuple-element.66.rest_0_), channel_id=1, source_target_pairs={{0,24},{1,25},{2,26},{3,27},{4,28},{5,29},{6,30},{7,31},{8,0},{9,1... | collective-permute-start | bytes 983048 | tf_op jit(solution)/shard_map/ppermute | solution.py:316
  7.7 3.0 %collective-permute-start.3 = (bf16[160,1024]{1,0:T(8,128)(2,1)}, bf16[160,1024]{1,0:T(8,128)(2,1)}, u32[]{:S(2)}, u32[]{:S(2)}) collective-permute-start(bf16[160,1024]{1,0:T(8,128)(2,1)} %get-tuple-element.82.rest_0_), channel_id=1, source_target_pairs={{0,6},{1,7},{2,0},{3,1},{4,2},{5,3},{6,4},{7,5},{8,14},{9,15},{10,... | collective-permute-start | bytes 983048 | tf_op jit(solution)/shard_map/ppermute | solution.py:316
  11.4 9.4 %collective-permute-done.rest_2_ = bf16[160,1024]{1,0:T(8,128)(2,1)} collective-permute-done((bf16[160,1024]{1,0:T(8,128)(2,1)}, bf16[160,1024]{1,0:T(8,128)(2,1)}, u32[]{:S(2)}, u32[]{:S(2)}) %collective-permute-start) | collective-permute-done | bytes 327712 | tf_op jit(solution)/shard_map/ppermute | solution.py:316
  22.4 6.9 %prep.1 = (f32[4,32,4,16,128]{4,3,2,1,0:T(8,128)S(1)}, s32[4,8,16,128]{3,2,1,0:T(8,128)S(1)}, s32[4,16,128]{2,1,0:T(8,128)S(1)}) custom-call(s32[4]{0:T(128)S(1)} %pad_add_fusion.pos_ref, s32[4,8,16384]{2,1,0:T(8,128)S(1)} %bitcast.31, s32[4,16384]{1,0:T(4,128)S(1)} %bitcast.33), custom_call_target="tpu_custom_call" | custom-call | flops 40000000 | bytes 9000000 | tf_op jit(solution)/shard_map/prep/pallas_call | solution.py:74
  31.5 3.0 %copy.25 = bf16[1024,1280]{0,1:T(8,128)(2,1)S(1)} copy(bf16[1024,1280]{1,0:T(8,128)(2,1)} %param.17) | data formatting | bytes 5242880 | tf_op args[7]
  34.5 2.5 %copy.24 = bf16[1024,24,16]{0,2,1:T(8,128)(2,1)} copy(bf16[1024,24,16]{0,1,2:T(8,128)(2,1)} %bitcast.36) | data formatting | bytes 1572864 | tf_op jit(solution)/shard_map/transpose | solution.py:358
  38.1 3.7 %collective-permute-start.6 = (bf16[160,1024]{1,0:T(8,128)(2,1)S(1)}, bf16[160,1024]{1,0:T(8,128)(2,1)S(1)}, u32[]{:S(2)}, u32[]{:S(2)}) collective-permute-start(bf16[160,1024]{1,0:T(8,128)(2,1)S(1)} %get-tuple-element.62.rest_0_), channel_id=1, source_target_pairs={{0,24},{1,25},{2,26},{3,27},{4,28},{5,29},{6,30},{7,31},{8,0},{9,1... | collective-permute-start | bytes 983048 | tf_op jit(solution)/shard_map/ppermute | solution.py:316
  43.9 12.1 %collective-permute-done.6.rest_2_ = bf16[160,1024]{1,0:T(8,128)(2,1)S(1)} collective-permute-done((bf16[160,1024]{1,0:T(8,128)(2,1)S(1)}, bf16[160,1024]{1,0:T(8,128)(2,1)S(1)}, u32[]{:S(2)}, u32[]{:S(2)}) %collective-permute-start.6) | collective-permute-done | bytes 327712 | tf_op jit(solution)/shard_map/ppermute | solution.py:316
  56.5 3.0 %collective-permute-done.8.rest_6_ = bf16[160,1024]{1,0:T(8,128)(2,1)S(1)} collective-permute-done((bf16[160,1024]{1,0:T(8,128)(2,1)S(1)}, bf16[160,1024]{1,0:T(8,128)(2,1)S(1)}, u32[]{:S(2)}, u32[]{:S(2)}) %collective-permute-start.8) | collective-permute-done | bytes 327712 | tf_op jit(solution)/shard_map/ppermute | solution.py:316
  63.4 8.7 %pool.4 = (bf16[4,160,128]{2,1,0:T(8,128)(2,1)S(1)}, bf16[4,160,128]{2,1,0:T(8,128)(2,1)S(1)}, bf16[4,160,128]{2,1,0:T(8,128)(2,1)S(1)}, bf16[4,160,128]{2,1,0:T(8,128)(2,1)S(1)}) custom-call(s32[16]{0:T(128)S(1)} %get-tuple-element.137.mask_ref, f32[4,32,4,16,128]{4,3,2,1,0:T(8,128)S(1)} %copy-done.4, s32[4,8,16,128]{3,2,1,0:T(8,128)S(1)} %get-tuple-element.65.lid_ref, ...), custom_call_target="tpu_custom_call" | custom-call | flops 8589934592 | bytes 5000000 | tf_op jit(solution)/shard_map/pool/pallas_call | solution.py:185
  75.7 3.2 %collective-permute-start.14 = (bf16[4,160,128]{2,1,0:T(8,128)(2,1)S(1)}, bf16[4,160,128]{2,1,0:T(8,128)(2,1)S(1)}, u32[]{:S(2)}, u32[]{:S(2)}) collective-permute-start(bf16[4,160,128]{2,1,0:T(8,128)(2,1)S(1)} %get-tuple-element.76), channel_id=1, source_target_pairs={{0,4},{1,5},{2,6},{3,7},{4,0},{5,1},{6,2},{7,3},{8,12},{9,13},{10,... | collective-permute-start | bytes 491528 | tf_op jit(solution)/shard_map/ppermute | solution.py:327
  79.4 8.7 %pool.5 = (bf16[4,160,128]{2,1,0:T(8,128)(2,1)S(1)}, bf16[4,160,128]{2,1,0:T(8,128)(2,1)S(1)}, bf16[4,160,128]{2,1,0:T(8,128)(2,1)S(1)}, bf16[4,160,128]{2,1,0:T(8,128)(2,1)S(1)}) custom-call(s32[16]{0:T(128)S(1)} %get-tuple-element.81.mask_ref, f32[4,32,4,16,128]{4,3,2,1,0:T(8,128)S(1)} %copy-done.4, s32[4,8,16,128]{3,2,1,0:T(8,128)S(1)} %get-tuple-element.65.lid_ref, ...), custom_call_target="tpu_custom_call" | custom-call | flops 8589934592 | bytes 5000000 | tf_op jit(solution)/shard_map/pool/pallas_call | solution.py:185
  90.0 4.9 %collective-permute-done.13 = bf16[4,160,128]{2,1,0:T(8,128)(2,1)S(1)} collective-permute-done((bf16[4,160,128]{2,1,0:T(8,128)(2,1)S(1)}, bf16[4,160,128]{2,1,0:T(8,128)(2,1)S(1)}, u32[]{:S(2)}, u32[]{:S(2)}) %collective-permute-start.13) | collective-permute-done | bytes 163872 | tf_op jit(solution)/shard_map/ppermute | solution.py:327
  96.9 2.5 %collective-permute-start.24 = (bf16[4,160,128]{2,1,0:T(8,128)(2,1)S(1)}, bf16[4,160,128]{2,1,0:T(8,128)(2,1)S(1)}, u32[]{:S(2)}, u32[]{:S(2)}) collective-permute-start(bf16[4,160,128]{2,1,0:T(8,128)(2,1)S(1)} %get-tuple-element.92), channel_id=1, source_target_pairs={{0,16},{1,17},{2,18},{3,19},{4,20},{5,21},{6,22},{7,23},{8,24},{9,... | collective-permute-start | bytes 491528 | tf_op jit(solution)/shard_map/ppermute | solution.py:327
  99.5 6.9 %collective-permute-done.23 = bf16[4,160,128]{2,1,0:T(8,128)(2,1)S(1)} collective-permute-done((bf16[4,160,128]{2,1,0:T(8,128)(2,1)S(1)}, bf16[4,160,128]{2,1,0:T(8,128)(2,1)S(1)}, u32[]{:S(2)}, u32[]{:S(2)}) %collective-permute-start.23) | collective-permute-done | bytes 163872 | tf_op jit(solution)/shard_map/ppermute | solution.py:327
  107.6 5.4 %collective-permute-done.25 = bf16[4,160,128]{2,1,0:T(8,128)(2,1)S(1)} collective-permute-done((bf16[4,160,128]{2,1,0:T(8,128)(2,1)S(1)}, bf16[4,160,128]{2,1,0:T(8,128)(2,1)S(1)}, u32[]{:S(2)}, u32[]{:S(2)}) %collective-permute-start.25) | collective-permute-done | bytes 163872 | tf_op jit(solution)/shard_map/ppermute | solution.py:327
  115.1 8.6 %pool.6 = (bf16[4,160,128]{2,1,0:T(8,128)(2,1)S(1)}, bf16[4,160,128]{2,1,0:T(8,128)(2,1)S(1)}, bf16[4,160,128]{2,1,0:T(8,128)(2,1)S(1)}, bf16[4,160,128]{2,1,0:T(8,128)(2,1)S(1)}) custom-call(s32[16]{0:T(128)S(1)} %get-tuple-element.95.mask_ref, f32[4,32,4,16,128]{4,3,2,1,0:T(8,128)S(1)} %copy-done.4, s32[4,8,16,128]{3,2,1,0:T(8,128)S(1)} %copy-done.6, ...), custom_call_target="tpu_custom_call" | custom-call | flops 8589934592 | bytes 5000000 | tf_op jit(solution)/shard_map/pool/pallas_call | solution.py:185
  123.8 7.9 %pool.7 = (bf16[4,160,128]{2,1,0:T(8,128)(2,1)S(1)}, bf16[4,160,128]{2,1,0:T(8,128)(2,1)S(1)}, bf16[4,160,128]{2,1,0:T(8,128)(2,1)S(1)}, bf16[4,160,128]{2,1,0:T(8,128)(2,1)S(1)}) custom-call(s32[16]{0:T(128)S(1)} %get-tuple-element.107.mask_ref, f32[4,32,4,16,128]{4,3,2,1,0:T(8,128)S(1)} %copy-done.4, s32[4,8,16,128]{3,2,1,0:T(8,128)S(1)} %copy-done.6, ...), custom_call_target="tpu_custom_call" | custom-call | flops 8589934592 | bytes 5000000 | tf_op jit(solution)/shard_map/pool/pallas_call | solution.py:185
  131.8 3.0 %collective-permute-start.41 = (bf16[4,160,128]{2,1,0:T(8,128)(2,1)S(1)}, bf16[4,160,128]{2,1,0:T(8,128)(2,1)S(1)}, u32[]{:S(2)}, u32[]{:S(2)}) collective-permute-start(bf16[4,160,128]{2,1,0:T(8,128)(2,1)S(1)} %get-tuple-element.113), channel_id=1, source_target_pairs={{0,16},{1,17},{2,18},{3,19},{4,20},{5,21},{6,22},{7,23},{8,24},{9,... | collective-permute-start | bytes 491528 | tf_op jit(solution)/shard_map/ppermute | solution.py:327
  137.4 2.5 %collective-permute-start.31 = (bf16[4,160,128]{2,1,0:T(8,128)(2,1)S(1)}, bf16[4,160,128]{2,1,0:T(8,128)(2,1)S(1)}, u32[]{:S(2)}, u32[]{:S(2)}) collective-permute-start(bf16[4,160,128]{2,1,0:T(8,128)(2,1)S(1)} %get-tuple-element.105), channel_id=1, source_target_pairs={{0,4},{1,5},{2,6},{3,7},{4,0},{5,1},{6,2},{7,3},{8,12},{9,13},{10,... | collective-permute-start | bytes 491528 | tf_op jit(solution)/shard_map/ppermute | solution.py:327
  148.8 4.2 %collective-permute-start.35 = (bf16[3,160,128]{2,1,0:T(8,128)(2,1)}, bf16[3,160,128]{2,1,0:T(8,128)(2,1)}, u32[]{:S(2)}, u32[]{:S(2)}) collective-permute-start(bf16[3,160,128]{2,1,0:T(8,128)(2,1)} %pad_maximum_fusion.3), channel_id=1, source_target_pairs={{0,96},{32,0},{64,32},{96,64},{1,97},{33,1},{65,33},{97,65},{2,98}... | collective-permute-start | bytes 368648 | tf_op jit(solution)/shard_map/ppermute | solution.py:384
  160.4 2.6 %collective-permute-start.45 = (bf16[1,160,128]{2,1,0:T(8,128)(2,1)}, bf16[1,160,128]{2,1,0:T(8,128)(2,1)S(1)}, u32[]{:S(2)}, u32[]{:S(2)}) collective-permute-start(bf16[1,160,128]{2,1,0:T(8,128)(2,1)} %get-tuple-element.121), channel_id=1, source_target_pairs={{0,96},{32,0},{64,32},{96,64},{1,97},{33,1},{65,33},{97,65},{2,98}... | collective-permute-start | bytes 122888 | tf_op jit(solution)/shard_map/ppermute | solution.py:384
  165.6 5.4 %tail.1 = bf16[16,160,128]{2,1,0:T(8,128)(2,1)} custom-call(s32[1]{0:T(128)} %bitcast.host_ref, s32[16]{0:T(128)S(1)} %copy-done.2, f32[24,16]{1,0:T(8,128)S(1)} %copy.27.proj_ref, f32[8,16]{1,0:T(8,128)S(1)} %convert_element_type.67.compress_ref, bf16[3,160,128]{2,1,0:T(8,128)(2,1)S(1)} %pad_maximum_fusion.rest_0_, ...), custom_call_target="tpu_custom_call" | custom-call | flops 1000000000 | bytes 8000000 | tf_op jit(solution)/shard_map/tail/pallas_call | solution.py:282
  (117 shorter events, 46.3 us)
Async XLA Ops:
  2.4 18.4 %collective-permute-start = (bf16[160,1024]{1,0:T(8,128)(2,1)}, bf16[160,1024]{1,0:T(8,128)(2,1)}, u32[]{:S(2)}, u32[]{:S(2)}) collective-permute-start(bf16[160,1024]{1,0:T(8,128)(2,1)} %get-tuple-element.66.rest_0_), channel_id=1, source_target_pairs={{0,24},{1,25},{2,26},{3,27},{4,28},{5,29},{6,30},{7,31},{8,0},{9,1... | collective-permute-start | bytes 983048 | tf_op jit(solution)/shard_map/ppermute | solution.py:316
  6.5 30.5 %collective-permute-start.1 = (bf16[160,1024]{1,0:T(8,128)(2,1)}, bf16[160,1024]{1,0:T(8,128)(2,1)}, u32[]{:S(2)}, u32[]{:S(2)}) collective-permute-start(bf16[160,1024]{1,0:T(8,128)(2,1)} %get-tuple-element.66.rest_0_), channel_id=1, source_target_pairs={{0,16},{1,17},{2,18},{3,19},{4,20},{5,21},{6,22},{7,23},{8,24},{9,... | collective-permute-start | bytes 983048 | tf_op jit(solution)/shard_map/ppermute | solution.py:316
  6.5 30.5 %collective-permute-start.2 = (bf16[160,1024]{1,0:T(8,128)(2,1)}, bf16[160,1024]{1,0:T(8,128)(2,1)}, u32[]{:S(2)}, u32[]{:S(2)}) collective-permute-start(bf16[160,1024]{1,0:T(8,128)(2,1)} %get-tuple-element.66.rest_0_), channel_id=1, source_target_pairs={{0,8},{1,9},{2,10},{3,11},{4,12},{5,13},{6,14},{7,15},{8,16},{9,17... | collective-permute-start | bytes 983048 | tf_op jit(solution)/shard_map/ppermute | solution.py:316
  7.7 29.2 %collective-permute-start.3 = (bf16[160,1024]{1,0:T(8,128)(2,1)}, bf16[160,1024]{1,0:T(8,128)(2,1)}, u32[]{:S(2)}, u32[]{:S(2)}) collective-permute-start(bf16[160,1024]{1,0:T(8,128)(2,1)} %get-tuple-element.82.rest_0_), channel_id=1, source_target_pairs={{0,6},{1,7},{2,0},{3,1},{4,2},{5,3},{6,4},{7,5},{8,14},{9,15},{10,... | collective-permute-start | bytes 983048 | tf_op jit(solution)/shard_map/ppermute | solution.py:316
  10.7 26.2 %collective-permute-start.4 = (bf16[160,1024]{1,0:T(8,128)(2,1)}, bf16[160,1024]{1,0:T(8,128)(2,1)}, u32[]{:S(2)}, u32[]{:S(2)}) collective-permute-start(bf16[160,1024]{1,0:T(8,128)(2,1)} %get-tuple-element.82.rest_0_), channel_id=1, source_target_pairs={{0,4},{1,5},{2,6},{3,7},{4,0},{5,1},{6,2},{7,3},{8,12},{9,13},{10,... | collective-permute-start | bytes 983048 | tf_op jit(solution)/shard_map/ppermute | solution.py:316
  20.8 16.2 %collective-permute-start.5 = (bf16[160,1024]{1,0:T(8,128)(2,1)}, bf16[160,1024]{1,0:T(8,128)(2,1)}, u32[]{:S(2)}, u32[]{:S(2)}) collective-permute-start(bf16[160,1024]{1,0:T(8,128)(2,1)} %get-tuple-element.82.rest_0_), channel_id=1, source_target_pairs={{0,2},{1,3},{2,4},{3,5},{4,6},{5,7},{6,0},{7,1},{8,10},{9,11},{10,... | collective-permute-start | bytes 983048 | tf_op jit(solution)/shard_map/ppermute | solution.py:316
  38.1 17.9 %collective-permute-start.6 = (bf16[160,1024]{1,0:T(8,128)(2,1)S(1)}, bf16[160,1024]{1,0:T(8,128)(2,1)S(1)}, u32[]{:S(2)}, u32[]{:S(2)}) collective-permute-start(bf16[160,1024]{1,0:T(8,128)(2,1)S(1)} %get-tuple-element.62.rest_0_), channel_id=1, source_target_pairs={{0,24},{1,25},{2,26},{3,27},{4,28},{5,29},{6,30},{7,31},{8,0},{9,1... | collective-permute-start | bytes 983048 | tf_op jit(solution)/shard_map/ppermute | solution.py:316
  41.8 14.3 %collective-permute-start.7 = (bf16[160,1024]{1,0:T(8,128)(2,1)S(1)}, bf16[160,1024]{1,0:T(8,128)(2,1)S(1)}, u32[]{:S(2)}, u32[]{:S(2)}) collective-permute-start(bf16[160,1024]{1,0:T(8,128)(2,1)S(1)} %get-tuple-element.62.rest_0_), channel_id=1, source_target_pairs={{0,16},{1,17},{2,18},{3,19},{4,20},{5,21},{6,22},{7,23},{8,24},{9,... | collective-permute-start | bytes 983048 | tf_op jit(solution)/shard_map/ppermute | solution.py:316
  41.8 17.7 %collective-permute-start.8 = (bf16[160,1024]{1,0:T(8,128)(2,1)S(1)}, bf16[160,1024]{1,0:T(8,128)(2,1)S(1)}, u32[]{:S(2)}, u32[]{:S(2)}) collective-permute-start(bf16[160,1024]{1,0:T(8,128)(2,1)S(1)} %get-tuple-element.62.rest_0_), channel_id=1, source_target_pairs={{0,8},{1,9},{2,10},{3,11},{4,12},{5,13},{6,14},{7,15},{8,16},{9,17... | collective-permute-start | bytes 983048 | tf_op jit(solution)/shard_map/ppermute | solution.py:316
  43.4 28.8 %collective-permute-start.19 = (bf16[160,1024]{1,0:T(8,128)(2,1)}, bf16[160,1024]{1,0:T(8,128)(2,1)S(1)}, u32[]{:S(2)}, u32[]{:S(2)}) collective-permute-start(bf16[160,1024]{1,0:T(8,128)(2,1)} %get-tuple-element.82.rest_0_), channel_id=1, source_target_pairs={{0,1},{1,0},{2,3},{3,2},{4,5},{5,4},{6,7},{7,6},{8,9},{9,8},{10,11... | collective-permute-start | bytes 983048 | tf_op jit(solution)/shard_map/ppermute | solution.py:321
  43.4 30.8 %collective-permute-start.20 = (bf16[160,1024]{1,0:T(8,128)(2,1)}, bf16[160,1024]{1,0:T(8,128)(2,1)S(1)}, u32[]{:S(2)}, u32[]{:S(2)}) collective-permute-start(bf16[160,1024]{1,0:T(8,128)(2,1)} %collective-permute-done.3.rest_2_), channel_id=1, source_target_pairs={{0,1},{1,0},{2,3},{3,2},{4,5},{5,4},{6,7},{7,6},{8,9},{9,8},{10,11... | collective-permute-start | bytes 983048 | tf_op jit(solution)/shard_map/ppermute | solution.py:321
  56.0 18.9 %collective-permute-start.21 = (bf16[160,1024]{1,0:T(8,128)(2,1)}, bf16[160,1024]{1,0:T(8,128)(2,1)S(1)}, u32[]{:S(2)}, u32[]{:S(2)}) collective-permute-start(bf16[160,1024]{1,0:T(8,128)(2,1)} %collective-permute-done.4.rest_4_), channel_id=1, source_target_pairs={{0,1},{1,0},{2,3},{3,2},{4,5},{5,4},{6,7},{7,6},{8,9},{9,8},{10,11... | collective-permute-start | bytes 983048 | tf_op jit(solution)/shard_map/ppermute | solution.py:321
  56.0 19.7 %collective-permute-start.22 = (bf16[160,1024]{1,0:T(8,128)(2,1)}, bf16[160,1024]{1,0:T(8,128)(2,1)S(1)}, u32[]{:S(2)}, u32[]{:S(2)}) collective-permute-start(bf16[160,1024]{1,0:T(8,128)(2,1)} %collective-permute-done.5.rest_6_), channel_id=1, source_target_pairs={{0,1},{1,0},{2,3},{3,2},{4,5},{5,4},{6,7},{7,6},{8,9},{9,8},{10,11... | collective-permute-start | bytes 983048 | tf_op jit(solution)/shard_map/ppermute | solution.py:321
  59.5 19.4 %collective-permute-start.16 = (bf16[160,1024]{1,0:T(8,128)(2,1)S(1)}, bf16[160,1024]{1,0:T(8,128)(2,1)S(1)}, u32[]{:S(2)}, u32[]{:S(2)}) collective-permute-start(bf16[160,1024]{1,0:T(8,128)(2,1)S(1)} %get-tuple-element.78.rest_0_), channel_id=1, source_target_pairs={{0,6},{1,7},{2,0},{3,1},{4,2},{5,3},{6,4},{7,5},{8,14},{9,15},{10,... | collective-permute-start | bytes 983048 | tf_op jit(solution)/shard_map/ppermute | solution.py:316
  72.1 16.0 %collective-permute-start.17 = (bf16[160,1024]{1,0:T(8,128)(2,1)S(1)}, bf16[160,1024]{1,0:T(8,128)(2,1)S(1)}, u32[]{:S(2)}, u32[]{:S(2)}) collective-permute-start(bf16[160,1024]{1,0:T(8,128)(2,1)S(1)} %get-tuple-element.78.rest_0_), channel_id=1, source_target_pairs={{0,4},{1,5},{2,6},{3,7},{4,0},{5,1},{6,2},{7,3},{8,12},{9,13},{10,... | collective-permute-start | bytes 983048 | tf_op jit(solution)/shard_map/ppermute | solution.py:316
  74.2 15.8 %collective-permute-start.18 = (bf16[160,1024]{1,0:T(8,128)(2,1)S(1)}, bf16[160,1024]{1,0:T(8,128)(2,1)S(1)}, u32[]{:S(2)}, u32[]{:S(2)}) collective-permute-start(bf16[160,1024]{1,0:T(8,128)(2,1)S(1)} %get-tuple-element.78.rest_0_), channel_id=1, source_target_pairs={{0,2},{1,3},{2,4},{3,5},{4,6},{5,7},{6,0},{7,1},{8,10},{9,11},{10,... | collective-permute-start | bytes 983048 | tf_op jit(solution)/shard_map/ppermute | solution.py:316
  74.9 20.0 %collective-permute-start.13 = (bf16[4,160,128]{2,1,0:T(8,128)(2,1)S(1)}, bf16[4,160,128]{2,1,0:T(8,128)(2,1)S(1)}, u32[]{:S(2)}, u32[]{:S(2)}) collective-permute-start(bf16[4,160,128]{2,1,0:T(8,128)(2,1)S(1)} %get-tuple-element.75), channel_id=1, source_target_pairs={{0,2},{1,3},{2,4},{3,5},{4,6},{5,7},{6,0},{7,1},{8,10},{9,11},{10,... | collective-permute-start | bytes 491528 | tf_op jit(solution)/shard_map/ppermute | solution.py:327
  75.7 21.2 %collective-permute-start.14 = (bf16[4,160,128]{2,1,0:T(8,128)(2,1)S(1)}, bf16[4,160,128]{2,1,0:T(8,128)(2,1)S(1)}, u32[]{:S(2)}, u32[]{:S(2)}) collective-permute-start(bf16[4,160,128]{2,1,0:T(8,128)(2,1)S(1)} %get-tuple-element.76), channel_id=1, source_target_pairs={{0,4},{1,5},{2,6},{3,7},{4,0},{5,1},{6,2},{7,3},{8,12},{9,13},{10,... | collective-permute-start | bytes 491528 | tf_op jit(solution)/shard_map/ppermute | solution.py:327
  78.9 18.0 %collective-permute-start.15 = (bf16[4,160,128]{2,1,0:T(8,128)(2,1)S(1)}, bf16[4,160,128]{2,1,0:T(8,128)(2,1)S(1)}, u32[]{:S(2)}, u32[]{:S(2)}) collective-permute-start(bf16[4,160,128]{2,1,0:T(8,128)(2,1)S(1)} %get-tuple-element.77), channel_id=1, source_target_pairs={{0,6},{1,7},{2,0},{3,1},{4,2},{5,3},{6,4},{7,5},{8,14},{9,15},{10,... | collective-permute-start | bytes 491528 | tf_op jit(solution)/shard_map/ppermute | solution.py:327
  88.1 25.0 %collective-permute-start.26 = (bf16[160,1024]{1,0:T(8,128)(2,1)S(1)}, bf16[160,1024]{1,0:T(8,128)(2,1)S(1)}, u32[]{:S(2)}, u32[]{:S(2)}) collective-permute-start(bf16[160,1024]{1,0:T(8,128)(2,1)S(1)} %get-tuple-element.62.rest_0_), channel_id=1, source_target_pairs={{0,1},{1,0},{2,3},{3,2},{4,5},{5,4},{6,7},{7,6},{8,9},{9,8},{10,11... | collective-permute-start | bytes 983048 | tf_op jit(solution)/shard_map/ppermute | solution.py:321
  90.0 23.7 %collective-permute-start.27 = (bf16[160,1024]{1,0:T(8,128)(2,1)S(1)}, bf16[160,1024]{1,0:T(8,128)(2,1)S(1)}, u32[]{:S(2)}, u32[]{:S(2)}) collective-permute-start(bf16[160,1024]{1,0:T(8,128)(2,1)S(1)} %collective-permute-done.6.rest_2_), channel_id=1, source_target_pairs={{0,1},{1,0},{2,3},{3,2},{4,5},{5,4},{6,7},{7,6},{8,9},{9,8},{10,11... | collective-permute-start | bytes 983048 | tf_op jit(solution)/shard_map/ppermute | solution.py:321
  94.8 18.9 %collective-permute-start.28 = (bf16[160,1024]{1,0:T(8,128)(2,1)S(1)}, bf16[160,1024]{1,0:T(8,128)(2,1)S(1)}, u32[]{:S(2)}, u32[]{:S(2)}) collective-permute-start(bf16[160,1024]{1,0:T(8,128)(2,1)S(1)} %collective-permute-done.7.rest_4_), channel_id=1, source_target_pairs={{0,1},{1,0},{2,3},{3,2},{4,5},{5,4},{6,7},{7,6},{8,9},{9,8},{10,11... | collective-permute-start | bytes 983048 | tf_op jit(solution)/shard_map/ppermute | solution.py:321
  143.4 16.9 %collective-permute-start.43 = (bf16[1,160,128]{2,1,0:T(8,128)(2,1)}, bf16[1,160,128]{2,1,0:T(8,128)(2,1)}, u32[]{:S(2)}, u32[]{:S(2)}) collective-permute-start(bf16[1,160,128]{2,1,0:T(8,128)(2,1)} %get-tuple-element.123), channel_id=1, source_target_pairs={{0,32},{32,64},{64,96},{96,0},{1,33},{33,65},{65,97},{97,1},{2,34}... | collective-permute-start | bytes 122888 | tf_op jit(solution)/shard_map/ppermute | solution.py:384
  148.8 16.2 %collective-permute-start.35 = (bf16[3,160,128]{2,1,0:T(8,128)(2,1)}, bf16[3,160,128]{2,1,0:T(8,128)(2,1)}, u32[]{:S(2)}, u32[]{:S(2)}) collective-permute-start(bf16[3,160,128]{2,1,0:T(8,128)(2,1)} %pad_maximum_fusion.3), channel_id=1, source_target_pairs={{0,96},{32,0},{64,32},{96,64},{1,97},{33,1},{65,33},{97,65},{2,98}... | collective-permute-start | bytes 368648 | tf_op jit(solution)/shard_map/ppermute | solution.py:384
  (32 other events, 352.4 us)

commit v3 on v1

--- a/solution.py
+++ b/solution.py
@@ -13,13 +13,13 @@
 GATHER = 8
 BLOCKS = GATHER * ROWS_DEV // SUB
 BAG_BLOCKS = 16
-STEPS = BAG_BLOCKS // 2
+PAIR = 2 * LANES
 
 
 def prep_kernel(pos_ref, idx_ref, len_ref, keys_ref, lid_ref, mask_ref):
     host, z, y, core = pos_ref[0], pos_ref[1], pos_ref[2], pos_ref[3]
     table = pl.program_id(0)
-    over_z = table % 2 == 0
+    over_z = table < 2
     slot = lax.broadcasted_iota(jnp.int32, (8, LANES), 0)
     pick = lax.broadcasted_iota(jnp.int32, (len_ref.shape[0], LANES), 0)
     for n in range(BAG_BLOCKS):
@@ -37,7 +37,9 @@
         )
         at_z, at_y, at_core = v >> 13, (v >> 11) & 3, (v >> 10) & 1
         here = jnp.where(over_z, at_y - y, at_z - z) == 0
-        shard = jnp.where(over_z, (at_z - z) & 3, (at_y - y) & 3) * 2 + (at_core ^ core)
+        away = jnp.where(over_z, (at_z - z) & 3, (at_y - y) & 3)
+        other = at_core ^ core
+        shard = jnp.where(away == 0, other, away + 1 + 3 * other)
         local = shard * ROWS_DEV + (v & (ROWS_DEV - 1))
         local = jnp.where(here & (slot < used), local, -1)
         for s in range(8):
@@ -97,13 +99,21 @@
     )(pos, idx, lens)
 
 
-def pool_kernel(mask_ref, keys_ref, lid_ref, *rest):
-    tabs = rest[:GATHER]
-    outs = rest[GATHER : GATHER + 4]
-    acc, counts, extra = rest[GATHER + 4 :]
-    step = pl.program_id(0)
+def pool_kernel(first_shard, n_shards, has_base, is_last, table0, *refs):
+    mask_ref, keys_ref, lid_ref = refs[:3]
+    tabs = refs[3 : 3 + n_shards]
+    refs = refs[3 + n_shards :]
+    if has_base:
+        base_ref, refs = refs[0], refs[1:]
+    if is_last:
+        outs, (sums, counts, extra) = refs[:4], refs[4:]
+    else:
+        sums, counts, extra = refs
+    table, step = pl.program_id(0), pl.program_id(1)
+    first_block = first_shard * (ROWS_DEV // SUB)
+    n_blocks = n_shards * (ROWS_DEV // SUB)
     row_ids = [
-        (lax.broadcasted_iota(jnp.int32, (16, LANES), 0) + c * 16)
+        (lax.broadcasted_iota(jnp.int32, (16, PAIR), 0) + c * 16)
         .astype(jnp.float32)
         .astype(jnp.bfloat16)
         for c in range(SUB // 16)
@@ -112,97 +122,135 @@
     def wide(x):
         return jnp.broadcast_to(x, (16, LANES)).astype(jnp.bfloat16)
 
-    for blk in range(BLOCKS):
-        for half in range(2):
-            row = pl.ds(2 * step + half, 1)
-            k1, m1, k2, m2 = (wide(keys_ref[0, blk, v, row, :]) for v in range(4))
+    for part in range(2):
+        bag = 4 * step + 2 * part
+        for blk in range(n_blocks):
+            k1, m1, k2, m2 = (
+                jnp.concatenate(
+                    [
+                        wide(keys_ref[0, first_block + blk, v, pl.ds(bag + half, 1), :])
+                        for half in range(2)
+                    ],
+                    axis=1,
+                )
+                for v in range(4)
+            )
             for c in range(SUB // 16):
-                counts[
-                    blk * SUB + c * 16 : blk * SUB + (c + 1) * 16,
-                    half * LANES : (half + 1) * LANES,
-                ] = jnp.where(
+                counts[part, blk * SUB + c * 16 : blk * SUB + (c + 1) * 16, :] = jnp.where(
                     k1 == row_ids[c], m1, jnp.where(k2 == row_ids[c], m2, jnp.bfloat16(0))
                 )
-    total = None
-    for g in range(GATHER):
-        part = jnp.dot(
-            tabs[g][...],
-            counts[g * ROWS_DEV : (g + 1) * ROWS_DEV, :],
-            preferred_element_type=jnp.float32,
-        )
-        total = part if total is None else total + part
-    acc[...] = total
-
-    mask = mask_ref[2 * step] | mask_ref[2 * step + 1]
-
-    @pl.when(mask != 0)
-    def _():
-        def fix(blk, carry):
-            @pl.when(((mask >> blk) & 1) == 1)
-            def _():
-                for half in range(2):
-                    row = pl.ds(2 * step + half, 1)
-                    k1 = keys_ref[0, blk, 0, row, :]
-                    k2 = keys_ref[0, blk, 2, row, :]
-                    left = []
-                    for s in range(8):
-                        x = lid_ref[0, s, row, :]
-                        low = jnp.where(
-                            (x >> 8) == blk, (x & (SUB - 1)).astype(jnp.float32), -1.0
-                        )
-                        left.append(wide(jnp.where((low == k1) | (low == k2), -1.0, low)))
-                    for c in range(SUB // 16):
-                        n = jnp.zeros((16, LANES), jnp.bfloat16)
-                        for k in left:
-                            n = n + jnp.where(k == row_ids[c], jnp.bfloat16(1), jnp.bfloat16(0))
-                        extra[c * 16 : (c + 1) * 16, half * LANES : (half + 1) * LANES] = n
-                columns = pl.ds(pl.multiple_of((blk & 3) * SUB, SUB), SUB)
-                for g in range(GATHER):
-
-                    @pl.when((blk >> 2) == g)
-                    def _(g=g):
-                        acc[...] += jnp.dot(
-                            tabs[g][:, columns], extra[...], preferred_element_type=jnp.float32
-                        )
-
-            return carry
-
-        lax.fori_loop(0, BLOCKS, fix, 0)
-
-    result = acc[...].astype(jnp.bfloat16)
-    place = (step % 2) * 2
-    for d in range(4):
-
-        @pl.when(step // 2 == d)
-        def _(d=d):
-            outs[d][pl.ds(place, 1), :, :] = result[None, :, :LANES]
-            outs[d][pl.ds(place + 1, 1), :, :] = result[None, :, LANES:]
-
-
-def pool(table, mask, keys, lids, shards):
-    emb, rows = shards[0].shape
+        total = base_ref[0, 0, part] if has_base else None
+        for g in range(n_shards):
+            product = jnp.dot(
+                tabs[g][0],
+                counts[part, g * ROWS_DEV : (g + 1) * ROWS_DEV, :],
+                preferred_element_type=jnp.float32,
+            )
+            total = product if total is None else total + product
+        sums[0, 0, part] = total
+
+    stage_bits = ((1 << n_blocks) - 1) << first_block
+    stage_bits = stage_bits - (1 << 32) if stage_bits >= 1 << 31 else stage_bits
+    for part in range(2):
+        bag = 4 * step + 2 * part
+        mask = mask_ref[table0 + table, bag] | mask_ref[table0 + table, bag + 1]
+
+        @pl.when((mask & jnp.int32(stage_bits)) != 0)
+        def _(part=part, bag=bag, mask=mask):
+            def fix(at, carry):
+                blk = first_block + at
+
+                @pl.when(((mask >> blk) & 1) == 1)
+                def _():
+                    for half in range(2):
+                        row = pl.ds(bag + half, 1)
+                        k1 = keys_ref[0, blk, 0, row, :]
+                        k2 = keys_ref[0, blk, 2, row, :]
+                        left = []
+                        for s in range(8):
+                            x = lid_ref[0, s, row, :]
+                            low = jnp.where(
+                                (x >> 8) == blk, (x & (SUB - 1)).astype(jnp.float32), -1.0
+                            )
+                            left.append(wide(jnp.where((low == k1) | (low == k2), -1.0, low)))
+                        for c in range(SUB // 16):
+                            n = jnp.zeros((16, LANES), jnp.bfloat16)
+                            for k in left:
+                                n = n + jnp.where(
+                                    k == row_ids[c][:, :LANES], jnp.bfloat16(1), jnp.bfloat16(0)
+                                )
+                            extra[c * 16 : (c + 1) * 16, half * LANES : (half + 1) * LANES] = n
+                    columns = pl.ds(pl.multiple_of((at & 3) * SUB, SUB), SUB)
+                    for g in range(n_shards):
+
+                        @pl.when((at >> 2) == g)
+                        def _(g=g):
+                            sums[0, 0, part] += jnp.dot(
+                                tabs[g][0, :, columns],
+                                extra[...],
+                                preferred_element_type=jnp.float32,
+                            )
+
+                return carry
+
+            lax.fori_loop(0, n_blocks, fix, 0)
+
+    if is_last:
+        for d in range(4):
+
+            @pl.when(step == d)
+            def _(d=d):
+                for part in range(2):
+                    result = sums[0, 0, part].astype(jnp.bfloat16)
+                    outs[d][0, 2 * part] = result[:, :LANES]
+                    outs[d][0, 2 * part + 1] = result[:, LANES:]
+
+
+def pool(first_shard, tables, masks, keys, lids, shards, base, is_last, name):
+    n_tables = len(tables)
+    table0 = tables[0]
+    n_shards = len(shards)
+    _, emb, rows = shards[0].shape
+    sums_block = (1, 1, 2, emb, PAIR)
+    sums_spec = pl.BlockSpec(sums_block, lambda j, i: (j, i, 0, 0, 0))
+    in_specs = [
+        pl.BlockSpec(memory_space=pltpu.SMEM),
+        pl.BlockSpec((1,) + keys.shape[1:], lambda j, i: (table0 + j, 0, 0, 0, 0)),
+        pl.BlockSpec((1,) + lids.shape[1:], lambda j, i: (table0 + j, 0, 0, 0)),
+    ] + [pl.BlockSpec((1, emb, rows), lambda j, i: (j, 0, 0))] * n_shards
+    args = [masks, keys, lids, *shards]
+    if base is not None:
+        from_table = base[1]
+        in_specs.append(pl.BlockSpec(sums_block, lambda j, i: (from_table + j, i, 0, 0, 0)))
+        args.append(base[0])
+    scratch = [
+        pltpu.VMEM((2, n_shards * rows, PAIR), jnp.bfloat16),
+        pltpu.VMEM((SUB, PAIR), jnp.bfloat16),
+    ]
+    if is_last:
+        out_specs = [pl.BlockSpec((1, 4, emb, LANES), lambda j, i: (j, 0, 0, 0))] * 4
+        out_shape = [jax.ShapeDtypeStruct((n_tables, 4, emb, LANES), jnp.bfloat16)] * 4
+        scratch = [pltpu.VMEM(sums_block, jnp.float32)] + scratch
+    else:
+        out_specs = sums_spec
+        out_shape = jax.ShapeDtypeStruct((n_tables, 4, 2, emb, PAIR), jnp.float32)
     return pl.pallas_call(
-        pool_kernel,
-        grid=(STEPS,),
-        in_specs=[
-            pl.BlockSpec(memory_space=pltpu.SMEM),
-            pl.BlockSpec((1,) + keys.shape[1:], lambda i: (table, 0, 0, 0, 0)),
-            pl.BlockSpec((1,) + lids.shape[1:], lambda i: (table, 0, 0, 0)),
-        ]
-        + [pl.BlockSpec((emb, rows), lambda i: (0, 0))] * GATHER,
-        out_specs=[pl.BlockSpec((4, emb, LANES), lambda i: (0, 0, 0))] * 4,
-        out_shape=[jax.ShapeDtypeStruct((4, emb, LANES), jnp.bfloat16)] * 4,
-        scratch_shapes=[
-            pltpu.VMEM((emb, 2 * LANES), jnp.float32),
-            pltpu.VMEM((GATHER * rows, 2 * LANES), jnp.bfloat16),
-            pltpu.VMEM((SUB, 2 * LANES), jnp.bfloat16),
-        ],
+        functools.partial(
+            pool_kernel, first_shard, n_shards, base is not None, is_last, table0
+        ),
+        grid=(n_tables, 4),
+        in_specs=in_specs,
+        out_specs=out_specs,
+        out_shape=out_shape,
+        scratch_shapes=scratch,
         compiler_params=pltpu.CompilerParams(vmem_limit_bytes=32 << 20),
         cost_estimate=pl.CostEstimate(
-            flops=2 * GATHER * rows * 2048 * 256, bytes_accessed=5_000_000, transcendentals=0
+            flops=2 * n_tables * n_shards * rows * 2048 * 256,
+            bytes_accessed=5_000_000,
+            transcendentals=0,
         ),
-        name="pool",
-    )(mask, keys, lids, *shards)
+        name=name,
+    )(*args)
 
 
 def tail_kernel(
@@ -212,14 +260,15 @@
     compress_ref,
     *rest,
 ):
-    parts = rest[:4]
-    fm_gain_ref, up_ref, down_ref, gain_ref, out_ref, emb, gram, summed = rest[4:]
+    parts = rest[:8]
+    fm_gain_ref, up_ref, down_ref, gain_ref, out_ref, emb, gram, summed = rest[8:]
     host = host_ref[0]
     for d in range(4):
         source = (host - d) & 3
         for j in range(4):
             at = order_ref[source * 4 + j]
-            emb[pl.ds(at, 1), :, :] = parts[d][j : j + 1, :, :].astype(jnp.float32)
+            part = parts[(j // 2) * 4 + d]
+            emb[pl.ds(at, 1), :, :] = part[j % 2 : j % 2 + 1, :, :].astype(jnp.float32)
     feats, width, lanes = emb.shape
     rank = proj_ref.shape[0]
 
@@ -279,7 +328,7 @@
     vmem = pl.BlockSpec(memory_space=pltpu.VMEM)
     return pl.pallas_call(
         tail_kernel,
-        in_specs=[smem] * 4 + [vmem] * 8,
+        in_specs=[smem] * 4 + [vmem] * 12,
         out_specs=vmem,
         out_shape=jax.ShapeDtypeStruct((feats, width, LANES), jnp.bfloat16),
         scratch_shapes=[
@@ -309,19 +358,23 @@
     return pairs
 
 
-def gather_shards(shard, axis):
-    near = [shard]
-    for rel in range(1, 4):
-        near.append(lax.ppermute(shard, "row", row_moves(axis, 4 - rel)))
-    far = [lax.ppermute(x, "row", row_moves("core", 1)) for x in near]
-    return [x for pair in zip(near, far) for x in pair]
+def near_shards(shard, axis):
+    return [lax.ppermute(shard, "row", row_moves(axis, 4 - rel)) for rel in range(1, 4)]
+
+
+def other_core(x):
+    return lax.ppermute(x, "row", row_moves("core", 1))
 
 
 def exchange(blocks, axis):
     total = blocks[0].astype(jnp.float32)
     for d in range(1, 4):
         total = total + lax.ppermute(blocks[d], "row", row_moves(axis, d)).astype(jnp.float32)
-    return total.astype(jnp.bfloat16)
+    total = total.astype(jnp.bfloat16)
+    return [total[:, 0]] + [
+        lax.ppermute(total[:, d], "hst", [(h, (h + d) % 4) for h in range(4)])
+        for d in range(1, 4)
+    ]
 
 
 def on_device(
@@ -345,36 +398,42 @@
     width = up_weight.shape[1]
 
     flipped = jnp.swapaxes(tables, 1, 2)
-    shards = [
-        gather_shards(flipped[j], "z" if j % 2 == 0 else "y") for j in range(n_tables)
-    ]
     keys, lids, masks = prep(pos, jnp.transpose(indices, (1, 2, 0)), lengths.T)
     masks = lax.reduce(masks, jnp.int32(0), lax.bitwise_or, (2,))
-    sums = []
-    for j in range(n_tables):
-        blocks = pool(j, masks[j], keys, lids, shards[j])
-        sums.append(exchange(blocks, "y" if j % 2 == 0 else "z"))
-
-    parts = []
-    for d in range(4):
-        block = jnp.stack([s[d] for s in sums])
-        if d:
-            block = lax.ppermute(block, "hst", [(h, (h + d) % 4) for h in range(4)])
-        parts.append(block)
     up = jnp.transpose(up_weight.reshape(feats, rank, width), (2, 1, 0)).reshape(
         width, rank * feats
     )
-    result = tail(
-        pos[:1],
+    small = (
         feature_order,
         proj_weight.astype(jnp.float32),
         compress_weight.astype(jnp.float32),
-        parts,
         fm_gain.reshape(feats, rank),
-        up,
-        down_weight.T,
         out_gain.T,
     )
+    masks, up, down, small = lax.optimization_barrier((masks, up, down_weight.T, small))
+    order, proj, compress, fm_gain, gain = small
+
+    own_far = other_core(flipped)
+    pairs = [(0, 1), (2, 3)]
+    axes = ["z", "y"]
+    near = [near_shards(flipped[2 * p : 2 * p + 2], axes[p]) for p in range(2)]
+    sums = pool(
+        0, (0, 1, 2, 3), masks, keys, lids, [flipped, own_far], None, False, "pool_own"
+    )
+    near, sums = lax.optimization_barrier((near, sums))
+    far = [[other_core(x) for x in near[p]] for p in range(2)]
+    parts = []
+    sums = [
+        pool(2, pairs[p], masks, keys, lids, near[p], (sums, 2 * p), False, "pool_near")
+        for p in range(2)
+    ]
+    far, sums = lax.optimization_barrier((far, sums))
+    for p in range(2):
+        blocks = pool(5, pairs[p], masks, keys, lids, far[p], (sums[p], 0), True, "pool_far")
+        if p == 0:
+            blocks, sums[1] = lax.optimization_barrier((blocks, sums[1]))
+        parts += exchange(blocks, axes[1 - p])
+    result = tail(pos[:1], order, proj, compress, parts, fm_gain, up, down, gain)
     return jnp.transpose(result, (2, 0, 1))
 
 

time: 175 us -> 145 us (0.83)
  Pallas kernels: 69.8 us -> 51.8 us
  starting transfers between devices: 46.5 us -> 33.4 us
  other arithmetic: 4.15 us -> 0.57 us
  waiting for transfers between devices: 32.1 us -> 34.9 us
    pallas_call x5 -> x6, Pallas kernels: 62.9 us -> 44.9 us  [the longest x5 39.4 us: pool(): pl.pallas_call(functools.partial(pool_kernel, first_shard, n_shards, base...]
    ppermute x12 -> x6, starting transfers between devices: 17.6 us -> 10.2 us  [exchange(): lax.ppermute(blocks[d], 'row', row_moves(axis, d)).astype(jnp.float32)]
    ppermute x31 -> x19, starting transfers between devices: 28.9 us -> 23.2 us  [the longest x6 12.3 us: near_shards(): lax.ppermute(shard, 'row', row_moves(axis, 4 - rel))]
    another operation x4 -> x0, other arithmetic: 2.88 us -> none  [on_device(): block = jnp.stack([s[d] for s in sums])]
    ppermute x12 -> x6, waiting for transfers between devices: 7.2 us -> 10 us  [exchange(): lax.ppermute(blocks[d], 'row', row_moves(axis, d)).astype(jnp.float32)]
    unnamed x38 -> x35, local copies, waits for them, and re-layouts: 14.6 us -> 14.3 us
    ppermute x31 -> x19, waiting for transfers between devices: 24.9 us -> 24.9 us  [the longest x6 20.7 us: near_shards(): lax.ppermute(shard, 'row', row_moves(axis, 4 - rel))]
  transfers between devices with their start and end apart: 43 -> 25, of which waited for: 9 -> 7; matrix products, arithmetic and copies ran while one was open for 7% -> 9% of each run, Pallas kernels for 37% -> 23%
where the time goes in v3:
time: 145 us; the launch traced here: 143 us
  Pallas kernels  51.8 us (36%)
  waiting for transfers between devices  34.9 us (24%)
  starting transfers between devices  33.4 us (23%)
  local copies, waits for them, and re-layouts  22.5 us (16%)
    pallas_call x5, Pallas kernels, pool(): pl.pallas_call(functools.partial(pool_kernel, first_shard, n_shards, base...  39.4 us
    ppermute x6, waiting for transfers between devices, near_shards(): lax.ppermute(shard, 'row', row_moves(axis, 4 - rel))  20.7 us
    unnamed x35, local copies, waits for them, and re-layouts  14.3 us
    ppermute x6, starting transfers between devices, near_shards(): lax.ppermute(shard, 'row', row_moves(axis, 4 - rel))  12.3 us
    ppermute x6, starting transfers between devices, exchange(): lax.ppermute(blocks[d], 'row', row_moves(axis, d)).astype(jnp.float32)  10.2 us
    ppermute x6, waiting for transfers between devices, exchange(): lax.ppermute(blocks[d], 'row', row_moves(axis, d)).astype(jnp.float32)  10 us
    ppermute x6, starting transfers between devices, exchange(): lax.ppermute(total[:, d], 'hst', [(h, (h + d) % 4) for h in range(4)])  9.72 us
    pallas_call x1, Pallas kernels, prep(): pl.pallas_call(prep_kernel, grid=(tables,), in_specs=[pl.BlockSpec(memory...  6.9 us
  transfers between devices with their start and end apart: 25, of which 7 were waited for; matrix products, arithmetic and copies ran while one was open for 9% of the time, Pallas kernels for 23%

profile of v3, /device:TPU:0, one launch (start us, length us, event | category | flops | bytes accessed | tf_op | source)
XLA Modules:
  0.0 143.4 jit_solution(1757578295504578193)
XLA Ops:
  0.0 2.6 %fusion = (bf16[2,160,1024]{2,1,0:T(8,128)(2,1)}, bf16[2,160,1024]{2,1,0:T(8,128)(2,1)}) fusion(bf16[4,160,1024]{2,1,0:T(8,128)(2,1)} %bitcast.33), kind=kLoop, calls=%fused_computation.11 | loop fusion | bytes 2621440 | tf_op jit(solution)/shard_map/slice | solution.py:419
  2.7 4.1 %collective-permute-start = (bf16[2,160,1024]{2,1,0:T(8,128)(2,1)}, bf16[2,160,1024]{2,1,0:T(8,128)(2,1)S(1)}, u32[]{:S(2)}, u32[]{:S(2)}) collective-permute-start(bf16[2,160,1024]{2,1,0:T(8,128)(2,1)} %get-tuple-element.84), channel_id=1, source_target_pairs={{0,24},{1,25},{2,26},{3,27},{4,28},{5,29},{6,30},{7,31},{8,0},{9,1... | collective-permute-start | bytes 1966088 | tf_op jit(solution)/shard_map/ppermute | solution.py:362
  8.1 3.0 %collective-permute-start.3 = (bf16[2,160,1024]{2,1,0:T(8,128)(2,1)}, bf16[2,160,1024]{2,1,0:T(8,128)(2,1)}, u32[]{:S(2)}, u32[]{:S(2)}) collective-permute-start(bf16[2,160,1024]{2,1,0:T(8,128)(2,1)} %get-tuple-element.83), channel_id=1, source_target_pairs={{0,6},{1,7},{2,0},{3,1},{4,2},{5,3},{6,4},{7,5},{8,14},{9,15},{10,... | collective-permute-start | bytes 1966088 | tf_op jit(solution)/shard_map/ppermute | solution.py:362
  11.2 6.9 %prep.1 = (f32[4,32,4,16,128]{4,3,2,1,0:T(8,128)S(1)}, s32[4,8,16,128]{3,2,1,0:T(8,128)S(1)}, s32[4,16,128]{2,1,0:T(8,128)S(1)}) custom-call(s32[4]{0:T(128)S(1)} %pad_add_fusion.pos_ref, s32[4,8,16384]{2,1,0:T(8,128)S(1)} %bitcast.31, s32[4,16384]{1,0:T(4,128)S(1)} %bitcast.36), custom_call_target="tpu_custom_call" | custom-call | flops 40000000 | bytes 9000000 | tf_op jit(solution)/shard_map/prep/pallas_call | solution.py:76
  18.1 2.0 %copy-done.8 = f32[4,32,4,16,128]{4,3,2,1,0:T(8,128)} copy-done((f32[4,32,4,16,128]{4,3,2,1,0:T(8,128)}, f32[4,32,4,16,128]{4,3,2,1,0:T(8,128)S(1)}, u32[]{:S(2)}) %copy-start.8) | copy-done | bytes 4194328
  20.9 3.0 %copy.36 = bf16[1024,1280]{0,1:T(8,128)(2,1)S(1)} copy(bf16[1024,1280]{1,0:T(8,128)(2,1)} %param.17) | data formatting | bytes 5242880 | tf_op args[7]
  24.0 2.5 %copy.35 = bf16[1024,24,16]{0,2,1:T(8,128)(2,1)} copy(bf16[1024,24,16]{0,1,2:T(8,128)(2,1)} %bitcast.38) | data formatting | bytes 1572864 | tf_op jit(solution)/shard_map/transpose | solution.py:403
  27.4 8.3 %collective-permute-done.refs_3_ = bf16[2,160,1024]{2,1,0:T(8,128)(2,1)S(1)} collective-permute-done((bf16[2,160,1024]{2,1,0:T(8,128)(2,1)}, bf16[2,160,1024]{2,1,0:T(8,128)(2,1)S(1)}, u32[]{:S(2)}, u32[]{:S(2)}) %collective-permute-start) | collective-permute-done | bytes 655392 | tf_op jit(solution)/shard_map/ppermute | solution.py:362
  35.7 3.2 %collective-permute-start.4 = (bf16[2,160,1024]{2,1,0:T(8,128)(2,1)}, bf16[2,160,1024]{2,1,0:T(8,128)(2,1)S(1)}, u32[]{:S(2)}, u32[]{:S(2)}) collective-permute-start(bf16[2,160,1024]{2,1,0:T(8,128)(2,1)} %get-tuple-element.83), channel_id=1, source_target_pairs={{0,4},{1,5},{2,6},{3,7},{4,0},{5,1},{6,2},{7,3},{8,12},{9,13},{10,... | collective-permute-start | bytes 1966088 | tf_op jit(solution)/shard_map/ppermute | solution.py:362
  40.9 2.2 %copy-done.9 = f32[4,32,4,16,128]{4,3,2,1,0:T(8,128)S(1)} copy-done((f32[4,32,4,16,128]{4,3,2,1,0:T(8,128)S(1)}, f32[4,32,4,16,128]{4,3,2,1,0:T(8,128)}, u32[]{:S(2)}) %copy-start.9) | copy-done | bytes 4194328
  44.0 11.2 %pool_own.1.refs_6_ = f32[4,4,2,160,256]{4,3,2,1,0:T(8,128)S(1)} custom-call(s32[4,16]{1,0:T(4,128)S(1)} %reduce.7.refs_0_, f32[4,32,4,16,128]{4,3,2,1,0:T(8,128)S(1)} %copy-done.9, s32[4,8,16,128]{3,2,1,0:T(8,128)S(1)} %copy-done.11, bf16[4,160,1024]{2,1,0:T(8,128)(2,1)S(1)} %bitcast.34, bf16[4,160,1024]{2,1,0:T(8,128)(2,1)} %collective-permute-done.6.refs_4_), custom_call_target="tpu_custom_call" | custom-call | flops 8589934592 | bytes 5000000 | tf_op jit(solution)/shard_map/pool_own/pallas_call | solution.py:237
  55.3 12.4 %collective-permute-done.5.refs_5_ = bf16[2,160,1024]{2,1,0:T(8,128)(2,1)S(1)} collective-permute-done((bf16[2,160,1024]{2,1,0:T(8,128)(2,1)}, bf16[2,160,1024]{2,1,0:T(8,128)(2,1)S(1)}, u32[]{:S(2)}, u32[]{:S(2)}) %collective-permute-start.5) | collective-permute-done | bytes 655392 | tf_op jit(solution)/shard_map/ppermute | solution.py:362
  68.7 2.0 %collective-permute-done.10.refs_3_ = bf16[2,160,1024]{2,1,0:T(8,128)(2,1)S(1)} collective-permute-done((bf16[2,160,1024]{2,1,0:T(8,128)(2,1)}, bf16[2,160,1024]{2,1,0:T(8,128)(2,1)S(1)}, u32[]{:S(2)}, u32[]{:S(2)}) %collective-permute-start.10) | collective-permute-done | bytes 655392 | tf_op jit(solution)/shard_map/ppermute | solution.py:366
  70.9 7.2 %pool_near.3.refs_6_ = f32[2,4,2,160,256]{4,3,2,1,0:T(8,128)S(1)} custom-call(s32[4,16]{1,0:T(4,128)S(1)} %reduce.7.refs_0_, f32[4,32,4,16,128]{4,3,2,1,0:T(8,128)S(1)} %copy-done.9, s32[4,8,16,128]{3,2,1,0:T(8,128)S(1)} %copy-done.11, bf16[2,160,1024]{2,1,0:T(8,128)(2,1)} %collective-permute-done.3.refs_3_, ...), custom_call_target="tpu_custom_call" | custom-call | flops 6442450944 | bytes 5000000 | tf_op jit(solution)/shard_map/pool_near/pallas_call | solution.py:237
  78.1 7.5 %pool_near.2.refs_6_ = f32[2,4,2,160,256]{4,3,2,1,0:T(8,128)S(1)} custom-call(s32[4,16]{1,0:T(4,128)S(1)} %reduce.7.refs_0_, f32[4,32,4,16,128]{4,3,2,1,0:T(8,128)S(1)} %copy-done.9, s32[4,8,16,128]{3,2,1,0:T(8,128)S(1)} %copy-done.11, bf16[2,160,1024]{2,1,0:T(8,128)(2,1)S(1)} %collective-permute-done.refs_3_, ...), custom_call_target="tpu_custom_call" | custom-call | flops 6442450944 | bytes 5000000 | tf_op jit(solution)/shard_map/pool_near/pallas_call | solution.py:237
  85.6 6.8 %pool_far.2 = (bf16[2,4,160,128]{3,2,1,0:T(8,128)(2,1)S(1)}, bf16[2,4,160,128]{3,2,1,0:T(8,128)(2,1)S(1)}, bf16[2,4,160,128]{3,2,1,0:T(8,128)(2,1)S(1)}, bf16[2,4,160,128]{3,2,1,0:T(8,128)(2,1)S(1)}) custom-call(s32[4,16]{1,0:T(4,128)S(1)} %reduce.7.refs_0_, f32[4,32,4,16,128]{4,3,2,1,0:T(8,128)S(1)} %copy-done.9, s32[4,8,16,128]{3,2,1,0:T(8,128)S(1)} %copy-done.11, ...), custom_call_target="tpu_custom_call" | custom-call | flops 6442450944 | bytes 5000000 | tf_op jit(solution)/shard_map/pool_far/pallas_call | solution.py:237
  92.4 6.7 %pool_far.3 = (bf16[2,4,160,128]{3,2,1,0:T(8,128)(2,1)S(1)}, bf16[2,4,160,128]{3,2,1,0:T(8,128)(2,1)S(1)}, bf16[2,4,160,128]{3,2,1,0:T(8,128)(2,1)S(1)}, bf16[2,4,160,128]{3,2,1,0:T(8,128)(2,1)S(1)}) custom-call(s32[4,16]{1,0:T(4,128)S(1)} %reduce.7.refs_0_, f32[4,32,4,16,128]{4,3,2,1,0:T(8,128)S(1)} %copy-done.9, s32[4,8,16,128]{3,2,1,0:T(8,128)S(1)} %copy-done.11, ...), custom_call_target="tpu_custom_call" | custom-call | flops 6442450944 | bytes 5000000 | tf_op jit(solution)/shard_map/pool_far/pallas_call | solution.py:237
  99.2 5.7 %collective-permute-start.20 = (bf16[2,4,160,128]{3,2,0,1:T(8,128)(2,1)S(1)}, bf16[2,4,160,128]{3,2,0,1:T(8,128)(2,1)S(1)}, u32[]{:S(2)}, u32[]{:S(2)}) collective-permute-start(bf16[2,4,160,128]{3,2,0,1:T(8,128)(2,1)S(1)} %copy.45), channel_id=1, source_target_pairs={{0,16},{1,17},{2,18},{3,19},{4,20},{5,21},{6,22},{7,23},{8,24},{9,... | collective-permute-start | bytes 983048 | tf_op jit(solution)/shard_map/ppermute | solution.py:372
  108.0 3.2 %collective-permute-done.19 = bf16[2,4,160,128]{3,2,0,1:T(8,128)(2,1)S(1)} collective-permute-done((bf16[2,4,160,128]{3,2,0,1:T(8,128)(2,1)S(1)}, bf16[2,4,160,128]{3,2,0,1:T(8,128)(2,1)S(1)}, u32[]{:S(2)}, u32[]{:S(2)}) %collective-permute-start.19) | collective-permute-done | bytes 327712 | tf_op jit(solution)/shard_map/ppermute | solution.py:372
  112.7 6.8 %collective-permute-done.20 = bf16[2,4,160,128]{3,2,0,1:T(8,128)(2,1)S(1)} collective-permute-done((bf16[2,4,160,128]{3,2,0,1:T(8,128)(2,1)S(1)}, bf16[2,4,160,128]{3,2,0,1:T(8,128)(2,1)S(1)}, u32[]{:S(2)}, u32[]{:S(2)}) %collective-permute-start.20) | collective-permute-done | bytes 327712 | tf_op jit(solution)/shard_map/ppermute | solution.py:372
  120.3 1.7 %collective-permute-start.22 = (bf16[2,160,128]{2,1,0:T(8,128)(2,1)S(1)}, bf16[2,160,128]{2,1,0:T(8,128)(2,1)S(1)}, u32[]{:S(2)}, u32[]{:S(2)}) collective-permute-start(bf16[2,160,128]{2,1,0:T(8,128)(2,1)S(1)} %get-tuple-element.87), channel_id=1, source_target_pairs={{0,32},{32,64},{64,96},{96,0},{1,33},{33,65},{65,97},{97,1},{2,34}... | collective-permute-start | bytes 245768 | tf_op jit(solution)/shard_map/ppermute | solution.py:375
  122.0 3.3 %collective-permute-start.23 = (bf16[2,160,128]{2,1,0:T(8,128)(2,1)}, bf16[2,160,128]{2,1,0:T(8,128)(2,1)}, u32[]{:S(2)}, u32[]{:S(2)}) collective-permute-start(bf16[2,160,128]{2,1,0:T(8,128)(2,1)} %get-tuple-element.86), channel_id=1, source_target_pairs={{0,64},{32,96},{64,0},{96,32},{1,65},{33,97},{65,1},{97,33},{2,66}... | collective-permute-start | bytes 245768 | tf_op jit(solution)/shard_map/ppermute | solution.py:375
  129.9 1.7 %collective-permute-start.18 = (bf16[2,160,128]{2,1,0:T(8,128)(2,1)}, bf16[2,160,128]{2,1,0:T(8,128)(2,1)}, u32[]{:S(2)}, u32[]{:S(2)}) collective-permute-start(bf16[2,160,128]{2,1,0:T(8,128)(2,1)} %get-tuple-element.89), channel_id=1, source_target_pairs={{0,96},{32,0},{64,32},{96,64},{1,97},{33,1},{65,33},{97,65},{2,98}... | collective-permute-start | bytes 245768 | tf_op jit(solution)/shard_map/ppermute | solution.py:375
  137.9 5.5 %tail.1 = bf16[16,160,128]{2,1,0:T(8,128)(2,1)} custom-call(s32[1]{0:T(128)} %bitcast.host_ref, s32[16]{0:T(128)S(1)} %copy-done.7, f32[24,16]{1,0:T(8,128)S(1)} %convert_element_type.36.proj_ref, f32[8,16]{1,0:T(8,128)S(1)} %convert_element_type.37.compress_ref, bf16[2,160,128]{2,1,0:T(8,128)(2,1)S(1)} %copy-done.2, ...), custom_call_target="tpu_custom_call" | custom-call | flops 1000000000 | bytes 8000000 | tf_op jit(solution)/shard_map/tail/pallas_call | solution.py:329
  (86 shorter events, 23.6 us)
Async XLA Ops:
  0.0 38.9 %collective-permute-start.6 = (bf16[4,160,1024]{2,1,0:T(8,128)(2,1)}, bf16[4,160,1024]{2,1,0:T(8,128)(2,1)}, u32[]{:S(2)}, u32[]{:S(2)}) collective-permute-start(bf16[4,160,1024]{2,1,0:T(8,128)(2,1)} %bitcast.32), channel_id=1, source_target_pairs={{0,1},{1,0},{2,3},{3,2},{4,5},{5,4},{6,7},{7,6},{8,9},{9,8},{10,11... | collective-permute-start | bytes 3932168 | tf_op jit(solution)/shard_map/ppermute | solution.py:366
  2.7 33.0 %collective-permute-start = (bf16[2,160,1024]{2,1,0:T(8,128)(2,1)}, bf16[2,160,1024]{2,1,0:T(8,128)(2,1)S(1)}, u32[]{:S(2)}, u32[]{:S(2)}) collective-permute-start(bf16[2,160,1024]{2,1,0:T(8,128)(2,1)} %get-tuple-element.84), channel_id=1, source_target_pairs={{0,24},{1,25},{2,26},{3,27},{4,28},{5,29},{6,30},{7,31},{8,0},{9,1... | collective-permute-start | bytes 1966088 | tf_op jit(solution)/shard_map/ppermute | solution.py:362
  6.8 48.4 %collective-permute-start.1 = (bf16[2,160,1024]{2,1,0:T(8,128)(2,1)}, bf16[2,160,1024]{2,1,0:T(8,128)(2,1)}, u32[]{:S(2)}, u32[]{:S(2)}) collective-permute-start(bf16[2,160,1024]{2,1,0:T(8,128)(2,1)} %get-tuple-element.84), channel_id=1, source_target_pairs={{0,16},{1,17},{2,18},{3,19},{4,20},{5,21},{6,22},{7,23},{8,24},{9,... | collective-permute-start | bytes 1966088 | tf_op jit(solution)/shard_map/ppermute | solution.py:362
  6.8 48.5 %collective-permute-start.2 = (bf16[2,160,1024]{2,1,0:T(8,128)(2,1)}, bf16[2,160,1024]{2,1,0:T(8,128)(2,1)}, u32[]{:S(2)}, u32[]{:S(2)}) collective-permute-start(bf16[2,160,1024]{2,1,0:T(8,128)(2,1)} %get-tuple-element.84), channel_id=1, source_target_pairs={{0,8},{1,9},{2,10},{3,11},{4,12},{5,13},{6,14},{7,15},{8,16},{9,17... | collective-permute-start | bytes 1966088 | tf_op jit(solution)/shard_map/ppermute | solution.py:362
  8.1 47.2 %collective-permute-start.3 = (bf16[2,160,1024]{2,1,0:T(8,128)(2,1)}, bf16[2,160,1024]{2,1,0:T(8,128)(2,1)}, u32[]{:S(2)}, u32[]{:S(2)}) collective-permute-start(bf16[2,160,1024]{2,1,0:T(8,128)(2,1)} %get-tuple-element.83), channel_id=1, source_target_pairs={{0,6},{1,7},{2,0},{3,1},{4,2},{5,3},{6,4},{7,5},{8,14},{9,15},{10,... | collective-permute-start | bytes 1966088 | tf_op jit(solution)/shard_map/ppermute | solution.py:362
  35.7 19.6 %collective-permute-start.4 = (bf16[2,160,1024]{2,1,0:T(8,128)(2,1)}, bf16[2,160,1024]{2,1,0:T(8,128)(2,1)S(1)}, u32[]{:S(2)}, u32[]{:S(2)}) collective-permute-start(bf16[2,160,1024]{2,1,0:T(8,128)(2,1)} %get-tuple-element.83), channel_id=1, source_target_pairs={{0,4},{1,5},{2,6},{3,7},{4,0},{5,1},{6,2},{7,3},{8,12},{9,13},{10,... | collective-permute-start | bytes 1966088 | tf_op jit(solution)/shard_map/ppermute | solution.py:362
  38.9 28.8 %collective-permute-start.5 = (bf16[2,160,1024]{2,1,0:T(8,128)(2,1)}, bf16[2,160,1024]{2,1,0:T(8,128)(2,1)S(1)}, u32[]{:S(2)}, u32[]{:S(2)}) collective-permute-start(bf16[2,160,1024]{2,1,0:T(8,128)(2,1)} %get-tuple-element.83), channel_id=1, source_target_pairs={{0,2},{1,3},{2,4},{3,5},{4,6},{5,7},{6,0},{7,1},{8,10},{9,11},{10,... | collective-permute-start | bytes 1966088 | tf_op jit(solution)/shard_map/ppermute | solution.py:362
  67.7 17.9 %collective-permute-start.11 = (bf16[2,160,1024]{2,1,0:T(8,128)(2,1)S(1)}, bf16[2,160,1024]{2,1,0:T(8,128)(2,1)S(1)}, u32[]{:S(2)}, u32[]{:S(2)}) collective-permute-start(bf16[2,160,1024]{2,1,0:T(8,128)(2,1)S(1)} %collective-permute-done.4.refs_4_), channel_id=1, source_target_pairs={{0,1},{1,0},{2,3},{3,2},{4,5},{5,4},{6,7},{7,6},{8,9},{9,8},{10,11... | collective-permute-start | bytes 1966088 | tf_op jit(solution)/shard_map/ppermute | solution.py:366
  68.1 17.4 %collective-permute-start.12 = (bf16[2,160,1024]{2,1,0:T(8,128)(2,1)S(1)}, bf16[2,160,1024]{2,1,0:T(8,128)(2,1)S(1)}, u32[]{:S(2)}, u32[]{:S(2)}) collective-permute-start(bf16[2,160,1024]{2,1,0:T(8,128)(2,1)S(1)} %collective-permute-done.5.refs_5_), channel_id=1, source_target_pairs={{0,1},{1,0},{2,3},{3,2},{4,5},{5,4},{6,7},{7,6},{8,9},{9,8},{10,11... | collective-permute-start | bytes 1966088 | tf_op jit(solution)/shard_map/ppermute | solution.py:366
  68.2 17.4 %collective-permute-start.7 = (bf16[2,160,1024]{2,1,0:T(8,128)(2,1)S(1)}, bf16[2,160,1024]{2,1,0:T(8,128)(2,1)S(1)}, u32[]{:S(2)}, u32[]{:S(2)}) collective-permute-start(bf16[2,160,1024]{2,1,0:T(8,128)(2,1)S(1)} %collective-permute-done.refs_3_), channel_id=1, source_target_pairs={{0,1},{1,0},{2,3},{3,2},{4,5},{5,4},{6,7},{7,6},{8,9},{9,8},{10,11... | collective-permute-start | bytes 1966088 | tf_op jit(solution)/shard_map/ppermute | solution.py:366
  68.7 16.9 %collective-permute-start.8 = (bf16[2,160,1024]{2,1,0:T(8,128)(2,1)}, bf16[2,160,1024]{2,1,0:T(8,128)(2,1)S(1)}, u32[]{:S(2)}, u32[]{:S(2)}) collective-permute-start(bf16[2,160,1024]{2,1,0:T(8,128)(2,1)} %collective-permute-done.1.refs_4_), channel_id=1, source_target_pairs={{0,1},{1,0},{2,3},{3,2},{4,5},{5,4},{6,7},{7,6},{8,9},{9,8},{10,11... | collective-permute-start | bytes 1966088 | tf_op jit(solution)/shard_map/ppermute | solution.py:366
  70.7 14.9 %collective-permute-start.9 = (bf16[2,160,1024]{2,1,0:T(8,128)(2,1)}, bf16[2,160,1024]{2,1,0:T(8,128)(2,1)S(1)}, u32[]{:S(2)}, u32[]{:S(2)}) collective-permute-start(bf16[2,160,1024]{2,1,0:T(8,128)(2,1)} %collective-permute-done.2.refs_5_), channel_id=1, source_target_pairs={{0,1},{1,0},{2,3},{3,2},{4,5},{5,4},{6,7},{7,6},{8,9},{9,8},{10,11... | collective-permute-start | bytes 1966088 | tf_op jit(solution)/shard_map/ppermute | solution.py:366
  99.1 12.1 %collective-permute-start.19 = (bf16[2,4,160,128]{3,2,0,1:T(8,128)(2,1)S(1)}, bf16[2,4,160,128]{3,2,0,1:T(8,128)(2,1)S(1)}, u32[]{:S(2)}, u32[]{:S(2)}) collective-permute-start(bf16[2,4,160,128]{3,2,0,1:T(8,128)(2,1)S(1)} %copy.44), channel_id=1, source_target_pairs={{0,8},{1,9},{2,10},{3,11},{4,12},{5,13},{6,14},{7,15},{8,16},{9,17... | collective-permute-start | bytes 983048 | tf_op jit(solution)/shard_map/ppermute | solution.py:372
  99.2 20.2 %collective-permute-start.20 = (bf16[2,4,160,128]{3,2,0,1:T(8,128)(2,1)S(1)}, bf16[2,4,160,128]{3,2,0,1:T(8,128)(2,1)S(1)}, u32[]{:S(2)}, u32[]{:S(2)}) collective-permute-start(bf16[2,4,160,128]{3,2,0,1:T(8,128)(2,1)S(1)} %copy.45), channel_id=1, source_target_pairs={{0,16},{1,17},{2,18},{3,19},{4,20},{5,21},{6,22},{7,23},{8,24},{9,... | collective-permute-start | bytes 983048 | tf_op jit(solution)/shard_map/ppermute | solution.py:372
  105.0 14.4 %collective-permute-start.21 = (bf16[2,4,160,128]{3,2,0,1:T(8,128)(2,1)S(1)}, bf16[2,4,160,128]{3,2,0,1:T(8,128)(2,1)S(1)}, u32[]{:S(2)}, u32[]{:S(2)}) collective-permute-start(bf16[2,4,160,128]{3,2,0,1:T(8,128)(2,1)S(1)} %copy.46), channel_id=1, source_target_pairs={{0,24},{1,25},{2,26},{3,27},{4,28},{5,29},{6,30},{7,31},{8,0},{9,1... | collective-permute-start | bytes 983048 | tf_op jit(solution)/shard_map/ppermute | solution.py:372
  105.1 20.2 %collective-permute-start.13 = (bf16[2,4,160,128]{3,2,0,1:T(8,128)(2,1)S(1)}, bf16[2,4,160,128]{3,2,0,1:T(8,128)(2,1)S(1)}, u32[]{:S(2)}, u32[]{:S(2)}) collective-permute-start(bf16[2,4,160,128]{3,2,0,1:T(8,128)(2,1)S(1)} %copy.40), channel_id=1, source_target_pairs={{0,2},{1,3},{2,4},{3,5},{4,6},{5,7},{6,0},{7,1},{8,10},{9,11},{10,... | collective-permute-start | bytes 983048 | tf_op jit(solution)/shard_map/ppermute | solution.py:372
  106.6 20.0 %collective-permute-start.14 = (bf16[2,4,160,128]{3,2,0,1:T(8,128)(2,1)S(1)}, bf16[2,4,160,128]{3,2,0,1:T(8,128)(2,1)S(1)}, u32[]{:S(2)}, u32[]{:S(2)}) collective-permute-start(bf16[2,4,160,128]{3,2,0,1:T(8,128)(2,1)S(1)} %copy.41), channel_id=1, source_target_pairs={{0,4},{1,5},{2,6},{3,7},{4,0},{5,1},{6,2},{7,3},{8,12},{9,13},{10,... | collective-permute-start | bytes 983048 | tf_op jit(solution)/shard_map/ppermute | solution.py:372
  111.2 15.4 %collective-permute-start.15 = (bf16[2,4,160,128]{3,2,0,1:T(8,128)(2,1)S(1)}, bf16[2,4,160,128]{3,2,0,1:T(8,128)(2,1)S(1)}, u32[]{:S(2)}, u32[]{:S(2)}) collective-permute-start(bf16[2,4,160,128]{3,2,0,1:T(8,128)(2,1)S(1)} %copy.42), channel_id=1, source_target_pairs={{0,6},{1,7},{2,0},{3,1},{4,2},{5,3},{6,4},{7,5},{8,14},{9,15},{10,... | collective-permute-start | bytes 983048 | tf_op jit(solution)/shard_map/ppermute | solution.py:372
  120.3 8.9 %collective-permute-start.22 = (bf16[2,160,128]{2,1,0:T(8,128)(2,1)S(1)}, bf16[2,160,128]{2,1,0:T(8,128)(2,1)S(1)}, u32[]{:S(2)}, u32[]{:S(2)}) collective-permute-start(bf16[2,160,128]{2,1,0:T(8,128)(2,1)S(1)} %get-tuple-element.87), channel_id=1, source_target_pairs={{0,32},{32,64},{64,96},{96,0},{1,33},{33,65},{65,97},{97,1},{2,34}... | collective-permute-start | bytes 245768 | tf_op jit(solution)/shard_map/ppermute | solution.py:375
  122.0 11.0 %collective-permute-start.23 = (bf16[2,160,128]{2,1,0:T(8,128)(2,1)}, bf16[2,160,128]{2,1,0:T(8,128)(2,1)}, u32[]{:S(2)}, u32[]{:S(2)}) collective-permute-start(bf16[2,160,128]{2,1,0:T(8,128)(2,1)} %get-tuple-element.86), channel_id=1, source_target_pairs={{0,64},{32,96},{64,0},{96,32},{1,65},{33,97},{65,1},{97,33},{2,66}... | collective-permute-start | bytes 245768 | tf_op jit(solution)/shard_map/ppermute | solution.py:375
  125.3 7.7 %collective-permute-start.24 = (bf16[2,160,128]{2,1,0:T(8,128)(2,1)}, bf16[2,160,128]{2,1,0:T(8,128)(2,1)}, u32[]{:S(2)}, u32[]{:S(2)}) collective-permute-start(bf16[2,160,128]{2,1,0:T(8,128)(2,1)} %get-tuple-element.85), channel_id=1, source_target_pairs={{0,96},{32,0},{64,32},{96,64},{1,97},{33,1},{65,33},{97,65},{2,98}... | collective-permute-start | bytes 245768 | tf_op jit(solution)/shard_map/ppermute | solution.py:375
  127.6 7.1 %collective-permute-start.16 = (bf16[2,160,128]{2,1,0:T(8,128)(2,1)}, bf16[2,160,128]{2,1,0:T(8,128)(2,1)}, u32[]{:S(2)}, u32[]{:S(2)}) collective-permute-start(bf16[2,160,128]{2,1,0:T(8,128)(2,1)} %get-tuple-element.91), channel_id=1, source_target_pairs={{0,32},{32,64},{64,96},{96,0},{1,33},{33,65},{65,97},{97,1},{2,34}... | collective-permute-start | bytes 245768 | tf_op jit(solution)/shard_map/ppermute | solution.py:375
  128.3 6.4 %collective-permute-start.17 = (bf16[2,160,128]{2,1,0:T(8,128)(2,1)}, bf16[2,160,128]{2,1,0:T(8,128)(2,1)}, u32[]{:S(2)}, u32[]{:S(2)}) collective-permute-start(bf16[2,160,128]{2,1,0:T(8,128)(2,1)} %get-tuple-element.90), channel_id=1, source_target_pairs={{0,64},{32,96},{64,0},{96,32},{1,65},{33,97},{65,1},{97,33},{2,66}... | collective-permute-start | bytes 245768 | tf_op jit(solution)/shard_map/ppermute | solution.py:375
  129.9 5.4 %collective-permute-start.18 = (bf16[2,160,128]{2,1,0:T(8,128)(2,1)}, bf16[2,160,128]{2,1,0:T(8,128)(2,1)}, u32[]{:S(2)}, u32[]{:S(2)}) collective-permute-start(bf16[2,160,128]{2,1,0:T(8,128)(2,1)} %get-tuple-element.89), channel_id=1, source_target_pairs={{0,96},{32,0},{64,32},{96,64},{1,97},{33,1},{65,33},{97,65},{2,98}... | collective-permute-start | bytes 245768 | tf_op jit(solution)/shard_map/ppermute | solution.py:375
  (17 other events, 76.0 us)

commit v4 on v3

--- a/solution.py
+++ b/solution.py
@@ -37,9 +37,10 @@
         )
         at_z, at_y, at_core = v >> 13, (v >> 11) & 3, (v >> 10) & 1
         here = jnp.where(over_z, at_y - y, at_z - z) == 0
-        away = jnp.where(over_z, (at_z - z) & 3, (at_y - y) & 3)
+        away = (at_y - y) & 3
         other = at_core ^ core
-        shard = jnp.where(away == 0, other, away + 1 + 3 * other)
+        ring = jnp.where(away == 0, other, away + 1 + 3 * other)
+        shard = jnp.where(over_z, at_z * 2 + at_core, ring)
         local = shard * ROWS_DEV + (v & (ROWS_DEV - 1))
         local = jnp.where(here & (slot < used), local, -1)
         for s in range(8):
@@ -91,7 +92,7 @@
             jax.ShapeDtypeStruct((tables, 8, BAG_BLOCKS, LANES), jnp.int32),
             jax.ShapeDtypeStruct((tables, BAG_BLOCKS, LANES), jnp.int32),
         ],
-        compiler_params=pltpu.CompilerParams(vmem_limit_bytes=32 << 20),
+        compiler_params=pltpu.CompilerParams(vmem_limit_bytes=60 << 20),
         cost_estimate=pl.CostEstimate(
             flops=40_000_000, bytes_accessed=9_000_000, transcendentals=0
         ),
@@ -202,34 +203,40 @@
             def _(d=d):
                 for part in range(2):
                     result = sums[0, 0, part].astype(jnp.bfloat16)
-                    outs[d][0, 2 * part] = result[:, :LANES]
-                    outs[d][0, 2 * part + 1] = result[:, LANES:]
+                    outs[d][2 * part, 0] = result[:, :LANES]
+                    outs[d][2 * part + 1, 0] = result[:, LANES:]
+
+
+def piece(array, first_table=0, stacked=None):
+    block = (1,) + array.shape[-2:]
+    if stacked is None:
+        return array, pl.BlockSpec(block, lambda j, i: (first_table + j, 0, 0))
+    return array, pl.BlockSpec((None,) + block, lambda j, i: (stacked, j, 0, 0))
 
 
 def pool(first_shard, tables, masks, keys, lids, shards, base, is_last, name):
     n_tables = len(tables)
     table0 = tables[0]
     n_shards = len(shards)
-    _, emb, rows = shards[0].shape
+    emb, rows = shards[0][0].shape[-2:]
     sums_block = (1, 1, 2, emb, PAIR)
     sums_spec = pl.BlockSpec(sums_block, lambda j, i: (j, i, 0, 0, 0))
     in_specs = [
         pl.BlockSpec(memory_space=pltpu.SMEM),
         pl.BlockSpec((1,) + keys.shape[1:], lambda j, i: (table0 + j, 0, 0, 0, 0)),
         pl.BlockSpec((1,) + lids.shape[1:], lambda j, i: (table0 + j, 0, 0, 0)),
-    ] + [pl.BlockSpec((1, emb, rows), lambda j, i: (j, 0, 0))] * n_shards
-    args = [masks, keys, lids, *shards]
+    ] + [spec for _, spec in shards]
+    args = [masks, keys, lids] + [array for array, _ in shards]
     if base is not None:
-        from_table = base[1]
-        in_specs.append(pl.BlockSpec(sums_block, lambda j, i: (from_table + j, i, 0, 0, 0)))
-        args.append(base[0])
+        in_specs.append(sums_spec)
+        args.append(base)
     scratch = [
         pltpu.VMEM((2, n_shards * rows, PAIR), jnp.bfloat16),
         pltpu.VMEM((SUB, PAIR), jnp.bfloat16),
     ]
     if is_last:
-        out_specs = [pl.BlockSpec((1, 4, emb, LANES), lambda j, i: (j, 0, 0, 0))] * 4
-        out_shape = [jax.ShapeDtypeStruct((n_tables, 4, emb, LANES), jnp.bfloat16)] * 4
+        out_specs = [pl.BlockSpec((4, 1, emb, LANES), lambda j, i: (0, j, 0, 0))] * 4
+        out_shape = [jax.ShapeDtypeStruct((4, n_tables, emb, LANES), jnp.bfloat16)] * 4
         scratch = [pltpu.VMEM(sums_block, jnp.float32)] + scratch
     else:
         out_specs = sums_spec
@@ -243,7 +250,7 @@
         out_specs=out_specs,
         out_shape=out_shape,
         scratch_shapes=scratch,
-        compiler_params=pltpu.CompilerParams(vmem_limit_bytes=32 << 20),
+        compiler_params=pltpu.CompilerParams(vmem_limit_bytes=60 << 20),
         cost_estimate=pl.CostEstimate(
             flops=2 * n_tables * n_shards * rows * 2048 * 256,
             bytes_accessed=5_000_000,
@@ -256,19 +263,18 @@
 def tail_kernel(
     host_ref,
     order_ref,
-    proj_ref,
     compress_ref,
     *rest,
 ):
     parts = rest[:8]
-    fm_gain_ref, up_ref, down_ref, gain_ref, out_ref, emb, gram, summed = rest[8:]
+    proj_ref, fm_gain_ref, up_ref, down_ref, gain_ref, out_ref, emb, gram, summed = rest[8:]
     host = host_ref[0]
     for d in range(4):
         source = (host - d) & 3
         for j in range(4):
             at = order_ref[source * 4 + j]
             part = parts[(j // 2) * 4 + d]
-            emb[pl.ds(at, 1), :, :] = part[j % 2 : j % 2 + 1, :, :].astype(jnp.float32)
+            emb[at] = part[j % 2].astype(jnp.float32)
     feats, width, lanes = emb.shape
     rank = proj_ref.shape[0]
 
@@ -279,11 +285,12 @@
             gram[f, g : g + 1, :] = dot
             if g != f:
                 gram[g, f : f + 1, :] = dot
+    proj = [jnp.broadcast_to(proj_ref[:, g : g + 1], (rank, lanes)) for g in range(feats)]
     rows = []
-    for k in range(rank):
+    for f in range(feats):
         row = None
         for g in range(feats):
-            term = proj_ref[k, g] * gram[g]
+            term = proj[g] * gram[f, g : g + 1, :]
             row = term if row is None else row + term
         rows.append(row)
     inv = 1.0 / (rank * feats)
@@ -292,7 +299,7 @@
     spread = jnp.sum(sum(r * r for r in rows), axis=0, keepdims=True) * inv
     scale = 1.0 / jnp.sqrt(spread + 1e-05)
     normed = jnp.concatenate(
-        [rows[k] * scale * fm_gain_ref[:, k : k + 1] for k in range(rank)], axis=0
+        [rows[f] * scale * fm_gain_ref[:, f : f + 1] for f in range(feats)], axis=0
     ).astype(jnp.bfloat16)
     hidden = jnp.maximum(
         jnp.dot(up_ref[...], normed, preferred_element_type=jnp.float32), 0.0
@@ -323,12 +330,15 @@
 
 
 def tail(host, order, proj, compress, parts, fm_gain, up, down, gain):
-    feats, width = order.shape[0], parts[0].shape[1]
+    feats, width = order.shape[0], parts[0].shape[2]
     smem = pl.BlockSpec(memory_space=pltpu.SMEM)
     vmem = pl.BlockSpec(memory_space=pltpu.VMEM)
+    mine = pl.BlockSpec((None,) + parts[0].shape[1:], lambda i: (0, 0, 0, 0))
+    there = pl.BlockSpec(parts[1].shape, lambda i: (0, 0, 0))
     return pl.pallas_call(
         tail_kernel,
-        in_specs=[smem] * 4 + [vmem] * 12,
+        grid=(1,),
+        in_specs=[smem] * 3 + ([mine] + [there] * 3) * 2 + [vmem] * 5,
         out_specs=vmem,
         out_shape=jax.ShapeDtypeStruct((feats, width, LANES), jnp.bfloat16),
         scratch_shapes=[
@@ -341,7 +351,7 @@
             flops=1_000_000_000, bytes_accessed=8_000_000, transcendentals=0
         ),
         name="tail",
-    )(host, order, proj, compress, *parts, fm_gain, up, down, gain)
+    )(host, order, compress, *parts, proj, fm_gain, up, down, gain)
 
 
 def row_moves(axis, step):
@@ -366,14 +376,16 @@
     return lax.ppermute(x, "row", row_moves("core", 1))
 
 
-def exchange(blocks, axis):
-    total = blocks[0].astype(jnp.float32)
-    for d in range(1, 4):
-        total = total + lax.ppermute(blocks[d], "row", row_moves(axis, d)).astype(jnp.float32)
-    total = total.astype(jnp.bfloat16)
-    return [total[:, 0]] + [
-        lax.ppermute(total[:, d], "hst", [(h, (h + d) % 4) for h in range(4)])
-        for d in range(1, 4)
+def to_owners(blocks, axis):
+    return [blocks[0]] + [
+        lax.ppermute(blocks[d], "row", row_moves(axis, d)) for d in range(1, 4)
+    ]
+
+
+def to_hosts(blocks):
+    total = sum(b.astype(jnp.float32) for b in blocks).astype(jnp.bfloat16)
+    return [total] + [
+        lax.ppermute(total[d], "hst", [(h, (h + d) % 4) for h in range(4)]) for d in range(1, 4)
     ]
 
 
@@ -392,47 +404,65 @@
     host = lax.axis_index("hst")
     row = lax.axis_index("row")
     pos = jnp.stack([host, row // 8, (row // 2) % 4, row % 2]).astype(jnp.int32)
-    n_tables = tables.shape[0]
-    feats, emb = out_gain.shape
+    feats = out_gain.shape[0]
     rank = proj_weight.shape[0]
-    width = up_weight.shape[1]
 
     flipped = jnp.swapaxes(tables, 1, 2)
     keys, lids, masks = prep(pos, jnp.transpose(indices, (1, 2, 0)), lengths.T)
     masks = lax.reduce(masks, jnp.int32(0), lax.bitwise_or, (2,))
-    up = jnp.transpose(up_weight.reshape(feats, rank, width), (2, 1, 0)).reshape(
-        width, rank * feats
-    )
     small = (
         feature_order,
         proj_weight.astype(jnp.float32),
         compress_weight.astype(jnp.float32),
-        fm_gain.reshape(feats, rank),
+        fm_gain.reshape(feats, rank).T,
         out_gain.T,
     )
-    masks, up, down, small = lax.optimization_barrier((masks, up, down_weight.T, small))
+    masks, up, down, small = lax.optimization_barrier(
+        (masks, up_weight.T, down_weight.T, small)
+    )
     order, proj, compress, fm_gain, gain = small
 
-    own_far = other_core(flipped)
-    pairs = [(0, 1), (2, 3)]
-    axes = ["z", "y"]
-    near = [near_shards(flipped[2 * p : 2 * p + 2], axes[p]) for p in range(2)]
+    ring = flipped[2:]
+    own_far = other_core(ring)
+    near = near_shards(ring, "y")
+    whole = lax.all_gather(
+        flipped[:2],
+        "row",
+        axis_index_groups=[
+            [z * 8 + y * 2 + core for z in range(4) for core in range(2)] for y in range(4)
+        ],
+    )
     sums = pool(
-        0, (0, 1, 2, 3), masks, keys, lids, [flipped, own_far], None, False, "pool_own"
+        0,
+        (2, 3),
+        masks,
+        keys,
+        lids,
+        [piece(flipped, 2), piece(own_far)],
+        None,
+        False,
+        "pool_own",
     )
     near, sums = lax.optimization_barrier((near, sums))
-    far = [[other_core(x) for x in near[p]] for p in range(2)]
-    parts = []
-    sums = [
-        pool(2, pairs[p], masks, keys, lids, near[p], (sums, 2 * p), False, "pool_near")
-        for p in range(2)
-    ]
+    far = [other_core(x) for x in near]
+    sums = pool(2, (2, 3), masks, keys, lids, [piece(x) for x in near], sums, False, "pool_near")
     far, sums = lax.optimization_barrier((far, sums))
-    for p in range(2):
-        blocks = pool(5, pairs[p], masks, keys, lids, far[p], (sums[p], 0), True, "pool_far")
-        if p == 0:
-            blocks, sums[1] = lax.optimization_barrier((blocks, sums[1]))
-        parts += exchange(blocks, axes[1 - p])
+    blocks = pool(5, (2, 3), masks, keys, lids, [piece(x) for x in far], sums, True, "pool_far")
+    masks, _ = lax.optimization_barrier((masks, blocks))
+    arrived = to_owners(blocks, "z")
+    blocks = pool(
+        0,
+        (0, 1),
+        masks,
+        keys,
+        lids,
+        [piece(whole, stacked=g) for g in range(GATHER)],
+        None,
+        True,
+        "pool_whole",
+    )
+    blocks, arrived = lax.optimization_barrier((blocks, arrived))
+    parts = to_hosts(to_owners(blocks, "y")) + to_hosts(arrived)
     result = tail(pos[:1], order, proj, compress, parts, fm_gain, up, down, gain)
     return jnp.transpose(result, (2, 0, 1))
 

time: 145 us -> 131 us (0.903)
  waiting for transfers between devices: 34.9 us -> 18.4 us
  local copies, waits for them, and re-layouts: 22.5 us -> 7.35 us
  between operations: 0.32 us -> 13.6 us
  Pallas kernels: 51.8 us -> 60.1 us
  starting transfers between devices: 33.4 us -> 26.6 us
  other arithmetic: 0.57 us -> 4.64 us
    ppermute x6 -> x3, waiting for transfers between devices: 20.7 us -> 6.74 us  [near_shards(): lax.ppermute(shard, 'row', row_moves(axis, 4 - rel))]
    unnamed x35 -> x16, local copies, waits for them, and re-layouts: 14.3 us -> 4.74 us
    ppermute x6 -> x3, starting transfers between devices: 12.3 us -> 4.77 us  [near_shards(): lax.ppermute(shard, 'row', row_moves(axis, 4 - rel))]
    pallas_call x5 -> x4, Pallas kernels: 39.4 us -> 46.5 us  [pool(): pl.pallas_call(functools.partial(pool_kernel, first_shard, n_shards, base...]
    transpose x1 -> x0, local copies, waits for them, and re-layouts: 2.46 us -> none  [on_device(): jnp.transpose(up_weight.reshape(feats, rank, width), (2, 1, 0))]
    convert_element_type x2, other arithmetic: 0.35 us -> 2.49 us  [to_hosts(): total = sum((b.astype(jnp.float32) for b in blocks)).astype(jnp.bfloat16)]
    ppermute x7 -> x4, waiting for transfers between devices: 2.05 us -> 0.01 us  [other_core(): return lax.ppermute(x, 'row', row_moves('core', 1))]
    pallas_call x1, Pallas kernels: 6.9 us -> 8.59 us  [prep(): pl.pallas_call(prep_kernel, grid=(tables,), in_specs=[pl.BlockSpec(memory...]
  transfers between devices with their start and end apart: 25 -> 20, of which waited for: 7 -> 5; matrix products, arithmetic and copies ran while one was open for 9% -> 7% of each run, Pallas kernels for 23% -> 42%
where the time goes in v4:
time: 131 us
  Pallas kernels  60.1 us (46%)
  starting transfers between devices  26.6 us (20%)
  waiting for transfers between devices  18.4 us (14%)
  between operations  13.6 us (10%)
  local copies, waits for them, and re-layouts  7.35 us (6%)
  other arithmetic  4.64 us (4%)
    pallas_call x4, Pallas kernels, pool(): pl.pallas_call(functools.partial(pool_kernel, first_shard, n_shards, base...  46.5 us
    ppermute x6, starting transfers between devices, to_owners(): lax.ppermute(blocks[d], 'row', row_moves(axis, d))  10.6 us
    ppermute x6, starting transfers between devices, to_hosts(): lax.ppermute(total[d], 'hst', [(h, (h + d) % 4) for h in range(4)])  10.6 us
    pallas_call x1, Pallas kernels, prep(): pl.pallas_call(prep_kernel, grid=(tables,), in_specs=[pl.BlockSpec(memory...  8.59 us
    ppermute x6, waiting for transfers between devices, to_owners(): lax.ppermute(blocks[d], 'row', row_moves(axis, d))  7.68 us
    ppermute x3, waiting for transfers between devices, near_shards(): lax.ppermute(shard, 'row', row_moves(axis, 4 - rel))  6.74 us
    pallas_call x1, Pallas kernels, tail(): pl.pallas_call(tail_kernel, grid=(1,), in_specs=[smem] * 3 + ([mine] + [t...  5.03 us
    ppermute x3, starting transfers between devices, near_shards(): lax.ppermute(shard, 'row', row_moves(axis, 4 - rel))  4.77 us
  transfers between devices with their start and end apart: 20, of which 5 were waited for; matrix products, arithmetic and copies ran while one was open for 7% of the time, Pallas kernels for 42%

profile of v4, /device:TPU:0, one launch (start us, length us, event | category | flops | bytes accessed | tf_op | source)
XLA Modules:
  0.0 130.6 jit_solution(13644788858302983624)
XLA Ops:
  6.5 2.4 %fusion = (bf16[2,160,1024]{2,1,0:T(8,128)(2,1)}, bf16[2,160,1024]{2,1,0:T(8,128)(2,1)}) fusion(bf16[4,160,1024]{2,1,0:T(8,128)(2,1)} %bitcast.30), kind=kLoop, calls=%fused_computation.9 | loop fusion | bytes 2621440 | tf_op jit(solution)/shard_map/slice | solution.py:429
  9.1 3.2 %collective-permute-start = (bf16[2,160,1024]{2,1,0:T(8,128)(2,1)}, bf16[2,160,1024]{2,1,0:T(8,128)(2,1)}, u32[]{:S(2)}, u32[]{:S(2)}) collective-permute-start(bf16[2,160,1024]{2,1,0:T(8,128)(2,1)} %get-tuple-element.78), channel_id=1, source_target_pairs={{0,6},{1,7},{2,0},{3,1},{4,2},{5,3},{6,4},{7,5},{8,14},{9,15},{10,... | collective-permute-start | bytes 1966088 | tf_op jit(solution)/shard_map/ppermute | solution.py:372
  14.5 8.6 %prep.1 = (f32[4,32,4,16,128]{4,3,2,1,0:T(8,128)}, s32[4,8,16,128]{3,2,1,0:T(8,128)}, s32[4,16,128]{2,1,0:T(8,128)}) custom-call(s32[4]{0:T(128)} %pad_add_fusion.pos_ref, s32[4,8,16384]{2,1,0:T(8,128)} %bitcast.29, s32[4,16384]{1,0:T(4,128)} %bitcast.32), custom_call_target="tpu_custom_call" | custom-call | flops 40000000 | bytes 9000000 | tf_op jit(solution)/shard_map/prep/pallas_call | solution.py:77
  23.1 1.5 %reduce.7.refs_0_ = s32[4,16]{1,0:T(4,128)} reduce(s32[4,16,128]{2,1,0:T(8,128)} %get-tuple-element.41, s32[]{:T(128)} %constant.48.clone.1), dimensions={2}, to_apply=%region_0.1 | reduce | flops 8128 | bytes 33028 | tf_op jit(solution)/shard_map/reduce | solution.py:412
  24.6 3.0 %copy.21 = bf16[1024,1280]{0,1:T(8,128)(2,1)S(1)} copy(bf16[1024,1280]{1,0:T(8,128)(2,1)} %param.17) | data formatting | bytes 5242880 | tf_op args[7]
  27.6 1.5 %copy.20 = bf16[384,1024]{0,1:T(8,128)(2,1)S(1)} copy(bf16[384,1024]{1,0:T(8,128)(2,1)} %param.16) | data formatting | bytes 1572864 | tf_op args[6]
  29.5 8.6 %pool_own.1.refs_6_ = f32[2,4,2,160,256]{4,3,2,1,0:T(8,128)} custom-call(s32[4,16]{1,0:T(4,128)} %reduce.7.refs_0_, f32[4,32,4,16,128]{4,3,2,1,0:T(8,128)} %get-tuple-element.45.refs_1_, s32[4,8,16,128]{3,2,1,0:T(8,128)} %get-tuple-element.46.refs_2_, bf16[4,160,1024]{2,1,0:T(8,128)(2,1)} %bitcast.31, bf16[2,160,1024]{2,1,0:T(8,128)(2,1)} %collective-permute-done.3.refs_4_), custom_call_target="tpu_custom_call" | custom-call | flops 4294967296 | bytes 5000000 | tf_op jit(solution)/shard_map/pool_own/pallas_call | solution.py:244
  38.2 3.0 %collective-permute-done.refs_3_ = bf16[2,160,1024]{2,1,0:T(8,128)(2,1)} collective-permute-done((bf16[2,160,1024]{2,1,0:T(8,128)(2,1)}, bf16[2,160,1024]{2,1,0:T(8,128)(2,1)}, u32[]{:S(2)}, u32[]{:S(2)}) %collective-permute-start) | collective-permute-done | bytes 655392 | tf_op jit(solution)/shard_map/ppermute | solution.py:372
  41.2 3.7 %collective-permute-done.2.refs_5_ = bf16[2,160,1024]{2,1,0:T(8,128)(2,1)} collective-permute-done((bf16[2,160,1024]{2,1,0:T(8,128)(2,1)}, bf16[2,160,1024]{2,1,0:T(8,128)(2,1)}, u32[]{:S(2)}, u32[]{:S(2)}) %collective-permute-start.2) | collective-permute-done | bytes 655392 | tf_op jit(solution)/shard_map/ppermute | solution.py:372
  45.4 10.2 %pool_near.1.refs_6_ = f32[2,4,2,160,256]{4,3,2,1,0:T(8,128)} custom-call(s32[4,16]{1,0:T(4,128)} %reduce.7.refs_0_, f32[4,32,4,16,128]{4,3,2,1,0:T(8,128)} %get-tuple-element.45.refs_1_, s32[4,8,16,128]{3,2,1,0:T(8,128)} %get-tuple-element.46.refs_2_, bf16[2,160,1024]{2,1,0:T(8,128)(2,1)} %collective-permute-done.refs_3_, ...), custom_call_target="tpu_custom_call" | custom-call | flops 6442450944 | bytes 5000000 | tf_op jit(solution)/shard_map/pool_near/pallas_call | solution.py:244
  55.7 10.2 %pool_far.1 = (bf16[4,2,160,128]{3,2,1,0:T(8,128)(2,1)}, bf16[4,2,160,128]{3,2,1,0:T(8,128)(2,1)}, bf16[4,2,160,128]{3,2,1,0:T(8,128)(2,1)}, bf16[4,2,160,128]{3,2,1,0:T(8,128)(2,1)}) custom-call(s32[4,16]{1,0:T(4,128)} %reduce.7.refs_0_, f32[4,32,4,16,128]{4,3,2,1,0:T(8,128)} %get-tuple-element.45.refs_1_, s32[4,8,16,128]{3,2,1,0:T(8,128)} %get-tuple-element.46.refs_2_, ...), custom_call_target="tpu_custom_call" | custom-call | flops 6442450944 | bytes 5000000 | tf_op jit(solution)/shard_map/pool_far/pallas_call | solution.py:244
  65.9 2.3 %collective-permute-start.7 = (bf16[4,2,160,128]{3,2,1,0:T(8,128)(2,1)}, bf16[4,2,160,128]{3,2,1,0:T(8,128)(2,1)}, u32[]{:S(2)}, u32[]{:S(2)}) collective-permute-start(bf16[4,2,160,128]{3,2,1,0:T(8,128)(2,1)} %get-tuple-element.56), channel_id=1, source_target_pairs={{0,8},{1,9},{2,10},{3,11},{4,12},{5,13},{6,14},{7,15},{8,16},{9,17... | collective-permute-start | bytes 983048 | tf_op jit(solution)/shard_map/ppermute | solution.py:381
  68.3 3.2 %collective-permute-start.8 = (bf16[4,2,160,128]{3,2,1,0:T(8,128)(2,1)}, bf16[4,2,160,128]{3,2,1,0:T(8,128)(2,1)}, u32[]{:S(2)}, u32[]{:S(2)}) collective-permute-start(bf16[4,2,160,128]{3,2,1,0:T(8,128)(2,1)} %get-tuple-element.57), channel_id=1, source_target_pairs={{0,16},{1,17},{2,18},{3,19},{4,20},{5,21},{6,22},{7,23},{8,24},{9,... | collective-permute-start | bytes 983048 | tf_op jit(solution)/shard_map/ppermute | solution.py:381
  71.4 1.4 %collective-permute-start.9 = (bf16[4,2,160,128]{3,2,1,0:T(8,128)(2,1)}, bf16[4,2,160,128]{3,2,1,0:T(8,128)(2,1)}, u32[]{:S(2)}, u32[]{:S(2)}) collective-permute-start(bf16[4,2,160,128]{3,2,1,0:T(8,128)(2,1)} %get-tuple-element.58), channel_id=1, source_target_pairs={{0,24},{1,25},{2,26},{3,27},{4,28},{5,29},{6,30},{7,31},{8,0},{9,1... | collective-permute-start | bytes 983048 | tf_op jit(solution)/shard_map/ppermute | solution.py:381
  72.9 17.4 %pool_whole.1 = (bf16[4,2,160,128]{3,2,1,0:T(8,128)(2,1)}, bf16[4,2,160,128]{3,2,1,0:T(8,128)(2,1)}, bf16[4,2,160,128]{3,2,1,0:T(8,128)(2,1)}, bf16[4,2,160,128]{3,2,1,0:T(8,128)(2,1)}) custom-call(s32[4,16]{1,0:T(4,128)} %reduce.7.refs_0_, f32[4,32,4,16,128]{4,3,2,1,0:T(8,128)} %get-tuple-element.45.refs_1_, s32[4,8,16,128]{3,2,1,0:T(8,128)} %get-tuple-element.46.refs_2_, ...), custom_call_target="tpu_custom_call" | custom-call | flops 17179869184 | bytes 5000000 | tf_op jit(solution)/shard_map/pool_whole/pallas_call | solution.py:244
  90.4 2.3 %collective-permute-start.11 = (bf16[4,2,160,128]{3,2,1,0:T(8,128)(2,1)}, bf16[4,2,160,128]{3,2,1,0:T(8,128)(2,1)S(1)}, u32[]{:S(2)}, u32[]{:S(2)}) collective-permute-start(bf16[4,2,160,128]{3,2,1,0:T(8,128)(2,1)} %get-tuple-element.66), channel_id=1, source_target_pairs={{0,4},{1,5},{2,6},{3,7},{4,0},{5,1},{6,2},{7,3},{8,12},{9,13},{10,... | collective-permute-start | bytes 983048 | tf_op jit(solution)/shard_map/ppermute | solution.py:381
  92.6 1.4 %collective-permute-start.12 = (bf16[4,2,160,128]{3,2,1,0:T(8,128)(2,1)}, bf16[4,2,160,128]{3,2,1,0:T(8,128)(2,1)S(1)}, u32[]{:S(2)}, u32[]{:S(2)}) collective-permute-start(bf16[4,2,160,128]{3,2,1,0:T(8,128)(2,1)} %get-tuple-element.67), channel_id=1, source_target_pairs={{0,6},{1,7},{2,0},{3,1},{4,2},{5,3},{6,4},{7,5},{8,14},{9,15},{10,... | collective-permute-start | bytes 983048 | tf_op jit(solution)/shard_map/ppermute | solution.py:381
  96.7 2.6 %collective-permute-start.17 = (bf16[2,160,128]{2,1,0:T(8,128)(2,1)S(1)}, bf16[2,160,128]{2,1,0:T(8,128)(2,1)S(1)}, u32[]{:S(2)}, u32[]{:S(2)}) collective-permute-start(bf16[2,160,128]{2,1,0:T(8,128)(2,1)S(1)} %get-tuple-element.80), channel_id=1, source_target_pairs={{0,64},{32,96},{64,0},{96,32},{1,65},{33,97},{65,1},{97,33},{2,66}... | collective-permute-start | bytes 245768 | tf_op jit(solution)/shard_map/ppermute | solution.py:388
  99.3 7.7 %collective-permute-done.10 = bf16[4,2,160,128]{3,2,1,0:T(8,128)(2,1)S(1)} collective-permute-done((bf16[4,2,160,128]{3,2,1,0:T(8,128)(2,1)}, bf16[4,2,160,128]{3,2,1,0:T(8,128)(2,1)S(1)}, u32[]{:S(2)}, u32[]{:S(2)}) %collective-permute-start.10) | collective-permute-done | bytes 327712 | tf_op jit(solution)/shard_map/ppermute | solution.py:381
  106.9 3.2 %collective-permute-start.18 = (bf16[2,160,128]{2,1,0:T(8,128)(2,1)S(1)}, bf16[2,160,128]{2,1,0:T(8,128)(2,1)S(1)}, u32[]{:S(2)}, u32[]{:S(2)}) collective-permute-start(bf16[2,160,128]{2,1,0:T(8,128)(2,1)S(1)} %get-tuple-element.79), channel_id=1, source_target_pairs={{0,96},{32,0},{64,32},{96,64},{1,97},{33,1},{65,33},{97,65},{2,98}... | collective-permute-start | bytes 245768 | tf_op jit(solution)/shard_map/ppermute | solution.py:388
  111.4 2.1 %collective-permute-start.14 = (bf16[2,160,128]{2,1,0:T(8,128)(2,1)S(1)}, bf16[2,160,128]{2,1,0:T(8,128)(2,1)S(1)}, u32[]{:S(2)}, u32[]{:S(2)}) collective-permute-start(bf16[2,160,128]{2,1,0:T(8,128)(2,1)S(1)} %get-tuple-element.83), channel_id=1, source_target_pairs={{0,64},{32,96},{64,0},{96,32},{1,65},{33,97},{65,1},{97,33},{2,66}... | collective-permute-start | bytes 245768 | tf_op jit(solution)/shard_map/ppermute | solution.py:388
  113.5 1.4 %collective-permute-start.15 = (bf16[2,160,128]{2,1,0:T(8,128)(2,1)S(1)}, bf16[2,160,128]{2,1,0:T(8,128)(2,1)S(1)}, u32[]{:S(2)}, u32[]{:S(2)}) collective-permute-start(bf16[2,160,128]{2,1,0:T(8,128)(2,1)S(1)} %get-tuple-element.82), channel_id=1, source_target_pairs={{0,96},{32,0},{64,32},{96,64},{1,97},{33,1},{65,33},{97,65},{2,98}... | collective-permute-start | bytes 245768 | tf_op jit(solution)/shard_map/ppermute | solution.py:388
  114.8 3.1 %collective-permute-done.13.rest_1_ = bf16[2,160,128]{2,1,0:T(8,128)(2,1)S(1)} collective-permute-done((bf16[2,160,128]{2,1,0:T(8,128)(2,1)S(1)}, bf16[2,160,128]{2,1,0:T(8,128)(2,1)S(1)}, u32[]{:S(2)}, u32[]{:S(2)}) %collective-permute-start.13) | collective-permute-done | bytes 81952 | tf_op jit(solution)/shard_map/ppermute | solution.py:388
  118.8 5.0 %tail.1 = bf16[16,160,128]{2,1,0:T(8,128)(2,1)} custom-call(s32[1]{0:T(128)} %bitcast.host_ref, s32[16]{0:T(128)S(1)} %copy-done, f32[8,16]{1,0:T(8,128)S(1)} %convert_element_type.37.compress_ref, bf16[4,2,160,128]{3,2,1,0:T(8,128)(2,1)S(1)} %add_convert_fusion.1.rest_0_, bf16[2,160,128]{2,1,0:T(8,128)(2,1)S(1)} %collective-permute-done.13.rest_1_, ...), custom_call_target="tpu_custom_call" | custom-call | flops 1000000000 | bytes 8000000 | tf_op jit(solution)/shard_map/tail/pallas_call | solution.py:338
  (50 shorter events, 8.1 us)
Async XLA Ops:
  6.5 66.3 %all-gather.3.cloned.1.call-start = ((), (), s32[]{:S(2)}) async-start(), calls=%async_computation | async-start | bytes 5898240 | tf_op jit(solution)/shard_map/all_gather | solution.py:428
  9.0 20.5 %collective-permute-start.3 = (bf16[2,160,1024]{2,1,0:T(8,128)(2,1)}, bf16[2,160,1024]{2,1,0:T(8,128)(2,1)}, u32[]{:S(2)}, u32[]{:S(2)}) collective-permute-start(bf16[2,160,1024]{2,1,0:T(8,128)(2,1)} %get-tuple-element.78), channel_id=1, source_target_pairs={{0,1},{1,0},{2,3},{3,2},{4,5},{5,4},{6,7},{7,6},{8,9},{9,8},{10,11... | collective-permute-start | bytes 1966088 | tf_op jit(solution)/shard_map/ppermute | solution.py:376
  9.1 32.1 %collective-permute-start = (bf16[2,160,1024]{2,1,0:T(8,128)(2,1)}, bf16[2,160,1024]{2,1,0:T(8,128)(2,1)}, u32[]{:S(2)}, u32[]{:S(2)}) collective-permute-start(bf16[2,160,1024]{2,1,0:T(8,128)(2,1)} %get-tuple-element.78), channel_id=1, source_target_pairs={{0,6},{1,7},{2,0},{3,1},{4,2},{5,3},{6,4},{7,5},{8,14},{9,15},{10,... | collective-permute-start | bytes 1966088 | tf_op jit(solution)/shard_map/ppermute | solution.py:372
  12.2 29.0 %collective-permute-start.1 = (bf16[2,160,1024]{2,1,0:T(8,128)(2,1)}, bf16[2,160,1024]{2,1,0:T(8,128)(2,1)}, u32[]{:S(2)}, u32[]{:S(2)}) collective-permute-start(bf16[2,160,1024]{2,1,0:T(8,128)(2,1)} %get-tuple-element.78), channel_id=1, source_target_pairs={{0,4},{1,5},{2,6},{3,7},{4,0},{5,1},{6,2},{7,3},{8,12},{9,13},{10,... | collective-permute-start | bytes 1966088 | tf_op jit(solution)/shard_map/ppermute | solution.py:372
  12.9 32.0 %collective-permute-start.2 = (bf16[2,160,1024]{2,1,0:T(8,128)(2,1)}, bf16[2,160,1024]{2,1,0:T(8,128)(2,1)}, u32[]{:S(2)}, u32[]{:S(2)}) collective-permute-start(bf16[2,160,1024]{2,1,0:T(8,128)(2,1)} %get-tuple-element.78), channel_id=1, source_target_pairs={{0,2},{1,3},{2,4},{3,5},{4,6},{5,7},{6,0},{7,1},{8,10},{9,11},{10,... | collective-permute-start | bytes 1966088 | tf_op jit(solution)/shard_map/ppermute | solution.py:372
  24.6 4.8 %copy-start.3 = (bf16[24,16]{0,1:T(8,128)(2,1)S(1)}, bf16[24,16]{0,1:T(8,128)(2,1)}, u32[]{:S(2)}) copy-start(bf16[24,16]{0,1:T(8,128)(2,1)} %param.14) | copy-start | bytes 2308
  24.6 4.9 %copy-start.5 = (bf16[8,16]{1,0:T(8,128)(2,1)S(1)}, bf16[8,16]{1,0:T(8,128)(2,1)}, u32[]{:S(2)}) copy-start(bf16[8,16]{1,0:T(8,128)(2,1)} %param.18) | copy-start | bytes 772
  44.9 10.7 %collective-permute-start.4 = (bf16[2,160,1024]{2,1,0:T(8,128)(2,1)}, bf16[2,160,1024]{2,1,0:T(8,128)(2,1)}, u32[]{:S(2)}, u32[]{:S(2)}) collective-permute-start(bf16[2,160,1024]{2,1,0:T(8,128)(2,1)} %collective-permute-done.refs_3_), channel_id=1, source_target_pairs={{0,1},{1,0},{2,3},{3,2},{4,5},{5,4},{6,7},{7,6},{8,9},{9,8},{10,11... | collective-permute-start | bytes 1966088 | tf_op jit(solution)/shard_map/ppermute | solution.py:376
  44.9 10.7 %collective-permute-start.5 = (bf16[2,160,1024]{2,1,0:T(8,128)(2,1)}, bf16[2,160,1024]{2,1,0:T(8,128)(2,1)}, u32[]{:S(2)}, u32[]{:S(2)}) collective-permute-start(bf16[2,160,1024]{2,1,0:T(8,128)(2,1)} %collective-permute-done.1.refs_4_), channel_id=1, source_target_pairs={{0,1},{1,0},{2,3},{3,2},{4,5},{5,4},{6,7},{7,6},{8,9},{9,8},{10,11... | collective-permute-start | bytes 1966088 | tf_op jit(solution)/shard_map/ppermute | solution.py:376
  45.4 10.2 %collective-permute-start.6 = (bf16[2,160,1024]{2,1,0:T(8,128)(2,1)}, bf16[2,160,1024]{2,1,0:T(8,128)(2,1)}, u32[]{:S(2)}, u32[]{:S(2)}) collective-permute-start(bf16[2,160,1024]{2,1,0:T(8,128)(2,1)} %collective-permute-done.2.refs_5_), channel_id=1, source_target_pairs={{0,1},{1,0},{2,3},{3,2},{4,5},{5,4},{6,7},{7,6},{8,9},{9,8},{10,11... | collective-permute-start | bytes 1966088 | tf_op jit(solution)/shard_map/ppermute | solution.py:376
  65.9 24.4 %collective-permute-start.7 = (bf16[4,2,160,128]{3,2,1,0:T(8,128)(2,1)}, bf16[4,2,160,128]{3,2,1,0:T(8,128)(2,1)}, u32[]{:S(2)}, u32[]{:S(2)}) collective-permute-start(bf16[4,2,160,128]{3,2,1,0:T(8,128)(2,1)} %get-tuple-element.56), channel_id=1, source_target_pairs={{0,8},{1,9},{2,10},{3,11},{4,12},{5,13},{6,14},{7,15},{8,16},{9,17... | collective-permute-start | bytes 983048 | tf_op jit(solution)/shard_map/ppermute | solution.py:381
  68.3 22.0 %collective-permute-start.8 = (bf16[4,2,160,128]{3,2,1,0:T(8,128)(2,1)}, bf16[4,2,160,128]{3,2,1,0:T(8,128)(2,1)}, u32[]{:S(2)}, u32[]{:S(2)}) collective-permute-start(bf16[4,2,160,128]{3,2,1,0:T(8,128)(2,1)} %get-tuple-element.57), channel_id=1, source_target_pairs={{0,16},{1,17},{2,18},{3,19},{4,20},{5,21},{6,22},{7,23},{8,24},{9,... | collective-permute-start | bytes 983048 | tf_op jit(solution)/shard_map/ppermute | solution.py:381
  71.4 18.9 %collective-permute-start.9 = (bf16[4,2,160,128]{3,2,1,0:T(8,128)(2,1)}, bf16[4,2,160,128]{3,2,1,0:T(8,128)(2,1)}, u32[]{:S(2)}, u32[]{:S(2)}) collective-permute-start(bf16[4,2,160,128]{3,2,1,0:T(8,128)(2,1)} %get-tuple-element.58), channel_id=1, source_target_pairs={{0,24},{1,25},{2,26},{3,27},{4,28},{5,29},{6,30},{7,31},{8,0},{9,1... | collective-permute-start | bytes 983048 | tf_op jit(solution)/shard_map/ppermute | solution.py:381
  72.9 21.1 %copy-start.1 = (bf16[4,2,160,128]{3,2,1,0:T(8,128)(2,1)S(1)}, bf16[4,2,160,128]{3,2,1,0:T(8,128)(2,1)}, u32[]{:S(2)}) copy-start(bf16[4,2,160,128]{3,2,1,0:T(8,128)(2,1)} %get-tuple-element.68) | copy-start | bytes 983044
  90.3 28.5 %copy-start = (s32[16]{0:T(128)S(1)}, s32[16]{0:T(128)}, u32[]{:S(2)}) copy-start(s32[16]{0:T(128)} %order_ref) | copy-start | bytes 196
  90.3 16.6 %collective-permute-start.10 = (bf16[4,2,160,128]{3,2,1,0:T(8,128)(2,1)}, bf16[4,2,160,128]{3,2,1,0:T(8,128)(2,1)S(1)}, u32[]{:S(2)}, u32[]{:S(2)}) collective-permute-start(bf16[4,2,160,128]{3,2,1,0:T(8,128)(2,1)} %get-tuple-element.65), channel_id=1, source_target_pairs={{0,2},{1,3},{2,4},{3,5},{4,6},{5,7},{6,0},{7,1},{8,10},{9,11},{10,... | collective-permute-start | bytes 983048 | tf_op jit(solution)/shard_map/ppermute | solution.py:381
  90.4 19.8 %collective-permute-start.11 = (bf16[4,2,160,128]{3,2,1,0:T(8,128)(2,1)}, bf16[4,2,160,128]{3,2,1,0:T(8,128)(2,1)S(1)}, u32[]{:S(2)}, u32[]{:S(2)}) collective-permute-start(bf16[4,2,160,128]{3,2,1,0:T(8,128)(2,1)} %get-tuple-element.66), channel_id=1, source_target_pairs={{0,4},{1,5},{2,6},{3,7},{4,0},{5,1},{6,2},{7,3},{8,12},{9,13},{10,... | collective-permute-start | bytes 983048 | tf_op jit(solution)/shard_map/ppermute | solution.py:381
  92.6 17.5 %collective-permute-start.12 = (bf16[4,2,160,128]{3,2,1,0:T(8,128)(2,1)}, bf16[4,2,160,128]{3,2,1,0:T(8,128)(2,1)S(1)}, u32[]{:S(2)}, u32[]{:S(2)}) collective-permute-start(bf16[4,2,160,128]{3,2,1,0:T(8,128)(2,1)} %get-tuple-element.67), channel_id=1, source_target_pairs={{0,6},{1,7},{2,0},{3,1},{4,2},{5,3},{6,4},{7,5},{8,14},{9,15},{10,... | collective-permute-start | bytes 983048 | tf_op jit(solution)/shard_map/ppermute | solution.py:381
  95.4 18.1 %collective-permute-start.16 = (bf16[2,160,128]{2,1,0:T(8,128)(2,1)S(1)}, bf16[2,160,128]{2,1,0:T(8,128)(2,1)S(1)}, u32[]{:S(2)}, u32[]{:S(2)}) collective-permute-start(bf16[2,160,128]{2,1,0:T(8,128)(2,1)S(1)} %get-tuple-element.81), channel_id=1, source_target_pairs={{0,32},{32,64},{64,96},{96,0},{1,33},{33,65},{65,97},{97,1},{2,34}... | collective-permute-start | bytes 245768 | tf_op jit(solution)/shard_map/ppermute | solution.py:388
  96.7 18.2 %collective-permute-start.17 = (bf16[2,160,128]{2,1,0:T(8,128)(2,1)S(1)}, bf16[2,160,128]{2,1,0:T(8,128)(2,1)S(1)}, u32[]{:S(2)}, u32[]{:S(2)}) collective-permute-start(bf16[2,160,128]{2,1,0:T(8,128)(2,1)S(1)} %get-tuple-element.80), channel_id=1, source_target_pairs={{0,64},{32,96},{64,0},{96,32},{1,65},{33,97},{65,1},{97,33},{2,66}... | collective-permute-start | bytes 245768 | tf_op jit(solution)/shard_map/ppermute | solution.py:388
  106.9 7.9 %collective-permute-start.18 = (bf16[2,160,128]{2,1,0:T(8,128)(2,1)S(1)}, bf16[2,160,128]{2,1,0:T(8,128)(2,1)S(1)}, u32[]{:S(2)}, u32[]{:S(2)}) collective-permute-start(bf16[2,160,128]{2,1,0:T(8,128)(2,1)S(1)} %get-tuple-element.79), channel_id=1, source_target_pairs={{0,96},{32,0},{64,32},{96,64},{1,97},{33,1},{65,33},{97,65},{2,98}... | collective-permute-start | bytes 245768 | tf_op jit(solution)/shard_map/ppermute | solution.py:388
  111.3 6.6 %collective-permute-start.13 = (bf16[2,160,128]{2,1,0:T(8,128)(2,1)S(1)}, bf16[2,160,128]{2,1,0:T(8,128)(2,1)S(1)}, u32[]{:S(2)}, u32[]{:S(2)}) collective-permute-start(bf16[2,160,128]{2,1,0:T(8,128)(2,1)S(1)} %get-tuple-element.84), channel_id=1, source_target_pairs={{0,32},{32,64},{64,96},{96,0},{1,33},{33,65},{65,97},{97,1},{2,34}... | collective-permute-start | bytes 245768 | tf_op jit(solution)/shard_map/ppermute | solution.py:388
  111.4 6.5 %collective-permute-start.14 = (bf16[2,160,128]{2,1,0:T(8,128)(2,1)S(1)}, bf16[2,160,128]{2,1,0:T(8,128)(2,1)S(1)}, u32[]{:S(2)}, u32[]{:S(2)}) collective-permute-start(bf16[2,160,128]{2,1,0:T(8,128)(2,1)S(1)} %get-tuple-element.83), channel_id=1, source_target_pairs={{0,64},{32,96},{64,0},{96,32},{1,65},{33,97},{65,1},{97,33},{2,66}... | collective-permute-start | bytes 245768 | tf_op jit(solution)/shard_map/ppermute | solution.py:388
  113.5 5.3 %collective-permute-start.15 = (bf16[2,160,128]{2,1,0:T(8,128)(2,1)S(1)}, bf16[2,160,128]{2,1,0:T(8,128)(2,1)S(1)}, u32[]{:S(2)}, u32[]{:S(2)}) collective-permute-start(bf16[2,160,128]{2,1,0:T(8,128)(2,1)S(1)} %get-tuple-element.82), channel_id=1, source_target_pairs={{0,96},{32,0},{64,32},{96,64},{1,97},{33,1},{65,33},{97,65},{2,98}... | collective-permute-start | bytes 245768 | tf_op jit(solution)/shard_map/ppermute | solution.py:388
  (2 other events, 9.2 us)
Sparse Core Ops, SparseCore 0:
  9.1 40.1 all-gather.2

commit v5 on v4

--- a/solution.py
+++ b/solution.py
@@ -37,10 +37,10 @@
         )
         at_z, at_y, at_core = v >> 13, (v >> 11) & 3, (v >> 10) & 1
         here = jnp.where(over_z, at_y - y, at_z - z) == 0
-        away = (at_y - y) & 3
+        away = jnp.where(over_z, at_z - z, at_y - y) & 3
+        shard = jnp.where(away == 2, 4, 2 + (away >> 1))
         other = at_core ^ core
-        ring = jnp.where(away == 0, other, away + 1 + 3 * other)
-        shard = jnp.where(over_z, at_z * 2 + at_core, ring)
+        shard = jnp.where(away == 0, other, shard + 3 * other)
         local = shard * ROWS_DEV + (v & (ROWS_DEV - 1))
         local = jnp.where(here & (slot < used), local, -1)
         for s in range(8):
@@ -100,10 +100,12 @@
     )(pos, idx, lens)
 
 
-def pool_kernel(first_shard, n_shards, has_base, is_last, table0, *refs):
-    mask_ref, keys_ref, lid_ref = refs[:3]
-    tabs = refs[3 : 3 + n_shards]
-    refs = refs[3 + n_shards :]
+def pool_kernel(layout, has_base, is_last, table0, *refs):
+    n_pieces = len(layout)
+    mask_ref, lid_ref = refs[:2]
+    keys = refs[2 : 2 + n_pieces]
+    tabs = refs[2 + n_pieces : 2 + 2 * n_pieces]
+    refs = refs[2 + 2 * n_pieces :]
     if has_base:
         base_ref, refs = refs[0], refs[1:]
     if is_last:
@@ -111,8 +113,8 @@
     else:
         sums, counts, extra = refs
     table, step = pl.program_id(0), pl.program_id(1)
-    first_block = first_shard * (ROWS_DEV // SUB)
-    n_blocks = n_shards * (ROWS_DEV // SUB)
+    first_block = layout[0][0]
+    n_blocks = sum(n for _, n in layout)
     row_ids = [
         (lax.broadcasted_iota(jnp.int32, (16, PAIR), 0) + c * 16)
         .astype(jnp.float32)
@@ -125,27 +127,25 @@
 
     for part in range(2):
         bag = 4 * step + 2 * part
-        for blk in range(n_blocks):
-            k1, m1, k2, m2 = (
-                jnp.concatenate(
-                    [
-                        wide(keys_ref[0, first_block + blk, v, pl.ds(bag + half, 1), :])
-                        for half in range(2)
-                    ],
-                    axis=1,
+        for (first, n), key in zip(layout, keys):
+            for b in range(n):
+                k1, m1, k2, m2 = (
+                    jnp.concatenate(
+                        [wide(key[0, 0, b, v, pl.ds(bag + half, 1), :]) for half in range(2)],
+                        axis=1,
+                    )
+                    for v in range(4)
                 )
-                for v in range(4)
-            )
-            for c in range(SUB // 16):
-                counts[part, blk * SUB + c * 16 : blk * SUB + (c + 1) * 16, :] = jnp.where(
-                    k1 == row_ids[c], m1, jnp.where(k2 == row_ids[c], m2, jnp.bfloat16(0))
-                )
+                row = (first - first_block + b) * SUB
+                for c in range(SUB // 16):
+                    counts[part, row + c * 16 : row + (c + 1) * 16, :] = jnp.where(
+                        k1 == row_ids[c], m1, jnp.where(k2 == row_ids[c], m2, jnp.bfloat16(0))
+                    )
         total = base_ref[0, 0, part] if has_base else None
-        for g in range(n_shards):
+        for (first, n), tab in zip(layout, tabs):
+            row = (first - first_block) * SUB
             product = jnp.dot(
-                tabs[g][0],
-                counts[part, g * ROWS_DEV : (g + 1) * ROWS_DEV, :],
-                preferred_element_type=jnp.float32,
+                tab[0], counts[part, row : row + n * SUB, :], preferred_element_type=jnp.float32
             )
             total = product if total is None else total + product
         sums[0, 0, part] = total
@@ -165,15 +165,18 @@
                 def _():
                     for half in range(2):
                         row = pl.ds(bag + half, 1)
-                        k1 = keys_ref[0, blk, 0, row, :]
-                        k2 = keys_ref[0, blk, 2, row, :]
-                        left = []
-                        for s in range(8):
-                            x = lid_ref[0, s, row, :]
-                            low = jnp.where(
-                                (x >> 8) == blk, (x & (SUB - 1)).astype(jnp.float32), -1.0
-                            )
-                            left.append(wide(jnp.where((low == k1) | (low == k2), -1.0, low)))
+                        lids = [lid_ref[0, s, row, :] for s in range(8)]
+                        low = [
+                            jnp.where((x >> 8) == blk, (x & (SUB - 1)).astype(jnp.float32), -1.0)
+                            for x in lids
+                        ]
+                        last = functools.reduce(jnp.maximum, low)
+                        first = functools.reduce(
+                            jnp.minimum, [jnp.where(x < 0.0, 511.0, x) for x in low]
+                        )
+                        left = [
+                            wide(jnp.where((x == first) | (x == last), -1.0, x)) for x in low
+                        ]
                         for c in range(SUB // 16):
                             n = jnp.zeros((16, LANES), jnp.bfloat16)
                             for k in left:
@@ -181,13 +184,13 @@
                                     k == row_ids[c][:, :LANES], jnp.bfloat16(1), jnp.bfloat16(0)
                                 )
                             extra[c * 16 : (c + 1) * 16, half * LANES : (half + 1) * LANES] = n
-                    columns = pl.ds(pl.multiple_of((at & 3) * SUB, SUB), SUB)
-                    for g in range(n_shards):
-
-                        @pl.when((at >> 2) == g)
-                        def _(g=g):
+                    for (first, n), tab in zip(layout, tabs):
+
+                        @pl.when((blk >= first) & (blk < first + n))
+                        def _(first=first, tab=tab):
+                            columns = pl.ds(pl.multiple_of((blk - first) * SUB, SUB), SUB)
                             sums[0, 0, part] += jnp.dot(
-                                tabs[g][0, :, columns],
+                                tab[0, :, columns],
                                 extra[...],
                                 preferred_element_type=jnp.float32,
                             )
@@ -207,31 +210,43 @@
                     outs[d][2 * part + 1, 0] = result[:, LANES:]
 
 
-def piece(array, first_table=0, stacked=None):
-    block = (1,) + array.shape[-2:]
-    if stacked is None:
-        return array, pl.BlockSpec(block, lambda j, i: (first_table + j, 0, 0))
-    return array, pl.BlockSpec((None,) + block, lambda j, i: (stacked, j, 0, 0))
-
-
-def pool(first_shard, tables, masks, keys, lids, shards, base, is_last, name):
+def pool(tables, masks, keys, lids, pieces, base, is_last, name):
     n_tables = len(tables)
     table0 = tables[0]
-    n_shards = len(shards)
-    emb, rows = shards[0][0].shape[-2:]
+    emb = pieces[0][0].shape[1]
     sums_block = (1, 1, 2, emb, PAIR)
     sums_spec = pl.BlockSpec(sums_block, lambda j, i: (j, i, 0, 0, 0))
+    layout, key_specs, tab_specs = [], [], []
+    for array, start_table, shard, start in pieces:
+        n = array.shape[2] // SUB
+        layout.append(((shard * ROWS_DEV + start) // SUB, n))
+        key_specs.append(
+            pl.BlockSpec(
+                (1, 1, n) + keys.shape[3:],
+                lambda j, i, shard=shard, at=start // SUB // n: (table0 + j, shard, at, 0, 0, 0),
+            )
+        )
+        tab_specs.append(
+            pl.BlockSpec(
+                (1,) + array.shape[1:], lambda j, i, skip=table0 - start_table: (skip + j, 0, 0)
+            )
+        )
+    rows = sum(n for _, n in layout) * SUB
     in_specs = [
         pl.BlockSpec(memory_space=pltpu.SMEM),
-        pl.BlockSpec((1,) + keys.shape[1:], lambda j, i: (table0 + j, 0, 0, 0, 0)),
         pl.BlockSpec((1,) + lids.shape[1:], lambda j, i: (table0 + j, 0, 0, 0)),
-    ] + [spec for _, spec in shards]
-    args = [masks, keys, lids] + [array for array, _ in shards]
+        *key_specs,
+        *tab_specs,
+    ]
+    args = [masks, lids] + [keys] * len(pieces) + [p[0] for p in pieces]
     if base is not None:
-        in_specs.append(sums_spec)
-        args.append(base)
+        array, start_table = base
+        in_specs.append(
+            pl.BlockSpec(sums_block, lambda j, i: (table0 - start_table + j, i, 0, 0, 0))
+        )
+        args.append(array)
     scratch = [
-        pltpu.VMEM((2, n_shards * rows, PAIR), jnp.bfloat16),
+        pltpu.VMEM((2, rows, PAIR), jnp.bfloat16),
         pltpu.VMEM((SUB, PAIR), jnp.bfloat16),
     ]
     if is_last:
@@ -242,9 +257,7 @@
         out_specs = sums_spec
         out_shape = jax.ShapeDtypeStruct((n_tables, 4, 2, emb, PAIR), jnp.float32)
     return pl.pallas_call(
-        functools.partial(
-            pool_kernel, first_shard, n_shards, base is not None, is_last, table0
-        ),
+        functools.partial(pool_kernel, tuple(layout), base is not None, is_last, table0),
         grid=(n_tables, 4),
         in_specs=in_specs,
         out_specs=out_specs,
@@ -252,7 +265,7 @@
         scratch_shapes=scratch,
         compiler_params=pltpu.CompilerParams(vmem_limit_bytes=60 << 20),
         cost_estimate=pl.CostEstimate(
-            flops=2 * n_tables * n_shards * rows * 2048 * 256,
+            flops=2 * n_tables * rows * 2048 * 256,
             bytes_accessed=5_000_000,
             transcendentals=0,
         ),
@@ -368,10 +381,6 @@
     return pairs
 
 
-def near_shards(shard, axis):
-    return [lax.ppermute(shard, "row", row_moves(axis, 4 - rel)) for rel in range(1, 4)]
-
-
 def other_core(x):
     return lax.ppermute(x, "row", row_moves("core", 1))
 
@@ -422,47 +431,67 @@
     )
     order, proj, compress, fm_gain, gain = small
 
-    ring = flipped[2:]
-    own_far = other_core(ring)
-    near = near_shards(ring, "y")
-    whole = lax.all_gather(
-        flipped[:2],
-        "row",
-        axis_index_groups=[
-            [z * 8 + y * 2 + core for z in range(4) for core in range(2)] for y in range(4)
-        ],
-    )
+    keys = keys.reshape((keys.shape[0], GATHER, ROWS_DEV // SUB) + keys.shape[2:])
+    pairs = [(0, 1), (2, 3)]
+    axes = ["z", "y"]
+
+    def move(x, axis, step):
+        return lax.ppermute(x, "row", row_moves(axis, step))
+
+    sides = []
+    for p in range(2):
+        mine = flipped[2 * p : 2 * p + 2]
+        sides.append([move(mine, axes[p], 3), move(mine, axes[p], 1)])
+    own_far = other_core(flipped)
+    sides, masks = lax.optimization_barrier((sides, masks))
+    half = ROWS_DEV // 2
+    beyond = [
+        [move(up1[:, :, :half], axis, 3), move(down1[:, :, half:], axis, 1)]
+        for (up1, down1), axis in zip(sides, axes)
+    ]
+
+    def stage(p, arrays, shard):
+        one, three, two_a, two_b = arrays
+        start = pairs[p][0]
+        return [
+            (one, start, shard, 0),
+            (three, start, shard + 1, 0),
+            (two_a, start, shard + 2, 0),
+            (two_b, start, shard + 2, half),
+        ]
+
     sums = pool(
-        0,
-        (2, 3),
+        (0, 1, 2, 3),
         masks,
         keys,
         lids,
-        [piece(flipped, 2), piece(own_far)],
+        [(flipped, 0, 0, 0), (own_far, 0, 1, 0)],
         None,
         False,
         "pool_own",
     )
-    near, sums = lax.optimization_barrier((near, sums))
-    far = [other_core(x) for x in near]
-    sums = pool(2, (2, 3), masks, keys, lids, [piece(x) for x in near], sums, False, "pool_near")
-    far, sums = lax.optimization_barrier((far, sums))
-    blocks = pool(5, (2, 3), masks, keys, lids, [piece(x) for x in far], sums, True, "pool_far")
+    sums, beyond, masks = lax.optimization_barrier((sums, beyond, masks))
+    near = [sides[p] + beyond[p] for p in range(2)]
+    far = [[other_core(x) for x in near[p]] for p in range(2)]
+    after = []
+    for p in range(2):
+        after.append(
+            pool(
+                pairs[p], masks, keys, lids, stage(p, near[p], 2), (sums, 0), False, "pool_near"
+            )
+        )
+        masks, _ = lax.optimization_barrier((masks, after[p]))
+    blocks = pool(
+        pairs[0], masks, keys, lids, stage(0, far[0], 5), (after[0], 0), True, "pool_far"
+    )
     masks, _ = lax.optimization_barrier((masks, blocks))
-    arrived = to_owners(blocks, "z")
+    arrived = to_owners(blocks, axes[1])
     blocks = pool(
-        0,
-        (0, 1),
-        masks,
-        keys,
-        lids,
-        [piece(whole, stacked=g) for g in range(GATHER)],
-        None,
-        True,
-        "pool_whole",
+        pairs[1], masks, keys, lids, stage(1, far[1], 5), (after[1], 2), True, "pool_far"
     )
     blocks, arrived = lax.optimization_barrier((blocks, arrived))
-    parts = to_hosts(to_owners(blocks, "y")) + to_hosts(arrived)
+    parts_b = to_hosts(to_owners(blocks, axes[0]))
+    parts = to_hosts(arrived) + parts_b
     result = tail(pos[:1], order, proj, compress, parts, fm_gain, up, down, gain)
     return jnp.transpose(result, (2, 0, 1))
 

time: 131 us -> 140 us (1.069)
  between operations: 13.6 us -> 0.19 us
  starting transfers between devices: 26.6 us -> 36.1 us
  Pallas kernels: 60.1 us -> 67.8 us
  local copies, waits for them, and re-layouts: 7.35 us -> 14 us
  waiting for transfers between devices: 18.4 us -> 16.2 us
    pallas_call x4 -> x5, Pallas kernels: 46.5 us -> 54.2 us  [pool(): pl.pallas_call(functools.partial(pool_kernel, tuple(layout), base is not...]
    ppermute x3 -> x8, starting transfers between devices: 4.77 us -> 12.1 us  [move(): return lax.ppermute(x, 'row', row_moves(axis, step))]
    slice x1 -> x5, local copies, waits for them, and re-layouts: 2.42 us -> 8.6 us  [the longest x2 3.45 us: on_device(): up1[:, :, :half]]
    ppermute x3 -> x8, waiting for transfers between devices: 6.74 us -> 2.52 us  [move(): return lax.ppermute(x, 'row', row_moves(axis, step))]
    ppermute x6, waiting for transfers between devices: 7.68 us -> 10.2 us  [to_owners(): lax.ppermute(blocks[d], 'row', row_moves(axis, d))]
    ppermute x4 -> x9, starting transfers between devices: 0.61 us -> 2.33 us  [other_core(): return lax.ppermute(x, 'row', row_moves('core', 1))]
    ppermute x6, starting transfers between devices: 10.6 us -> 12 us  [to_hosts(): lax.ppermute(total[d], 'hst', [(h, (h + d) % 4) for h in range(4)])]
    unnamed x16 -> x18, local copies, waits for them, and re-layouts: 4.74 us -> 5.17 us
  transfers between devices with their start and end apart: 20 -> 29, of which waited for: 5 -> 8; matrix products, arithmetic and copies ran while one was open for 7% -> 13% of each run, Pallas kernels for 42% -> 45%
where the time goes in v5:
time: 140 us; the launch traced here: 139 us
  Pallas kernels  67.8 us (48%)
  starting transfers between devices  36.1 us (26%)
  waiting for transfers between devices  16.2 us (12%)
  local copies, waits for them, and re-layouts  14 us (10%)
  other arithmetic  4.62 us (3%)
    pallas_call x5, Pallas kernels, pool(): pl.pallas_call(functools.partial(pool_kernel, tuple(layout), base is not...  54.2 us
    ppermute x8, starting transfers between devices, move(): return lax.ppermute(x, 'row', row_moves(axis, step))  12.1 us
    ppermute x6, starting transfers between devices, to_hosts(): lax.ppermute(total[d], 'hst', [(h, (h + d) % 4) for h in range(4)])  12 us
    ppermute x6, waiting for transfers between devices, to_owners(): lax.ppermute(blocks[d], 'row', row_moves(axis, d))  10.2 us
    ppermute x6, starting transfers between devices, to_owners(): lax.ppermute(blocks[d], 'row', row_moves(axis, d))  9.64 us
    pallas_call x1, Pallas kernels, prep(): pl.pallas_call(prep_kernel, grid=(tables,), in_specs=[pl.BlockSpec(memory...  8.57 us
    unnamed x18, local copies, waits for them, and re-layouts  5.17 us
    pallas_call x1, Pallas kernels, tail(): pl.pallas_call(tail_kernel, grid=(1,), in_specs=[smem] * 3 + ([mine] + [t...  5.03 us
  transfers between devices with their start and end apart: 29, of which 8 were waited for; matrix products, arithmetic and copies ran while one was open for 13% of the time, Pallas kernels for 45%

profile of v5, /device:TPU:0, one launch (start us, length us, event | category | flops | bytes accessed | tf_op | source)
XLA Modules:
  0.0 138.9 jit_solution(4293662259517492349)
XLA Ops:
  0.0 2.4 %fusion = (bf16[2,160,1024]{2,1,0:T(8,128)(2,1)}, bf16[2,160,1024]{2,1,0:T(8,128)(2,1)}) fusion(bf16[4,160,1024]{2,1,0:T(8,128)(2,1)} %bitcast.49), kind=kLoop, calls=%fused_computation.9 | loop fusion | bytes 2621440 | tf_op jit(solution)/shard_map/slice | solution.py:443
  2.5 4.1 %collective-permute-start = (bf16[2,160,1024]{2,1,0:T(8,128)(2,1)}, bf16[2,160,1024]{2,1,0:T(8,128)(2,1)}, u32[]{:S(2)}, u32[]{:S(2)}) collective-permute-start(bf16[2,160,1024]{2,1,0:T(8,128)(2,1)} %get-tuple-element.88), channel_id=1, source_target_pairs={{0,24},{1,25},{2,26},{3,27},{4,28},{5,29},{6,30},{7,31},{8,0},{9,1... | collective-permute-start | bytes 1966088 | tf_op jit(solution)/shard_map/ppermute | solution.py:439
  6.6 3.0 %collective-permute-start.2 = (bf16[2,160,1024]{2,1,0:T(8,128)(2,1)}, bf16[2,160,1024]{2,1,0:T(8,128)(2,1)}, u32[]{:S(2)}, u32[]{:S(2)}) collective-permute-start(bf16[2,160,1024]{2,1,0:T(8,128)(2,1)} %get-tuple-element.87), channel_id=1, source_target_pairs={{0,6},{1,7},{2,0},{3,1},{4,2},{5,3},{6,4},{7,5},{8,14},{9,15},{10,... | collective-permute-start | bytes 1966088 | tf_op jit(solution)/shard_map/ppermute | solution.py:439
  10.2 8.6 %prep.1 = (f32[4,32,4,16,128]{4,3,2,1,0:T(8,128)}, s32[4,8,16,128]{3,2,1,0:T(8,128)}, s32[4,16,128]{2,1,0:T(8,128)}) custom-call(s32[4]{0:T(128)} %pad_add_fusion.pos_ref, s32[4,8,16384]{2,1,0:T(8,128)} %bitcast.47, s32[4,16384]{1,0:T(4,128)} %bitcast.51), custom_call_target="tpu_custom_call" | custom-call | flops 40000000 | bytes 9000000 | tf_op jit(solution)/shard_map/prep/pallas_call | solution.py:77
  20.2 3.0 %copy.16 = bf16[1024,1280]{0,1:T(8,128)(2,1)S(1)} copy(bf16[1024,1280]{1,0:T(8,128)(2,1)} %param.17) | data formatting | bytes 5242880 | tf_op args[7]
  25.2 2.5 %collective-permute-done.3.refs_7_ = bf16[2,160,1024]{2,1,0:T(8,128)(2,1)} collective-permute-done((bf16[2,160,1024]{2,1,0:T(8,128)(2,1)}, bf16[2,160,1024]{2,1,0:T(8,128)(2,1)}, u32[]{:S(2)}, u32[]{:S(2)}) %collective-permute-start.3) | collective-permute-done | bytes 655392 | tf_op jit(solution)/shard_map/ppermute | solution.py:439
  28.8 1.7 %slice.38 = bf16[2,160,512]{2,1,0:T(8,128)(2,1)} slice(bf16[2,160,1024]{2,1,0:T(8,128)(2,1)} %collective-permute-done.refs_6_), slice={[0:2], [0:160], [0:512]} | slice | bytes 655360 | tf_op jit(solution)/shard_map/slice | solution.py:449
  30.5 3.0 %collective-permute-start.5 = (bf16[2,160,512]{2,1,0:T(8,128)(2,1)}, bf16[2,160,512]{2,1,0:T(8,128)(2,1)}, u32[]{:S(2)}, u32[]{:S(2)}) collective-permute-start(bf16[2,160,512]{2,1,0:T(8,128)(2,1)} %slice.38), channel_id=1, source_target_pairs={{0,24},{1,25},{2,26},{3,27},{4,28},{5,29},{6,30},{7,31},{8,0},{9,1... | collective-permute-start | bytes 983048 | tf_op jit(solution)/shard_map/ppermute | solution.py:439
  33.5 1.7 %slice.40 = bf16[2,160,512]{2,1,0:T(8,128)(2,1)} slice(bf16[2,160,1024]{2,1,0:T(8,128)(2,1)} %collective-permute-done.2.refs_6_), slice={[0:2], [0:160], [0:512]} | slice | bytes 655360 | tf_op jit(solution)/shard_map/slice | solution.py:449
  38.9 13.9 %pool_own.1.refs_10_ = f32[4,4,2,160,256]{4,3,2,1,0:T(8,128)} custom-call(s32[4,16]{1,0:T(4,128)} %reduce.7.refs_0_, s32[4,8,16,128]{3,2,1,0:T(8,128)} %get-tuple-element.51.refs_1_, f32[4,8,4,4,16,128]{5,4,3,2,1,0:T(8,128)} %bitcast.29, f32[4,8,4,4,16,128]{5,4,3,2,1,0:T(8,128)} %bitcast.30, bf16[4,160,1024]{2,1,0:T(8,128)(2,1)} %bitcast.50, ...), custom_call_target="tpu_custom_call" | custom-call | flops 8589934592 | bytes 5000000 | tf_op jit(solution)/shard_map/pool_own/pallas_call | solution.py:259
  53.9 9.7 %pool_near.2.refs_10_ = f32[2,4,2,160,256]{4,3,2,1,0:T(8,128)} custom-call(s32[4,16]{1,0:T(4,128)} %reduce.7.refs_0_, s32[4,8,16,128]{3,2,1,0:T(8,128)} %get-tuple-element.51.refs_1_, f32[4,8,4,4,16,128]{5,4,3,2,1,0:T(8,128)} %bitcast.31, f32[4,8,4,4,16,128]{5,4,3,2,1,0:T(8,128)} %bitcast.32, f32[4,8,4,4,16,128]{5,4,3,2,1,0:T(8,128)} %bitcast.33, ...), custom_call_target="tpu_custom_call" | custom-call | flops 6442450944 | bytes 5000000 | tf_op jit(solution)/shard_map/pool_near/pallas_call | solution.py:259
  63.8 9.7 %pool_near.3.refs_10_ = f32[2,4,2,160,256]{4,3,2,1,0:T(8,128)} custom-call(s32[4,16]{1,0:T(4,128)} %reduce.7.refs_0_, s32[4,8,16,128]{3,2,1,0:T(8,128)} %get-tuple-element.51.refs_1_, f32[4,8,4,4,16,128]{5,4,3,2,1,0:T(8,128)} %bitcast.35, f32[4,8,4,4,16,128]{5,4,3,2,1,0:T(8,128)} %bitcast.36, f32[4,8,4,4,16,128]{5,4,3,2,1,0:T(8,128)} %bitcast.37, ...), custom_call_target="tpu_custom_call" | custom-call | flops 6442450944 | bytes 5000000 | tf_op jit(solution)/shard_map/pool_near/pallas_call | solution.py:259
  75.0 10.0 %pool_far.2 = (bf16[4,2,160,128]{3,2,1,0:T(8,128)(2,1)}, bf16[4,2,160,128]{3,2,1,0:T(8,128)(2,1)}, bf16[4,2,160,128]{3,2,1,0:T(8,128)(2,1)}, bf16[4,2,160,128]{3,2,1,0:T(8,128)(2,1)}) custom-call(s32[4,16]{1,0:T(4,128)} %reduce.7.refs_0_, s32[4,8,16,128]{3,2,1,0:T(8,128)} %get-tuple-element.51.refs_1_, f32[4,8,4,4,16,128]{5,4,3,2,1,0:T(8,128)} %bitcast.39, ...), custom_call_target="tpu_custom_call" | custom-call | flops 6442450944 | bytes 5000000 | tf_op jit(solution)/shard_map/pool_far/pallas_call | solution.py:259
  86.6 2.8 %collective-permute-start.18 = (bf16[4,2,160,128]{3,2,1,0:T(8,128)(2,1)}, bf16[4,2,160,128]{3,2,1,0:T(8,128)(2,1)}, u32[]{:S(2)}, u32[]{:S(2)}) collective-permute-start(bf16[4,2,160,128]{3,2,1,0:T(8,128)(2,1)} %get-tuple-element.67), channel_id=1, source_target_pairs={{0,4},{1,5},{2,6},{3,7},{4,0},{5,1},{6,2},{7,3},{8,12},{9,13},{10,... | collective-permute-start | bytes 983048 | tf_op jit(solution)/shard_map/ppermute | solution.py:390
  90.1 10.9 %pool_far.3 = (bf16[4,2,160,128]{3,2,1,0:T(8,128)(2,1)}, bf16[4,2,160,128]{3,2,1,0:T(8,128)(2,1)}, bf16[4,2,160,128]{3,2,1,0:T(8,128)(2,1)}, bf16[4,2,160,128]{3,2,1,0:T(8,128)(2,1)}) custom-call(s32[4,16]{1,0:T(4,128)} %reduce.7.refs_0_, s32[4,8,16,128]{3,2,1,0:T(8,128)} %get-tuple-element.51.refs_1_, f32[4,8,4,4,16,128]{5,4,3,2,1,0:T(8,128)} %bitcast.43, ...), custom_call_target="tpu_custom_call" | custom-call | flops 6442450944 | bytes 5000000 | tf_op jit(solution)/shard_map/pool_far/pallas_call | solution.py:259
  101.0 3.8 %collective-permute-done.18 = bf16[4,2,160,128]{3,2,1,0:T(8,128)(2,1)} collective-permute-done((bf16[4,2,160,128]{3,2,1,0:T(8,128)(2,1)}, bf16[4,2,160,128]{3,2,1,0:T(8,128)(2,1)}, u32[]{:S(2)}, u32[]{:S(2)}) %collective-permute-start.18) | collective-permute-done | bytes 327712 | tf_op jit(solution)/shard_map/ppermute | solution.py:390
  104.8 4.5 %collective-permute-start.24 = (bf16[4,2,160,128]{3,2,1,0:T(8,128)(2,1)}, bf16[4,2,160,128]{3,2,1,0:T(8,128)(2,1)S(1)}, u32[]{:S(2)}, u32[]{:S(2)}) collective-permute-start(bf16[4,2,160,128]{3,2,1,0:T(8,128)(2,1)} %get-tuple-element.80), channel_id=1, source_target_pairs={{0,16},{1,17},{2,18},{3,19},{4,20},{5,21},{6,22},{7,23},{8,24},{9,... | collective-permute-start | bytes 983048 | tf_op jit(solution)/shard_map/ppermute | solution.py:390
  110.8 2.0 %collective-permute-start.20 = (bf16[2,160,128]{2,1,0:T(8,128)(2,1)S(1)}, bf16[2,160,128]{2,1,0:T(8,128)(2,1)S(1)}, u32[]{:S(2)}, u32[]{:S(2)}) collective-permute-start(bf16[2,160,128]{2,1,0:T(8,128)(2,1)S(1)} %get-tuple-element.94), channel_id=1, source_target_pairs={{0,32},{32,64},{64,96},{96,0},{1,33},{33,65},{65,97},{97,1},{2,34}... | collective-permute-start | bytes 245768 | tf_op jit(solution)/shard_map/ppermute | solution.py:397
  112.8 2.4 %collective-permute-start.21 = (bf16[2,160,128]{2,1,0:T(8,128)(2,1)S(1)}, bf16[2,160,128]{2,1,0:T(8,128)(2,1)S(1)}, u32[]{:S(2)}, u32[]{:S(2)}) collective-permute-start(bf16[2,160,128]{2,1,0:T(8,128)(2,1)S(1)} %get-tuple-element.93), channel_id=1, source_target_pairs={{0,64},{32,96},{64,0},{96,32},{1,65},{33,97},{65,1},{97,33},{2,66}... | collective-permute-start | bytes 245768 | tf_op jit(solution)/shard_map/ppermute | solution.py:397
  115.1 1.9 %collective-permute-done.23 = bf16[4,2,160,128]{3,2,1,0:T(8,128)(2,1)S(1)} collective-permute-done((bf16[4,2,160,128]{3,2,1,0:T(8,128)(2,1)}, bf16[4,2,160,128]{3,2,1,0:T(8,128)(2,1)S(1)}, u32[]{:S(2)}, u32[]{:S(2)}) %collective-permute-start.23) | collective-permute-done | bytes 327712 | tf_op jit(solution)/shard_map/ppermute | solution.py:390
  118.6 4.5 %collective-permute-done.24 = bf16[4,2,160,128]{3,2,1,0:T(8,128)(2,1)S(1)} collective-permute-done((bf16[4,2,160,128]{3,2,1,0:T(8,128)(2,1)}, bf16[4,2,160,128]{3,2,1,0:T(8,128)(2,1)S(1)}, u32[]{:S(2)}, u32[]{:S(2)}) %collective-permute-start.24) | collective-permute-done | bytes 327712 | tf_op jit(solution)/shard_map/ppermute | solution.py:390
  124.4 2.2 %collective-permute-start.26 = (bf16[2,160,128]{2,1,0:T(8,128)(2,1)S(1)}, bf16[2,160,128]{2,1,0:T(8,128)(2,1)S(1)}, u32[]{:S(2)}, u32[]{:S(2)}) collective-permute-start(bf16[2,160,128]{2,1,0:T(8,128)(2,1)S(1)} %get-tuple-element.91), channel_id=1, source_target_pairs={{0,32},{32,64},{64,96},{96,0},{1,33},{33,65},{65,97},{97,1},{2,34}... | collective-permute-start | bytes 245768 | tf_op jit(solution)/shard_map/ppermute | solution.py:397
  126.6 2.8 %collective-permute-start.27 = (bf16[2,160,128]{2,1,0:T(8,128)(2,1)S(1)}, bf16[2,160,128]{2,1,0:T(8,128)(2,1)S(1)}, u32[]{:S(2)}, u32[]{:S(2)}) collective-permute-start(bf16[2,160,128]{2,1,0:T(8,128)(2,1)S(1)} %get-tuple-element.90), channel_id=1, source_target_pairs={{0,64},{32,96},{64,0},{96,32},{1,65},{33,97},{65,1},{97,33},{2,66}... | collective-permute-start | bytes 245768 | tf_op jit(solution)/shard_map/ppermute | solution.py:397
  133.9 5.0 %tail.1 = bf16[16,160,128]{2,1,0:T(8,128)(2,1)} custom-call(s32[1]{0:T(128)} %bitcast.host_ref, s32[16]{0:T(128)S(1)} %copy-done, f32[8,16]{1,0:T(8,128)S(1)} %convert_element_type.37.compress_ref, bf16[4,2,160,128]{3,2,1,0:T(8,128)(2,1)S(1)} %add_convert_fusion.1.rest_0_, bf16[2,160,128]{2,1,0:T(8,128)(2,1)S(1)} %collective-permute-done.20.rest_1_, ...), custom_call_target="tpu_custom_call" | custom-call | flops 1000000000 | bytes 8000000 | tf_op jit(solution)/shard_map/tail/pallas_call | solution.py:351
  (74 shorter events, 22.4 us)
Async XLA Ops:
  0.0 37.9 %collective-permute-start.4 = (bf16[4,160,1024]{2,1,0:T(8,128)(2,1)}, bf16[4,160,1024]{2,1,0:T(8,128)(2,1)}, u32[]{:S(2)}, u32[]{:S(2)}) collective-permute-start(bf16[4,160,1024]{2,1,0:T(8,128)(2,1)} %bitcast.48), channel_id=1, source_target_pairs={{0,1},{1,0},{2,3},{3,2},{4,5},{5,4},{6,7},{7,6},{8,9},{9,8},{10,11... | collective-permute-start | bytes 3932168 | tf_op jit(solution)/shard_map/ppermute | solution.py:385
  2.5 22.7 %collective-permute-start = (bf16[2,160,1024]{2,1,0:T(8,128)(2,1)}, bf16[2,160,1024]{2,1,0:T(8,128)(2,1)}, u32[]{:S(2)}, u32[]{:S(2)}) collective-permute-start(bf16[2,160,1024]{2,1,0:T(8,128)(2,1)} %get-tuple-element.88), channel_id=1, source_target_pairs={{0,24},{1,25},{2,26},{3,27},{4,28},{5,29},{6,30},{7,31},{8,0},{9,1... | collective-permute-start | bytes 1966088 | tf_op jit(solution)/shard_map/ppermute | solution.py:439
  6.6 18.6 %collective-permute-start.1 = (bf16[2,160,1024]{2,1,0:T(8,128)(2,1)}, bf16[2,160,1024]{2,1,0:T(8,128)(2,1)}, u32[]{:S(2)}, u32[]{:S(2)}) collective-permute-start(bf16[2,160,1024]{2,1,0:T(8,128)(2,1)} %get-tuple-element.88), channel_id=1, source_target_pairs={{0,8},{1,9},{2,10},{3,11},{4,12},{5,13},{6,14},{7,15},{8,16},{9,17... | collective-permute-start | bytes 1966088 | tf_op jit(solution)/shard_map/ppermute | solution.py:439
  6.6 18.6 %collective-permute-start.2 = (bf16[2,160,1024]{2,1,0:T(8,128)(2,1)}, bf16[2,160,1024]{2,1,0:T(8,128)(2,1)}, u32[]{:S(2)}, u32[]{:S(2)}) collective-permute-start(bf16[2,160,1024]{2,1,0:T(8,128)(2,1)} %get-tuple-element.87), channel_id=1, source_target_pairs={{0,6},{1,7},{2,0},{3,1},{4,2},{5,3},{6,4},{7,5},{8,14},{9,15},{10,... | collective-permute-start | bytes 1966088 | tf_op jit(solution)/shard_map/ppermute | solution.py:439
  9.6 18.1 %collective-permute-start.3 = (bf16[2,160,1024]{2,1,0:T(8,128)(2,1)}, bf16[2,160,1024]{2,1,0:T(8,128)(2,1)}, u32[]{:S(2)}, u32[]{:S(2)}) collective-permute-start(bf16[2,160,1024]{2,1,0:T(8,128)(2,1)} %get-tuple-element.87), channel_id=1, source_target_pairs={{0,2},{1,3},{2,4},{3,5},{4,6},{5,7},{6,0},{7,1},{8,10},{9,11},{10,... | collective-permute-start | bytes 1966088 | tf_op jit(solution)/shard_map/ppermute | solution.py:439
  28.7 34.9 %collective-permute-start.10 = (bf16[2,160,1024]{2,1,0:T(8,128)(2,1)}, bf16[2,160,1024]{2,1,0:T(8,128)(2,1)}, u32[]{:S(2)}, u32[]{:S(2)}) collective-permute-start(bf16[2,160,1024]{2,1,0:T(8,128)(2,1)} %collective-permute-done.1.refs_7_), channel_id=1, source_target_pairs={{0,1},{1,0},{2,3},{3,2},{4,5},{5,4},{6,7},{7,6},{8,9},{9,8},{10,11... | collective-permute-start | bytes 1966088 | tf_op jit(solution)/shard_map/ppermute | solution.py:385
  30.5 22.3 %collective-permute-start.5 = (bf16[2,160,512]{2,1,0:T(8,128)(2,1)}, bf16[2,160,512]{2,1,0:T(8,128)(2,1)}, u32[]{:S(2)}, u32[]{:S(2)}) collective-permute-start(bf16[2,160,512]{2,1,0:T(8,128)(2,1)} %slice.38), channel_id=1, source_target_pairs={{0,24},{1,25},{2,26},{3,27},{4,28},{5,29},{6,30},{7,31},{8,0},{9,1... | collective-permute-start | bytes 983048 | tf_op jit(solution)/shard_map/ppermute | solution.py:439
  33.5 19.4 %collective-permute-start.6 = (bf16[2,160,512]{2,1,0:T(8,128)(2,1)S(1)}, bf16[2,160,512]{2,1,0:T(8,128)(2,1)}, u32[]{:S(2)}, u32[]{:S(2)}) collective-permute-start(bf16[2,160,512]{2,1,0:T(8,128)(2,1)S(1)} %slice.39), channel_id=1, source_target_pairs={{0,8},{1,9},{2,10},{3,11},{4,12},{5,13},{6,14},{7,15},{8,16},{9,17... | collective-permute-start | bytes 983048 | tf_op jit(solution)/shard_map/ppermute | solution.py:439
  35.2 18.2 %collective-permute-start.7 = (bf16[2,160,512]{2,1,0:T(8,128)(2,1)}, bf16[2,160,512]{2,1,0:T(8,128)(2,1)}, u32[]{:S(2)}, u32[]{:S(2)}) collective-permute-start(bf16[2,160,512]{2,1,0:T(8,128)(2,1)} %slice.40), channel_id=1, source_target_pairs={{0,6},{1,7},{2,0},{3,1},{4,2},{5,3},{6,4},{7,5},{8,14},{9,15},{10,... | collective-permute-start | bytes 983048 | tf_op jit(solution)/shard_map/ppermute | solution.py:439
  37.9 15.5 %collective-permute-start.8 = (bf16[2,160,512]{2,1,0:T(8,128)(2,1)}, bf16[2,160,512]{2,1,0:T(8,128)(2,1)}, u32[]{:S(2)}, u32[]{:S(2)}) collective-permute-start(bf16[2,160,512]{2,1,0:T(8,128)(2,1)} %slice.41), channel_id=1, source_target_pairs={{0,2},{1,3},{2,4},{3,5},{4,6},{5,7},{6,0},{7,1},{8,10},{9,11},{10,... | collective-permute-start | bytes 983048 | tf_op jit(solution)/shard_map/ppermute | solution.py:439
  52.9 20.7 %collective-permute-start.9 = (bf16[2,160,1024]{2,1,0:T(8,128)(2,1)}, bf16[2,160,1024]{2,1,0:T(8,128)(2,1)}, u32[]{:S(2)}, u32[]{:S(2)}) collective-permute-start(bf16[2,160,1024]{2,1,0:T(8,128)(2,1)} %collective-permute-done.refs_6_), channel_id=1, source_target_pairs={{0,1},{1,0},{2,3},{3,2},{4,5},{5,4},{6,7},{7,6},{8,9},{9,8},{10,11... | collective-permute-start | bytes 1966088 | tf_op jit(solution)/shard_map/ppermute | solution.py:385
  52.9 33.7 %collective-permute-start.13 = (bf16[2,160,1024]{2,1,0:T(8,128)(2,1)}, bf16[2,160,1024]{2,1,0:T(8,128)(2,1)}, u32[]{:S(2)}, u32[]{:S(2)}) collective-permute-start(bf16[2,160,1024]{2,1,0:T(8,128)(2,1)} %collective-permute-done.2.refs_6_), channel_id=1, source_target_pairs={{0,1},{1,0},{2,3},{3,2},{4,5},{5,4},{6,7},{7,6},{8,9},{9,8},{10,11... | collective-permute-start | bytes 1966088 | tf_op jit(solution)/shard_map/ppermute | solution.py:385
  53.4 36.0 %collective-permute-start.14 = (bf16[2,160,1024]{2,1,0:T(8,128)(2,1)}, bf16[2,160,1024]{2,1,0:T(8,128)(2,1)}, u32[]{:S(2)}, u32[]{:S(2)}) collective-permute-start(bf16[2,160,1024]{2,1,0:T(8,128)(2,1)} %collective-permute-done.3.refs_7_), channel_id=1, source_target_pairs={{0,1},{1,0},{2,3},{3,2},{4,5},{5,4},{6,7},{7,6},{8,9},{9,8},{10,11... | collective-permute-start | bytes 1966088 | tf_op jit(solution)/shard_map/ppermute | solution.py:385
  53.5 20.8 %collective-permute-start.11 = (bf16[2,160,512]{2,1,0:T(8,128)(2,1)}, bf16[2,160,512]{2,1,0:T(8,128)(2,1)S(1)}, u32[]{:S(2)}, u32[]{:S(2)}) collective-permute-start(bf16[2,160,512]{2,1,0:T(8,128)(2,1)} %collective-permute-done.5.refs_8_), channel_id=1, source_target_pairs={{0,1},{1,0},{2,3},{3,2},{4,5},{5,4},{6,7},{7,6},{8,9},{9,8},{10,11... | collective-permute-start | bytes 983048 | tf_op jit(solution)/shard_map/ppermute | solution.py:385
  73.5 16.6 %collective-permute-start.15 = (bf16[2,160,512]{2,1,0:T(8,128)(2,1)}, bf16[2,160,512]{2,1,0:T(8,128)(2,1)}, u32[]{:S(2)}, u32[]{:S(2)}) collective-permute-start(bf16[2,160,512]{2,1,0:T(8,128)(2,1)} %collective-permute-done.7.refs_8_), channel_id=1, source_target_pairs={{0,1},{1,0},{2,3},{3,2},{4,5},{5,4},{6,7},{7,6},{8,9},{9,8},{10,11... | collective-permute-start | bytes 983048 | tf_op jit(solution)/shard_map/ppermute | solution.py:385
  74.3 15.8 %collective-permute-start.16 = (bf16[2,160,512]{2,1,0:T(8,128)(2,1)}, bf16[2,160,512]{2,1,0:T(8,128)(2,1)}, u32[]{:S(2)}, u32[]{:S(2)}) collective-permute-start(bf16[2,160,512]{2,1,0:T(8,128)(2,1)} %collective-permute-done.8.refs_9_), channel_id=1, source_target_pairs={{0,1},{1,0},{2,3},{3,2},{4,5},{5,4},{6,7},{7,6},{8,9},{9,8},{10,11... | collective-permute-start | bytes 983048 | tf_op jit(solution)/shard_map/ppermute | solution.py:385
  85.0 16.0 %collective-permute-start.17 = (bf16[4,2,160,128]{3,2,1,0:T(8,128)(2,1)}, bf16[4,2,160,128]{3,2,1,0:T(8,128)(2,1)}, u32[]{:S(2)}, u32[]{:S(2)}) collective-permute-start(bf16[4,2,160,128]{3,2,1,0:T(8,128)(2,1)} %get-tuple-element.66), channel_id=1, source_target_pairs={{0,2},{1,3},{2,4},{3,5},{4,6},{5,7},{6,0},{7,1},{8,10},{9,11},{10,... | collective-permute-start | bytes 983048 | tf_op jit(solution)/shard_map/ppermute | solution.py:390
  86.6 18.2 %collective-permute-start.18 = (bf16[4,2,160,128]{3,2,1,0:T(8,128)(2,1)}, bf16[4,2,160,128]{3,2,1,0:T(8,128)(2,1)}, u32[]{:S(2)}, u32[]{:S(2)}) collective-permute-start(bf16[4,2,160,128]{3,2,1,0:T(8,128)(2,1)} %get-tuple-element.67), channel_id=1, source_target_pairs={{0,4},{1,5},{2,6},{3,7},{4,0},{5,1},{6,2},{7,3},{8,12},{9,13},{10,... | collective-permute-start | bytes 983048 | tf_op jit(solution)/shard_map/ppermute | solution.py:390
  89.4 15.4 %collective-permute-start.19 = (bf16[4,2,160,128]{3,2,1,0:T(8,128)(2,1)}, bf16[4,2,160,128]{3,2,1,0:T(8,128)(2,1)}, u32[]{:S(2)}, u32[]{:S(2)}) collective-permute-start(bf16[4,2,160,128]{3,2,1,0:T(8,128)(2,1)} %get-tuple-element.68), channel_id=1, source_target_pairs={{0,6},{1,7},{2,0},{3,1},{4,2},{5,3},{6,4},{7,5},{8,14},{9,15},{10,... | collective-permute-start | bytes 983048 | tf_op jit(solution)/shard_map/ppermute | solution.py:390
  104.8 18.3 %collective-permute-start.24 = (bf16[4,2,160,128]{3,2,1,0:T(8,128)(2,1)}, bf16[4,2,160,128]{3,2,1,0:T(8,128)(2,1)S(1)}, u32[]{:S(2)}, u32[]{:S(2)}) collective-permute-start(bf16[4,2,160,128]{3,2,1,0:T(8,128)(2,1)} %get-tuple-element.80), channel_id=1, source_target_pairs={{0,16},{1,17},{2,18},{3,19},{4,20},{5,21},{6,22},{7,23},{8,24},{9,... | collective-permute-start | bytes 983048 | tf_op jit(solution)/shard_map/ppermute | solution.py:390
  109.3 13.8 %collective-permute-start.25 = (bf16[4,2,160,128]{3,2,1,0:T(8,128)(2,1)}, bf16[4,2,160,128]{3,2,1,0:T(8,128)(2,1)S(1)}, u32[]{:S(2)}, u32[]{:S(2)}) collective-permute-start(bf16[4,2,160,128]{3,2,1,0:T(8,128)(2,1)} %get-tuple-element.81), channel_id=1, source_target_pairs={{0,24},{1,25},{2,26},{3,27},{4,28},{5,29},{6,30},{7,31},{8,0},{9,1... | collective-permute-start | bytes 983048 | tf_op jit(solution)/shard_map/ppermute | solution.py:390
  110.8 18.7 %collective-permute-start.20 = (bf16[2,160,128]{2,1,0:T(8,128)(2,1)S(1)}, bf16[2,160,128]{2,1,0:T(8,128)(2,1)S(1)}, u32[]{:S(2)}, u32[]{:S(2)}) collective-permute-start(bf16[2,160,128]{2,1,0:T(8,128)(2,1)S(1)} %get-tuple-element.94), channel_id=1, source_target_pairs={{0,32},{32,64},{64,96},{96,0},{1,33},{33,65},{65,97},{97,1},{2,34}... | collective-permute-start | bytes 245768 | tf_op jit(solution)/shard_map/ppermute | solution.py:397
  112.8 17.7 %collective-permute-start.21 = (bf16[2,160,128]{2,1,0:T(8,128)(2,1)S(1)}, bf16[2,160,128]{2,1,0:T(8,128)(2,1)S(1)}, u32[]{:S(2)}, u32[]{:S(2)}) collective-permute-start(bf16[2,160,128]{2,1,0:T(8,128)(2,1)S(1)} %get-tuple-element.93), channel_id=1, source_target_pairs={{0,64},{32,96},{64,0},{96,32},{1,65},{33,97},{65,1},{97,33},{2,66}... | collective-permute-start | bytes 245768 | tf_op jit(solution)/shard_map/ppermute | solution.py:397
  117.1 13.4 %collective-permute-start.22 = (bf16[2,160,128]{2,1,0:T(8,128)(2,1)S(1)}, bf16[2,160,128]{2,1,0:T(8,128)(2,1)S(1)}, u32[]{:S(2)}, u32[]{:S(2)}) collective-permute-start(bf16[2,160,128]{2,1,0:T(8,128)(2,1)S(1)} %get-tuple-element.92), channel_id=1, source_target_pairs={{0,96},{32,0},{64,32},{96,64},{1,97},{33,1},{65,33},{97,65},{2,98}... | collective-permute-start | bytes 245768 | tf_op jit(solution)/shard_map/ppermute | solution.py:397
  (12 other events, 116.0 us)

commit v6 on v5

--- a/solution.py
+++ b/solution.py
@@ -67,9 +67,10 @@
             keys_ref[0, blk, 3, rows, :] = n_last
             return mask | jnp.where(more, jnp.int32(1) << blk, 0)
 
-        mask_ref[0, rows, :] = lax.fori_loop(
-            0, BLOCKS, one_block, jnp.zeros((8, LANES), jnp.int32)
-        )
+        mask = lax.fori_loop(0, BLOCKS, one_block, jnp.zeros((8, LANES), jnp.int32))
+        for shift in (64, 32, 16, 8, 4, 2, 1):
+            mask = mask | pltpu.roll(mask, shift, 1)
+        mask_ref[0, rows, :] = mask
 
 
 def prep(pos, idx, lens):
@@ -92,7 +93,7 @@
             jax.ShapeDtypeStruct((tables, 8, BAG_BLOCKS, LANES), jnp.int32),
             jax.ShapeDtypeStruct((tables, BAG_BLOCKS, LANES), jnp.int32),
         ],
-        compiler_params=pltpu.CompilerParams(vmem_limit_bytes=60 << 20),
+        compiler_params=pltpu.CompilerParams(vmem_limit_bytes=24 << 20),
         cost_estimate=pl.CostEstimate(
             flops=40_000_000, bytes_accessed=9_000_000, transcendentals=0
         ),
@@ -154,7 +155,7 @@
     stage_bits = stage_bits - (1 << 32) if stage_bits >= 1 << 31 else stage_bits
     for part in range(2):
         bag = 4 * step + 2 * part
-        mask = mask_ref[table0 + table, bag] | mask_ref[table0 + table, bag + 1]
+        mask = mask_ref[table0 + table, bag, 0] | mask_ref[table0 + table, bag + 1, 0]
 
         @pl.when((mask & jnp.int32(stage_bits)) != 0)
         def _(part=part, bag=bag, mask=mask):
@@ -263,7 +264,7 @@
         out_specs=out_specs,
         out_shape=out_shape,
         scratch_shapes=scratch,
-        compiler_params=pltpu.CompilerParams(vmem_limit_bytes=60 << 20),
+        compiler_params=pltpu.CompilerParams(vmem_limit_bytes=24 << 20),
         cost_estimate=pl.CostEstimate(
             flops=2 * n_tables * rows * 2048 * 256,
             bytes_accessed=5_000_000,
@@ -313,16 +314,15 @@
     scale = 1.0 / jnp.sqrt(spread + 1e-05)
     normed = jnp.concatenate(
         [rows[f] * scale * fm_gain_ref[:, f : f + 1] for f in range(feats)], axis=0
+    )
+    hidden = jnp.maximum(
+        jnp.dot(normed.T.astype(jnp.bfloat16), up_ref[...], preferred_element_type=jnp.float32),
+        0.0,
     ).astype(jnp.bfloat16)
-    hidden = jnp.maximum(
-        jnp.dot(up_ref[...], normed, preferred_element_type=jnp.float32), 0.0
-    ).astype(jnp.bfloat16)
+    fm_block = jnp.dot(hidden, down_ref[...], preferred_element_type=jnp.float32).T
     half = feats // 2
     for m in range(half):
-        block = jnp.dot(
-            down_ref[m * width : (m + 1) * width, :], hidden, preferred_element_type=jnp.float32
-        )
-        summed[m] = block + emb[m]
+        summed[m] = fm_block[m * width : (m + 1) * width, :] + emb[m]
         acc = emb[half + m]
         for f in range(feats):
             acc = acc + compress_ref[m, f] * emb[f]
@@ -391,8 +391,11 @@
     ]
 
 
-def to_hosts(blocks):
-    total = sum(b.astype(jnp.float32) for b in blocks).astype(jnp.bfloat16)
+def add_up(blocks):
+    return sum(b.astype(jnp.float32) for b in blocks).astype(jnp.bfloat16)
+
+
+def to_hosts(total):
     return [total] + [
         lax.ppermute(total[d], "hst", [(h, (h + d) % 4) for h in range(4)]) for d in range(1, 4)
     ]
@@ -418,7 +421,6 @@
 
     flipped = jnp.swapaxes(tables, 1, 2)
     keys, lids, masks = prep(pos, jnp.transpose(indices, (1, 2, 0)), lengths.T)
-    masks = lax.reduce(masks, jnp.int32(0), lax.bitwise_or, (2,))
     small = (
         feature_order,
         proj_weight.astype(jnp.float32),
@@ -427,7 +429,7 @@
         out_gain.T,
     )
     masks, up, down, small = lax.optimization_barrier(
-        (masks, up_weight.T, down_weight.T, small)
+        (masks, up_weight, down_weight, small)
     )
     order, proj, compress, fm_gain, gain = small
 
@@ -438,27 +440,14 @@
     def move(x, axis, step):
         return lax.ppermute(x, "row", row_moves(axis, step))
 
-    sides = []
-    for p in range(2):
-        mine = flipped[2 * p : 2 * p + 2]
-        sides.append([move(mine, axes[p], 3), move(mine, axes[p], 1)])
+    mine = [flipped[2 * p : 2 * p + 2] for p in range(2)]
+    sides = [[move(mine[p], axes[p], 3), move(mine[p], axes[p], 1)] for p in range(2)]
     own_far = other_core(flipped)
-    sides, masks = lax.optimization_barrier((sides, masks))
-    half = ROWS_DEV // 2
-    beyond = [
-        [move(up1[:, :, :half], axis, 3), move(down1[:, :, half:], axis, 1)]
-        for (up1, down1), axis in zip(sides, axes)
-    ]
+    sides, mine, masks = lax.optimization_barrier((sides, mine, masks))
+    beyond = [move(mine[p], axes[p], 2) for p in range(2)]
 
     def stage(p, arrays, shard):
-        one, three, two_a, two_b = arrays
-        start = pairs[p][0]
-        return [
-            (one, start, shard, 0),
-            (three, start, shard + 1, 0),
-            (two_a, start, shard + 2, 0),
-            (two_b, start, shard + 2, half),
-        ]
+        return [(x, pairs[p][0], shard + k, 0) for k, x in enumerate(arrays)]
 
     sums = pool(
         (0, 1, 2, 3),
@@ -470,28 +459,38 @@
         False,
         "pool_own",
     )
-    sums, beyond, masks = lax.optimization_barrier((sums, beyond, masks))
-    near = [sides[p] + beyond[p] for p in range(2)]
-    far = [[other_core(x) for x in near[p]] for p in range(2)]
-    after = []
-    for p in range(2):
-        after.append(
-            pool(
-                pairs[p], masks, keys, lids, stage(p, near[p], 2), (sums, 0), False, "pool_near"
-            )
+    early = [other_core(x) for x in (sides[0][0], sides[0][1], sides[1][0])]
+    sums, sides, beyond, early, masks = lax.optimization_barrier(
+        (sums, sides, beyond, early, masks)
+    )
+    near = [sides[p] + [beyond[p]] for p in range(2)]
+    late = [other_core(x) for x in (beyond[0], sides[1][1], beyond[1])]
+
+    def pool_pair(p, base, masks):
+        near_sums = pool(
+            pairs[p], masks, keys, lids, stage(p, near[p], 2), base, False, "pool_near"
         )
-        masks, _ = lax.optimization_barrier((masks, after[p]))
+        masks, _ = lax.optimization_barrier((masks, near_sums))
+        return near_sums, masks
+
+    near_sums, masks = pool_pair(0, (sums, 0), masks)
+    late, masks = lax.optimization_barrier((late, masks))
+    far = [[early[0], early[1], late[0]], [early[2], late[1], late[2]]]
     blocks = pool(
-        pairs[0], masks, keys, lids, stage(0, far[0], 5), (after[0], 0), True, "pool_far"
+        pairs[0], masks, keys, lids, stage(0, far[0], 5), (near_sums, 0), True, "pool_far"
     )
     masks, _ = lax.optimization_barrier((masks, blocks))
     arrived = to_owners(blocks, axes[1])
+    near_sums, masks = pool_pair(1, (sums, 0), masks)
+    arrived, masks = lax.optimization_barrier((arrived, masks))
+    total = add_up(arrived)
+    total, masks = lax.optimization_barrier((total, masks))
+    parts = to_hosts(total)
     blocks = pool(
-        pairs[1], masks, keys, lids, stage(1, far[1], 5), (after[1], 2), True, "pool_far"
-    )
-    blocks, arrived = lax.optimization_barrier((blocks, arrived))
-    parts_b = to_hosts(to_owners(blocks, axes[0]))
-    parts = to_hosts(arrived) + parts_b
+        pairs[1], masks, keys, lids, stage(1, far[1], 5), (near_sums, 2), True, "pool_far"
+    )
+    blocks, parts = lax.optimization_barrier((blocks, parts))
+    parts += to_hosts(add_up(to_owners(blocks, axes[0])))
     result = tail(pos[:1], order, proj, compress, parts, fm_gain, up, down, gain)
     return jnp.transpose(result, (2, 0, 1))
 

time: 140 us -> 126 us (0.900)
  waiting for transfers between devices: 16.2 us -> 33.1 us
  Pallas kernels: 67.8 us -> 56.7 us
  local copies, waits for them, and re-layouts: 14 us -> 6 us
  starting transfers between devices: 36.1 us -> 28.1 us
  other arithmetic: 4.62 us -> 1.12 us
    pallas_call x5, Pallas kernels: 54.2 us -> 41.4 us  [pool(): pl.pallas_call(functools.partial(pool_kernel, tuple(layout), base is not...]
    ppermute x6, waiting for transfers between devices: 10.2 us -> 20.4 us  [to_owners(): lax.ppermute(blocks[d], 'row', row_moves(axis, d))]
    ppermute x8 -> x6, waiting for transfers between devices: 2.52 us -> 8.62 us  [move(): return lax.ppermute(x, 'row', row_moves(axis, step))]
    slice x5 -> x1, local copies, waits for them, and re-layouts: 8.6 us -> 2.57 us  [on_device(): mine = [flipped[2 * p:2 * p + 2] for p in range(2)]]
    ppermute x8 -> x6, starting transfers between devices: 12.1 us -> 8.73 us  [move(): return lax.ppermute(x, 'row', row_moves(axis, step))]
    unnamed x18 -> x14, local copies, waits for them, and re-layouts: 5.17 us -> 2.56 us
    ppermute x6, starting transfers between devices: 12 us -> 9.49 us  [to_hosts(): lax.ppermute(total[d], 'hst', [(h, (h + d) % 4) for h in range(4)])]
    convert_element_type x2, other arithmetic: 2.56 us -> 0.35 us  [add_up(): return sum((b.astype(jnp.float32) for b in blocks)).astype(jnp.bfloat16)]
  transfers between devices with their start and end apart: 29 -> 25, of which waited for: 8 -> 10; matrix products, arithmetic and copies ran while one was open for 13% -> 5% of each run, Pallas kernels for 45% -> 36%
where the time goes in v6:
time: 126 us; the launch traced here: 125 us
  Pallas kernels  56.7 us (45%)
  waiting for transfers between devices  33.1 us (26%)
  starting transfers between devices  28.1 us (22%)
  local copies, waits for them, and re-layouts  6 us (5%)
    pallas_call x5, Pallas kernels, pool(): pl.pallas_call(functools.partial(pool_kernel, tuple(layout), base is not...  41.4 us
    ppermute x6, waiting for transfers between devices, to_owners(): lax.ppermute(blocks[d], 'row', row_moves(axis, d))  20.4 us
    pallas_call x1, Pallas kernels, prep(): pl.pallas_call(prep_kernel, grid=(tables,), in_specs=[pl.BlockSpec(memory...  10.7 us
    ppermute x6, starting transfers between devices, to_hosts(): lax.ppermute(total[d], 'hst', [(h, (h + d) % 4) for h in range(4)])  9.49 us
    ppermute x6, starting transfers between devices, move(): return lax.ppermute(x, 'row', row_moves(axis, step))  8.73 us
    ppermute x6, starting transfers between devices, to_owners(): lax.ppermute(blocks[d], 'row', row_moves(axis, d))  8.66 us
    ppermute x6, waiting for transfers between devices, move(): return lax.ppermute(x, 'row', row_moves(axis, step))  8.62 us
    pallas_call x1, Pallas kernels, tail(): pl.pallas_call(tail_kernel, grid=(1,), in_specs=[smem] * 3 + ([mine] + [t...  4.58 us
  transfers between devices with their start and end apart: 25, of which 10 were waited for; matrix products, arithmetic and copies ran while one was open for 5% of the time, Pallas kernels for 36%

profile of v6, /device:TPU:0, one launch (start us, length us, event | category | flops | bytes accessed | tf_op | source)
XLA Modules:
  0.0 125.2 jit_solution(14318107160934441364)
XLA Ops:
  0.0 2.6 %fusion = (bf16[2,160,1024]{2,1,0:T(8,128)(2,1)}, bf16[2,160,1024]{2,1,0:T(8,128)(2,1)}) fusion(bf16[4,160,1024]{2,1,0:T(8,128)(2,1)} %bitcast.25), kind=kLoop, calls=%fused_computation.9 | loop fusion | bytes 2621440 | tf_op jit(solution)/shard_map/slice | solution.py:443
  2.6 4.1 %collective-permute-start = (bf16[2,160,1024]{2,1,0:T(8,128)(2,1)}, bf16[2,160,1024]{2,1,0:T(8,128)(2,1)}, u32[]{:S(2)}, u32[]{:S(2)}) collective-permute-start(bf16[2,160,1024]{2,1,0:T(8,128)(2,1)} %get-tuple-element.75), channel_id=1, source_target_pairs={{0,24},{1,25},{2,26},{3,27},{4,28},{5,29},{6,30},{7,31},{8,0},{9,1... | collective-permute-start | bytes 1966088 | tf_op jit(solution)/shard_map/ppermute | solution.py:441
  6.7 3.0 %collective-permute-start.2 = (bf16[2,160,1024]{2,1,0:T(8,128)(2,1)}, bf16[2,160,1024]{2,1,0:T(8,128)(2,1)}, u32[]{:S(2)}, u32[]{:S(2)}) collective-permute-start(bf16[2,160,1024]{2,1,0:T(8,128)(2,1)} %get-tuple-element.76), channel_id=1, source_target_pairs={{0,6},{1,7},{2,0},{3,1},{4,2},{5,3},{6,4},{7,5},{8,14},{9,15},{10,... | collective-permute-start | bytes 1966088 | tf_op jit(solution)/shard_map/ppermute | solution.py:441
  13.9 10.7 %prep.1 = (f32[4,32,4,16,128]{4,3,2,1,0:T(8,128)S(1)}, s32[4,8,16,128]{3,2,1,0:T(8,128)S(1)}, s32[4,16,128]{2,1,0:T(8,128)S(1)}) custom-call(s32[4]{0:T(128)S(1)} %pad_add_fusion.pos_ref, s32[4,8,16384]{2,1,0:T(8,128)S(1)} %bitcast.23, s32[4,16384]{1,0:T(4,128)S(1)} %bitcast.28), custom_call_target="tpu_custom_call" | custom-call | flops 40000000 | bytes 9000000 | tf_op jit(solution)/shard_map/prep/pallas_call | solution.py:78
  25.3 2.7 %collective-permute-done.3.refs_6_ = bf16[2,160,1024]{2,1,0:T(8,128)(2,1)} collective-permute-done((bf16[2,160,1024]{2,1,0:T(8,128)(2,1)}, bf16[2,160,1024]{2,1,0:T(8,128)(2,1)}, u32[]{:S(2)}, u32[]{:S(2)}) %collective-permute-start.3) | collective-permute-done | bytes 655392 | tf_op jit(solution)/shard_map/ppermute | solution.py:441
  28.0 1.6 %collective-permute-start.5 = (bf16[2,160,1024]{2,1,0:T(8,128)(2,1)}, bf16[2,160,1024]{2,1,0:T(8,128)(2,1)S(1)}, u32[]{:S(2)}, u32[]{:S(2)}) collective-permute-start(bf16[2,160,1024]{2,1,0:T(8,128)(2,1)} %get-tuple-element.75), channel_id=1, source_target_pairs={{0,16},{1,17},{2,18},{3,19},{4,20},{5,21},{6,22},{7,23},{8,24},{9,... | collective-permute-start | bytes 1966088 | tf_op jit(solution)/shard_map/ppermute | solution.py:441
  30.1 11.4 %pool_own.1.refs_8_ = f32[4,4,2,160,256]{4,3,2,1,0:T(8,128)S(1)} custom-call(s32[4,16,128]{2,1,0:T(8,128)S(1)} %get-tuple-element.101.refs_0_, s32[4,8,16,128]{3,2,1,0:T(8,128)S(1)} %get-tuple-element.69.refs_1_, f32[4,8,4,4,16,128]{5,4,3,2,1,0:T(8,128)S(1)} %bitcast.30, f32[4,8,4,4,16,128]{5,4,3,2,1,0:T(8,128)S(1)} %bitcast.31, ...), custom_call_target="tpu_custom_call" | custom-call | flops 8589934592 | bytes 5000000 | tf_op jit(solution)/shard_map/pool_own/pallas_call | solution.py:260
  41.5 4.2 %collective-permute-done.5.refs_7_ = bf16[2,160,1024]{2,1,0:T(8,128)(2,1)S(1)} collective-permute-done((bf16[2,160,1024]{2,1,0:T(8,128)(2,1)}, bf16[2,160,1024]{2,1,0:T(8,128)(2,1)S(1)}, u32[]{:S(2)}, u32[]{:S(2)}) %collective-permute-start.5) | collective-permute-done | bytes 655392 | tf_op jit(solution)/shard_map/ppermute | solution.py:441
  47.4 7.3 %pool_near.2.refs_8_ = f32[2,4,2,160,256]{4,3,2,1,0:T(8,128)S(1)} custom-call(s32[4,16,128]{2,1,0:T(8,128)S(1)} %get-tuple-element.101.refs_0_, s32[4,8,16,128]{3,2,1,0:T(8,128)S(1)} %get-tuple-element.69.refs_1_, f32[4,8,4,4,16,128]{5,4,3,2,1,0:T(8,128)S(1)} %bitcast.32, f32[4,8,4,4,16,128]{5,4,3,2,1,0:T(8,128)S(1)} %bitcast.33, ...), custom_call_target="tpu_custom_call" | custom-call | flops 6442450944 | bytes 5000000 | tf_op jit(solution)/shard_map/pool_near/pallas_call | solution.py:260
  54.8 7.4 %pool_far.2 = (bf16[4,2,160,128]{3,2,1,0:T(8,128)(2,1)S(1)}, bf16[4,2,160,128]{3,2,1,0:T(8,128)(2,1)S(1)}, bf16[4,2,160,128]{3,2,1,0:T(8,128)(2,1)S(1)}, bf16[4,2,160,128]{3,2,1,0:T(8,128)(2,1)S(1)}) custom-call(s32[4,16,128]{2,1,0:T(8,128)S(1)} %get-tuple-element.101.refs_0_, s32[4,8,16,128]{3,2,1,0:T(8,128)S(1)} %get-tuple-element.69.refs_1_, ...), custom_call_target="tpu_custom_call" | custom-call | flops 6442450944 | bytes 5000000 | tf_op jit(solution)/shard_map/pool_far/pallas_call | solution.py:260
  62.3 2.7 %collective-permute-start.14 = (bf16[4,2,160,128]{3,2,1,0:T(8,128)(2,1)S(1)}, bf16[4,2,160,128]{3,2,1,0:T(8,128)(2,1)S(1)}, u32[]{:S(2)}, u32[]{:S(2)}) collective-permute-start(bf16[4,2,160,128]{3,2,1,0:T(8,128)(2,1)S(1)} %get-tuple-element.91), channel_id=1, source_target_pairs={{0,4},{1,5},{2,6},{3,7},{4,0},{5,1},{6,2},{7,3},{8,12},{9,13},{10,... | collective-permute-start | bytes 983048 | tf_op jit(solution)/shard_map/ppermute | solution.py:390
  65.8 7.9 %pool_near.3.refs_8_ = f32[2,4,2,160,256]{4,3,2,1,0:T(8,128)S(1)} custom-call(s32[4,16,128]{2,1,0:T(8,128)S(1)} %get-tuple-element.101.refs_0_, s32[4,8,16,128]{3,2,1,0:T(8,128)S(1)} %get-tuple-element.69.refs_1_, f32[4,8,4,4,16,128]{5,4,3,2,1,0:T(8,128)S(1)} %bitcast.38, f32[4,8,4,4,16,128]{5,4,3,2,1,0:T(8,128)S(1)} %bitcast.39, ...), custom_call_target="tpu_custom_call" | custom-call | flops 6442450944 | bytes 5000000 | tf_op jit(solution)/shard_map/pool_near/pallas_call | solution.py:260
  73.7 7.3 %collective-permute-done.13 = bf16[4,2,160,128]{3,2,1,0:T(8,128)(2,1)S(1)} collective-permute-done((bf16[4,2,160,128]{3,2,1,0:T(8,128)(2,1)S(1)}, bf16[4,2,160,128]{3,2,1,0:T(8,128)(2,1)S(1)}, u32[]{:S(2)}, u32[]{:S(2)}) %collective-permute-start.13) | collective-permute-done | bytes 327712 | tf_op jit(solution)/shard_map/ppermute | solution.py:390
  81.8 1.1 collective-permute-start.16
  82.9 2.7 %collective-permute-start.17 = (bf16[2,160,128]{2,1,0:T(8,128)(2,1)S(1)}, bf16[2,160,128]{2,1,0:T(8,128)(2,1)S(1)}, u32[]{:S(2)}, u32[]{:S(2)}) collective-permute-start(bf16[2,160,128]{2,1,0:T(8,128)(2,1)S(1)} %get-tuple-element.129), channel_id=1, source_target_pairs={{0,64},{32,96},{64,0},{96,32},{1,65},{33,97},{65,1},{97,33},{2,66}... | collective-permute-start | bytes 245768 | tf_op jit(solution)/shard_map/ppermute | solution.py:400
  85.7 2.4 %collective-permute-start.18 = (bf16[2,160,128]{2,1,0:T(8,128)(2,1)S(1)}, bf16[2,160,128]{2,1,0:T(8,128)(2,1)S(1)}, u32[]{:S(2)}, u32[]{:S(2)}) collective-permute-start(bf16[2,160,128]{2,1,0:T(8,128)(2,1)S(1)} %get-tuple-element.128), channel_id=1, source_target_pairs={{0,96},{32,0},{64,32},{96,64},{1,97},{33,1},{65,33},{97,65},{2,98}... | collective-permute-start | bytes 245768 | tf_op jit(solution)/shard_map/ppermute | solution.py:400
  88.0 7.4 %pool_far.3 = (bf16[4,2,160,128]{3,2,1,0:T(8,128)(2,1)S(1)}, bf16[4,2,160,128]{3,2,1,0:T(8,128)(2,1)S(1)}, bf16[4,2,160,128]{3,2,1,0:T(8,128)(2,1)S(1)}, bf16[4,2,160,128]{3,2,1,0:T(8,128)(2,1)S(1)}) custom-call(s32[4,16,128]{2,1,0:T(8,128)S(1)} %get-tuple-element.101.refs_0_, s32[4,8,16,128]{3,2,1,0:T(8,128)S(1)} %get-tuple-element.69.refs_1_, ...), custom_call_target="tpu_custom_call" | custom-call | flops 6442450944 | bytes 5000000 | tf_op jit(solution)/shard_map/pool_far/pallas_call | solution.py:260
  95.5 2.3 %collective-permute-start.19 = (bf16[4,2,160,128]{3,2,1,0:T(8,128)(2,1)S(1)}, bf16[4,2,160,128]{3,2,1,0:T(8,128)(2,1)S(1)}, u32[]{:S(2)}, u32[]{:S(2)}) collective-permute-start(bf16[4,2,160,128]{3,2,1,0:T(8,128)(2,1)S(1)} %get-tuple-element.115), channel_id=1, source_target_pairs={{0,8},{1,9},{2,10},{3,11},{4,12},{5,13},{6,14},{7,15},{8,16},{9,17... | collective-permute-start | bytes 983048 | tf_op jit(solution)/shard_map/ppermute | solution.py:390
  97.8 2.8 %collective-permute-start.21 = (bf16[4,2,160,128]{3,2,1,0:T(8,128)(2,1)S(1)}, bf16[4,2,160,128]{3,2,1,0:T(8,128)(2,1)S(1)}, u32[]{:S(2)}, u32[]{:S(2)}) collective-permute-start(bf16[4,2,160,128]{3,2,1,0:T(8,128)(2,1)S(1)} %get-tuple-element.117), channel_id=1, source_target_pairs={{0,24},{1,25},{2,26},{3,27},{4,28},{5,29},{6,30},{7,31},{8,0},{9,1... | collective-permute-start | bytes 983048 | tf_op jit(solution)/shard_map/ppermute | solution.py:390
  100.6 11.8 %collective-permute-done.19 = bf16[4,2,160,128]{3,2,1,0:T(8,128)(2,1)S(1)} collective-permute-done((bf16[4,2,160,128]{3,2,1,0:T(8,128)(2,1)S(1)}, bf16[4,2,160,128]{3,2,1,0:T(8,128)(2,1)S(1)}, u32[]{:S(2)}, u32[]{:S(2)}) %collective-permute-start.19) | collective-permute-done | bytes 327712 | tf_op jit(solution)/shard_map/ppermute | solution.py:390
  113.3 2.2 %collective-permute-start.23 = (bf16[2,160,128]{2,1,0:T(8,128)(2,1)S(1)}, bf16[2,160,128]{2,1,0:T(8,128)(2,1)S(1)}, u32[]{:S(2)}, u32[]{:S(2)}) collective-permute-start(bf16[2,160,128]{2,1,0:T(8,128)(2,1)S(1)} %get-tuple-element.126), channel_id=1, source_target_pairs={{0,64},{32,96},{64,0},{96,32},{1,65},{33,97},{65,1},{97,33},{2,66}... | collective-permute-start | bytes 245768 | tf_op jit(solution)/shard_map/ppermute | solution.py:400
  115.5 1.0 collective-permute-start.24
  116.5 3.3 %collective-permute-done.22.rest_5_ = bf16[2,160,128]{2,1,0:T(8,128)(2,1)S(1)} collective-permute-done((bf16[2,160,128]{2,1,0:T(8,128)(2,1)S(1)}, bf16[2,160,128]{2,1,0:T(8,128)(2,1)S(1)}, u32[]{:S(2)}, u32[]{:S(2)}) %collective-permute-start.22) | collective-permute-done | bytes 81952 | tf_op jit(solution)/shard_map/ppermute | solution.py:400
  120.7 4.6 %tail.1 = bf16[16,160,128]{2,1,0:T(8,128)(2,1)} custom-call(s32[1]{0:T(128)} %bitcast.host_ref, s32[16]{0:T(128)S(1)} %copy-done.5, f32[8,16]{1,0:T(8,128)S(1)} %convert_element_type.37.compress_ref, bf16[4,2,160,128]{3,2,1,0:T(8,128)(2,1)S(1)} %add_convert_fusion.1.rest_0_, bf16[2,160,128]{2,1,0:T(8,128)(2,1)S(1)} %collective-permute-done.16.rest_1_, ...), custom_call_target="tpu_custom_call" | custom-call | flops 1000000000 | bytes 8000000 | tf_op jit(solution)/shard_map/tail/pallas_call | solution.py:351
  (57 shorter events, 10.6 us)
Async XLA Ops:
  0.0 30.1 %collective-permute-start.4 = (bf16[4,160,1024]{2,1,0:T(8,128)(2,1)}, bf16[4,160,1024]{2,1,0:T(8,128)(2,1)}, u32[]{:S(2)}, u32[]{:S(2)}) collective-permute-start(bf16[4,160,1024]{2,1,0:T(8,128)(2,1)} %bitcast.24), channel_id=1, source_target_pairs={{0,1},{1,0},{2,3},{3,2},{4,5},{5,4},{6,7},{7,6},{8,9},{9,8},{10,11... | collective-permute-start | bytes 3932168 | tf_op jit(solution)/shard_map/ppermute | solution.py:385
  2.6 22.0 %collective-permute-start = (bf16[2,160,1024]{2,1,0:T(8,128)(2,1)}, bf16[2,160,1024]{2,1,0:T(8,128)(2,1)}, u32[]{:S(2)}, u32[]{:S(2)}) collective-permute-start(bf16[2,160,1024]{2,1,0:T(8,128)(2,1)} %get-tuple-element.75), channel_id=1, source_target_pairs={{0,24},{1,25},{2,26},{3,27},{4,28},{5,29},{6,30},{7,31},{8,0},{9,1... | collective-permute-start | bytes 1966088 | tf_op jit(solution)/shard_map/ppermute | solution.py:441
  6.7 18.6 %collective-permute-start.1 = (bf16[2,160,1024]{2,1,0:T(8,128)(2,1)}, bf16[2,160,1024]{2,1,0:T(8,128)(2,1)}, u32[]{:S(2)}, u32[]{:S(2)}) collective-permute-start(bf16[2,160,1024]{2,1,0:T(8,128)(2,1)} %get-tuple-element.75), channel_id=1, source_target_pairs={{0,8},{1,9},{2,10},{3,11},{4,12},{5,13},{6,14},{7,15},{8,16},{9,17... | collective-permute-start | bytes 1966088 | tf_op jit(solution)/shard_map/ppermute | solution.py:441
  6.7 18.6 %collective-permute-start.2 = (bf16[2,160,1024]{2,1,0:T(8,128)(2,1)}, bf16[2,160,1024]{2,1,0:T(8,128)(2,1)}, u32[]{:S(2)}, u32[]{:S(2)}) collective-permute-start(bf16[2,160,1024]{2,1,0:T(8,128)(2,1)} %get-tuple-element.76), channel_id=1, source_target_pairs={{0,6},{1,7},{2,0},{3,1},{4,2},{5,3},{6,4},{7,5},{8,14},{9,15},{10,... | collective-permute-start | bytes 1966088 | tf_op jit(solution)/shard_map/ppermute | solution.py:441
  9.7 18.3 %collective-permute-start.3 = (bf16[2,160,1024]{2,1,0:T(8,128)(2,1)}, bf16[2,160,1024]{2,1,0:T(8,128)(2,1)}, u32[]{:S(2)}, u32[]{:S(2)}) collective-permute-start(bf16[2,160,1024]{2,1,0:T(8,128)(2,1)} %get-tuple-element.76), channel_id=1, source_target_pairs={{0,2},{1,3},{2,4},{3,5},{4,6},{5,7},{6,0},{7,1},{8,10},{9,11},{10,... | collective-permute-start | bytes 1966088 | tf_op jit(solution)/shard_map/ppermute | solution.py:441
  28.0 17.7 %collective-permute-start.5 = (bf16[2,160,1024]{2,1,0:T(8,128)(2,1)}, bf16[2,160,1024]{2,1,0:T(8,128)(2,1)S(1)}, u32[]{:S(2)}, u32[]{:S(2)}) collective-permute-start(bf16[2,160,1024]{2,1,0:T(8,128)(2,1)} %get-tuple-element.75), channel_id=1, source_target_pairs={{0,16},{1,17},{2,18},{3,19},{4,20},{5,21},{6,22},{7,23},{8,24},{9,... | collective-permute-start | bytes 1966088 | tf_op jit(solution)/shard_map/ppermute | solution.py:441
  29.6 17.1 %collective-permute-start.6 = (bf16[2,160,1024]{2,1,0:T(8,128)(2,1)}, bf16[2,160,1024]{2,1,0:T(8,128)(2,1)S(1)}, u32[]{:S(2)}, u32[]{:S(2)}) collective-permute-start(bf16[2,160,1024]{2,1,0:T(8,128)(2,1)} %get-tuple-element.76), channel_id=1, source_target_pairs={{0,4},{1,5},{2,6},{3,7},{4,0},{5,1},{6,2},{7,3},{8,12},{9,13},{10,... | collective-permute-start | bytes 1966088 | tf_op jit(solution)/shard_map/ppermute | solution.py:441
  29.6 17.1 %collective-permute-start.7 = (bf16[2,160,1024]{2,1,0:T(8,128)(2,1)}, bf16[2,160,1024]{2,1,0:T(8,128)(2,1)S(1)}, u32[]{:S(2)}, u32[]{:S(2)}) collective-permute-start(bf16[2,160,1024]{2,1,0:T(8,128)(2,1)} %collective-permute-done.refs_5_), channel_id=1, source_target_pairs={{0,1},{1,0},{2,3},{3,2},{4,5},{5,4},{6,7},{7,6},{8,9},{9,8},{10,11... | collective-permute-start | bytes 1966088 | tf_op jit(solution)/shard_map/ppermute | solution.py:385
  29.6 17.1 %collective-permute-start.8 = (bf16[2,160,1024]{2,1,0:T(8,128)(2,1)}, bf16[2,160,1024]{2,1,0:T(8,128)(2,1)S(1)}, u32[]{:S(2)}, u32[]{:S(2)}) collective-permute-start(bf16[2,160,1024]{2,1,0:T(8,128)(2,1)} %collective-permute-done.1.refs_6_), channel_id=1, source_target_pairs={{0,1},{1,0},{2,3},{3,2},{4,5},{5,4},{6,7},{7,6},{8,9},{9,8},{10,11... | collective-permute-start | bytes 1966088 | tf_op jit(solution)/shard_map/ppermute | solution.py:385
  30.1 16.6 %collective-permute-start.9 = (bf16[2,160,1024]{2,1,0:T(8,128)(2,1)}, bf16[2,160,1024]{2,1,0:T(8,128)(2,1)S(1)}, u32[]{:S(2)}, u32[]{:S(2)}) collective-permute-start(bf16[2,160,1024]{2,1,0:T(8,128)(2,1)} %collective-permute-done.2.refs_5_), channel_id=1, source_target_pairs={{0,1},{1,0},{2,3},{3,2},{4,5},{5,4},{6,7},{7,6},{8,9},{9,8},{10,11... | collective-permute-start | bytes 1966088 | tf_op jit(solution)/shard_map/ppermute | solution.py:385
  46.7 8.0 %collective-permute-start.10 = (bf16[2,160,1024]{2,1,0:T(8,128)(2,1)S(1)}, bf16[2,160,1024]{2,1,0:T(8,128)(2,1)S(1)}, u32[]{:S(2)}, u32[]{:S(2)}) collective-permute-start(bf16[2,160,1024]{2,1,0:T(8,128)(2,1)S(1)} %collective-permute-done.5.refs_7_), channel_id=1, source_target_pairs={{0,1},{1,0},{2,3},{3,2},{4,5},{5,4},{6,7},{7,6},{8,9},{9,8},{10,11... | collective-permute-start | bytes 1966088 | tf_op jit(solution)/shard_map/ppermute | solution.py:385
  46.8 8.0 %collective-permute-start.11 = (bf16[2,160,1024]{2,1,0:T(8,128)(2,1)}, bf16[2,160,1024]{2,1,0:T(8,128)(2,1)S(1)}, u32[]{:S(2)}, u32[]{:S(2)}) collective-permute-start(bf16[2,160,1024]{2,1,0:T(8,128)(2,1)} %collective-permute-done.3.refs_6_), channel_id=1, source_target_pairs={{0,1},{1,0},{2,3},{3,2},{4,5},{5,4},{6,7},{7,6},{8,9},{9,8},{10,11... | collective-permute-start | bytes 1966088 | tf_op jit(solution)/shard_map/ppermute | solution.py:385
  47.3 7.5 %collective-permute-start.12 = (bf16[2,160,1024]{2,1,0:T(8,128)(2,1)S(1)}, bf16[2,160,1024]{2,1,0:T(8,128)(2,1)S(1)}, u32[]{:S(2)}, u32[]{:S(2)}) collective-permute-start(bf16[2,160,1024]{2,1,0:T(8,128)(2,1)S(1)} %collective-permute-done.6.refs_7_), channel_id=1, source_target_pairs={{0,1},{1,0},{2,3},{3,2},{4,5},{5,4},{6,7},{7,6},{8,9},{9,8},{10,11... | collective-permute-start | bytes 1966088 | tf_op jit(solution)/shard_map/ppermute | solution.py:385
  62.2 18.8 %collective-permute-start.13 = (bf16[4,2,160,128]{3,2,1,0:T(8,128)(2,1)S(1)}, bf16[4,2,160,128]{3,2,1,0:T(8,128)(2,1)S(1)}, u32[]{:S(2)}, u32[]{:S(2)}) collective-permute-start(bf16[4,2,160,128]{3,2,1,0:T(8,128)(2,1)S(1)} %get-tuple-element.90), channel_id=1, source_target_pairs={{0,2},{1,3},{2,4},{3,5},{4,6},{5,7},{6,0},{7,1},{8,10},{9,11},{10,... | collective-permute-start | bytes 983048 | tf_op jit(solution)/shard_map/ppermute | solution.py:390
  62.3 18.7 %collective-permute-start.14 = (bf16[4,2,160,128]{3,2,1,0:T(8,128)(2,1)S(1)}, bf16[4,2,160,128]{3,2,1,0:T(8,128)(2,1)S(1)}, u32[]{:S(2)}, u32[]{:S(2)}) collective-permute-start(bf16[4,2,160,128]{3,2,1,0:T(8,128)(2,1)S(1)} %get-tuple-element.91), channel_id=1, source_target_pairs={{0,4},{1,5},{2,6},{3,7},{4,0},{5,1},{6,2},{7,3},{8,12},{9,13},{10,... | collective-permute-start | bytes 983048 | tf_op jit(solution)/shard_map/ppermute | solution.py:390
  65.0 16.7 %collective-permute-start.15 = (bf16[4,2,160,128]{3,2,1,0:T(8,128)(2,1)S(1)}, bf16[4,2,160,128]{3,2,1,0:T(8,128)(2,1)S(1)}, u32[]{:S(2)}, u32[]{:S(2)}) collective-permute-start(bf16[4,2,160,128]{3,2,1,0:T(8,128)(2,1)S(1)} %get-tuple-element.92), channel_id=1, source_target_pairs={{0,6},{1,7},{2,0},{3,1},{4,2},{5,3},{6,4},{7,5},{8,14},{9,15},{10,... | collective-permute-start | bytes 983048 | tf_op jit(solution)/shard_map/ppermute | solution.py:390
  81.8 13.6 %collective-permute-start.16 = (bf16[2,160,128]{2,1,0:T(8,128)(2,1)S(1)}, bf16[2,160,128]{2,1,0:T(8,128)(2,1)S(1)}, u32[]{:S(2)}, u32[]{:S(2)}) collective-permute-start(bf16[2,160,128]{2,1,0:T(8,128)(2,1)S(1)} %get-tuple-element.130), channel_id=1, source_target_pairs={{0,32},{32,64},{64,96},{96,0},{1,33},{33,65},{65,97},{97,1},{2,34}... | collective-permute-start | bytes 245768 | tf_op jit(solution)/shard_map/ppermute | solution.py:400
  82.9 12.6 %collective-permute-start.17 = (bf16[2,160,128]{2,1,0:T(8,128)(2,1)S(1)}, bf16[2,160,128]{2,1,0:T(8,128)(2,1)S(1)}, u32[]{:S(2)}, u32[]{:S(2)}) collective-permute-start(bf16[2,160,128]{2,1,0:T(8,128)(2,1)S(1)} %get-tuple-element.129), channel_id=1, source_target_pairs={{0,64},{32,96},{64,0},{96,32},{1,65},{33,97},{65,1},{97,33},{2,66}... | collective-permute-start | bytes 245768 | tf_op jit(solution)/shard_map/ppermute | solution.py:400
  85.7 9.8 %collective-permute-start.18 = (bf16[2,160,128]{2,1,0:T(8,128)(2,1)S(1)}, bf16[2,160,128]{2,1,0:T(8,128)(2,1)S(1)}, u32[]{:S(2)}, u32[]{:S(2)}) collective-permute-start(bf16[2,160,128]{2,1,0:T(8,128)(2,1)S(1)} %get-tuple-element.128), channel_id=1, source_target_pairs={{0,96},{32,0},{64,32},{96,64},{1,97},{33,1},{65,33},{97,65},{2,98}... | collective-permute-start | bytes 245768 | tf_op jit(solution)/shard_map/ppermute | solution.py:400
  95.5 16.9 %collective-permute-start.19 = (bf16[4,2,160,128]{3,2,1,0:T(8,128)(2,1)S(1)}, bf16[4,2,160,128]{3,2,1,0:T(8,128)(2,1)S(1)}, u32[]{:S(2)}, u32[]{:S(2)}) collective-permute-start(bf16[4,2,160,128]{3,2,1,0:T(8,128)(2,1)S(1)} %get-tuple-element.115), channel_id=1, source_target_pairs={{0,8},{1,9},{2,10},{3,11},{4,12},{5,13},{6,14},{7,15},{8,16},{9,17... | collective-permute-start | bytes 983048 | tf_op jit(solution)/shard_map/ppermute | solution.py:390
  97.8 14.6 %collective-permute-start.20 = (bf16[4,2,160,128]{3,2,1,0:T(8,128)(2,1)S(1)}, bf16[4,2,160,128]{3,2,1,0:T(8,128)(2,1)S(1)}, u32[]{:S(2)}, u32[]{:S(2)}) collective-permute-start(bf16[4,2,160,128]{3,2,1,0:T(8,128)(2,1)S(1)} %get-tuple-element.116), channel_id=1, source_target_pairs={{0,16},{1,17},{2,18},{3,19},{4,20},{5,21},{6,22},{7,23},{8,24},{9,... | collective-permute-start | bytes 983048 | tf_op jit(solution)/shard_map/ppermute | solution.py:390
  97.8 15.2 %collective-permute-start.21 = (bf16[4,2,160,128]{3,2,1,0:T(8,128)(2,1)S(1)}, bf16[4,2,160,128]{3,2,1,0:T(8,128)(2,1)S(1)}, u32[]{:S(2)}, u32[]{:S(2)}) collective-permute-start(bf16[4,2,160,128]{3,2,1,0:T(8,128)(2,1)S(1)} %get-tuple-element.117), channel_id=1, source_target_pairs={{0,24},{1,25},{2,26},{3,27},{4,28},{5,29},{6,30},{7,31},{8,0},{9,1... | collective-permute-start | bytes 983048 | tf_op jit(solution)/shard_map/ppermute | solution.py:390
  113.2 6.6 %collective-permute-start.22 = (bf16[2,160,128]{2,1,0:T(8,128)(2,1)S(1)}, bf16[2,160,128]{2,1,0:T(8,128)(2,1)S(1)}, u32[]{:S(2)}, u32[]{:S(2)}) collective-permute-start(bf16[2,160,128]{2,1,0:T(8,128)(2,1)S(1)} %get-tuple-element.127), channel_id=1, source_target_pairs={{0,32},{32,64},{64,96},{96,0},{1,33},{33,65},{65,97},{97,1},{2,34}... | collective-permute-start | bytes 245768 | tf_op jit(solution)/shard_map/ppermute | solution.py:400
  113.3 6.5 %collective-permute-start.23 = (bf16[2,160,128]{2,1,0:T(8,128)(2,1)S(1)}, bf16[2,160,128]{2,1,0:T(8,128)(2,1)S(1)}, u32[]{:S(2)}, u32[]{:S(2)}) collective-permute-start(bf16[2,160,128]{2,1,0:T(8,128)(2,1)S(1)} %get-tuple-element.126), channel_id=1, source_target_pairs={{0,64},{32,96},{64,0},{96,32},{1,65},{33,97},{65,1},{97,33},{2,66}... | collective-permute-start | bytes 245768 | tf_op jit(solution)/shard_map/ppermute | solution.py:400
  (7 other events, 142.0 us)

commit v7 on v6

--- a/solution.py
+++ b/solution.py
@@ -5,6 +5,7 @@
 from jax import lax
 from jax.experimental import pallas as pl
 from jax.experimental.pallas import tpu as pltpu
+from jax.sharding import Mesh
 from jax.sharding import PartitionSpec as P
 
 LANES = 128
@@ -23,12 +24,12 @@
     slot = lax.broadcasted_iota(jnp.int32, (8, LANES), 0)
     pick = lax.broadcasted_iota(jnp.int32, (len_ref.shape[0], LANES), 0)
     for n in range(BAG_BLOCKS):
-        dest, hrel = n // 4, n % 4
-        owner_host = (host + hrel) & 3
+        high_part, low_part = n // 4, n % 4
+        owner_host = jnp.where(over_z, (host + low_part) & 3, high_part)
         row_dev = jnp.where(
             over_z,
-            z * 8 + ((y + dest) & 3) * 2 + core,
-            ((z + dest) & 3) * 8 + y * 2 + core,
+            z * 8 + ((y + high_part) & 3) * 2 + core,
+            low_part * 8 + y * 2 + core,
         )
         start = pl.multiple_of((owner_host * 32 + row_dev) * LANES, LANES)
         v = idx_ref[0, :, pl.ds(start, LANES)]
@@ -68,9 +69,14 @@
             return mask | jnp.where(more, jnp.int32(1) << blk, 0)
 
         mask = lax.fori_loop(0, BLOCKS, one_block, jnp.zeros((8, LANES), jnp.int32))
+        mask_ref[table, rows, :] = mask
+
+    @pl.when(table == pl.num_programs(0) - 1)
+    def _():
+        masks = mask_ref[...]
         for shift in (64, 32, 16, 8, 4, 2, 1):
-            mask = mask | pltpu.roll(mask, shift, 1)
-        mask_ref[0, rows, :] = mask
+            masks = masks | pltpu.roll(masks, shift, 2)
+        mask_ref[...] = masks
 
 
 def prep(pos, idx, lens):
@@ -86,7 +92,7 @@
         out_specs=[
             pl.BlockSpec((1, BLOCKS, 4, BAG_BLOCKS, LANES), lambda j: (j, 0, 0, 0, 0)),
             pl.BlockSpec((1, 8, BAG_BLOCKS, LANES), lambda j: (j, 0, 0, 0)),
-            pl.BlockSpec((1, BAG_BLOCKS, LANES), lambda j: (j, 0, 0)),
+            pl.BlockSpec((tables, BAG_BLOCKS, LANES), lambda j: (0, 0, 0)),
         ],
         out_shape=[
             jax.ShapeDtypeStruct((tables, BLOCKS, 4, BAG_BLOCKS, LANES), jnp.float32),
@@ -101,7 +107,7 @@
     )(pos, idx, lens)
 
 
-def pool_kernel(layout, has_base, is_last, table0, *refs):
+def pool_kernel(layout, has_base, n_outs, table0, *refs):
     n_pieces = len(layout)
     mask_ref, lid_ref = refs[:2]
     keys = refs[2 : 2 + n_pieces]
@@ -109,8 +115,8 @@
     refs = refs[2 + 2 * n_pieces :]
     if has_base:
         base_ref, refs = refs[0], refs[1:]
-    if is_last:
-        outs, (sums, counts, extra) = refs[:4], refs[4:]
+    if n_outs:
+        outs, (sums, counts, extra) = refs[:n_outs], refs[n_outs:]
     else:
         sums, counts, extra = refs
     table, step = pl.program_id(0), pl.program_id(1)
@@ -200,18 +206,22 @@
 
             lax.fori_loop(0, n_blocks, fix, 0)
 
-    if is_last:
-        for d in range(4):
-
-            @pl.when(step == d)
-            def _(d=d):
-                for part in range(2):
-                    result = sums[0, 0, part].astype(jnp.bfloat16)
-                    outs[d][2 * part, 0] = result[:, :LANES]
-                    outs[d][2 * part + 1, 0] = result[:, LANES:]
-
-
-def pool(tables, masks, keys, lids, pieces, base, is_last, name):
+    def finish(out):
+        for part in range(2):
+            result = sums[0, 0, part].astype(jnp.bfloat16)
+            out[2 * part, 0] = result[:, :LANES]
+            out[2 * part + 1, 0] = result[:, LANES:]
+
+    if n_outs == 1:
+        finish(outs[0])
+    for d in range(n_outs if n_outs > 1 else 0):
+
+        @pl.when(step == d)
+        def _(d=d):
+            finish(outs[d])
+
+
+def pool(tables, masks, keys, lids, pieces, base, n_outs, name):
     n_tables = len(tables)
     table0 = tables[0]
     emb = pieces[0][0].shape[1]
@@ -250,15 +260,20 @@
         pltpu.VMEM((2, rows, PAIR), jnp.bfloat16),
         pltpu.VMEM((SUB, PAIR), jnp.bfloat16),
     ]
-    if is_last:
-        out_specs = [pl.BlockSpec((4, 1, emb, LANES), lambda j, i: (0, j, 0, 0))] * 4
-        out_shape = [jax.ShapeDtypeStruct((4, n_tables, emb, LANES), jnp.bfloat16)] * 4
+    if n_outs:
+        places = BAG_BLOCKS // n_outs
+        out_specs = [
+            pl.BlockSpec((4, 1, emb, LANES), lambda j, i: (i if n_outs == 1 else 0, j, 0, 0))
+        ] * n_outs
+        out_shape = [
+            jax.ShapeDtypeStruct((places, n_tables, emb, LANES), jnp.bfloat16)
+        ] * n_outs
         scratch = [pltpu.VMEM(sums_block, jnp.float32)] + scratch
     else:
         out_specs = sums_spec
         out_shape = jax.ShapeDtypeStruct((n_tables, 4, 2, emb, PAIR), jnp.float32)
     return pl.pallas_call(
-        functools.partial(pool_kernel, tuple(layout), base is not None, is_last, table0),
+        functools.partial(pool_kernel, tuple(layout), base is not None, n_outs, table0),
         grid=(n_tables, 4),
         in_specs=in_specs,
         out_specs=out_specs,
@@ -274,23 +289,25 @@
     )(*args)
 
 
-def tail_kernel(
-    host_ref,
-    order_ref,
-    compress_ref,
-    *rest,
-):
-    parts = rest[:8]
-    proj_ref, fm_gain_ref, up_ref, down_ref, gain_ref, out_ref, emb, gram, summed = rest[8:]
+def tail_kernel(host_ref, order_ref, *rest):
+    parts, summed_here = rest[:4], rest[4]
+    proj_ref, fm_gain_ref, up_ref, down_ref, compress_ref, gain_ref, out_ref = rest[5:12]
+    emb, gram, summed = rest[12:]
     host = host_ref[0]
     for d in range(4):
         source = (host - d) & 3
-        for j in range(4):
-            at = order_ref[source * 4 + j]
-            part = parts[(j // 2) * 4 + d]
-            emb[at] = part[j % 2].astype(jnp.float32)
+        for j in range(2):
+            emb[order_ref[source * 4 + j]] = parts[d][j].astype(jnp.float32)
+            total = summed_here[4 * d, j].astype(jnp.float32)
+            for k in range(1, 4):
+                total = total + summed_here[4 * d + k, j].astype(jnp.float32)
+            emb[order_ref[d * 4 + 2 + j]] = total.astype(jnp.bfloat16).astype(jnp.float32)
     feats, width, lanes = emb.shape
-    rank = proj_ref.shape[0]
+    rank = proj_ref.shape[1]
+    proj_weight = proj_ref[...].astype(jnp.float32).T
+    fm_gain = fm_gain_ref[...].T
+    compress = compress_ref[...].astype(jnp.float32)
+    gain = gain_ref[...].T
 
     for f in range(feats):
         x = emb[f]
@@ -299,7 +316,7 @@
             gram[f, g : g + 1, :] = dot
             if g != f:
                 gram[g, f : f + 1, :] = dot
-    proj = [jnp.broadcast_to(proj_ref[:, g : g + 1], (rank, lanes)) for g in range(feats)]
+    proj = [jnp.broadcast_to(proj_weight[:, g : g + 1], (rank, lanes)) for g in range(feats)]
     rows = []
     for f in range(feats):
         row = None
@@ -312,8 +329,13 @@
     rows = [r - mean for r in rows]
     spread = jnp.sum(sum(r * r for r in rows), axis=0, keepdims=True) * inv
     scale = 1.0 / jnp.sqrt(spread + 1e-05)
+    normed = jnp.concatenate([r * scale for r in rows], axis=0)
     normed = jnp.concatenate(
-        [rows[f] * scale * fm_gain_ref[:, f : f + 1] for f in range(feats)], axis=0
+        [
+            normed[c * lanes : (c + 1) * lanes] * fm_gain[:, c : c + 1]
+            for c in range(rank * feats // lanes)
+        ],
+        axis=0,
     )
     hidden = jnp.maximum(
         jnp.dot(normed.T.astype(jnp.bfloat16), up_ref[...], preferred_element_type=jnp.float32),
@@ -325,7 +347,7 @@
         summed[m] = fm_block[m * width : (m + 1) * width, :] + emb[m]
         acc = emb[half + m]
         for f in range(feats):
-            acc = acc + compress_ref[m, f] * emb[f]
+            acc = acc + compress[m : m + 1, f : f + 1] * emb[f]
         summed[half + m] = acc
     inv = 1.0 / (feats * width)
     total = summed[0]
@@ -339,10 +361,10 @@
     spread = jnp.sum(square, axis=0, keepdims=True) * inv
     scale = 1.0 / jnp.sqrt(spread + 1e-05)
     for f in range(feats):
-        out_ref[f] = ((summed[f] - mean) * scale * gain_ref[:, f : f + 1]).astype(jnp.bfloat16)
-
-
-def tail(host, order, proj, compress, parts, fm_gain, up, down, gain):
+        out_ref[f] = ((summed[f] - mean) * scale * gain[:, f : f + 1]).astype(jnp.bfloat16)
+
+
+def tail(host, order, parts, *weights):
     feats, width = order.shape[0], parts[0].shape[2]
     smem = pl.BlockSpec(memory_space=pltpu.SMEM)
     vmem = pl.BlockSpec(memory_space=pltpu.VMEM)
@@ -351,7 +373,7 @@
     return pl.pallas_call(
         tail_kernel,
         grid=(1,),
-        in_specs=[smem] * 3 + ([mine] + [there] * 3) * 2 + [vmem] * 5,
+        in_specs=[smem] * 2 + [mine] + [there] * 3 + [vmem] * 7,
         out_specs=vmem,
         out_shape=jax.ShapeDtypeStruct((feats, width, LANES), jnp.bfloat16),
         scratch_shapes=[
@@ -364,31 +386,20 @@
             flops=1_000_000_000, bytes_accessed=8_000_000, transcendentals=0
         ),
         name="tail",
-    )(host, order, compress, *parts, proj, fm_gain, up, down, gain)
-
-
-def row_moves(axis, step):
-    pairs = []
-    for z in range(4):
-        for y in range(4):
-            for core in range(2):
-                to = {
-                    "z": (((z + step) % 4) * 8 + y * 2 + core),
-                    "y": (z * 8 + ((y + step) % 4) * 2 + core),
-                    "core": (z * 8 + y * 2 + (core + step) % 2),
-                }[axis]
-                pairs.append((z * 8 + y * 2 + core, to))
-    return pairs
+    )(host, order, *parts, *weights)
+
+
+def move(x, axis, step):
+    size = 2 if axis == "core" else 4
+    return lax.ppermute(x, axis, [(i, (i + step) % size) for i in range(size)])
 
 
 def other_core(x):
-    return lax.ppermute(x, "row", row_moves("core", 1))
+    return move(x, "core", 1)
 
 
 def to_owners(blocks, axis):
-    return [blocks[0]] + [
-        lax.ppermute(blocks[d], "row", row_moves(axis, d)) for d in range(1, 4)
-    ]
+    return [blocks[0]] + [move(blocks[d], axis, d) for d in range(1, 4)]
 
 
 def add_up(blocks):
@@ -396,9 +407,7 @@
 
 
 def to_hosts(total):
-    return [total] + [
-        lax.ppermute(total[d], "hst", [(h, (h + d) % 4) for h in range(4)]) for d in range(1, 4)
-    ]
+    return [total] + [move(total[d], "hst", d) for d in range(1, 4)]
 
 
 def on_device(
@@ -413,32 +422,13 @@
     compress_weight,
     out_gain,
 ):
-    host = lax.axis_index("hst")
-    row = lax.axis_index("row")
-    pos = jnp.stack([host, row // 8, (row // 2) % 4, row % 2]).astype(jnp.int32)
-    feats = out_gain.shape[0]
-    rank = proj_weight.shape[0]
+    pos = jnp.stack([lax.axis_index(a) for a in ("hst", "z", "y", "core")]).astype(jnp.int32)
 
     flipped = jnp.swapaxes(tables, 1, 2)
     keys, lids, masks = prep(pos, jnp.transpose(indices, (1, 2, 0)), lengths.T)
-    small = (
-        feature_order,
-        proj_weight.astype(jnp.float32),
-        compress_weight.astype(jnp.float32),
-        fm_gain.reshape(feats, rank).T,
-        out_gain.T,
-    )
-    masks, up, down, small = lax.optimization_barrier(
-        (masks, up_weight, down_weight, small)
-    )
-    order, proj, compress, fm_gain, gain = small
-
     keys = keys.reshape((keys.shape[0], GATHER, ROWS_DEV // SUB) + keys.shape[2:])
     pairs = [(0, 1), (2, 3)]
     axes = ["z", "y"]
-
-    def move(x, axis, step):
-        return lax.ppermute(x, "row", row_moves(axis, step))
 
     mine = [flipped[2 * p : 2 * p + 2] for p in range(2)]
     sides = [[move(mine[p], axes[p], 3), move(mine[p], axes[p], 1)] for p in range(2)]
@@ -456,7 +446,7 @@
         lids,
         [(flipped, 0, 0, 0), (own_far, 0, 1, 0)],
         None,
-        False,
+        0,
         "pool_own",
     )
     early = [other_core(x) for x in (sides[0][0], sides[0][1], sides[1][0])]
@@ -468,7 +458,7 @@
 
     def pool_pair(p, base, masks):
         near_sums = pool(
-            pairs[p], masks, keys, lids, stage(p, near[p], 2), base, False, "pool_near"
+            pairs[p], masks, keys, lids, stage(p, near[p], 2), base, 0, "pool_near"
         )
         masks, _ = lax.optimization_barrier((masks, near_sums))
         return near_sums, masks
@@ -477,27 +467,37 @@
     late, masks = lax.optimization_barrier((late, masks))
     far = [[early[0], early[1], late[0]], [early[2], late[1], late[2]]]
     blocks = pool(
-        pairs[0], masks, keys, lids, stage(0, far[0], 5), (near_sums, 0), True, "pool_far"
+        pairs[0], masks, keys, lids, stage(0, far[0], 5), (near_sums, 0), 4, "pool_far"
     )
     masks, _ = lax.optimization_barrier((masks, blocks))
     arrived = to_owners(blocks, axes[1])
     near_sums, masks = pool_pair(1, (sums, 0), masks)
-    arrived, masks = lax.optimization_barrier((arrived, masks))
-    total = add_up(arrived)
-    total, masks = lax.optimization_barrier((total, masks))
+    (blocks,) = pool(
+        pairs[1], masks, keys, lids, stage(1, far[1], 5), (near_sums, 2), 1, "pool_far"
+    )
+    arrived, blocks = lax.optimization_barrier((arrived, blocks))
+    total, blocks = lax.optimization_barrier((add_up(arrived), blocks))
     parts = to_hosts(total)
-    blocks = pool(
-        pairs[1], masks, keys, lids, stage(1, far[1], 5), (near_sums, 2), True, "pool_far"
-    )
-    blocks, parts = lax.optimization_barrier((blocks, parts))
-    parts += to_hosts(add_up(to_owners(blocks, axes[0])))
-    result = tail(pos[:1], order, proj, compress, parts, fm_gain, up, down, gain)
+    parts.append(lax.all_to_all(blocks, ("hst", axes[0]), 0, 0, tiled=True))
+    result = tail(
+        pos[:1],
+        feature_order,
+        parts,
+        proj_weight.T,
+        fm_gain.reshape(-1, LANES),
+        up_weight,
+        down_weight,
+        compress_weight,
+        out_gain,
+    )
     return jnp.transpose(result, (2, 0, 1))
 
 
 def solution(mesh):
+    fine = Mesh(mesh.devices.reshape(4, 4, 4, 2), ("hst", "z", "y", "core"))
+    row = ("z", "y", "core")
     in_specs = (
-        P("hst", "row", None),
+        P("hst", row, None),
         P(None, "hst", None),
         P(None, "hst"),
         P(),
@@ -508,7 +508,7 @@
         P(),
         P(),
     )
-    out_specs = P(("hst", "row"), None, None)
+    out_specs = P(("hst",) + row, None, None)
     return jax.shard_map(
-        on_device, mesh=mesh, in_specs=in_specs, out_specs=out_specs, check_vma=False
-    )
+        on_device, mesh=fine, in_specs=in_specs, out_specs=out_specs, check_vma=False
+    )

time: 126 us -> 119 us (0.944)
  Pallas kernels: 56.7 us -> 54.2 us
  starting transfers between devices: 28.1 us -> 26.1 us
    ppermute x25 -> x19, starting transfers between devices: 28.1 us -> 19.2 us  [move(): return lax.ppermute(x, axis, [(i, (i + step) % size) for i in range(size)])]
    all_to_all x0 -> x1, starting transfers between devices: none -> 6.87 us  [on_device(): parts.append(lax.all_to_all(blocks, ('hst', axes[0]), 0, 0, tiled=True))]
    pallas_call x1, Pallas kernels: 10.7 us -> 7.41 us  [prep(): pl.pallas_call(prep_kernel, grid=(tables,), in_specs=[pl.BlockSpec(memory...]
    ppermute x25 -> x19, waiting for transfers between devices: 33.1 us -> 32.4 us  [move(): return lax.ppermute(x, axis, [(i, (i + step) % size) for i in range(size)])]
    unnamed x14 -> x20, local copies, waits for them, and re-layouts: 2.56 us -> 2.72 us
  transfers between devices with their start and end apart: 25 -> 20, of which waited for: 10 -> 7; matrix products, arithmetic and copies ran while one was open for 5% -> 2% of each run, Pallas kernels for 36% -> 35%
where the time goes in v7:
time: 119 us; the launch traced here: 118 us
  Pallas kernels  54.2 us (46%)
  waiting for transfers between devices  32.4 us (27%)
  starting transfers between devices  26.1 us (22%)
  local copies, waits for them, and re-layouts  5.32 us (4%)
    pallas_call x5, Pallas kernels, pool(): pl.pallas_call(functools.partial(pool_kernel, tuple(layout), base is not...  42.2 us
    ppermute x19, waiting for transfers between devices, move(): return lax.ppermute(x, axis, [(i, (i + step) % size) for i in range(size)])  32.4 us
    ppermute x19, starting transfers between devices, move(): return lax.ppermute(x, axis, [(i, (i + step) % size) for i in range(size)])  19.2 us
    pallas_call x1, Pallas kernels, prep(): pl.pallas_call(prep_kernel, grid=(tables,), in_specs=[pl.BlockSpec(memory...  7.41 us
    all_to_all x1, starting transfers between devices, on_device(): parts.append(lax.all_to_all(blocks, ('hst', axes[0]), 0, 0, tiled=True))  6.87 us
    pallas_call x1, Pallas kernels, tail(): pl.pallas_call(tail_kernel, grid=(1,), in_specs=[smem] * 2 + [mine] + [th...  4.54 us
    unnamed x20, local copies, waits for them, and re-layouts  2.72 us
    slice x1, local copies, waits for them, and re-layouts, on_device(): mine = [flipped[2 * p:2 * p + 2] for p in range(2)]  2.58 us
  transfers between devices with their start and end apart: 20, of which 7 were waited for; matrix products, arithmetic and copies ran while one was open for 2% of the time, Pallas kernels for 35%

profile of v7, /device:TPU:0, one launch (start us, length us, event | category | flops | bytes accessed | tf_op | source)
XLA Modules:
  0.0 118.5 jit_solution(12650643041912993054)
XLA Ops:
  0.0 2.6 %fusion = (bf16[2,160,1024]{2,1,0:T(8,128)(2,1)}, bf16[2,160,1024]{2,1,0:T(8,128)(2,1)}) fusion(bf16[4,160,1024]{2,1,0:T(8,128)(2,1)} %bitcast.19), kind=kLoop, calls=%fused_computation.5 | loop fusion | bytes 2621440 | tf_op jit(solution)/shard_map/slice | solution.py:433
  2.6 4.1 %collective-permute-start = (bf16[2,160,1024]{2,1,0:T(8,128)(2,1)}, bf16[2,160,1024]{2,1,0:T(8,128)(2,1)}, u32[]{:S(2)}, u32[]{:S(2)}) collective-permute-start(bf16[2,160,1024]{2,1,0:T(8,128)(2,1)} %get-tuple-element.52), channel_id=1, source_target_pairs={{0,24},{8,0},{16,8},{24,16},{1,25},{9,1},{17,9},{25,17},{2,26},{10... | collective-permute-start | bytes 1966088 | tf_op jit(solution)/shard_map/ppermute | solution.py:394
  6.7 3.0 %collective-permute-start.2 = (bf16[2,160,1024]{2,1,0:T(8,128)(2,1)}, bf16[2,160,1024]{2,1,0:T(8,128)(2,1)}, u32[]{:S(2)}, u32[]{:S(2)}) collective-permute-start(bf16[2,160,1024]{2,1,0:T(8,128)(2,1)} %get-tuple-element.53), channel_id=1, source_target_pairs={{0,6},{2,0},{4,2},{6,4},{1,7},{3,1},{5,3},{7,5},{8,14},{10,8},{12,... | collective-permute-start | bytes 1966088 | tf_op jit(solution)/shard_map/ppermute | solution.py:394
  10.8 7.4 %prep.1 = (f32[4,32,4,16,128]{4,3,2,1,0:T(8,128)S(1)}, s32[4,8,16,128]{3,2,1,0:T(8,128)S(1)}, s32[4,16,128]{2,1,0:T(8,128)S(1)}) custom-call(s32[4]{0:T(128)S(1)} %pad_add_fusion.pos_ref, s32[4,8,16384]{2,1,0:T(8,128)S(1)} %bitcast.17, s32[4,16384]{1,0:T(4,128)S(1)} %bitcast.21), custom_call_target="tpu_custom_call" | custom-call | flops 40000000 | bytes 9000000 | tf_op jit(solution)/shard_map/prep/pallas_call | solution.py:84
  18.2 3.7 %collective-permute-done.refs_5_ = bf16[2,160,1024]{2,1,0:T(8,128)(2,1)} collective-permute-done((bf16[2,160,1024]{2,1,0:T(8,128)(2,1)}, bf16[2,160,1024]{2,1,0:T(8,128)(2,1)}, u32[]{:S(2)}, u32[]{:S(2)}) %collective-permute-start) | collective-permute-done | bytes 655392 | tf_op jit(solution)/shard_map/ppermute | solution.py:394
  21.9 3.4 %collective-permute-done.1.refs_6_ = bf16[2,160,1024]{2,1,0:T(8,128)(2,1)} collective-permute-done((bf16[2,160,1024]{2,1,0:T(8,128)(2,1)}, bf16[2,160,1024]{2,1,0:T(8,128)(2,1)}, u32[]{:S(2)}, u32[]{:S(2)}) %collective-permute-start.1) | collective-permute-done | bytes 655392 | tf_op jit(solution)/shard_map/ppermute | solution.py:394
  25.3 2.7 %collective-permute-done.3.refs_6_ = bf16[2,160,1024]{2,1,0:T(8,128)(2,1)} collective-permute-done((bf16[2,160,1024]{2,1,0:T(8,128)(2,1)}, bf16[2,160,1024]{2,1,0:T(8,128)(2,1)}, u32[]{:S(2)}, u32[]{:S(2)}) %collective-permute-start.3) | collective-permute-done | bytes 655392 | tf_op jit(solution)/shard_map/ppermute | solution.py:394
  28.6 1.6 %collective-permute-start.5 = (bf16[2,160,1024]{2,1,0:T(8,128)(2,1)}, bf16[2,160,1024]{2,1,0:T(8,128)(2,1)S(1)}, u32[]{:S(2)}, u32[]{:S(2)}) collective-permute-start(bf16[2,160,1024]{2,1,0:T(8,128)(2,1)} %get-tuple-element.52), channel_id=1, source_target_pairs={{0,16},{8,24},{16,0},{24,8},{1,17},{9,25},{17,1},{25,9},{2,18},{10... | collective-permute-start | bytes 1966088 | tf_op jit(solution)/shard_map/ppermute | solution.py:394
  30.2 11.7 %pool_own.1.refs_8_ = f32[4,4,2,160,256]{4,3,2,1,0:T(8,128)S(1)} custom-call(s32[4,16,128]{2,1,0:T(8,128)S(1)} %get-tuple-element.72.refs_0_, s32[4,8,16,128]{3,2,1,0:T(8,128)S(1)} %get-tuple-element.46.refs_1_, f32[4,8,4,4,16,128]{5,4,3,2,1,0:T(8,128)S(1)} %bitcast.24, f32[4,8,4,4,16,128]{5,4,3,2,1,0:T(8,128)S(1)} %bitcast.25, ...), custom_call_target="tpu_custom_call" | custom-call | flops 8589934592 | bytes 5000000 | tf_op jit(solution)/shard_map/pool_own/pallas_call | solution.py:275
  41.9 5.5 %collective-permute-done.5.refs_7_ = bf16[2,160,1024]{2,1,0:T(8,128)(2,1)S(1)} collective-permute-done((bf16[2,160,1024]{2,1,0:T(8,128)(2,1)}, bf16[2,160,1024]{2,1,0:T(8,128)(2,1)S(1)}, u32[]{:S(2)}, u32[]{:S(2)}) %collective-permute-start.5) | collective-permute-done | bytes 655392 | tf_op jit(solution)/shard_map/ppermute | solution.py:394
  47.4 1.3 %collective-permute-done.6.refs_7_ = bf16[2,160,1024]{2,1,0:T(8,128)(2,1)S(1)} collective-permute-done((bf16[2,160,1024]{2,1,0:T(8,128)(2,1)}, bf16[2,160,1024]{2,1,0:T(8,128)(2,1)S(1)}, u32[]{:S(2)}, u32[]{:S(2)}) %collective-permute-start.6) | collective-permute-done | bytes 655392 | tf_op jit(solution)/shard_map/ppermute | solution.py:394
  49.2 7.3 %pool_near.2.refs_8_ = f32[2,4,2,160,256]{4,3,2,1,0:T(8,128)S(1)} custom-call(s32[4,16,128]{2,1,0:T(8,128)S(1)} %get-tuple-element.72.refs_0_, s32[4,8,16,128]{3,2,1,0:T(8,128)S(1)} %get-tuple-element.46.refs_1_, f32[4,8,4,4,16,128]{5,4,3,2,1,0:T(8,128)S(1)} %bitcast.26, f32[4,8,4,4,16,128]{5,4,3,2,1,0:T(8,128)S(1)} %bitcast.27, ...), custom_call_target="tpu_custom_call" | custom-call | flops 6442450944 | bytes 5000000 | tf_op jit(solution)/shard_map/pool_near/pallas_call | solution.py:275
  56.6 7.8 %pool_far.2 = (bf16[4,2,160,128]{3,2,1,0:T(8,128)(2,1)S(1)}, bf16[4,2,160,128]{3,2,1,0:T(8,128)(2,1)S(1)}, bf16[4,2,160,128]{3,2,1,0:T(8,128)(2,1)S(1)}, bf16[4,2,160,128]{3,2,1,0:T(8,128)(2,1)S(1)}) custom-call(s32[4,16,128]{2,1,0:T(8,128)S(1)} %get-tuple-element.72.refs_0_, s32[4,8,16,128]{3,2,1,0:T(8,128)S(1)} %get-tuple-element.46.refs_1_, ...), custom_call_target="tpu_custom_call" | custom-call | flops 6442450944 | bytes 5000000 | tf_op jit(solution)/shard_map/pool_far/pallas_call | solution.py:275
  65.8 2.0 %collective-permute-start.15 = (bf16[4,2,160,128]{3,2,1,0:T(8,128)(2,1)S(1)}, bf16[4,2,160,128]{3,2,1,0:T(8,128)(2,1)S(1)}, u32[]{:S(2)}, u32[]{:S(2)}) collective-permute-start(bf16[4,2,160,128]{3,2,1,0:T(8,128)(2,1)S(1)} %get-tuple-element.69), channel_id=1, source_target_pairs={{0,6},{2,0},{4,2},{6,4},{1,7},{3,1},{5,3},{7,5},{8,14},{10,8},{12,... | collective-permute-start | bytes 983048 | tf_op jit(solution)/shard_map/ppermute | solution.py:394
  67.8 7.4 %pool_near.3.refs_8_ = f32[2,4,2,160,256]{4,3,2,1,0:T(8,128)S(1)} custom-call(s32[4,16,128]{2,1,0:T(8,128)S(1)} %get-tuple-element.72.refs_0_, s32[4,8,16,128]{3,2,1,0:T(8,128)S(1)} %get-tuple-element.46.refs_1_, f32[4,8,4,4,16,128]{5,4,3,2,1,0:T(8,128)S(1)} %bitcast.32, f32[4,8,4,4,16,128]{5,4,3,2,1,0:T(8,128)S(1)} %bitcast.33, ...), custom_call_target="tpu_custom_call" | custom-call | flops 6442450944 | bytes 5000000 | tf_op jit(solution)/shard_map/pool_near/pallas_call | solution.py:275
  75.2 7.9 %pool_far.3 = bf16[16,2,160,128]{3,2,1,0:T(8,128)(2,1)} custom-call(s32[4,16,128]{2,1,0:T(8,128)S(1)} %get-tuple-element.72.refs_0_, s32[4,8,16,128]{3,2,1,0:T(8,128)S(1)} %get-tuple-element.46.refs_1_, f32[4,8,4,4,16,128]{5,4,3,2,1,0:T(8,128)S(1)} %bitcast.35, f32[4,8,4,4,16,128]{5,4,3,2,1,0:T(8,128)S(1)} %bitcast.36, ...), custom_call_target="tpu_custom_call" | custom-call | flops 6442450944 | bytes 5000000 | tf_op jit(solution)/shard_map/pool_far/pallas_call | solution.py:275
  83.4 6.9 %all-to-all-start = ((bf16[16,2,160,128]{3,2,1,0:T(8,128)(2,1)}), bf16[16,2,160,128]{3,2,1,0:T(8,128)(2,1)S(1)}, u32[]{:S(2)}, u32[]{:S(2)}) async-start(bf16[16,2,160,128]{3,2,1,0:T(8,128)(2,1)} %pool_far.3), calls=%async_computation | async-start | bytes 2621440 | tf_op jit(solution)/shard_map/all_to_all | solution.py:481
  90.3 2.0 %collective-permute-start.16 = (bf16[2,160,128]{2,1,0:T(8,128)(2,1)S(1)}, bf16[2,160,128]{2,1,0:T(8,128)(2,1)S(1)}, u32[]{:S(2)}, u32[]{:S(2)}) collective-permute-start(bf16[2,160,128]{2,1,0:T(8,128)(2,1)S(1)} %get-tuple-element.87), channel_id=1, source_target_pairs={{0,32},{32,64},{64,96},{96,0},{1,33},{33,65},{65,97},{97,1},{2,34}... | collective-permute-start | bytes 245768 | tf_op jit(solution)/shard_map/ppermute | solution.py:394
  92.3 2.7 %collective-permute-start.17 = (bf16[2,160,128]{2,1,0:T(8,128)(2,1)S(1)}, bf16[2,160,128]{2,1,0:T(8,128)(2,1)S(1)}, u32[]{:S(2)}, u32[]{:S(2)}) collective-permute-start(bf16[2,160,128]{2,1,0:T(8,128)(2,1)S(1)} %get-tuple-element.86), channel_id=1, source_target_pairs={{0,64},{32,96},{64,0},{96,32},{1,65},{33,97},{65,1},{97,33},{2,66}... | collective-permute-start | bytes 245768 | tf_op jit(solution)/shard_map/ppermute | solution.py:394
  94.9 1.5 %collective-permute-start.18 = (bf16[2,160,128]{2,1,0:T(8,128)(2,1)S(1)}, bf16[2,160,128]{2,1,0:T(8,128)(2,1)S(1)}, u32[]{:S(2)}, u32[]{:S(2)}) collective-permute-start(bf16[2,160,128]{2,1,0:T(8,128)(2,1)S(1)} %get-tuple-element.85), channel_id=1, source_target_pairs={{0,96},{32,0},{64,32},{96,64},{1,97},{33,1},{65,33},{97,65},{2,98}... | collective-permute-start | bytes 245768 | tf_op jit(solution)/shard_map/ppermute | solution.py:394
  96.4 14.1 %collective-permute-done.16.rest_1_ = bf16[2,160,128]{2,1,0:T(8,128)(2,1)S(1)} collective-permute-done((bf16[2,160,128]{2,1,0:T(8,128)(2,1)S(1)}, bf16[2,160,128]{2,1,0:T(8,128)(2,1)S(1)}, u32[]{:S(2)}, u32[]{:S(2)}) %collective-permute-start.16) | collective-permute-done | bytes 81952 | tf_op jit(solution)/shard_map/ppermute | solution.py:394
  110.5 1.6 %collective-permute-done.17.rest_2_ = bf16[2,160,128]{2,1,0:T(8,128)(2,1)S(1)} collective-permute-done((bf16[2,160,128]{2,1,0:T(8,128)(2,1)S(1)}, bf16[2,160,128]{2,1,0:T(8,128)(2,1)S(1)}, u32[]{:S(2)}, u32[]{:S(2)}) %collective-permute-start.17) | collective-permute-done | bytes 81952 | tf_op jit(solution)/shard_map/ppermute | solution.py:394
  112.2 1.7 %copy-done = bf16[1024,1280]{1,0:T(8,128)(2,1)S(1)} copy-done((bf16[1024,1280]{1,0:T(8,128)(2,1)S(1)}, bf16[1024,1280]{1,0:T(8,128)(2,1)}, u32[]{:S(2)}) %copy-start) | copy-done | bytes 2621464
  113.9 4.5 %tail.1 = bf16[16,160,128]{2,1,0:T(8,128)(2,1)} custom-call(s32[1]{0:T(128)} %bitcast.host_ref, s32[16]{0:T(128)S(1)} %copy-done.9, bf16[4,2,160,128]{3,2,1,0:T(8,128)(2,1)S(1)} %add_convert_fusion.rest_0_, bf16[2,160,128]{2,1,0:T(8,128)(2,1)S(1)} %collective-permute-done.16.rest_1_, bf16[2,160,128]{2,1,0:T(8,128)(2,1)S(1)} %collective-permute-done.17.rest_2_, ...), custom_call_target="tpu_custom_call" | custom-call | flops 1000000000 | bytes 8000000 | tf_op jit(solution)/shard_map/tail/pallas_call | solution.py:373
  (47 shorter events, 3.7 us)
Async XLA Ops:
  0.0 30.2 %copy-start.2 = (bf16[4,1024,160]{1,2,0:T(8,128)(2,1)S(1)}, bf16[4,1024,160]{1,2,0:T(8,128)(2,1)}, u32[]{:S(2)}) copy-start(bf16[4,1024,160]{1,2,0:T(8,128)(2,1)} %param.10) | copy-start | bytes 3932164
  0.0 30.1 %collective-permute-start.4 = (bf16[4,160,1024]{2,1,0:T(8,128)(2,1)}, bf16[4,160,1024]{2,1,0:T(8,128)(2,1)}, u32[]{:S(2)}, u32[]{:S(2)}) collective-permute-start(bf16[4,160,1024]{2,1,0:T(8,128)(2,1)} %bitcast.18), channel_id=1, source_target_pairs={{0,1},{1,0},{2,3},{3,2},{4,5},{5,4},{6,7},{7,6},{8,9},{9,8},{10,11... | collective-permute-start | bytes 3932168 | tf_op jit(solution)/shard_map/ppermute | solution.py:394
  2.6 19.3 %collective-permute-start = (bf16[2,160,1024]{2,1,0:T(8,128)(2,1)}, bf16[2,160,1024]{2,1,0:T(8,128)(2,1)}, u32[]{:S(2)}, u32[]{:S(2)}) collective-permute-start(bf16[2,160,1024]{2,1,0:T(8,128)(2,1)} %get-tuple-element.52), channel_id=1, source_target_pairs={{0,24},{8,0},{16,8},{24,16},{1,25},{9,1},{17,9},{25,17},{2,26},{10... | collective-permute-start | bytes 1966088 | tf_op jit(solution)/shard_map/ppermute | solution.py:394
  6.7 18.6 %collective-permute-start.1 = (bf16[2,160,1024]{2,1,0:T(8,128)(2,1)}, bf16[2,160,1024]{2,1,0:T(8,128)(2,1)}, u32[]{:S(2)}, u32[]{:S(2)}) collective-permute-start(bf16[2,160,1024]{2,1,0:T(8,128)(2,1)} %get-tuple-element.52), channel_id=1, source_target_pairs={{0,8},{8,16},{16,24},{24,0},{1,9},{9,17},{17,25},{25,1},{2,10},{10... | collective-permute-start | bytes 1966088 | tf_op jit(solution)/shard_map/ppermute | solution.py:394
  6.7 18.6 %collective-permute-start.2 = (bf16[2,160,1024]{2,1,0:T(8,128)(2,1)}, bf16[2,160,1024]{2,1,0:T(8,128)(2,1)}, u32[]{:S(2)}, u32[]{:S(2)}) collective-permute-start(bf16[2,160,1024]{2,1,0:T(8,128)(2,1)} %get-tuple-element.53), channel_id=1, source_target_pairs={{0,6},{2,0},{4,2},{6,4},{1,7},{3,1},{5,3},{7,5},{8,14},{10,8},{12,... | collective-permute-start | bytes 1966088 | tf_op jit(solution)/shard_map/ppermute | solution.py:394
  9.7 18.3 %collective-permute-start.3 = (bf16[2,160,1024]{2,1,0:T(8,128)(2,1)}, bf16[2,160,1024]{2,1,0:T(8,128)(2,1)}, u32[]{:S(2)}, u32[]{:S(2)}) collective-permute-start(bf16[2,160,1024]{2,1,0:T(8,128)(2,1)} %get-tuple-element.53), channel_id=1, source_target_pairs={{0,2},{2,4},{4,6},{6,0},{1,3},{3,5},{5,7},{7,1},{8,10},{10,12},{12... | collective-permute-start | bytes 1966088 | tf_op jit(solution)/shard_map/ppermute | solution.py:394
  28.0 13.8 %collective-permute-start.7 = (bf16[2,160,1024]{2,1,0:T(8,128)(2,1)}, bf16[2,160,1024]{2,1,0:T(8,128)(2,1)S(1)}, u32[]{:S(2)}, u32[]{:S(2)}) collective-permute-start(bf16[2,160,1024]{2,1,0:T(8,128)(2,1)} %collective-permute-done.refs_5_), channel_id=1, source_target_pairs={{0,1},{1,0},{2,3},{3,2},{4,5},{5,4},{6,7},{7,6},{8,9},{9,8},{10,11... | collective-permute-start | bytes 1966088 | tf_op jit(solution)/shard_map/ppermute | solution.py:394
  28.1 13.9 %collective-permute-start.8 = (bf16[2,160,1024]{2,1,0:T(8,128)(2,1)}, bf16[2,160,1024]{2,1,0:T(8,128)(2,1)S(1)}, u32[]{:S(2)}, u32[]{:S(2)}) collective-permute-start(bf16[2,160,1024]{2,1,0:T(8,128)(2,1)} %collective-permute-done.1.refs_6_), channel_id=1, source_target_pairs={{0,1},{1,0},{2,3},{3,2},{4,5},{5,4},{6,7},{7,6},{8,9},{9,8},{10,11... | collective-permute-start | bytes 1966088 | tf_op jit(solution)/shard_map/ppermute | solution.py:394
  28.6 13.4 %collective-permute-start.9 = (bf16[2,160,1024]{2,1,0:T(8,128)(2,1)}, bf16[2,160,1024]{2,1,0:T(8,128)(2,1)S(1)}, u32[]{:S(2)}, u32[]{:S(2)}) collective-permute-start(bf16[2,160,1024]{2,1,0:T(8,128)(2,1)} %collective-permute-done.2.refs_5_), channel_id=1, source_target_pairs={{0,1},{1,0},{2,3},{3,2},{4,5},{5,4},{6,7},{7,6},{8,9},{9,8},{10,11... | collective-permute-start | bytes 1966088 | tf_op jit(solution)/shard_map/ppermute | solution.py:394
  28.6 18.9 %collective-permute-start.5 = (bf16[2,160,1024]{2,1,0:T(8,128)(2,1)}, bf16[2,160,1024]{2,1,0:T(8,128)(2,1)S(1)}, u32[]{:S(2)}, u32[]{:S(2)}) collective-permute-start(bf16[2,160,1024]{2,1,0:T(8,128)(2,1)} %get-tuple-element.52), channel_id=1, source_target_pairs={{0,16},{8,24},{16,0},{24,8},{1,17},{9,25},{17,1},{25,9},{2,18},{10... | collective-permute-start | bytes 1966088 | tf_op jit(solution)/shard_map/ppermute | solution.py:394
  30.1 18.6 %collective-permute-start.6 = (bf16[2,160,1024]{2,1,0:T(8,128)(2,1)}, bf16[2,160,1024]{2,1,0:T(8,128)(2,1)S(1)}, u32[]{:S(2)}, u32[]{:S(2)}) collective-permute-start(bf16[2,160,1024]{2,1,0:T(8,128)(2,1)} %get-tuple-element.53), channel_id=1, source_target_pairs={{0,4},{2,6},{4,0},{6,2},{1,5},{3,7},{5,1},{7,3},{8,12},{10,14},{12... | collective-permute-start | bytes 1966088 | tf_op jit(solution)/shard_map/ppermute | solution.py:394
  48.7 7.9 %collective-permute-start.10 = (bf16[2,160,1024]{2,1,0:T(8,128)(2,1)S(1)}, bf16[2,160,1024]{2,1,0:T(8,128)(2,1)S(1)}, u32[]{:S(2)}, u32[]{:S(2)}) collective-permute-start(bf16[2,160,1024]{2,1,0:T(8,128)(2,1)S(1)} %collective-permute-done.5.refs_7_), channel_id=1, source_target_pairs={{0,1},{1,0},{2,3},{3,2},{4,5},{5,4},{6,7},{7,6},{8,9},{9,8},{10,11... | collective-permute-start | bytes 1966088 | tf_op jit(solution)/shard_map/ppermute | solution.py:394
  48.7 7.9 %collective-permute-start.11 = (bf16[2,160,1024]{2,1,0:T(8,128)(2,1)}, bf16[2,160,1024]{2,1,0:T(8,128)(2,1)S(1)}, u32[]{:S(2)}, u32[]{:S(2)}) collective-permute-start(bf16[2,160,1024]{2,1,0:T(8,128)(2,1)} %collective-permute-done.3.refs_6_), channel_id=1, source_target_pairs={{0,1},{1,0},{2,3},{3,2},{4,5},{5,4},{6,7},{7,6},{8,9},{9,8},{10,11... | collective-permute-start | bytes 1966088 | tf_op jit(solution)/shard_map/ppermute | solution.py:394
  49.2 7.4 %collective-permute-start.12 = (bf16[2,160,1024]{2,1,0:T(8,128)(2,1)S(1)}, bf16[2,160,1024]{2,1,0:T(8,128)(2,1)S(1)}, u32[]{:S(2)}, u32[]{:S(2)}) collective-permute-start(bf16[2,160,1024]{2,1,0:T(8,128)(2,1)S(1)} %collective-permute-done.6.refs_7_), channel_id=1, source_target_pairs={{0,1},{1,0},{2,3},{3,2},{4,5},{5,4},{6,7},{7,6},{8,9},{9,8},{10,11... | collective-permute-start | bytes 1966088 | tf_op jit(solution)/shard_map/ppermute | solution.py:394
  64.5 18.7 %collective-permute-start.13 = (bf16[4,2,160,128]{3,2,1,0:T(8,128)(2,1)S(1)}, bf16[4,2,160,128]{3,2,1,0:T(8,128)(2,1)S(1)}, u32[]{:S(2)}, u32[]{:S(2)}) collective-permute-start(bf16[4,2,160,128]{3,2,1,0:T(8,128)(2,1)S(1)} %get-tuple-element.67), channel_id=1, source_target_pairs={{0,2},{2,4},{4,6},{6,0},{1,3},{3,5},{5,7},{7,1},{8,10},{10,12},{12... | collective-permute-start | bytes 983048 | tf_op jit(solution)/shard_map/ppermute | solution.py:394
  64.6 18.6 %collective-permute-start.14 = (bf16[4,2,160,128]{3,2,1,0:T(8,128)(2,1)S(1)}, bf16[4,2,160,128]{3,2,1,0:T(8,128)(2,1)S(1)}, u32[]{:S(2)}, u32[]{:S(2)}) collective-permute-start(bf16[4,2,160,128]{3,2,1,0:T(8,128)(2,1)S(1)} %get-tuple-element.68), channel_id=1, source_target_pairs={{0,4},{2,6},{4,0},{6,2},{1,5},{3,7},{5,1},{7,3},{8,12},{10,14},{12... | collective-permute-start | bytes 983048 | tf_op jit(solution)/shard_map/ppermute | solution.py:394
  65.8 17.4 %collective-permute-start.15 = (bf16[4,2,160,128]{3,2,1,0:T(8,128)(2,1)S(1)}, bf16[4,2,160,128]{3,2,1,0:T(8,128)(2,1)S(1)}, u32[]{:S(2)}, u32[]{:S(2)}) collective-permute-start(bf16[4,2,160,128]{3,2,1,0:T(8,128)(2,1)S(1)} %get-tuple-element.69), channel_id=1, source_target_pairs={{0,6},{2,0},{4,2},{6,4},{1,7},{3,1},{5,3},{7,5},{8,14},{10,8},{12,... | collective-permute-start | bytes 983048 | tf_op jit(solution)/shard_map/ppermute | solution.py:394
  83.1 29.0 %copy-start.7 = (f32[384]{0:T(512)S(1)}, f32[384]{0:T(512)}, u32[]{:S(2)}) copy-start(f32[384]{0:T(512)} %param.15) | copy-start | bytes 4612
  83.1 29.0 %copy-start.8 = (bf16[8,16]{1,0:T(8,128)(2,1)S(1)}, bf16[8,16]{1,0:T(8,128)(2,1)}, u32[]{:S(2)}) copy-start(bf16[8,16]{1,0:T(8,128)(2,1)} %rest_9_.1) | copy-start | bytes 772
  83.2 29.0 %copy-start.9 = (s32[16]{0:T(128)S(1)}, s32[16]{0:T(128)}, u32[]{:S(2)}) copy-start(s32[16]{0:T(128)} %order_ref.1) | copy-start | bytes 196
  83.4 28.8 %all-to-all-start = ((bf16[16,2,160,128]{3,2,1,0:T(8,128)(2,1)}), bf16[16,2,160,128]{3,2,1,0:T(8,128)(2,1)S(1)}, u32[]{:S(2)}, u32[]{:S(2)}) async-start(bf16[16,2,160,128]{3,2,1,0:T(8,128)(2,1)} %pool_far.3), calls=%async_computation | async-start | bytes 2621440 | tf_op jit(solution)/shard_map/all_to_all | solution.py:481
  90.3 20.3 %collective-permute-start.16 = (bf16[2,160,128]{2,1,0:T(8,128)(2,1)S(1)}, bf16[2,160,128]{2,1,0:T(8,128)(2,1)S(1)}, u32[]{:S(2)}, u32[]{:S(2)}) collective-permute-start(bf16[2,160,128]{2,1,0:T(8,128)(2,1)S(1)} %get-tuple-element.87), channel_id=1, source_target_pairs={{0,32},{32,64},{64,96},{96,0},{1,33},{33,65},{65,97},{97,1},{2,34}... | collective-permute-start | bytes 245768 | tf_op jit(solution)/shard_map/ppermute | solution.py:394
  92.3 19.9 %collective-permute-start.17 = (bf16[2,160,128]{2,1,0:T(8,128)(2,1)S(1)}, bf16[2,160,128]{2,1,0:T(8,128)(2,1)S(1)}, u32[]{:S(2)}, u32[]{:S(2)}) collective-permute-start(bf16[2,160,128]{2,1,0:T(8,128)(2,1)S(1)} %get-tuple-element.86), channel_id=1, source_target_pairs={{0,64},{32,96},{64,0},{96,32},{1,65},{33,97},{65,1},{97,33},{2,66}... | collective-permute-start | bytes 245768 | tf_op jit(solution)/shard_map/ppermute | solution.py:394
  94.9 17.2 %collective-permute-start.18 = (bf16[2,160,128]{2,1,0:T(8,128)(2,1)S(1)}, bf16[2,160,128]{2,1,0:T(8,128)(2,1)S(1)}, u32[]{:S(2)}, u32[]{:S(2)}) collective-permute-start(bf16[2,160,128]{2,1,0:T(8,128)(2,1)S(1)} %get-tuple-element.85), channel_id=1, source_target_pairs={{0,96},{32,0},{64,32},{96,64},{1,97},{33,1},{65,33},{97,65},{2,98}... | collective-permute-start | bytes 245768 | tf_op jit(solution)/shard_map/ppermute | solution.py:394
  (6 other events, 99.6 us)

commit v8 on v7

--- a/solution.py
+++ b/solution.py
@@ -39,9 +39,9 @@
         at_z, at_y, at_core = v >> 13, (v >> 11) & 3, (v >> 10) & 1
         here = jnp.where(over_z, at_y - y, at_z - z) == 0
         away = jnp.where(over_z, at_z - z, at_y - y) & 3
-        shard = jnp.where(away == 2, 4, 2 + (away >> 1))
         other = at_core ^ core
-        shard = jnp.where(away == 0, other, shard + 3 * other)
+        shard = jnp.where(away == 2, 6 + other, 2 + (away >> 1) + 2 * other)
+        shard = jnp.where(away == 0, other, shard)
         local = shard * ROWS_DEV + (v & (ROWS_DEV - 1))
         local = jnp.where(here & (slot < used), local, -1)
         for s in range(8):
@@ -433,51 +433,37 @@
     mine = [flipped[2 * p : 2 * p + 2] for p in range(2)]
     sides = [[move(mine[p], axes[p], 3), move(mine[p], axes[p], 1)] for p in range(2)]
     own_far = other_core(flipped)
-    sides, mine, masks = lax.optimization_barrier((sides, mine, masks))
+
+    def stage(tables, arrays, shard, base, n_outs, name):
+        pieces = [(x, 0 if x.shape[0] == 4 else tables[0]) for x in arrays]
+        pieces = [(x, start, shard + k, 0) for k, (x, start) in enumerate(pieces)]
+        return pool(tables, masks, keys, lids, pieces, base, n_outs, name)
+
+    sums = stage((0, 1, 2, 3), [flipped], 0, None, 0, "pool_own")
+    sums, sides, mine, masks = lax.optimization_barrier((sums, sides, mine, masks))
     beyond = [move(mine[p], axes[p], 2) for p in range(2)]
-
-    def stage(p, arrays, shard):
-        return [(x, pairs[p][0], shard + k, 0) for k, x in enumerate(arrays)]
-
-    sums = pool(
-        (0, 1, 2, 3),
-        masks,
-        keys,
-        lids,
-        [(flipped, 0, 0, 0), (own_far, 0, 1, 0)],
-        None,
-        0,
-        "pool_own",
-    )
     early = [other_core(x) for x in (sides[0][0], sides[0][1], sides[1][0])]
-    sums, sides, beyond, early, masks = lax.optimization_barrier(
-        (sums, sides, beyond, early, masks)
-    )
-    near = [sides[p] + [beyond[p]] for p in range(2)]
+    middle = []
+    for p in range(2):
+        middle.append(stage(pairs[p], [own_far] + sides[p], 1, (sums, 0), 0, "pool_sides"))
+        masks, _ = lax.optimization_barrier((masks, middle[p]))
+    sides, beyond, early, masks = lax.optimization_barrier((sides, beyond, early, masks))
     late = [other_core(x) for x in (beyond[0], sides[1][1], beyond[1])]
-
-    def pool_pair(p, base, masks):
-        near_sums = pool(
-            pairs[p], masks, keys, lids, stage(p, near[p], 2), base, 0, "pool_near"
-        )
-        masks, _ = lax.optimization_barrier((masks, near_sums))
-        return near_sums, masks
-
-    near_sums, masks = pool_pair(0, (sums, 0), masks)
-    late, masks = lax.optimization_barrier((late, masks))
-    far = [[early[0], early[1], late[0]], [early[2], late[1], late[2]]]
-    blocks = pool(
-        pairs[0], masks, keys, lids, stage(0, far[0], 5), (near_sums, 0), 4, "pool_far"
-    )
+    first = stage(pairs[0], early[:2], 4, (middle[0], 0), 0, "pool_other")
+    masks, _ = lax.optimization_barrier((masks, first))
+    blocks = stage(pairs[0], [beyond[0], late[0]], 6, (first, 0), 4, "pool_beyond")
     masks, _ = lax.optimization_barrier((masks, blocks))
     arrived = to_owners(blocks, axes[1])
-    near_sums, masks = pool_pair(1, (sums, 0), masks)
-    (blocks,) = pool(
-        pairs[1], masks, keys, lids, stage(1, far[1], 5), (near_sums, 2), 1, "pool_far"
+    (blocks,) = stage(
+        pairs[1],
+        [early[2], late[1], beyond[1], late[2]],
+        4,
+        (middle[1], 2),
+        1,
+        "pool_rest",
     )
     arrived, blocks = lax.optimization_barrier((arrived, blocks))
-    total, blocks = lax.optimization_barrier((add_up(arrived), blocks))
-    parts = to_hosts(total)
+    parts = to_hosts(add_up(arrived))
     parts.append(lax.all_to_all(blocks, ("hst", axes[0]), 0, 0, tiled=True))
     result = tail(
         pos[:1],

time: 119 us -> 114 us (0.958)
  waiting for transfers between devices: 32.4 us -> 25.3 us
  Pallas kernels: 54.2 us -> 56.2 us
    ppermute x19, waiting for transfers between devices: 32.4 us -> 25.3 us  [move(): return lax.ppermute(x, axis, [(i, (i + step) % size) for i in range(size)])]
    pallas_call x5 -> x6, Pallas kernels: 42.2 us -> 44.3 us  [pool(): pl.pallas_call(functools.partial(pool_kernel, tuple(layout), base is not...]
  transfers between devices with their start and end apart: 20 -> 20, of which waited for: 7 -> 7; matrix products, arithmetic and copies ran while one was open for 2% -> 3% of each run, Pallas kernels for 35% -> 45%
where the time goes in v8:
time: 114 us
  Pallas kernels  56.2 us (49%)
  starting transfers between devices  25.4 us (22%)
  waiting for transfers between devices  25.3 us (22%)
  local copies, waits for them, and re-layouts  5.32 us (5%)
  other arithmetic  1.22 us (1%)
    pallas_call x6, Pallas kernels, pool(): pl.pallas_call(functools.partial(pool_kernel, tuple(layout), base is not...  44.3 us
    ppermute x19, waiting for transfers between devices, move(): return lax.ppermute(x, axis, [(i, (i + step) % size) for i in range(size)])  25.3 us
    ppermute x19, starting transfers between devices, move(): return lax.ppermute(x, axis, [(i, (i + step) % size) for i in range(size)])  19.3 us
    pallas_call x1, Pallas kernels, prep(): pl.pallas_call(prep_kernel, grid=(tables,), in_specs=[pl.BlockSpec(memory...  7.41 us
    all_to_all x1, starting transfers between devices, on_device(): parts.append(lax.all_to_all(blocks, ('hst', axes[0]), 0, 0, tiled=True))  6.07 us
    pallas_call x1, Pallas kernels, tail(): pl.pallas_call(tail_kernel, grid=(1,), in_specs=[smem] * 2 + [mine] + [th...  4.53 us
    unnamed x20, local copies, waits for them, and re-layouts  2.72 us
    slice x1, local copies, waits for them, and re-layouts, on_device(): mine = [flipped[2 * p:2 * p + 2] for p in range(2)]  2.58 us
  transfers between devices with their start and end apart: 20, of which 7 were waited for; matrix products, arithmetic and copies ran while one was open for 3% of the time, Pallas kernels for 45%

profile of v8, /device:TPU:0, one launch (start us, length us, event | category | flops | bytes accessed | tf_op | source)
XLA Modules:
  0.0 113.7 jit_solution(16245458998987661766)
XLA Ops:
  0.0 2.6 %fusion = (bf16[2,160,1024]{2,1,0:T(8,128)(2,1)}, bf16[2,160,1024]{2,1,0:T(8,128)(2,1)}) fusion(bf16[4,160,1024]{2,1,0:T(8,128)(2,1)} %bitcast.19), kind=kLoop, calls=%fused_computation.5 | loop fusion | bytes 2621440 | tf_op jit(solution)/shard_map/slice | solution.py:433
  2.6 4.1 %collective-permute-start = (bf16[2,160,1024]{2,1,0:T(8,128)(2,1)}, bf16[2,160,1024]{2,1,0:T(8,128)(2,1)}, u32[]{:S(2)}, u32[]{:S(2)}) collective-permute-start(bf16[2,160,1024]{2,1,0:T(8,128)(2,1)} %get-tuple-element.43), channel_id=1, source_target_pairs={{0,24},{8,0},{16,8},{24,16},{1,25},{9,1},{17,9},{25,17},{2,26},{10... | collective-permute-start | bytes 1966088 | tf_op jit(solution)/shard_map/ppermute | solution.py:394
  6.7 3.0 %collective-permute-start.2 = (bf16[2,160,1024]{2,1,0:T(8,128)(2,1)}, bf16[2,160,1024]{2,1,0:T(8,128)(2,1)}, u32[]{:S(2)}, u32[]{:S(2)}) collective-permute-start(bf16[2,160,1024]{2,1,0:T(8,128)(2,1)} %get-tuple-element.44), channel_id=1, source_target_pairs={{0,6},{2,0},{4,2},{6,4},{1,7},{3,1},{5,3},{7,5},{8,14},{10,8},{12,... | collective-permute-start | bytes 1966088 | tf_op jit(solution)/shard_map/ppermute | solution.py:394
  10.8 7.4 %prep.1 = (f32[4,32,4,16,128]{4,3,2,1,0:T(8,128)S(1)}, s32[4,8,16,128]{3,2,1,0:T(8,128)S(1)}, s32[4,16,128]{2,1,0:T(8,128)S(1)}) custom-call(s32[4]{0:T(128)S(1)} %pad_add_fusion.pos_ref, s32[4,8,16384]{2,1,0:T(8,128)S(1)} %bitcast.17, s32[4,16384]{1,0:T(4,128)S(1)} %bitcast.21), custom_call_target="tpu_custom_call" | custom-call | flops 40000000 | bytes 9000000 | tf_op jit(solution)/shard_map/prep/pallas_call | solution.py:84
  18.2 7.3 %pool_own.1.refs_8_ = f32[4,4,2,160,256]{4,3,2,1,0:T(8,128)S(1)} custom-call(s32[4,16,128]{2,1,0:T(8,128)S(1)} %get-tuple-element.58.refs_0_, s32[4,8,16,128]{3,2,1,0:T(8,128)S(1)} %get-tuple-element.37.refs_1_, f32[4,8,4,4,16,128]{5,4,3,2,1,0:T(8,128)S(1)} %bitcast.24, bf16[4,160,1024]{2,1,0:T(8,128)(2,1)S(1)} %bitcast.20), custom_call_target="tpu_custom_call" | custom-call | flops 4294967296 | bytes 5000000 | tf_op jit(solution)/shard_map/pool_own/pallas_call | solution.py:275
  25.5 2.5 %collective-permute-done.3.refs_7_ = bf16[2,160,1024]{2,1,0:T(8,128)(2,1)} collective-permute-done((bf16[2,160,1024]{2,1,0:T(8,128)(2,1)}, bf16[2,160,1024]{2,1,0:T(8,128)(2,1)}, u32[]{:S(2)}, u32[]{:S(2)}) %collective-permute-start.3) | collective-permute-done | bytes 655392 | tf_op jit(solution)/shard_map/ppermute | solution.py:394
  28.6 1.6 %collective-permute-start.4 = (bf16[2,160,1024]{2,1,0:T(8,128)(2,1)}, bf16[2,160,1024]{2,1,0:T(8,128)(2,1)S(1)}, u32[]{:S(2)}, u32[]{:S(2)}) collective-permute-start(bf16[2,160,1024]{2,1,0:T(8,128)(2,1)} %get-tuple-element.43), channel_id=1, source_target_pairs={{0,16},{8,24},{16,0},{24,8},{1,17},{9,25},{17,1},{25,9},{2,18},{10... | collective-permute-start | bytes 1966088 | tf_op jit(solution)/shard_map/ppermute | solution.py:394
  30.3 7.5 %pool_sides.2.refs_6_ = f32[2,4,2,160,256]{4,3,2,1,0:T(8,128)S(1)} custom-call(s32[4,16,128]{2,1,0:T(8,128)S(1)} %get-tuple-element.58.refs_0_, s32[4,8,16,128]{3,2,1,0:T(8,128)S(1)} %get-tuple-element.37.refs_1_, f32[4,8,4,4,16,128]{5,4,3,2,1,0:T(8,128)S(1)} %bitcast.25, f32[4,8,4,4,16,128]{5,4,3,2,1,0:T(8,128)S(1)} %bitcast.26, ...), custom_call_target="tpu_custom_call" | custom-call | flops 6442450944 | bytes 5000000 | tf_op jit(solution)/shard_map/pool_sides/pallas_call | solution.py:275
  37.8 8.1 %pool_sides.3.refs_10_ = f32[2,4,2,160,256]{4,3,2,1,0:T(8,128)S(1)} custom-call(s32[4,16,128]{2,1,0:T(8,128)S(1)} %get-tuple-element.58.refs_0_, s32[4,8,16,128]{3,2,1,0:T(8,128)S(1)} %get-tuple-element.37.refs_1_, f32[4,8,4,4,16,128]{5,4,3,2,1,0:T(8,128)S(1)} %bitcast.28, f32[4,8,4,4,16,128]{5,4,3,2,1,0:T(8,128)S(1)} %bitcast.29, ...), custom_call_target="tpu_custom_call" | custom-call | flops 6442450944 | bytes 5000000 | tf_op jit(solution)/shard_map/pool_sides/pallas_call | solution.py:275
  46.0 1.4 %collective-permute-done.4.refs_4_ = bf16[2,160,1024]{2,1,0:T(8,128)(2,1)S(1)} collective-permute-done((bf16[2,160,1024]{2,1,0:T(8,128)(2,1)}, bf16[2,160,1024]{2,1,0:T(8,128)(2,1)S(1)}, u32[]{:S(2)}, u32[]{:S(2)}) %collective-permute-start.4) | collective-permute-done | bytes 655392 | tf_op jit(solution)/shard_map/ppermute | solution.py:394
  47.4 1.3 %collective-permute-done.5.refs_8_ = bf16[2,160,1024]{2,1,0:T(8,128)(2,1)S(1)} collective-permute-done((bf16[2,160,1024]{2,1,0:T(8,128)(2,1)}, bf16[2,160,1024]{2,1,0:T(8,128)(2,1)S(1)}, u32[]{:S(2)}, u32[]{:S(2)}) %collective-permute-start.5) | collective-permute-done | bytes 655392 | tf_op jit(solution)/shard_map/ppermute | solution.py:394
  49.2 5.6 %pool_other.1.refs_6_ = f32[2,4,2,160,256]{4,3,2,1,0:T(8,128)S(1)} custom-call(s32[4,16,128]{2,1,0:T(8,128)S(1)} %get-tuple-element.58.refs_0_, s32[4,8,16,128]{3,2,1,0:T(8,128)S(1)} %get-tuple-element.37.refs_1_, f32[4,8,4,4,16,128]{5,4,3,2,1,0:T(8,128)S(1)} %bitcast.31, f32[4,8,4,4,16,128]{5,4,3,2,1,0:T(8,128)S(1)} %bitcast.32, ...), custom_call_target="tpu_custom_call" | custom-call | flops 4294967296 | bytes 5000000 | tf_op jit(solution)/shard_map/pool_other/pallas_call | solution.py:275
  54.9 6.4 %pool_beyond.1 = (bf16[4,2,160,128]{3,2,1,0:T(8,128)(2,1)S(1)}, bf16[4,2,160,128]{3,2,1,0:T(8,128)(2,1)S(1)}, bf16[4,2,160,128]{3,2,1,0:T(8,128)(2,1)S(1)}, bf16[4,2,160,128]{3,2,1,0:T(8,128)(2,1)S(1)}) custom-call(s32[4,16,128]{2,1,0:T(8,128)S(1)} %get-tuple-element.58.refs_0_, s32[4,8,16,128]{3,2,1,0:T(8,128)S(1)} %get-tuple-element.37.refs_1_, ...), custom_call_target="tpu_custom_call" | custom-call | flops 4294967296 | bytes 5000000 | tf_op jit(solution)/shard_map/pool_beyond/pallas_call | solution.py:275
  61.4 2.5 %collective-permute-start.12 = (bf16[4,2,160,128]{3,2,1,0:T(8,128)(2,1)S(1)}, bf16[4,2,160,128]{3,2,1,0:T(8,128)(2,1)S(1)}, u32[]{:S(2)}, u32[]{:S(2)}) collective-permute-start(bf16[4,2,160,128]{3,2,1,0:T(8,128)(2,1)S(1)} %get-tuple-element.56), channel_id=1, source_target_pairs={{0,4},{2,6},{4,0},{6,2},{1,5},{3,7},{5,1},{7,3},{8,12},{10,14},{12... | collective-permute-start | bytes 983048 | tf_op jit(solution)/shard_map/ppermute | solution.py:394
  64.6 9.3 %pool_rest.1 = bf16[16,2,160,128]{3,2,1,0:T(8,128)(2,1)} custom-call(s32[4,16,128]{2,1,0:T(8,128)S(1)} %get-tuple-element.58.refs_0_, s32[4,8,16,128]{3,2,1,0:T(8,128)S(1)} %get-tuple-element.37.refs_1_, f32[4,8,4,4,16,128]{5,4,3,2,1,0:T(8,128)S(1)} %bitcast.35, f32[4,8,4,4,16,128]{5,4,3,2,1,0:T(8,128)S(1)} %bitcast.36, ...), custom_call_target="tpu_custom_call" | custom-call | flops 8589934592 | bytes 5000000 | tf_op jit(solution)/shard_map/pool_rest/pallas_call | solution.py:275
  74.0 5.4 %collective-permute-done.11 = bf16[4,2,160,128]{3,2,1,0:T(8,128)(2,1)S(1)} collective-permute-done((bf16[4,2,160,128]{3,2,1,0:T(8,128)(2,1)S(1)}, bf16[4,2,160,128]{3,2,1,0:T(8,128)(2,1)S(1)}, u32[]{:S(2)}, u32[]{:S(2)}) %collective-permute-start.11) | collective-permute-done | bytes 327712 | tf_op jit(solution)/shard_map/ppermute | solution.py:394
  80.1 6.1 %all-to-all-start = ((bf16[16,2,160,128]{3,2,1,0:T(8,128)(2,1)}), bf16[16,2,160,128]{3,2,1,0:T(8,128)(2,1)S(1)}, u32[]{:S(2)}, u32[]{:S(2)}) async-start(bf16[16,2,160,128]{3,2,1,0:T(8,128)(2,1)} %pool_rest.1), calls=%async_computation | async-start | bytes 2621440 | tf_op jit(solution)/shard_map/all_to_all | solution.py:467
  87.3 2.0 %collective-permute-start.16 = (bf16[2,160,128]{2,1,0:T(8,128)(2,1)S(1)}, bf16[2,160,128]{2,1,0:T(8,128)(2,1)S(1)}, u32[]{:S(2)}, u32[]{:S(2)}) collective-permute-start(bf16[2,160,128]{2,1,0:T(8,128)(2,1)S(1)} %get-tuple-element.71), channel_id=1, source_target_pairs={{0,32},{32,64},{64,96},{96,0},{1,33},{33,65},{65,97},{97,1},{2,34}... | collective-permute-start | bytes 245768 | tf_op jit(solution)/shard_map/ppermute | solution.py:394
  89.3 2.7 %collective-permute-start.17 = (bf16[2,160,128]{2,1,0:T(8,128)(2,1)S(1)}, bf16[2,160,128]{2,1,0:T(8,128)(2,1)S(1)}, u32[]{:S(2)}, u32[]{:S(2)}) collective-permute-start(bf16[2,160,128]{2,1,0:T(8,128)(2,1)S(1)} %get-tuple-element.70), channel_id=1, source_target_pairs={{0,64},{32,96},{64,0},{96,32},{1,65},{33,97},{65,1},{97,33},{2,66}... | collective-permute-start | bytes 245768 | tf_op jit(solution)/shard_map/ppermute | solution.py:394
  92.0 1.5 %collective-permute-start.18 = (bf16[2,160,128]{2,1,0:T(8,128)(2,1)S(1)}, bf16[2,160,128]{2,1,0:T(8,128)(2,1)S(1)}, u32[]{:S(2)}, u32[]{:S(2)}) collective-permute-start(bf16[2,160,128]{2,1,0:T(8,128)(2,1)S(1)} %get-tuple-element.69), channel_id=1, source_target_pairs={{0,96},{32,0},{64,32},{96,64},{1,97},{33,1},{65,33},{97,65},{2,98}... | collective-permute-start | bytes 245768 | tf_op jit(solution)/shard_map/ppermute | solution.py:394
  93.5 12.7 %collective-permute-done.16.rest_1_ = bf16[2,160,128]{2,1,0:T(8,128)(2,1)S(1)} collective-permute-done((bf16[2,160,128]{2,1,0:T(8,128)(2,1)S(1)}, bf16[2,160,128]{2,1,0:T(8,128)(2,1)S(1)}, u32[]{:S(2)}, u32[]{:S(2)}) %collective-permute-start.16) | collective-permute-done | bytes 81952 | tf_op jit(solution)/shard_map/ppermute | solution.py:394
  106.1 1.2 %collective-permute-done.17.rest_2_ = bf16[2,160,128]{2,1,0:T(8,128)(2,1)S(1)} collective-permute-done((bf16[2,160,128]{2,1,0:T(8,128)(2,1)S(1)}, bf16[2,160,128]{2,1,0:T(8,128)(2,1)S(1)}, u32[]{:S(2)}, u32[]{:S(2)}) %collective-permute-start.17) | collective-permute-done | bytes 81952 | tf_op jit(solution)/shard_map/ppermute | solution.py:394
  107.4 1.7 %copy-done = bf16[1024,1280]{1,0:T(8,128)(2,1)S(1)} copy-done((bf16[1024,1280]{1,0:T(8,128)(2,1)S(1)}, bf16[1024,1280]{1,0:T(8,128)(2,1)}, u32[]{:S(2)}) %copy-start) | copy-done | bytes 2621464
  109.1 4.5 %tail.1 = bf16[16,160,128]{2,1,0:T(8,128)(2,1)} custom-call(s32[1]{0:T(128)} %bitcast.host_ref, s32[16]{0:T(128)S(1)} %copy-done.9, bf16[4,2,160,128]{3,2,1,0:T(8,128)(2,1)S(1)} %add_convert_fusion.rest_0_, bf16[2,160,128]{2,1,0:T(8,128)(2,1)S(1)} %collective-permute-done.16.rest_1_, bf16[2,160,128]{2,1,0:T(8,128)(2,1)S(1)} %collective-permute-done.17.rest_2_, ...), custom_call_target="tpu_custom_call" | custom-call | flops 1000000000 | bytes 8000000 | tf_op jit(solution)/shard_map/tail/pallas_call | solution.py:373
  (48 shorter events, 4.9 us)
Async XLA Ops:
  0.0 30.1 %collective-permute-start.9 = (bf16[4,160,1024]{2,1,0:T(8,128)(2,1)}, bf16[4,160,1024]{2,1,0:T(8,128)(2,1)}, u32[]{:S(2)}, u32[]{:S(2)}) collective-permute-start(bf16[4,160,1024]{2,1,0:T(8,128)(2,1)} %bitcast.18), channel_id=1, source_target_pairs={{0,1},{1,0},{2,3},{3,2},{4,5},{5,4},{6,7},{7,6},{8,9},{9,8},{10,11... | collective-permute-start | bytes 3932168 | tf_op jit(solution)/shard_map/ppermute | solution.py:394
  2.6 22.9 %collective-permute-start = (bf16[2,160,1024]{2,1,0:T(8,128)(2,1)}, bf16[2,160,1024]{2,1,0:T(8,128)(2,1)}, u32[]{:S(2)}, u32[]{:S(2)}) collective-permute-start(bf16[2,160,1024]{2,1,0:T(8,128)(2,1)} %get-tuple-element.43), channel_id=1, source_target_pairs={{0,24},{8,0},{16,8},{24,16},{1,25},{9,1},{17,9},{25,17},{2,26},{10... | collective-permute-start | bytes 1966088 | tf_op jit(solution)/shard_map/ppermute | solution.py:394
  6.7 18.8 %collective-permute-start.1 = (bf16[2,160,1024]{2,1,0:T(8,128)(2,1)}, bf16[2,160,1024]{2,1,0:T(8,128)(2,1)}, u32[]{:S(2)}, u32[]{:S(2)}) collective-permute-start(bf16[2,160,1024]{2,1,0:T(8,128)(2,1)} %get-tuple-element.43), channel_id=1, source_target_pairs={{0,8},{8,16},{16,24},{24,0},{1,9},{9,17},{17,25},{25,1},{2,10},{10... | collective-permute-start | bytes 1966088 | tf_op jit(solution)/shard_map/ppermute | solution.py:394
  6.7 18.8 %collective-permute-start.2 = (bf16[2,160,1024]{2,1,0:T(8,128)(2,1)}, bf16[2,160,1024]{2,1,0:T(8,128)(2,1)}, u32[]{:S(2)}, u32[]{:S(2)}) collective-permute-start(bf16[2,160,1024]{2,1,0:T(8,128)(2,1)} %get-tuple-element.44), channel_id=1, source_target_pairs={{0,6},{2,0},{4,2},{6,4},{1,7},{3,1},{5,3},{7,5},{8,14},{10,8},{12,... | collective-permute-start | bytes 1966088 | tf_op jit(solution)/shard_map/ppermute | solution.py:394
  9.7 18.3 %collective-permute-start.3 = (bf16[2,160,1024]{2,1,0:T(8,128)(2,1)}, bf16[2,160,1024]{2,1,0:T(8,128)(2,1)}, u32[]{:S(2)}, u32[]{:S(2)}) collective-permute-start(bf16[2,160,1024]{2,1,0:T(8,128)(2,1)} %get-tuple-element.44), channel_id=1, source_target_pairs={{0,2},{2,4},{4,6},{6,0},{1,3},{3,5},{5,7},{7,1},{8,10},{10,12},{12... | collective-permute-start | bytes 1966088 | tf_op jit(solution)/shard_map/ppermute | solution.py:394
  28.0 17.9 %collective-permute-start.6 = (bf16[2,160,1024]{2,1,0:T(8,128)(2,1)}, bf16[2,160,1024]{2,1,0:T(8,128)(2,1)S(1)}, u32[]{:S(2)}, u32[]{:S(2)}) collective-permute-start(bf16[2,160,1024]{2,1,0:T(8,128)(2,1)} %collective-permute-done.refs_6_), channel_id=1, source_target_pairs={{0,1},{1,0},{2,3},{3,2},{4,5},{5,4},{6,7},{7,6},{8,9},{9,8},{10,11... | collective-permute-start | bytes 1966088 | tf_op jit(solution)/shard_map/ppermute | solution.py:394
  28.1 17.9 %collective-permute-start.7 = (bf16[2,160,1024]{2,1,0:T(8,128)(2,1)}, bf16[2,160,1024]{2,1,0:T(8,128)(2,1)S(1)}, u32[]{:S(2)}, u32[]{:S(2)}) collective-permute-start(bf16[2,160,1024]{2,1,0:T(8,128)(2,1)} %collective-permute-done.1.refs_7_), channel_id=1, source_target_pairs={{0,1},{1,0},{2,3},{3,2},{4,5},{5,4},{6,7},{7,6},{8,9},{9,8},{10,11... | collective-permute-start | bytes 1966088 | tf_op jit(solution)/shard_map/ppermute | solution.py:394
  28.6 17.4 %collective-permute-start.8 = (bf16[2,160,1024]{2,1,0:T(8,128)(2,1)}, bf16[2,160,1024]{2,1,0:T(8,128)(2,1)S(1)}, u32[]{:S(2)}, u32[]{:S(2)}) collective-permute-start(bf16[2,160,1024]{2,1,0:T(8,128)(2,1)} %collective-permute-done.2.refs_6_), channel_id=1, source_target_pairs={{0,1},{1,0},{2,3},{3,2},{4,5},{5,4},{6,7},{7,6},{8,9},{9,8},{10,11... | collective-permute-start | bytes 1966088 | tf_op jit(solution)/shard_map/ppermute | solution.py:394
  28.6 18.9 %collective-permute-start.4 = (bf16[2,160,1024]{2,1,0:T(8,128)(2,1)}, bf16[2,160,1024]{2,1,0:T(8,128)(2,1)S(1)}, u32[]{:S(2)}, u32[]{:S(2)}) collective-permute-start(bf16[2,160,1024]{2,1,0:T(8,128)(2,1)} %get-tuple-element.43), channel_id=1, source_target_pairs={{0,16},{8,24},{16,0},{24,8},{1,17},{9,25},{17,1},{25,9},{2,18},{10... | collective-permute-start | bytes 1966088 | tf_op jit(solution)/shard_map/ppermute | solution.py:394
  30.1 18.6 %collective-permute-start.5 = (bf16[2,160,1024]{2,1,0:T(8,128)(2,1)}, bf16[2,160,1024]{2,1,0:T(8,128)(2,1)S(1)}, u32[]{:S(2)}, u32[]{:S(2)}) collective-permute-start(bf16[2,160,1024]{2,1,0:T(8,128)(2,1)} %get-tuple-element.44), channel_id=1, source_target_pairs={{0,4},{2,6},{4,0},{6,2},{1,5},{3,7},{5,1},{7,3},{8,12},{10,14},{12... | collective-permute-start | bytes 1966088 | tf_op jit(solution)/shard_map/ppermute | solution.py:394
  48.7 6.1 %collective-permute-start.10 = (bf16[2,160,1024]{2,1,0:T(8,128)(2,1)S(1)}, bf16[2,160,1024]{2,1,0:T(8,128)(2,1)S(1)}, u32[]{:S(2)}, u32[]{:S(2)}) collective-permute-start(bf16[2,160,1024]{2,1,0:T(8,128)(2,1)S(1)} %collective-permute-done.4.refs_4_), channel_id=1, source_target_pairs={{0,1},{1,0},{2,3},{3,2},{4,5},{5,4},{6,7},{7,6},{8,9},{9,8},{10,11... | collective-permute-start | bytes 1966088 | tf_op jit(solution)/shard_map/ppermute | solution.py:394
  48.7 15.9 %collective-permute-start.14 = (bf16[2,160,1024]{2,1,0:T(8,128)(2,1)}, bf16[2,160,1024]{2,1,0:T(8,128)(2,1)S(1)}, u32[]{:S(2)}, u32[]{:S(2)}) collective-permute-start(bf16[2,160,1024]{2,1,0:T(8,128)(2,1)} %collective-permute-done.3.refs_7_), channel_id=1, source_target_pairs={{0,1},{1,0},{2,3},{3,2},{4,5},{5,4},{6,7},{7,6},{8,9},{9,8},{10,11... | collective-permute-start | bytes 1966088 | tf_op jit(solution)/shard_map/ppermute | solution.py:394
  49.2 15.4 %collective-permute-start.15 = (bf16[2,160,1024]{2,1,0:T(8,128)(2,1)S(1)}, bf16[2,160,1024]{2,1,0:T(8,128)(2,1)S(1)}, u32[]{:S(2)}, u32[]{:S(2)}) collective-permute-start(bf16[2,160,1024]{2,1,0:T(8,128)(2,1)S(1)} %collective-permute-done.5.refs_8_), channel_id=1, source_target_pairs={{0,1},{1,0},{2,3},{3,2},{4,5},{5,4},{6,7},{7,6},{8,9},{9,8},{10,11... | collective-permute-start | bytes 1966088 | tf_op jit(solution)/shard_map/ppermute | solution.py:394
  61.3 18.0 %collective-permute-start.11 = (bf16[4,2,160,128]{3,2,1,0:T(8,128)(2,1)S(1)}, bf16[4,2,160,128]{3,2,1,0:T(8,128)(2,1)S(1)}, u32[]{:S(2)}, u32[]{:S(2)}) collective-permute-start(bf16[4,2,160,128]{3,2,1,0:T(8,128)(2,1)S(1)} %get-tuple-element.55), channel_id=1, source_target_pairs={{0,2},{2,4},{4,6},{6,0},{1,3},{3,5},{5,7},{7,1},{8,10},{10,12},{12... | collective-permute-start | bytes 983048 | tf_op jit(solution)/shard_map/ppermute | solution.py:394
  61.4 17.9 %collective-permute-start.12 = (bf16[4,2,160,128]{3,2,1,0:T(8,128)(2,1)S(1)}, bf16[4,2,160,128]{3,2,1,0:T(8,128)(2,1)S(1)}, u32[]{:S(2)}, u32[]{:S(2)}) collective-permute-start(bf16[4,2,160,128]{3,2,1,0:T(8,128)(2,1)S(1)} %get-tuple-element.56), channel_id=1, source_target_pairs={{0,4},{2,6},{4,0},{6,2},{1,5},{3,7},{5,1},{7,3},{8,12},{10,14},{12... | collective-permute-start | bytes 983048 | tf_op jit(solution)/shard_map/ppermute | solution.py:394
  63.9 16.1 %collective-permute-start.13 = (bf16[4,2,160,128]{3,2,1,0:T(8,128)(2,1)S(1)}, bf16[4,2,160,128]{3,2,1,0:T(8,128)(2,1)}, u32[]{:S(2)}, u32[]{:S(2)}) collective-permute-start(bf16[4,2,160,128]{3,2,1,0:T(8,128)(2,1)S(1)} %get-tuple-element.57), channel_id=1, source_target_pairs={{0,6},{2,0},{4,2},{6,4},{1,7},{3,1},{5,3},{7,5},{8,14},{10,8},{12,... | collective-permute-start | bytes 983048 | tf_op jit(solution)/shard_map/ppermute | solution.py:394
  73.9 33.4 %copy-start.6 = (bf16[24,16]{0,1:T(8,128)(2,1)S(1)}, bf16[24,16]{0,1:T(8,128)(2,1)}, u32[]{:S(2)}) copy-start(bf16[24,16]{0,1:T(8,128)(2,1)} %param.14) | copy-start | bytes 2308
  73.9 33.4 %copy-start.7 = (f32[384]{0:T(512)S(1)}, f32[384]{0:T(512)}, u32[]{:S(2)}) copy-start(f32[384]{0:T(512)} %param.15) | copy-start | bytes 4612
  73.9 33.4 %copy-start.8 = (bf16[8,16]{1,0:T(8,128)(2,1)S(1)}, bf16[8,16]{1,0:T(8,128)(2,1)}, u32[]{:S(2)}) copy-start(bf16[8,16]{1,0:T(8,128)(2,1)} %rest_9_.1) | copy-start | bytes 772
  73.9 33.4 %copy-start.9 = (s32[16]{0:T(128)S(1)}, s32[16]{0:T(128)}, u32[]{:S(2)}) copy-start(s32[16]{0:T(128)} %order_ref.1) | copy-start | bytes 196
  80.1 27.2 %all-to-all-start = ((bf16[16,2,160,128]{3,2,1,0:T(8,128)(2,1)}), bf16[16,2,160,128]{3,2,1,0:T(8,128)(2,1)S(1)}, u32[]{:S(2)}, u32[]{:S(2)}) async-start(bf16[16,2,160,128]{3,2,1,0:T(8,128)(2,1)} %pool_rest.1), calls=%async_computation | async-start | bytes 2621440 | tf_op jit(solution)/shard_map/all_to_all | solution.py:467
  87.3 18.8 %collective-permute-start.16 = (bf16[2,160,128]{2,1,0:T(8,128)(2,1)S(1)}, bf16[2,160,128]{2,1,0:T(8,128)(2,1)S(1)}, u32[]{:S(2)}, u32[]{:S(2)}) collective-permute-start(bf16[2,160,128]{2,1,0:T(8,128)(2,1)S(1)} %get-tuple-element.71), channel_id=1, source_target_pairs={{0,32},{32,64},{64,96},{96,0},{1,33},{33,65},{65,97},{97,1},{2,34}... | collective-permute-start | bytes 245768 | tf_op jit(solution)/shard_map/ppermute | solution.py:394
  89.3 18.0 %collective-permute-start.17 = (bf16[2,160,128]{2,1,0:T(8,128)(2,1)S(1)}, bf16[2,160,128]{2,1,0:T(8,128)(2,1)S(1)}, u32[]{:S(2)}, u32[]{:S(2)}) collective-permute-start(bf16[2,160,128]{2,1,0:T(8,128)(2,1)S(1)} %get-tuple-element.70), channel_id=1, source_target_pairs={{0,64},{32,96},{64,0},{96,32},{1,65},{33,97},{65,1},{97,33},{2,66}... | collective-permute-start | bytes 245768 | tf_op jit(solution)/shard_map/ppermute | solution.py:394
  92.0 15.3 %collective-permute-start.18 = (bf16[2,160,128]{2,1,0:T(8,128)(2,1)S(1)}, bf16[2,160,128]{2,1,0:T(8,128)(2,1)S(1)}, u32[]{:S(2)}, u32[]{:S(2)}) collective-permute-start(bf16[2,160,128]{2,1,0:T(8,128)(2,1)S(1)} %get-tuple-element.69), channel_id=1, source_target_pairs={{0,96},{32,0},{64,32},{96,64},{1,97},{33,1},{65,33},{97,65},{2,98}... | collective-permute-start | bytes 245768 | tf_op jit(solution)/shard_map/ppermute | solution.py:394
  (6 other events, 97.5 us)

commit v9 on v8

--- a/solution.py
+++ b/solution.py
@@ -15,6 +15,8 @@
 BLOCKS = GATHER * ROWS_DEV // SUB
 BAG_BLOCKS = 16
 PAIR = 2 * LANES
+PARTS = 4
+STEPS = BAG_BLOCKS // (2 * PARTS)
 
 
 def prep_kernel(pos_ref, idx_ref, len_ref, keys_ref, lid_ref, mask_ref):
@@ -132,8 +134,8 @@
     def wide(x):
         return jnp.broadcast_to(x, (16, LANES)).astype(jnp.bfloat16)
 
-    for part in range(2):
-        bag = 4 * step + 2 * part
+    for part in range(PARTS):
+        bag = 2 * (PARTS * step + part)
         for (first, n), key in zip(layout, keys):
             for b in range(n):
                 k1, m1, k2, m2 = (
@@ -159,8 +161,8 @@
 
     stage_bits = ((1 << n_blocks) - 1) << first_block
     stage_bits = stage_bits - (1 << 32) if stage_bits >= 1 << 31 else stage_bits
-    for part in range(2):
-        bag = 4 * step + 2 * part
+    for part in range(PARTS):
+        bag = 2 * (PARTS * step + part)
         mask = mask_ref[table0 + table, bag, 0] | mask_ref[table0 + table, bag + 1, 0]
 
         @pl.when((mask & jnp.int32(stage_bits)) != 0)
@@ -206,26 +208,26 @@
 
             lax.fori_loop(0, n_blocks, fix, 0)
 
-    def finish(out):
-        for part in range(2):
-            result = sums[0, 0, part].astype(jnp.bfloat16)
-            out[2 * part, 0] = result[:, :LANES]
-            out[2 * part + 1, 0] = result[:, LANES:]
+    def finish(out, first_part, n_parts):
+        for k in range(n_parts):
+            result = sums[0, 0, first_part + k].astype(jnp.bfloat16)
+            out[2 * k, 0] = result[:, :LANES]
+            out[2 * k + 1, 0] = result[:, LANES:]
 
     if n_outs == 1:
-        finish(outs[0])
+        finish(outs[0], 0, PARTS)
     for d in range(n_outs if n_outs > 1 else 0):
 
-        @pl.when(step == d)
+        @pl.when(step == 2 * d // PARTS)
         def _(d=d):
-            finish(outs[d])
+            finish(outs[d], 2 * d % PARTS, 2)
 
 
 def pool(tables, masks, keys, lids, pieces, base, n_outs, name):
     n_tables = len(tables)
     table0 = tables[0]
     emb = pieces[0][0].shape[1]
-    sums_block = (1, 1, 2, emb, PAIR)
+    sums_block = (1, 1, PARTS, emb, PAIR)
     sums_spec = pl.BlockSpec(sums_block, lambda j, i: (j, i, 0, 0, 0))
     layout, key_specs, tab_specs = [], [], []
     for array, start_table, shard, start in pieces:
@@ -257,13 +259,16 @@
         )
         args.append(array)
     scratch = [
-        pltpu.VMEM((2, rows, PAIR), jnp.bfloat16),
+        pltpu.VMEM((PARTS, rows, PAIR), jnp.bfloat16),
         pltpu.VMEM((SUB, PAIR), jnp.bfloat16),
     ]
     if n_outs:
         places = BAG_BLOCKS // n_outs
         out_specs = [
-            pl.BlockSpec((4, 1, emb, LANES), lambda j, i: (i if n_outs == 1 else 0, j, 0, 0))
+            pl.BlockSpec(
+                (2 * PARTS if n_outs == 1 else places, 1, emb, LANES),
+                lambda j, i: (i if n_outs == 1 else 0, j, 0, 0),
+            )
         ] * n_outs
         out_shape = [
             jax.ShapeDtypeStruct((places, n_tables, emb, LANES), jnp.bfloat16)
@@ -271,10 +276,10 @@
         scratch = [pltpu.VMEM(sums_block, jnp.float32)] + scratch
     else:
         out_specs = sums_spec
-        out_shape = jax.ShapeDtypeStruct((n_tables, 4, 2, emb, PAIR), jnp.float32)
+        out_shape = jax.ShapeDtypeStruct((n_tables, STEPS, PARTS, emb, PAIR), jnp.float32)
     return pl.pallas_call(
         functools.partial(pool_kernel, tuple(layout), base is not None, n_outs, table0),
-        grid=(n_tables, 4),
+        grid=(n_tables, STEPS),
         in_specs=in_specs,
         out_specs=out_specs,
         out_shape=out_shape,
@@ -381,7 +386,7 @@
             pltpu.VMEM((feats, feats, LANES), jnp.float32),
             pltpu.VMEM((feats, width, LANES), jnp.float32),
         ],
-        compiler_params=pltpu.CompilerParams(vmem_limit_bytes=32 << 20),
+        compiler_params=pltpu.CompilerParams(vmem_limit_bytes=20 << 20),
         cost_estimate=pl.CostEstimate(
             flops=1_000_000_000, bytes_accessed=8_000_000, transcendentals=0
         ),

time: 114 us -> 113 us (level)
  Pallas kernels: 56.2 us -> 48.8 us
  waiting for transfers between devices: 25.3 us -> 31.6 us
    pallas_call x6, Pallas kernels: 44.3 us -> 36.9 us  [pool(): pl.pallas_call(functools.partial(pool_kernel, tuple(layout), base is not...]
    ppermute x19, waiting for transfers between devices: 25.3 us -> 31.6 us  [move(): return lax.ppermute(x, axis, [(i, (i + step) % size) for i in range(size)])]
  transfers between devices with their start and end apart: 20 -> 20, of which waited for: 7 -> 8; matrix products, arithmetic and copies ran while one was open for 3% -> 3% of each run, Pallas kernels for 45% -> 39%
where the time goes in v9:
time: 113 us
  Pallas kernels  48.8 us (43%)
  waiting for transfers between devices  31.6 us (28%)
  starting transfers between devices  25.4 us (22%)
  local copies, waits for them, and re-layouts  5.32 us (5%)
  other arithmetic  1.22 us (1%)
    pallas_call x6, Pallas kernels, pool(): pl.pallas_call(functools.partial(pool_kernel, tuple(layout), base is not...  36.9 us
    ppermute x19, waiting for transfers between devices, move(): return lax.ppermute(x, axis, [(i, (i + step) % size) for i in range(size)])  31.6 us
    ppermute x19, starting transfers between devices, move(): return lax.ppermute(x, axis, [(i, (i + step) % size) for i in range(size)])  19.2 us
    pallas_call x1, Pallas kernels, prep(): pl.pallas_call(prep_kernel, grid=(tables,), in_specs=[pl.BlockSpec(memory...  7.41 us
    all_to_all x1, starting transfers between devices, on_device(): parts.append(lax.all_to_all(blocks, ('hst', axes[0]), 0, 0, tiled=True))  6.18 us
    pallas_call x1, Pallas kernels, tail(): pl.pallas_call(tail_kernel, grid=(1,), in_specs=[smem] * 2 + [mine] + [th...  4.53 us
    unnamed x20, local copies, waits for them, and re-layouts  2.72 us
    slice x1, local copies, waits for them, and re-layouts, on_device(): mine = [flipped[2 * p:2 * p + 2] for p in range(2)]  2.58 us
  transfers between devices with their start and end apart: 20, of which 8 were waited for; matrix products, arithmetic and copies ran while one was open for 3% of the time, Pallas kernels for 39%

profile of v9, /device:TPU:0, one launch (start us, length us, event | category | flops | bytes accessed | tf_op | source)
XLA Modules:
  0.0 112.5 jit_solution(17468572554560687482)
XLA Ops:
  0.0 2.6 %fusion = (bf16[2,160,1024]{2,1,0:T(8,128)(2,1)}, bf16[2,160,1024]{2,1,0:T(8,128)(2,1)}) fusion(bf16[4,160,1024]{2,1,0:T(8,128)(2,1)} %bitcast.19), kind=kLoop, calls=%fused_computation.5 | loop fusion | bytes 2621440 | tf_op jit(solution)/shard_map/slice | solution.py:438
  2.6 4.1 %collective-permute-start = (bf16[2,160,1024]{2,1,0:T(8,128)(2,1)}, bf16[2,160,1024]{2,1,0:T(8,128)(2,1)}, u32[]{:S(2)}, u32[]{:S(2)}) collective-permute-start(bf16[2,160,1024]{2,1,0:T(8,128)(2,1)} %get-tuple-element.43), channel_id=1, source_target_pairs={{0,24},{8,0},{16,8},{24,16},{1,25},{9,1},{17,9},{25,17},{2,26},{10... | collective-permute-start | bytes 1966088 | tf_op jit(solution)/shard_map/ppermute | solution.py:399
  6.7 3.0 %collective-permute-start.2 = (bf16[2,160,1024]{2,1,0:T(8,128)(2,1)}, bf16[2,160,1024]{2,1,0:T(8,128)(2,1)}, u32[]{:S(2)}, u32[]{:S(2)}) collective-permute-start(bf16[2,160,1024]{2,1,0:T(8,128)(2,1)} %get-tuple-element.44), channel_id=1, source_target_pairs={{0,6},{2,0},{4,2},{6,4},{1,7},{3,1},{5,3},{7,5},{8,14},{10,8},{12,... | collective-permute-start | bytes 1966088 | tf_op jit(solution)/shard_map/ppermute | solution.py:399
  10.8 7.4 %prep.1 = (f32[4,32,4,16,128]{4,3,2,1,0:T(8,128)S(1)}, s32[4,8,16,128]{3,2,1,0:T(8,128)S(1)}, s32[4,16,128]{2,1,0:T(8,128)S(1)}) custom-call(s32[4]{0:T(128)S(1)} %pad_add_fusion.pos_ref, s32[4,8,16384]{2,1,0:T(8,128)S(1)} %bitcast.17, s32[4,16384]{1,0:T(4,128)S(1)} %bitcast.21), custom_call_target="tpu_custom_call" | custom-call | flops 40000000 | bytes 9000000 | tf_op jit(solution)/shard_map/prep/pallas_call | solution.py:86
  18.2 5.8 %pool_own.1.refs_8_ = f32[4,2,4,160,256]{4,3,2,1,0:T(8,128)S(1)} custom-call(s32[4,16,128]{2,1,0:T(8,128)S(1)} %get-tuple-element.58.refs_0_, s32[4,8,16,128]{3,2,1,0:T(8,128)S(1)} %get-tuple-element.37.refs_1_, f32[4,8,4,4,16,128]{5,4,3,2,1,0:T(8,128)S(1)} %bitcast.24, bf16[4,160,1024]{2,1,0:T(8,128)(2,1)S(1)} %bitcast.20), custom_call_target="tpu_custom_call" | custom-call | flops 4294967296 | bytes 5000000 | tf_op jit(solution)/shard_map/pool_own/pallas_call | solution.py:280
  24.0 1.3 %collective-permute-done.1.refs_7_ = bf16[2,160,1024]{2,1,0:T(8,128)(2,1)} collective-permute-done((bf16[2,160,1024]{2,1,0:T(8,128)(2,1)}, bf16[2,160,1024]{2,1,0:T(8,128)(2,1)}, u32[]{:S(2)}, u32[]{:S(2)}) %collective-permute-start.1) | collective-permute-done | bytes 655392 | tf_op jit(solution)/shard_map/ppermute | solution.py:399
  25.3 2.7 %collective-permute-done.3.refs_7_ = bf16[2,160,1024]{2,1,0:T(8,128)(2,1)} collective-permute-done((bf16[2,160,1024]{2,1,0:T(8,128)(2,1)}, bf16[2,160,1024]{2,1,0:T(8,128)(2,1)}, u32[]{:S(2)}, u32[]{:S(2)}) %collective-permute-start.3) | collective-permute-done | bytes 655392 | tf_op jit(solution)/shard_map/ppermute | solution.py:399
  28.6 1.6 %collective-permute-start.4 = (bf16[2,160,1024]{2,1,0:T(8,128)(2,1)}, bf16[2,160,1024]{2,1,0:T(8,128)(2,1)S(1)}, u32[]{:S(2)}, u32[]{:S(2)}) collective-permute-start(bf16[2,160,1024]{2,1,0:T(8,128)(2,1)} %get-tuple-element.43), channel_id=1, source_target_pairs={{0,16},{8,24},{16,0},{24,8},{1,17},{9,25},{17,1},{25,9},{2,18},{10... | collective-permute-start | bytes 1966088 | tf_op jit(solution)/shard_map/ppermute | solution.py:399
  30.2 6.3 %pool_sides.2.refs_6_ = f32[2,2,4,160,256]{4,3,2,1,0:T(8,128)S(1)} custom-call(s32[4,16,128]{2,1,0:T(8,128)S(1)} %get-tuple-element.58.refs_0_, s32[4,8,16,128]{3,2,1,0:T(8,128)S(1)} %get-tuple-element.37.refs_1_, f32[4,8,4,4,16,128]{5,4,3,2,1,0:T(8,128)S(1)} %bitcast.25, f32[4,8,4,4,16,128]{5,4,3,2,1,0:T(8,128)S(1)} %bitcast.26, ...), custom_call_target="tpu_custom_call" | custom-call | flops 6442450944 | bytes 5000000 | tf_op jit(solution)/shard_map/pool_sides/pallas_call | solution.py:280
  36.5 6.4 %pool_sides.3.refs_10_ = f32[2,2,4,160,256]{4,3,2,1,0:T(8,128)S(1)} custom-call(s32[4,16,128]{2,1,0:T(8,128)S(1)} %get-tuple-element.58.refs_0_, s32[4,8,16,128]{3,2,1,0:T(8,128)S(1)} %get-tuple-element.37.refs_1_, f32[4,8,4,4,16,128]{5,4,3,2,1,0:T(8,128)S(1)} %bitcast.28, f32[4,8,4,4,16,128]{5,4,3,2,1,0:T(8,128)S(1)} %bitcast.29, ...), custom_call_target="tpu_custom_call" | custom-call | flops 6442450944 | bytes 5000000 | tf_op jit(solution)/shard_map/pool_sides/pallas_call | solution.py:280
  42.9 4.5 %collective-permute-done.4.refs_4_ = bf16[2,160,1024]{2,1,0:T(8,128)(2,1)S(1)} collective-permute-done((bf16[2,160,1024]{2,1,0:T(8,128)(2,1)}, bf16[2,160,1024]{2,1,0:T(8,128)(2,1)S(1)}, u32[]{:S(2)}, u32[]{:S(2)}) %collective-permute-start.4) | collective-permute-done | bytes 655392 | tf_op jit(solution)/shard_map/ppermute | solution.py:399
  47.4 1.3 %collective-permute-done.5.refs_8_ = bf16[2,160,1024]{2,1,0:T(8,128)(2,1)S(1)} collective-permute-done((bf16[2,160,1024]{2,1,0:T(8,128)(2,1)}, bf16[2,160,1024]{2,1,0:T(8,128)(2,1)S(1)}, u32[]{:S(2)}, u32[]{:S(2)}) %collective-permute-start.5) | collective-permute-done | bytes 655392 | tf_op jit(solution)/shard_map/ppermute | solution.py:399
  49.2 4.8 %pool_other.1.refs_6_ = f32[2,2,4,160,256]{4,3,2,1,0:T(8,128)S(1)} custom-call(s32[4,16,128]{2,1,0:T(8,128)S(1)} %get-tuple-element.58.refs_0_, s32[4,8,16,128]{3,2,1,0:T(8,128)S(1)} %get-tuple-element.37.refs_1_, f32[4,8,4,4,16,128]{5,4,3,2,1,0:T(8,128)S(1)} %bitcast.31, f32[4,8,4,4,16,128]{5,4,3,2,1,0:T(8,128)S(1)} %bitcast.32, ...), custom_call_target="tpu_custom_call" | custom-call | flops 4294967296 | bytes 5000000 | tf_op jit(solution)/shard_map/pool_other/pallas_call | solution.py:280
  54.1 5.1 %pool_beyond.1 = (bf16[4,2,160,128]{3,2,1,0:T(8,128)(2,1)S(1)}, bf16[4,2,160,128]{3,2,1,0:T(8,128)(2,1)S(1)}, bf16[4,2,160,128]{3,2,1,0:T(8,128)(2,1)S(1)}, bf16[4,2,160,128]{3,2,1,0:T(8,128)(2,1)S(1)}) custom-call(s32[4,16,128]{2,1,0:T(8,128)S(1)} %get-tuple-element.58.refs_0_, s32[4,8,16,128]{3,2,1,0:T(8,128)S(1)} %get-tuple-element.37.refs_1_, ...), custom_call_target="tpu_custom_call" | custom-call | flops 4294967296 | bytes 5000000 | tf_op jit(solution)/shard_map/pool_beyond/pallas_call | solution.py:280
  59.3 2.5 %collective-permute-start.12 = (bf16[4,2,160,128]{3,2,1,0:T(8,128)(2,1)S(1)}, bf16[4,2,160,128]{3,2,1,0:T(8,128)(2,1)S(1)}, u32[]{:S(2)}, u32[]{:S(2)}) collective-permute-start(bf16[4,2,160,128]{3,2,1,0:T(8,128)(2,1)S(1)} %get-tuple-element.56), channel_id=1, source_target_pairs={{0,4},{2,6},{4,0},{6,2},{1,5},{3,7},{5,1},{7,3},{8,12},{10,14},{12... | collective-permute-start | bytes 983048 | tf_op jit(solution)/shard_map/ppermute | solution.py:399
  62.5 8.5 %pool_rest.1 = bf16[16,2,160,128]{3,2,1,0:T(8,128)(2,1)} custom-call(s32[4,16,128]{2,1,0:T(8,128)S(1)} %get-tuple-element.58.refs_0_, s32[4,8,16,128]{3,2,1,0:T(8,128)S(1)} %get-tuple-element.37.refs_1_, f32[4,8,4,4,16,128]{5,4,3,2,1,0:T(8,128)S(1)} %bitcast.35, f32[4,8,4,4,16,128]{5,4,3,2,1,0:T(8,128)S(1)} %bitcast.36, ...), custom_call_target="tpu_custom_call" | custom-call | flops 8589934592 | bytes 5000000 | tf_op jit(solution)/shard_map/pool_rest/pallas_call | solution.py:280
  71.0 6.6 %collective-permute-done.11 = bf16[4,2,160,128]{3,2,1,0:T(8,128)(2,1)S(1)} collective-permute-done((bf16[4,2,160,128]{3,2,1,0:T(8,128)(2,1)S(1)}, bf16[4,2,160,128]{3,2,1,0:T(8,128)(2,1)S(1)}, u32[]{:S(2)}, u32[]{:S(2)}) %collective-permute-start.11) | collective-permute-done | bytes 327712 | tf_op jit(solution)/shard_map/ppermute | solution.py:399
  78.4 6.2 %all-to-all-start = ((bf16[16,2,160,128]{3,2,1,0:T(8,128)(2,1)}), bf16[16,2,160,128]{3,2,1,0:T(8,128)(2,1)S(1)}, u32[]{:S(2)}, u32[]{:S(2)}) async-start(bf16[16,2,160,128]{3,2,1,0:T(8,128)(2,1)} %pool_rest.1), calls=%async_computation | async-start | bytes 2621440 | tf_op jit(solution)/shard_map/all_to_all | solution.py:472
  85.7 2.0 %collective-permute-start.16 = (bf16[2,160,128]{2,1,0:T(8,128)(2,1)S(1)}, bf16[2,160,128]{2,1,0:T(8,128)(2,1)S(1)}, u32[]{:S(2)}, u32[]{:S(2)}) collective-permute-start(bf16[2,160,128]{2,1,0:T(8,128)(2,1)S(1)} %get-tuple-element.71), channel_id=1, source_target_pairs={{0,32},{32,64},{64,96},{96,0},{1,33},{33,65},{65,97},{97,1},{2,34}... | collective-permute-start | bytes 245768 | tf_op jit(solution)/shard_map/ppermute | solution.py:399
  87.7 2.7 %collective-permute-start.17 = (bf16[2,160,128]{2,1,0:T(8,128)(2,1)S(1)}, bf16[2,160,128]{2,1,0:T(8,128)(2,1)S(1)}, u32[]{:S(2)}, u32[]{:S(2)}) collective-permute-start(bf16[2,160,128]{2,1,0:T(8,128)(2,1)S(1)} %get-tuple-element.70), channel_id=1, source_target_pairs={{0,64},{32,96},{64,0},{96,32},{1,65},{33,97},{65,1},{97,33},{2,66}... | collective-permute-start | bytes 245768 | tf_op jit(solution)/shard_map/ppermute | solution.py:399
  90.4 1.5 %collective-permute-start.18 = (bf16[2,160,128]{2,1,0:T(8,128)(2,1)S(1)}, bf16[2,160,128]{2,1,0:T(8,128)(2,1)S(1)}, u32[]{:S(2)}, u32[]{:S(2)}) collective-permute-start(bf16[2,160,128]{2,1,0:T(8,128)(2,1)S(1)} %get-tuple-element.69), channel_id=1, source_target_pairs={{0,96},{32,0},{64,32},{96,64},{1,97},{33,1},{65,33},{97,65},{2,98}... | collective-permute-start | bytes 245768 | tf_op jit(solution)/shard_map/ppermute | solution.py:399
  91.9 13.0 %collective-permute-done.16.rest_1_ = bf16[2,160,128]{2,1,0:T(8,128)(2,1)S(1)} collective-permute-done((bf16[2,160,128]{2,1,0:T(8,128)(2,1)S(1)}, bf16[2,160,128]{2,1,0:T(8,128)(2,1)S(1)}, u32[]{:S(2)}, u32[]{:S(2)}) %collective-permute-start.16) | collective-permute-done | bytes 81952 | tf_op jit(solution)/shard_map/ppermute | solution.py:399
  106.2 1.7 %copy-done = bf16[1024,1280]{1,0:T(8,128)(2,1)S(1)} copy-done((bf16[1024,1280]{1,0:T(8,128)(2,1)S(1)}, bf16[1024,1280]{1,0:T(8,128)(2,1)}, u32[]{:S(2)}) %copy-start) | copy-done | bytes 2621464
  108.0 4.5 %tail.1 = bf16[16,160,128]{2,1,0:T(8,128)(2,1)} custom-call(s32[1]{0:T(128)} %bitcast.host_ref, s32[16]{0:T(128)S(1)} %copy-done.9, bf16[4,2,160,128]{3,2,1,0:T(8,128)(2,1)S(1)} %add_convert_fusion.rest_0_, bf16[2,160,128]{2,1,0:T(8,128)(2,1)S(1)} %collective-permute-done.16.rest_1_, bf16[2,160,128]{2,1,0:T(8,128)(2,1)S(1)} %collective-permute-done.17.rest_2_, ...), custom_call_target="tpu_custom_call" | custom-call | flops 1000000000 | bytes 8000000 | tf_op jit(solution)/shard_map/tail/pallas_call | solution.py:378
  (48 shorter events, 6.1 us)
Async XLA Ops:
  0.0 30.1 %collective-permute-start.9 = (bf16[4,160,1024]{2,1,0:T(8,128)(2,1)}, bf16[4,160,1024]{2,1,0:T(8,128)(2,1)}, u32[]{:S(2)}, u32[]{:S(2)}) collective-permute-start(bf16[4,160,1024]{2,1,0:T(8,128)(2,1)} %bitcast.18), channel_id=1, source_target_pairs={{0,1},{1,0},{2,3},{3,2},{4,5},{5,4},{6,7},{7,6},{8,9},{9,8},{10,11... | collective-permute-start | bytes 3932168 | tf_op jit(solution)/shard_map/ppermute | solution.py:399
  2.6 21.4 %collective-permute-start = (bf16[2,160,1024]{2,1,0:T(8,128)(2,1)}, bf16[2,160,1024]{2,1,0:T(8,128)(2,1)}, u32[]{:S(2)}, u32[]{:S(2)}) collective-permute-start(bf16[2,160,1024]{2,1,0:T(8,128)(2,1)} %get-tuple-element.43), channel_id=1, source_target_pairs={{0,24},{8,0},{16,8},{24,16},{1,25},{9,1},{17,9},{25,17},{2,26},{10... | collective-permute-start | bytes 1966088 | tf_op jit(solution)/shard_map/ppermute | solution.py:399
  6.7 18.6 %collective-permute-start.1 = (bf16[2,160,1024]{2,1,0:T(8,128)(2,1)}, bf16[2,160,1024]{2,1,0:T(8,128)(2,1)}, u32[]{:S(2)}, u32[]{:S(2)}) collective-permute-start(bf16[2,160,1024]{2,1,0:T(8,128)(2,1)} %get-tuple-element.43), channel_id=1, source_target_pairs={{0,8},{8,16},{16,24},{24,0},{1,9},{9,17},{17,25},{25,1},{2,10},{10... | collective-permute-start | bytes 1966088 | tf_op jit(solution)/shard_map/ppermute | solution.py:399
  6.7 18.6 %collective-permute-start.2 = (bf16[2,160,1024]{2,1,0:T(8,128)(2,1)}, bf16[2,160,1024]{2,1,0:T(8,128)(2,1)}, u32[]{:S(2)}, u32[]{:S(2)}) collective-permute-start(bf16[2,160,1024]{2,1,0:T(8,128)(2,1)} %get-tuple-element.44), channel_id=1, source_target_pairs={{0,6},{2,0},{4,2},{6,4},{1,7},{3,1},{5,3},{7,5},{8,14},{10,8},{12,... | collective-permute-start | bytes 1966088 | tf_op jit(solution)/shard_map/ppermute | solution.py:399
  9.7 18.3 %collective-permute-start.3 = (bf16[2,160,1024]{2,1,0:T(8,128)(2,1)}, bf16[2,160,1024]{2,1,0:T(8,128)(2,1)}, u32[]{:S(2)}, u32[]{:S(2)}) collective-permute-start(bf16[2,160,1024]{2,1,0:T(8,128)(2,1)} %get-tuple-element.44), channel_id=1, source_target_pairs={{0,2},{2,4},{4,6},{6,0},{1,3},{3,5},{5,7},{7,1},{8,10},{10,12},{12... | collective-permute-start | bytes 1966088 | tf_op jit(solution)/shard_map/ppermute | solution.py:399
  28.0 14.8 %collective-permute-start.6 = (bf16[2,160,1024]{2,1,0:T(8,128)(2,1)}, bf16[2,160,1024]{2,1,0:T(8,128)(2,1)S(1)}, u32[]{:S(2)}, u32[]{:S(2)}) collective-permute-start(bf16[2,160,1024]{2,1,0:T(8,128)(2,1)} %collective-permute-done.refs_6_), channel_id=1, source_target_pairs={{0,1},{1,0},{2,3},{3,2},{4,5},{5,4},{6,7},{7,6},{8,9},{9,8},{10,11... | collective-permute-start | bytes 1966088 | tf_op jit(solution)/shard_map/ppermute | solution.py:399
  28.1 14.8 %collective-permute-start.7 = (bf16[2,160,1024]{2,1,0:T(8,128)(2,1)}, bf16[2,160,1024]{2,1,0:T(8,128)(2,1)S(1)}, u32[]{:S(2)}, u32[]{:S(2)}) collective-permute-start(bf16[2,160,1024]{2,1,0:T(8,128)(2,1)} %collective-permute-done.1.refs_7_), channel_id=1, source_target_pairs={{0,1},{1,0},{2,3},{3,2},{4,5},{5,4},{6,7},{7,6},{8,9},{9,8},{10,11... | collective-permute-start | bytes 1966088 | tf_op jit(solution)/shard_map/ppermute | solution.py:399
  28.6 14.3 %collective-permute-start.8 = (bf16[2,160,1024]{2,1,0:T(8,128)(2,1)}, bf16[2,160,1024]{2,1,0:T(8,128)(2,1)S(1)}, u32[]{:S(2)}, u32[]{:S(2)}) collective-permute-start(bf16[2,160,1024]{2,1,0:T(8,128)(2,1)} %collective-permute-done.2.refs_6_), channel_id=1, source_target_pairs={{0,1},{1,0},{2,3},{3,2},{4,5},{5,4},{6,7},{7,6},{8,9},{9,8},{10,11... | collective-permute-start | bytes 1966088 | tf_op jit(solution)/shard_map/ppermute | solution.py:399
  28.6 18.9 %collective-permute-start.4 = (bf16[2,160,1024]{2,1,0:T(8,128)(2,1)}, bf16[2,160,1024]{2,1,0:T(8,128)(2,1)S(1)}, u32[]{:S(2)}, u32[]{:S(2)}) collective-permute-start(bf16[2,160,1024]{2,1,0:T(8,128)(2,1)} %get-tuple-element.43), channel_id=1, source_target_pairs={{0,16},{8,24},{16,0},{24,8},{1,17},{9,25},{17,1},{25,9},{2,18},{10... | collective-permute-start | bytes 1966088 | tf_op jit(solution)/shard_map/ppermute | solution.py:399
  30.1 18.6 %collective-permute-start.5 = (bf16[2,160,1024]{2,1,0:T(8,128)(2,1)}, bf16[2,160,1024]{2,1,0:T(8,128)(2,1)S(1)}, u32[]{:S(2)}, u32[]{:S(2)}) collective-permute-start(bf16[2,160,1024]{2,1,0:T(8,128)(2,1)} %get-tuple-element.44), channel_id=1, source_target_pairs={{0,4},{2,6},{4,0},{6,2},{1,5},{3,7},{5,1},{7,3},{8,12},{10,14},{12... | collective-permute-start | bytes 1966088 | tf_op jit(solution)/shard_map/ppermute | solution.py:399
  48.7 5.3 %collective-permute-start.10 = (bf16[2,160,1024]{2,1,0:T(8,128)(2,1)S(1)}, bf16[2,160,1024]{2,1,0:T(8,128)(2,1)S(1)}, u32[]{:S(2)}, u32[]{:S(2)}) collective-permute-start(bf16[2,160,1024]{2,1,0:T(8,128)(2,1)S(1)} %collective-permute-done.4.refs_4_), channel_id=1, source_target_pairs={{0,1},{1,0},{2,3},{3,2},{4,5},{5,4},{6,7},{7,6},{8,9},{9,8},{10,11... | collective-permute-start | bytes 1966088 | tf_op jit(solution)/shard_map/ppermute | solution.py:399
  48.7 13.8 %collective-permute-start.14 = (bf16[2,160,1024]{2,1,0:T(8,128)(2,1)}, bf16[2,160,1024]{2,1,0:T(8,128)(2,1)S(1)}, u32[]{:S(2)}, u32[]{:S(2)}) collective-permute-start(bf16[2,160,1024]{2,1,0:T(8,128)(2,1)} %collective-permute-done.3.refs_7_), channel_id=1, source_target_pairs={{0,1},{1,0},{2,3},{3,2},{4,5},{5,4},{6,7},{7,6},{8,9},{9,8},{10,11... | collective-permute-start | bytes 1966088 | tf_op jit(solution)/shard_map/ppermute | solution.py:399
  49.2 13.3 %collective-permute-start.15 = (bf16[2,160,1024]{2,1,0:T(8,128)(2,1)S(1)}, bf16[2,160,1024]{2,1,0:T(8,128)(2,1)S(1)}, u32[]{:S(2)}, u32[]{:S(2)}) collective-permute-start(bf16[2,160,1024]{2,1,0:T(8,128)(2,1)S(1)} %collective-permute-done.5.refs_8_), channel_id=1, source_target_pairs={{0,1},{1,0},{2,3},{3,2},{4,5},{5,4},{6,7},{7,6},{8,9},{9,8},{10,11... | collective-permute-start | bytes 1966088 | tf_op jit(solution)/shard_map/ppermute | solution.py:399
  59.2 18.4 %collective-permute-start.11 = (bf16[4,2,160,128]{3,2,1,0:T(8,128)(2,1)S(1)}, bf16[4,2,160,128]{3,2,1,0:T(8,128)(2,1)S(1)}, u32[]{:S(2)}, u32[]{:S(2)}) collective-permute-start(bf16[4,2,160,128]{3,2,1,0:T(8,128)(2,1)S(1)} %get-tuple-element.55), channel_id=1, source_target_pairs={{0,2},{2,4},{4,6},{6,0},{1,3},{3,5},{5,7},{7,1},{8,10},{10,12},{12... | collective-permute-start | bytes 983048 | tf_op jit(solution)/shard_map/ppermute | solution.py:399
  59.3 18.4 %collective-permute-start.12 = (bf16[4,2,160,128]{3,2,1,0:T(8,128)(2,1)S(1)}, bf16[4,2,160,128]{3,2,1,0:T(8,128)(2,1)S(1)}, u32[]{:S(2)}, u32[]{:S(2)}) collective-permute-start(bf16[4,2,160,128]{3,2,1,0:T(8,128)(2,1)S(1)} %get-tuple-element.56), channel_id=1, source_target_pairs={{0,4},{2,6},{4,0},{6,2},{1,5},{3,7},{5,1},{7,3},{8,12},{10,14},{12... | collective-permute-start | bytes 983048 | tf_op jit(solution)/shard_map/ppermute | solution.py:399
  61.8 16.6 %collective-permute-start.13 = (bf16[4,2,160,128]{3,2,1,0:T(8,128)(2,1)S(1)}, bf16[4,2,160,128]{3,2,1,0:T(8,128)(2,1)}, u32[]{:S(2)}, u32[]{:S(2)}) collective-permute-start(bf16[4,2,160,128]{3,2,1,0:T(8,128)(2,1)S(1)} %get-tuple-element.57), channel_id=1, source_target_pairs={{0,6},{2,0},{4,2},{6,4},{1,7},{3,1},{5,3},{7,5},{8,14},{10,8},{12,... | collective-permute-start | bytes 983048 | tf_op jit(solution)/shard_map/ppermute | solution.py:399
  71.0 35.2 %copy-start.6 = (bf16[24,16]{0,1:T(8,128)(2,1)S(1)}, bf16[24,16]{0,1:T(8,128)(2,1)}, u32[]{:S(2)}) copy-start(bf16[24,16]{0,1:T(8,128)(2,1)} %param.14) | copy-start | bytes 2308
  71.0 35.2 %copy-start.7 = (f32[384]{0:T(512)S(1)}, f32[384]{0:T(512)}, u32[]{:S(2)}) copy-start(f32[384]{0:T(512)} %param.15) | copy-start | bytes 4612
  71.0 35.2 %copy-start.8 = (bf16[8,16]{1,0:T(8,128)(2,1)S(1)}, bf16[8,16]{1,0:T(8,128)(2,1)}, u32[]{:S(2)}) copy-start(bf16[8,16]{1,0:T(8,128)(2,1)} %rest_9_.1) | copy-start | bytes 772
  71.0 35.2 %copy-start.9 = (s32[16]{0:T(128)S(1)}, s32[16]{0:T(128)}, u32[]{:S(2)}) copy-start(s32[16]{0:T(128)} %order_ref.1) | copy-start | bytes 196
  78.4 27.8 %all-to-all-start = ((bf16[16,2,160,128]{3,2,1,0:T(8,128)(2,1)}), bf16[16,2,160,128]{3,2,1,0:T(8,128)(2,1)S(1)}, u32[]{:S(2)}, u32[]{:S(2)}) async-start(bf16[16,2,160,128]{3,2,1,0:T(8,128)(2,1)} %pool_rest.1), calls=%async_computation | async-start | bytes 2621440 | tf_op jit(solution)/shard_map/all_to_all | solution.py:472
  85.7 19.1 %collective-permute-start.16 = (bf16[2,160,128]{2,1,0:T(8,128)(2,1)S(1)}, bf16[2,160,128]{2,1,0:T(8,128)(2,1)S(1)}, u32[]{:S(2)}, u32[]{:S(2)}) collective-permute-start(bf16[2,160,128]{2,1,0:T(8,128)(2,1)S(1)} %get-tuple-element.71), channel_id=1, source_target_pairs={{0,32},{32,64},{64,96},{96,0},{1,33},{33,65},{65,97},{97,1},{2,34}... | collective-permute-start | bytes 245768 | tf_op jit(solution)/shard_map/ppermute | solution.py:399
  87.7 18.5 %collective-permute-start.17 = (bf16[2,160,128]{2,1,0:T(8,128)(2,1)S(1)}, bf16[2,160,128]{2,1,0:T(8,128)(2,1)S(1)}, u32[]{:S(2)}, u32[]{:S(2)}) collective-permute-start(bf16[2,160,128]{2,1,0:T(8,128)(2,1)S(1)} %get-tuple-element.70), channel_id=1, source_target_pairs={{0,64},{32,96},{64,0},{96,32},{1,65},{33,97},{65,1},{97,33},{2,66}... | collective-permute-start | bytes 245768 | tf_op jit(solution)/shard_map/ppermute | solution.py:399
  90.4 15.8 %collective-permute-start.18 = (bf16[2,160,128]{2,1,0:T(8,128)(2,1)S(1)}, bf16[2,160,128]{2,1,0:T(8,128)(2,1)S(1)}, u32[]{:S(2)}, u32[]{:S(2)}) collective-permute-start(bf16[2,160,128]{2,1,0:T(8,128)(2,1)S(1)} %get-tuple-element.69), channel_id=1, source_target_pairs={{0,96},{32,0},{64,32},{96,64},{1,97},{33,1},{65,33},{97,65},{2,98}... | collective-permute-start | bytes 245768 | tf_op jit(solution)/shard_map/ppermute | solution.py:399
  (6 other events, 101.1 us)

commit v10 on v9

--- a/solution.py
+++ b/solution.py
@@ -447,6 +447,7 @@
     sums = stage((0, 1, 2, 3), [flipped], 0, None, 0, "pool_own")
     sums, sides, mine, masks = lax.optimization_barrier((sums, sides, mine, masks))
     beyond = [move(mine[p], axes[p], 2) for p in range(2)]
+    sides, own_far = lax.optimization_barrier((sides, own_far))
     early = [other_core(x) for x in (sides[0][0], sides[0][1], sides[1][0])]
     middle = []
     for p in range(2):

time: 113 us -> 110 us (0.973)
  waiting for transfers between devices: 31.6 us -> 28.3 us
    ppermute x19, waiting for transfers between devices: 31.6 us -> 28.2 us  [move(): return lax.ppermute(x, axis, [(i, (i + step) % size) for i in range(size)])]
  transfers between devices with their start and end apart: 20 -> 20, of which waited for: 8 -> 9; matrix products, arithmetic and copies ran while one was open for 3% -> 3% of each run, Pallas kernels for 39% -> 41%
where the time goes in v10:
time: 110 us
  Pallas kernels  49.2 us (45%)
  waiting for transfers between devices  28.3 us (26%)
  starting transfers between devices  25.6 us (23%)
  local copies, waits for them, and re-layouts  5.33 us (5%)
  other arithmetic  1.22 us (1%)
    pallas_call x6, Pallas kernels, pool(): pl.pallas_call(functools.partial(pool_kernel, tuple(layout), base is not...  37.3 us
    ppermute x19, waiting for transfers between devices, move(): return lax.ppermute(x, axis, [(i, (i + step) % size) for i in range(size)])  28.2 us
    ppermute x19, starting transfers between devices, move(): return lax.ppermute(x, axis, [(i, (i + step) % size) for i in range(size)])  19.5 us
    pallas_call x1, Pallas kernels, prep(): pl.pallas_call(prep_kernel, grid=(tables,), in_specs=[pl.BlockSpec(memory...  7.41 us
    all_to_all x1, starting transfers between devices, on_device(): parts.append(lax.all_to_all(blocks, ('hst', axes[0]), 0, 0, tiled=True))  6.11 us
    pallas_call x1, Pallas kernels, tail(): pl.pallas_call(tail_kernel, grid=(1,), in_specs=[smem] * 2 + [mine] + [th...  4.53 us
    unnamed x20, local copies, waits for them, and re-layouts  2.72 us
    slice x1, local copies, waits for them, and re-layouts, on_device(): mine = [flipped[2 * p:2 * p + 2] for p in range(2)]  2.59 us
  transfers between devices with their start and end apart: 20, of which 9 were waited for; matrix products, arithmetic and copies ran while one was open for 3% of the time, Pallas kernels for 41%

profile of v10, /device:TPU:0, one launch (start us, length us, event | category | flops | bytes accessed | tf_op | source)
XLA Modules:
  0.0 109.8 jit_solution(14352571703546903698)
XLA Ops:
  0.0 2.6 %fusion = (bf16[2,160,1024]{2,1,0:T(8,128)(2,1)}, bf16[2,160,1024]{2,1,0:T(8,128)(2,1)}) fusion(bf16[4,160,1024]{2,1,0:T(8,128)(2,1)} %bitcast.19), kind=kLoop, calls=%fused_computation.5 | loop fusion | bytes 2621440 | tf_op jit(solution)/shard_map/slice | solution.py:438
  2.6 4.1 %collective-permute-start = (bf16[2,160,1024]{2,1,0:T(8,128)(2,1)}, bf16[2,160,1024]{2,1,0:T(8,128)(2,1)}, u32[]{:S(2)}, u32[]{:S(2)}) collective-permute-start(bf16[2,160,1024]{2,1,0:T(8,128)(2,1)} %get-tuple-element.52), channel_id=1, source_target_pairs={{0,24},{8,0},{16,8},{24,16},{1,25},{9,1},{17,9},{25,17},{2,26},{10... | collective-permute-start | bytes 1966088 | tf_op jit(solution)/shard_map/ppermute | solution.py:399
  6.7 3.0 %collective-permute-start.2 = (bf16[2,160,1024]{2,1,0:T(8,128)(2,1)}, bf16[2,160,1024]{2,1,0:T(8,128)(2,1)}, u32[]{:S(2)}, u32[]{:S(2)}) collective-permute-start(bf16[2,160,1024]{2,1,0:T(8,128)(2,1)} %get-tuple-element.53), channel_id=1, source_target_pairs={{0,6},{2,0},{4,2},{6,4},{1,7},{3,1},{5,3},{7,5},{8,14},{10,8},{12,... | collective-permute-start | bytes 1966088 | tf_op jit(solution)/shard_map/ppermute | solution.py:399
  10.8 7.4 %prep.1 = (f32[4,32,4,16,128]{4,3,2,1,0:T(8,128)S(1)}, s32[4,8,16,128]{3,2,1,0:T(8,128)S(1)}, s32[4,16,128]{2,1,0:T(8,128)S(1)}) custom-call(s32[4]{0:T(128)S(1)} %pad_add_fusion.pos_ref, s32[4,8,16384]{2,1,0:T(8,128)S(1)} %bitcast.17, s32[4,16384]{1,0:T(4,128)S(1)} %bitcast.21), custom_call_target="tpu_custom_call" | custom-call | flops 40000000 | bytes 9000000 | tf_op jit(solution)/shard_map/prep/pallas_call | solution.py:86
  18.2 5.8 %pool_own.1.refs_8_ = f32[4,2,4,160,256]{4,3,2,1,0:T(8,128)S(1)} custom-call(s32[4,16,128]{2,1,0:T(8,128)S(1)} %get-tuple-element.68.refs_0_, s32[4,8,16,128]{3,2,1,0:T(8,128)S(1)} %get-tuple-element.42.refs_1_, f32[4,8,4,4,16,128]{5,4,3,2,1,0:T(8,128)S(1)} %bitcast.24, bf16[4,160,1024]{2,1,0:T(8,128)(2,1)S(1)} %bitcast.20), custom_call_target="tpu_custom_call" | custom-call | flops 4294967296 | bytes 5000000 | tf_op jit(solution)/shard_map/pool_own/pallas_call | solution.py:280
  24.0 1.3 %collective-permute-done.1.refs_7_ = bf16[2,160,1024]{2,1,0:T(8,128)(2,1)} collective-permute-done((bf16[2,160,1024]{2,1,0:T(8,128)(2,1)}, bf16[2,160,1024]{2,1,0:T(8,128)(2,1)}, u32[]{:S(2)}, u32[]{:S(2)}) %collective-permute-start.1) | collective-permute-done | bytes 655392 | tf_op jit(solution)/shard_map/ppermute | solution.py:399
  25.3 2.7 %collective-permute-done.3.refs_7_ = bf16[2,160,1024]{2,1,0:T(8,128)(2,1)} collective-permute-done((bf16[2,160,1024]{2,1,0:T(8,128)(2,1)}, bf16[2,160,1024]{2,1,0:T(8,128)(2,1)}, u32[]{:S(2)}, u32[]{:S(2)}) %collective-permute-start.3) | collective-permute-done | bytes 655392 | tf_op jit(solution)/shard_map/ppermute | solution.py:399
  28.1 1.6 %collective-permute-start.5 = (bf16[2,160,1024]{2,1,0:T(8,128)(2,1)}, bf16[2,160,1024]{2,1,0:T(8,128)(2,1)S(1)}, u32[]{:S(2)}, u32[]{:S(2)}) collective-permute-start(bf16[2,160,1024]{2,1,0:T(8,128)(2,1)} %get-tuple-element.52), channel_id=1, source_target_pairs={{0,16},{8,24},{16,0},{24,8},{1,17},{9,25},{17,1},{25,9},{2,18},{10... | collective-permute-start | bytes 1966088 | tf_op jit(solution)/shard_map/ppermute | solution.py:399
  30.2 6.3 %pool_sides.2.refs_6_ = f32[2,2,4,160,256]{4,3,2,1,0:T(8,128)S(1)} custom-call(s32[4,16,128]{2,1,0:T(8,128)S(1)} %get-tuple-element.68.refs_0_, s32[4,8,16,128]{3,2,1,0:T(8,128)S(1)} %get-tuple-element.42.refs_1_, f32[4,8,4,4,16,128]{5,4,3,2,1,0:T(8,128)S(1)} %bitcast.25, f32[4,8,4,4,16,128]{5,4,3,2,1,0:T(8,128)S(1)} %bitcast.26, ...), custom_call_target="tpu_custom_call" | custom-call | flops 6442450944 | bytes 5000000 | tf_op jit(solution)/shard_map/pool_sides/pallas_call | solution.py:280
  36.5 6.9 %pool_sides.3.refs_10_ = f32[2,2,4,160,256]{4,3,2,1,0:T(8,128)S(1)} custom-call(s32[4,16,128]{2,1,0:T(8,128)S(1)} %get-tuple-element.68.refs_0_, s32[4,8,16,128]{3,2,1,0:T(8,128)S(1)} %get-tuple-element.42.refs_1_, f32[4,8,4,4,16,128]{5,4,3,2,1,0:T(8,128)S(1)} %bitcast.28, f32[4,8,4,4,16,128]{5,4,3,2,1,0:T(8,128)S(1)} %bitcast.29, ...), custom_call_target="tpu_custom_call" | custom-call | flops 6442450944 | bytes 5000000 | tf_op jit(solution)/shard_map/pool_sides/pallas_call | solution.py:280
  43.4 2.3 %collective-permute-done.5.refs_4_ = bf16[2,160,1024]{2,1,0:T(8,128)(2,1)S(1)} collective-permute-done((bf16[2,160,1024]{2,1,0:T(8,128)(2,1)}, bf16[2,160,1024]{2,1,0:T(8,128)(2,1)S(1)}, u32[]{:S(2)}, u32[]{:S(2)}) %collective-permute-start.5) | collective-permute-done | bytes 655392 | tf_op jit(solution)/shard_map/ppermute | solution.py:399
  47.4 4.8 %pool_other.1.refs_6_ = f32[2,2,4,160,256]{4,3,2,1,0:T(8,128)S(1)} custom-call(s32[4,16,128]{2,1,0:T(8,128)S(1)} %get-tuple-element.68.refs_0_, s32[4,8,16,128]{3,2,1,0:T(8,128)S(1)} %get-tuple-element.42.refs_1_, f32[4,8,4,4,16,128]{5,4,3,2,1,0:T(8,128)S(1)} %bitcast.31, f32[4,8,4,4,16,128]{5,4,3,2,1,0:T(8,128)S(1)} %bitcast.32, ...), custom_call_target="tpu_custom_call" | custom-call | flops 4294967296 | bytes 5000000 | tf_op jit(solution)/shard_map/pool_other/pallas_call | solution.py:280
  52.2 5.1 %pool_beyond.1 = (bf16[4,2,160,128]{3,2,1,0:T(8,128)(2,1)S(1)}, bf16[4,2,160,128]{3,2,1,0:T(8,128)(2,1)S(1)}, bf16[4,2,160,128]{3,2,1,0:T(8,128)(2,1)S(1)}, bf16[4,2,160,128]{3,2,1,0:T(8,128)(2,1)S(1)}) custom-call(s32[4,16,128]{2,1,0:T(8,128)S(1)} %get-tuple-element.68.refs_0_, s32[4,8,16,128]{3,2,1,0:T(8,128)S(1)} %get-tuple-element.42.refs_1_, ...), custom_call_target="tpu_custom_call" | custom-call | flops 4294967296 | bytes 5000000 | tf_op jit(solution)/shard_map/pool_beyond/pallas_call | solution.py:280
  57.4 2.9 %collective-permute-start.12 = (bf16[4,2,160,128]{3,2,1,0:T(8,128)(2,1)S(1)}, bf16[4,2,160,128]{3,2,1,0:T(8,128)(2,1)S(1)}, u32[]{:S(2)}, u32[]{:S(2)}) collective-permute-start(bf16[4,2,160,128]{3,2,1,0:T(8,128)(2,1)S(1)} %get-tuple-element.66), channel_id=1, source_target_pairs={{0,4},{2,6},{4,0},{6,2},{1,5},{3,7},{5,1},{7,3},{8,12},{10,14},{12... | collective-permute-start | bytes 983048 | tf_op jit(solution)/shard_map/ppermute | solution.py:399
  60.7 8.5 %pool_rest.1 = bf16[16,2,160,128]{3,2,1,0:T(8,128)(2,1)} custom-call(s32[4,16,128]{2,1,0:T(8,128)S(1)} %get-tuple-element.68.refs_0_, s32[4,8,16,128]{3,2,1,0:T(8,128)S(1)} %get-tuple-element.42.refs_1_, f32[4,8,4,4,16,128]{5,4,3,2,1,0:T(8,128)S(1)} %bitcast.35, f32[4,8,4,4,16,128]{5,4,3,2,1,0:T(8,128)S(1)} %bitcast.36, ...), custom_call_target="tpu_custom_call" | custom-call | flops 8589934592 | bytes 5000000 | tf_op jit(solution)/shard_map/pool_rest/pallas_call | solution.py:280
  69.2 6.5 %collective-permute-done.11 = bf16[4,2,160,128]{3,2,1,0:T(8,128)(2,1)S(1)} collective-permute-done((bf16[4,2,160,128]{3,2,1,0:T(8,128)(2,1)S(1)}, bf16[4,2,160,128]{3,2,1,0:T(8,128)(2,1)S(1)}, u32[]{:S(2)}, u32[]{:S(2)}) %collective-permute-start.11) | collective-permute-done | bytes 327712 | tf_op jit(solution)/shard_map/ppermute | solution.py:399
  76.4 6.1 %all-to-all-start = ((bf16[16,2,160,128]{3,2,1,0:T(8,128)(2,1)}), bf16[16,2,160,128]{3,2,1,0:T(8,128)(2,1)S(1)}, u32[]{:S(2)}, u32[]{:S(2)}) async-start(bf16[16,2,160,128]{3,2,1,0:T(8,128)(2,1)} %pool_rest.1), calls=%async_computation | async-start | bytes 2621440 | tf_op jit(solution)/shard_map/all_to_all | solution.py:473
  83.7 2.0 %collective-permute-start.16 = (bf16[2,160,128]{2,1,0:T(8,128)(2,1)S(1)}, bf16[2,160,128]{2,1,0:T(8,128)(2,1)S(1)}, u32[]{:S(2)}, u32[]{:S(2)}) collective-permute-start(bf16[2,160,128]{2,1,0:T(8,128)(2,1)S(1)} %get-tuple-element.81), channel_id=1, source_target_pairs={{0,32},{32,64},{64,96},{96,0},{1,33},{33,65},{65,97},{97,1},{2,34}... | collective-permute-start | bytes 245768 | tf_op jit(solution)/shard_map/ppermute | solution.py:399
  85.7 2.7 %collective-permute-start.17 = (bf16[2,160,128]{2,1,0:T(8,128)(2,1)S(1)}, bf16[2,160,128]{2,1,0:T(8,128)(2,1)S(1)}, u32[]{:S(2)}, u32[]{:S(2)}) collective-permute-start(bf16[2,160,128]{2,1,0:T(8,128)(2,1)S(1)} %get-tuple-element.80), channel_id=1, source_target_pairs={{0,64},{32,96},{64,0},{96,32},{1,65},{33,97},{65,1},{97,33},{2,66}... | collective-permute-start | bytes 245768 | tf_op jit(solution)/shard_map/ppermute | solution.py:399
  88.4 1.5 %collective-permute-start.18 = (bf16[2,160,128]{2,1,0:T(8,128)(2,1)S(1)}, bf16[2,160,128]{2,1,0:T(8,128)(2,1)S(1)}, u32[]{:S(2)}, u32[]{:S(2)}) collective-permute-start(bf16[2,160,128]{2,1,0:T(8,128)(2,1)S(1)} %get-tuple-element.79), channel_id=1, source_target_pairs={{0,96},{32,0},{64,32},{96,64},{1,97},{33,1},{65,33},{97,65},{2,98}... | collective-permute-start | bytes 245768 | tf_op jit(solution)/shard_map/ppermute | solution.py:399
  89.8 12.4 %collective-permute-done.16.rest_1_ = bf16[2,160,128]{2,1,0:T(8,128)(2,1)S(1)} collective-permute-done((bf16[2,160,128]{2,1,0:T(8,128)(2,1)S(1)}, bf16[2,160,128]{2,1,0:T(8,128)(2,1)S(1)}, u32[]{:S(2)}, u32[]{:S(2)}) %collective-permute-start.16) | collective-permute-done | bytes 81952 | tf_op jit(solution)/shard_map/ppermute | solution.py:399
  102.2 1.2 %collective-permute-done.17.rest_2_ = bf16[2,160,128]{2,1,0:T(8,128)(2,1)S(1)} collective-permute-done((bf16[2,160,128]{2,1,0:T(8,128)(2,1)S(1)}, bf16[2,160,128]{2,1,0:T(8,128)(2,1)S(1)}, u32[]{:S(2)}, u32[]{:S(2)}) %collective-permute-start.17) | collective-permute-done | bytes 81952 | tf_op jit(solution)/shard_map/ppermute | solution.py:399
  103.6 1.7 %copy-done = bf16[1024,1280]{1,0:T(8,128)(2,1)S(1)} copy-done((bf16[1024,1280]{1,0:T(8,128)(2,1)S(1)}, bf16[1024,1280]{1,0:T(8,128)(2,1)}, u32[]{:S(2)}) %copy-start) | copy-done | bytes 2621464
  105.3 4.5 %tail.1 = bf16[16,160,128]{2,1,0:T(8,128)(2,1)} custom-call(s32[1]{0:T(128)} %bitcast.host_ref, s32[16]{0:T(128)S(1)} %copy-done.9, bf16[4,2,160,128]{3,2,1,0:T(8,128)(2,1)S(1)} %add_convert_fusion.rest_0_, bf16[2,160,128]{2,1,0:T(8,128)(2,1)S(1)} %collective-permute-done.16.rest_1_, bf16[2,160,128]{2,1,0:T(8,128)(2,1)S(1)} %collective-permute-done.17.rest_2_, ...), custom_call_target="tpu_custom_call" | custom-call | flops 1000000000 | bytes 8000000 | tf_op jit(solution)/shard_map/tail/pallas_call | solution.py:378
  (48 shorter events, 5.9 us)
Async XLA Ops:
  0.0 29.6 %collective-permute-start.4 = (bf16[4,160,1024]{2,1,0:T(8,128)(2,1)}, bf16[4,160,1024]{2,1,0:T(8,128)(2,1)}, u32[]{:S(2)}, u32[]{:S(2)}) collective-permute-start(bf16[4,160,1024]{2,1,0:T(8,128)(2,1)} %bitcast.18), channel_id=1, source_target_pairs={{0,1},{1,0},{2,3},{3,2},{4,5},{5,4},{6,7},{7,6},{8,9},{9,8},{10,11... | collective-permute-start | bytes 3932168 | tf_op jit(solution)/shard_map/ppermute | solution.py:399
  2.6 21.4 %collective-permute-start = (bf16[2,160,1024]{2,1,0:T(8,128)(2,1)}, bf16[2,160,1024]{2,1,0:T(8,128)(2,1)}, u32[]{:S(2)}, u32[]{:S(2)}) collective-permute-start(bf16[2,160,1024]{2,1,0:T(8,128)(2,1)} %get-tuple-element.52), channel_id=1, source_target_pairs={{0,24},{8,0},{16,8},{24,16},{1,25},{9,1},{17,9},{25,17},{2,26},{10... | collective-permute-start | bytes 1966088 | tf_op jit(solution)/shard_map/ppermute | solution.py:399
  6.7 18.6 %collective-permute-start.1 = (bf16[2,160,1024]{2,1,0:T(8,128)(2,1)}, bf16[2,160,1024]{2,1,0:T(8,128)(2,1)}, u32[]{:S(2)}, u32[]{:S(2)}) collective-permute-start(bf16[2,160,1024]{2,1,0:T(8,128)(2,1)} %get-tuple-element.52), channel_id=1, source_target_pairs={{0,8},{8,16},{16,24},{24,0},{1,9},{9,17},{17,25},{25,1},{2,10},{10... | collective-permute-start | bytes 1966088 | tf_op jit(solution)/shard_map/ppermute | solution.py:399
  6.7 18.6 %collective-permute-start.2 = (bf16[2,160,1024]{2,1,0:T(8,128)(2,1)}, bf16[2,160,1024]{2,1,0:T(8,128)(2,1)}, u32[]{:S(2)}, u32[]{:S(2)}) collective-permute-start(bf16[2,160,1024]{2,1,0:T(8,128)(2,1)} %get-tuple-element.53), channel_id=1, source_target_pairs={{0,6},{2,0},{4,2},{6,4},{1,7},{3,1},{5,3},{7,5},{8,14},{10,8},{12,... | collective-permute-start | bytes 1966088 | tf_op jit(solution)/shard_map/ppermute | solution.py:399
  9.7 18.3 %collective-permute-start.3 = (bf16[2,160,1024]{2,1,0:T(8,128)(2,1)}, bf16[2,160,1024]{2,1,0:T(8,128)(2,1)}, u32[]{:S(2)}, u32[]{:S(2)}) collective-permute-start(bf16[2,160,1024]{2,1,0:T(8,128)(2,1)} %get-tuple-element.53), channel_id=1, source_target_pairs={{0,2},{2,4},{4,6},{6,0},{1,3},{3,5},{5,7},{7,1},{8,10},{10,12},{12... | collective-permute-start | bytes 1966088 | tf_op jit(solution)/shard_map/ppermute | solution.py:399
  28.1 17.7 %collective-permute-start.5 = (bf16[2,160,1024]{2,1,0:T(8,128)(2,1)}, bf16[2,160,1024]{2,1,0:T(8,128)(2,1)S(1)}, u32[]{:S(2)}, u32[]{:S(2)}) collective-permute-start(bf16[2,160,1024]{2,1,0:T(8,128)(2,1)} %get-tuple-element.52), channel_id=1, source_target_pairs={{0,16},{8,24},{16,0},{24,8},{1,17},{9,25},{17,1},{25,9},{2,18},{10... | collective-permute-start | bytes 1966088 | tf_op jit(solution)/shard_map/ppermute | solution.py:399
  29.6 17.1 %collective-permute-start.6 = (bf16[2,160,1024]{2,1,0:T(8,128)(2,1)}, bf16[2,160,1024]{2,1,0:T(8,128)(2,1)S(1)}, u32[]{:S(2)}, u32[]{:S(2)}) collective-permute-start(bf16[2,160,1024]{2,1,0:T(8,128)(2,1)} %get-tuple-element.53), channel_id=1, source_target_pairs={{0,4},{2,6},{4,0},{6,2},{1,5},{3,7},{5,1},{7,3},{8,12},{10,14},{12... | collective-permute-start | bytes 1966088 | tf_op jit(solution)/shard_map/ppermute | solution.py:399
  29.6 17.1 %collective-permute-start.7 = (bf16[2,160,1024]{2,1,0:T(8,128)(2,1)}, bf16[2,160,1024]{2,1,0:T(8,128)(2,1)S(1)}, u32[]{:S(2)}, u32[]{:S(2)}) collective-permute-start(bf16[2,160,1024]{2,1,0:T(8,128)(2,1)} %collective-permute-done.refs_6_), channel_id=1, source_target_pairs={{0,1},{1,0},{2,3},{3,2},{4,5},{5,4},{6,7},{7,6},{8,9},{9,8},{10,11... | collective-permute-start | bytes 1966088 | tf_op jit(solution)/shard_map/ppermute | solution.py:399
  29.7 17.1 %collective-permute-start.8 = (bf16[2,160,1024]{2,1,0:T(8,128)(2,1)}, bf16[2,160,1024]{2,1,0:T(8,128)(2,1)S(1)}, u32[]{:S(2)}, u32[]{:S(2)}) collective-permute-start(bf16[2,160,1024]{2,1,0:T(8,128)(2,1)} %collective-permute-done.1.refs_7_), channel_id=1, source_target_pairs={{0,1},{1,0},{2,3},{3,2},{4,5},{5,4},{6,7},{7,6},{8,9},{9,8},{10,11... | collective-permute-start | bytes 1966088 | tf_op jit(solution)/shard_map/ppermute | solution.py:399
  30.2 16.6 %collective-permute-start.9 = (bf16[2,160,1024]{2,1,0:T(8,128)(2,1)}, bf16[2,160,1024]{2,1,0:T(8,128)(2,1)S(1)}, u32[]{:S(2)}, u32[]{:S(2)}) collective-permute-start(bf16[2,160,1024]{2,1,0:T(8,128)(2,1)} %collective-permute-done.2.refs_6_), channel_id=1, source_target_pairs={{0,1},{1,0},{2,3},{3,2},{4,5},{5,4},{6,7},{7,6},{8,9},{9,8},{10,11... | collective-permute-start | bytes 1966088 | tf_op jit(solution)/shard_map/ppermute | solution.py:399
  46.7 5.5 %collective-permute-start.10 = (bf16[2,160,1024]{2,1,0:T(8,128)(2,1)S(1)}, bf16[2,160,1024]{2,1,0:T(8,128)(2,1)S(1)}, u32[]{:S(2)}, u32[]{:S(2)}) collective-permute-start(bf16[2,160,1024]{2,1,0:T(8,128)(2,1)S(1)} %collective-permute-done.5.refs_4_), channel_id=1, source_target_pairs={{0,1},{1,0},{2,3},{3,2},{4,5},{5,4},{6,7},{7,6},{8,9},{9,8},{10,11... | collective-permute-start | bytes 1966088 | tf_op jit(solution)/shard_map/ppermute | solution.py:399
  46.8 13.8 %collective-permute-start.14 = (bf16[2,160,1024]{2,1,0:T(8,128)(2,1)}, bf16[2,160,1024]{2,1,0:T(8,128)(2,1)S(1)}, u32[]{:S(2)}, u32[]{:S(2)}) collective-permute-start(bf16[2,160,1024]{2,1,0:T(8,128)(2,1)} %collective-permute-done.3.refs_7_), channel_id=1, source_target_pairs={{0,1},{1,0},{2,3},{3,2},{4,5},{5,4},{6,7},{7,6},{8,9},{9,8},{10,11... | collective-permute-start | bytes 1966088 | tf_op jit(solution)/shard_map/ppermute | solution.py:399
  47.3 13.3 %collective-permute-start.15 = (bf16[2,160,1024]{2,1,0:T(8,128)(2,1)S(1)}, bf16[2,160,1024]{2,1,0:T(8,128)(2,1)S(1)}, u32[]{:S(2)}, u32[]{:S(2)}) collective-permute-start(bf16[2,160,1024]{2,1,0:T(8,128)(2,1)S(1)} %collective-permute-done.6.refs_8_), channel_id=1, source_target_pairs={{0,1},{1,0},{2,3},{3,2},{4,5},{5,4},{6,7},{7,6},{8,9},{9,8},{10,11... | collective-permute-start | bytes 1966088 | tf_op jit(solution)/shard_map/ppermute | solution.py:399
  57.3 18.3 %collective-permute-start.11 = (bf16[4,2,160,128]{3,2,1,0:T(8,128)(2,1)S(1)}, bf16[4,2,160,128]{3,2,1,0:T(8,128)(2,1)S(1)}, u32[]{:S(2)}, u32[]{:S(2)}) collective-permute-start(bf16[4,2,160,128]{3,2,1,0:T(8,128)(2,1)S(1)} %get-tuple-element.65), channel_id=1, source_target_pairs={{0,2},{2,4},{4,6},{6,0},{1,3},{3,5},{5,7},{7,1},{8,10},{10,12},{12... | collective-permute-start | bytes 983048 | tf_op jit(solution)/shard_map/ppermute | solution.py:399
  57.4 18.3 %collective-permute-start.12 = (bf16[4,2,160,128]{3,2,1,0:T(8,128)(2,1)S(1)}, bf16[4,2,160,128]{3,2,1,0:T(8,128)(2,1)S(1)}, u32[]{:S(2)}, u32[]{:S(2)}) collective-permute-start(bf16[4,2,160,128]{3,2,1,0:T(8,128)(2,1)S(1)} %get-tuple-element.66), channel_id=1, source_target_pairs={{0,4},{2,6},{4,0},{6,2},{1,5},{3,7},{5,1},{7,3},{8,12},{10,14},{12... | collective-permute-start | bytes 983048 | tf_op jit(solution)/shard_map/ppermute | solution.py:399
  60.3 16.1 %collective-permute-start.13 = (bf16[4,2,160,128]{3,2,1,0:T(8,128)(2,1)S(1)}, bf16[4,2,160,128]{3,2,1,0:T(8,128)(2,1)}, u32[]{:S(2)}, u32[]{:S(2)}) collective-permute-start(bf16[4,2,160,128]{3,2,1,0:T(8,128)(2,1)S(1)} %get-tuple-element.67), channel_id=1, source_target_pairs={{0,6},{2,0},{4,2},{6,4},{1,7},{3,1},{5,3},{7,5},{8,14},{10,8},{12,... | collective-permute-start | bytes 983048 | tf_op jit(solution)/shard_map/ppermute | solution.py:399
  69.1 34.4 %copy-start.6 = (bf16[24,16]{0,1:T(8,128)(2,1)S(1)}, bf16[24,16]{0,1:T(8,128)(2,1)}, u32[]{:S(2)}) copy-start(bf16[24,16]{0,1:T(8,128)(2,1)} %param.14) | copy-start | bytes 2308
  69.1 34.4 %copy-start.7 = (f32[384]{0:T(512)S(1)}, f32[384]{0:T(512)}, u32[]{:S(2)}) copy-start(f32[384]{0:T(512)} %param.15) | copy-start | bytes 4612
  69.1 34.4 %copy-start.8 = (bf16[8,16]{1,0:T(8,128)(2,1)S(1)}, bf16[8,16]{1,0:T(8,128)(2,1)}, u32[]{:S(2)}) copy-start(bf16[8,16]{1,0:T(8,128)(2,1)} %rest_9_.1) | copy-start | bytes 772
  69.1 34.4 %copy-start.9 = (s32[16]{0:T(128)S(1)}, s32[16]{0:T(128)}, u32[]{:S(2)}) copy-start(s32[16]{0:T(128)} %order_ref.1) | copy-start | bytes 196
  76.4 27.1 %all-to-all-start = ((bf16[16,2,160,128]{3,2,1,0:T(8,128)(2,1)}), bf16[16,2,160,128]{3,2,1,0:T(8,128)(2,1)S(1)}, u32[]{:S(2)}, u32[]{:S(2)}) async-start(bf16[16,2,160,128]{3,2,1,0:T(8,128)(2,1)} %pool_rest.1), calls=%async_computation | async-start | bytes 2621440 | tf_op jit(solution)/shard_map/all_to_all | solution.py:473
  83.7 18.5 %collective-permute-start.16 = (bf16[2,160,128]{2,1,0:T(8,128)(2,1)S(1)}, bf16[2,160,128]{2,1,0:T(8,128)(2,1)S(1)}, u32[]{:S(2)}, u32[]{:S(2)}) collective-permute-start(bf16[2,160,128]{2,1,0:T(8,128)(2,1)S(1)} %get-tuple-element.81), channel_id=1, source_target_pairs={{0,32},{32,64},{64,96},{96,0},{1,33},{33,65},{65,97},{97,1},{2,34}... | collective-permute-start | bytes 245768 | tf_op jit(solution)/shard_map/ppermute | solution.py:399
  85.7 17.7 %collective-permute-start.17 = (bf16[2,160,128]{2,1,0:T(8,128)(2,1)S(1)}, bf16[2,160,128]{2,1,0:T(8,128)(2,1)S(1)}, u32[]{:S(2)}, u32[]{:S(2)}) collective-permute-start(bf16[2,160,128]{2,1,0:T(8,128)(2,1)S(1)} %get-tuple-element.80), channel_id=1, source_target_pairs={{0,64},{32,96},{64,0},{96,32},{1,65},{33,97},{65,1},{97,33},{2,66}... | collective-permute-start | bytes 245768 | tf_op jit(solution)/shard_map/ppermute | solution.py:399
  88.4 15.0 %collective-permute-start.18 = (bf16[2,160,128]{2,1,0:T(8,128)(2,1)S(1)}, bf16[2,160,128]{2,1,0:T(8,128)(2,1)S(1)}, u32[]{:S(2)}, u32[]{:S(2)}) collective-permute-start(bf16[2,160,128]{2,1,0:T(8,128)(2,1)S(1)} %get-tuple-element.79), channel_id=1, source_target_pairs={{0,96},{32,0},{64,32},{96,64},{1,97},{33,1},{65,33},{97,65},{2,98}... | collective-permute-start | bytes 245768 | tf_op jit(solution)/shard_map/ppermute | solution.py:399
  (6 other events, 99.5 us)
